TPU v7x, 32 devices: a whole 2x2x4 slice. The times are simulated.
32 devices in a mesh: samp: 8 (over y, x, core), feat: 4 (over z).
Axes of the slice: x: 2, y: 2, z: 4, core: 2. Of those that a mesh axis runs over, the one named last changes fastest.
Arguments:
- labels: int32 [131072], P('samp'), may hold values 0 or 1
- beta: float32 [262144], P('feat'), may hold values from -1.2 to 1.2
- tile_rows: int32 [8, 4, 64], P('samp', 'feat'), may hold values from 0 to 127, as said below
- tile_cols: int32 [8, 4, 64], P('samp', 'feat'), may hold values from 0 to 511, as said below
- tile_values: bfloat16 [8, 4, 64, 128, 128], P('samp', 'feat'), may hold values from -0.5 to 0.5
- block_order: int32 [4, 4], P('feat'), may hold values from 0 to 511, as said below
- hess_inv: float32 [4, 4, 128, 128], P('feat')
Outputs:
- beta_new: float32 [262144], P('feat')
- residual: float32 [131072], P(('samp', 'feat'))
Inputs may be any that keep to these rules, and one draw needn't show every extreme that they name: `tile_rows`: row block numbers within a samp index. `tile_cols`: feature block numbers within a feat index. Each row of block_order holds 4 distinct block numbers.
All inputs are finite; a program needn't handle non-finite values. No bound on the sum of `labels` on one device may be relied on, other than what follows from the above.
Results may differ from a plain program's by a relative error of at most 0.0025.
Values sent between devices are 32-bit elements; how exact they have to be, the bound alone decides.
No kernel may reach another device: no remote copies, remote signals or barrier semaphores. Data moves between devices by JAX's collectives and lax.ppermute only.
A program may use at most 64 MiB of HBM per device.

v0:
```python
import jax
import jax.numpy as jnp
from jax import lax
from jax.sharding import PartitionSpec as P

exact_prec = lax.Precision.HIGHEST
l1_penalty = 0.25


def from_behind(value, axis, steps):
    count = lax.axis_size(axis)
    pairs = [(source, (source + steps) % count) for source in range(count)]
    return lax.ppermute(value, axis, pairs)


def per_device(labels, beta, tile_rows, tile_cols, tile_values, block_order, hess_inv):
    cycle_size = lax.axis_size("feat")
    my_index = lax.axis_index("feat")
    row_ids = tile_rows[0, 0]
    col_ids = tile_cols[0, 0]
    values = tile_values[0, 0]
    tile_edge = values.shape[-1]
    row_blocks = labels.shape[0] // tile_edge
    group_blocks = row_blocks // cycle_size
    blocks = beta.reshape(-1, tile_edge)
    picked = jnp.take(blocks.astype(jnp.bfloat16), col_ids, axis=0)
    products = jnp.einsum("krc,kc->kr", values, picked, preferred_element_type=jnp.float32)
    placing = (row_ids[:, None] == jnp.arange(row_blocks, dtype=jnp.int32)[None, :]).astype(
        jnp.float32
    )
    partial_sum = jnp.dot(placing.T, products, precision=exact_prec)
    margins = lax.psum_scatter(partial_sum, "feat", scatter_dimension=0, tiled=True)
    probability = jax.nn.sigmoid(margins)
    weight = probability * (1.0 - probability)
    own_labels = lax.dynamic_slice_in_dim(
        labels.reshape(row_blocks, tile_edge), my_index * group_blocks, group_blocks, 0
    )
    residual = own_labels.astype(jnp.float32) - probability
    sub_ids = jnp.arange(group_blocks, dtype=jnp.int32)
    inverses = hess_inv[0]
    targets = block_order[0]

    def run_section(section_index, carry):
        blocks, residual, weight = carry
        group_index = (my_index - section_index) % cycle_size
        target = lax.dynamic_index_in_dim(targets, section_index, 0, keepdims=False)
        inverse = lax.dynamic_index_in_dim(inverses, section_index, 0, keepdims=False)
        offsets = row_ids - group_index * group_blocks
        matches = (col_ids == target) & (offsets >= 0) & (offsets < group_blocks)
        chosen = (offsets[:, None] == sub_ids[None, :]) & matches[:, None]
        rounded = residual.astype(jnp.bfloat16)
        resid_tiles = jnp.dot(
            chosen.astype(jnp.bfloat16), rounded, preferred_element_type=jnp.float32
        ).astype(jnp.bfloat16)
        local_grad = jnp.einsum(
            "krc,kr->c", values, resid_tiles, preferred_element_type=jnp.float32
        )
        gradient = lax.psum(local_grad, "samp")
        current = lax.dynamic_index_in_dim(blocks, target, 0, keepdims=False)
        moved_block = current + jnp.dot(inverse, gradient, precision=exact_prec)
        shrunk = jnp.sign(moved_block) * jnp.maximum(jnp.abs(moved_block) - l1_penalty, 0.0)
        change = (shrunk - current).astype(jnp.bfloat16)
        image_rows = jnp.einsum("krc,c->kr", values, change, preferred_element_type=jnp.float32)
        landed = jnp.dot(chosen.astype(jnp.float32).T, image_rows, precision=exact_prec)
        residual = residual - weight * landed
        blocks = lax.dynamic_update_index_in_dim(blocks, shrunk, target, 0)
        residual, weight = from_behind((residual, weight), "feat", 1)
        return (blocks, residual, weight)

    blocks, residual, weight = lax.fori_loop(0, cycle_size, run_section, (blocks, residual, weight))
    return (blocks.reshape(-1), residual.reshape(-1))


def solution(mesh):
    placed = (
        P("samp"),
        P("feat"),
        P("samp", "feat", None),
        P("samp", "feat", None),
        P("samp", "feat", None, None, None),
        P("feat", None),
        P("feat", None, None, None),
    )
    return jax.shard_map(
        per_device,
        mesh=mesh,
        in_specs=placed,
        out_specs=(P("feat"), P(("samp", "feat"))),
        check_vma=False,
    )
```

profile of v0, /device:TPU:0, one launch (start us, length us, event | category | flops | bytes accessed | tf_op | source)
XLA Modules:
  0.0 137.3 jit_solution(14995622747265725093)
XLA Ops:
  7.3 1.1 copy.34
  8.4 0.7 compare_and_fusion.1
  9.0 0.7 fusion.30
  9.7 0.6 gather_fusion
  10.4 2.8 %fusion.26 = f32[64,1,128]{2,1,0:T(1,128)S(1)} fusion(bf16[64,128,1]{1,0,2:T(8,128)(2,1)S(1)} %select_bitcast_fusion, bf16[1,1,64,128,128]{4,3,2,1,0:T(8,128)(2,1)} %param.13), kind=kOutput, calls=%fused_computation.29 | convolution fusion | flops 2097152 | bytes 2146304 | tf_op jit(solution)/shard_map/krc,kc->kr/dot_general | solution.py:27
  13.2 1.0 fusion.28
  14.2 21.9 %reduce-scatter.2.cloned.1.call-done = f32[32,128]{1,0:T(8,128)} async-done(((f32[128,128]{1,0:T(8,128)}), f32[32,128]{1,0:T(8,128)}) %reduce-scatter.2.cloned.1.call-update) | async-done | bytes 16400 | tf_op jit(solution)/shard_map/reduce_scatter | solution.py:32
  36.1 0.7 subtract_multiply_fusion
  36.8 93.0 %while.20 = (s32[]{:T(128)}, f32[512,128]{1,0:T(8,128)S(1)}, f32[32,128]{1,0:T(8,128)S(1)}, f32[32,128]{1,0:T(8,128)S(1)}, s32[4]{0:T(128)S(1)}, /*index=5*/f32[...) while((s32[]{:T(128)}, f32[512,128]{1,0:T(8,128)S(1)}, ...), condition=%wide.region_3.4_spmd.clone, body=%wide.region_1.3_spmd.clone.sunk | while | flops 8091154 | bytes 4595052 | solution.py:70
  36.9 0.6 dynamic_slice.60
  38.8 0.7 compare_and_fusion.3
  39.5 0.2 fusion.59
  39.7 0.4 convolution_bitcast_fusion.3
  40.1 11.8 %psum.16 = f32[128]{0:T(128)S(1)} all-reduce(f32[128]{0:T(128)S(1)} %convolution_bitcast_fusion.3), channel_id=1, replica_groups=mesh['samp'=8,'feat'=4] {'samp'}, use_global_device_ids=true, to_apply=%region_2.2 | all-reduce | flops 128 | bytes 1024 | tf_op jit(solution)/shard_map/while/body/eval_jaxpr/psum | solution.py:58
  52.6 1.0 maximum_multiply_fusion.2
  53.6 0.7 fusion.60
  54.3 0.3 fusion.61
  54.6 1.2 collective-permute-start
  55.8 4.4 %collective-permute-done = f32[32,128]{1,0:T(8,128)S(1)} collective-permute-done((f32[32,128]{1,0:T(8,128)S(1)}, f32[32,128]{1,0:T(8,128)S(1)}, u32[]{:S(2)}, u32[]{:S(2)}) %collective-permute-start) | collective-permute-done | bytes 16416 | tf_op jit(solution)/shard_map/while/body/eval_jaxpr/ppermute | solution.py:13
  60.2 0.6 dynamic_slice.60
  62.1 0.7 compare_and_fusion.3
  62.7 0.2 fusion.59
  62.9 0.4 convolution_bitcast_fusion.3
  63.3 11.8 %psum.16 = f32[128]{0:T(128)S(1)} all-reduce(f32[128]{0:T(128)S(1)} %convolution_bitcast_fusion.3), channel_id=1, replica_groups=mesh['samp'=8,'feat'=4] {'samp'}, use_global_device_ids=true, to_apply=%region_2.2 | all-reduce | flops 128 | bytes 1024 | tf_op jit(solution)/shard_map/while/body/eval_jaxpr/psum | solution.py:58
  75.8 1.0 maximum_multiply_fusion.2
  76.8 0.7 fusion.60
  77.5 0.3 fusion.61
  77.8 0.9 collective-permute-start
  78.7 4.7 %collective-permute-done = f32[32,128]{1,0:T(8,128)S(1)} collective-permute-done((f32[32,128]{1,0:T(8,128)S(1)}, f32[32,128]{1,0:T(8,128)S(1)}, u32[]{:S(2)}, u32[]{:S(2)}) %collective-permute-start) | collective-permute-done | bytes 16416 | tf_op jit(solution)/shard_map/while/body/eval_jaxpr/ppermute | solution.py:13
  83.4 0.6 dynamic_slice.60
  85.3 0.7 compare_and_fusion.3
  86.1 0.4 convolution_bitcast_fusion.3
  86.5 11.8 %psum.16 = f32[128]{0:T(128)S(1)} all-reduce(f32[128]{0:T(128)S(1)} %convolution_bitcast_fusion.3), channel_id=1, replica_groups=mesh['samp'=8,'feat'=4] {'samp'}, use_global_device_ids=true, to_apply=%region_2.2 | all-reduce | flops 128 | bytes 1024 | tf_op jit(solution)/shard_map/while/body/eval_jaxpr/psum | solution.py:58
  99.0 1.0 maximum_multiply_fusion.2
  100.0 0.7 fusion.60
  100.7 0.3 fusion.61
  101.0 1.4 collective-permute-start
  102.4 4.2 %collective-permute-done = f32[32,128]{1,0:T(8,128)S(1)} collective-permute-done((f32[32,128]{1,0:T(8,128)S(1)}, f32[32,128]{1,0:T(8,128)S(1)}, u32[]{:S(2)}, u32[]{:S(2)}) %collective-permute-start) | collective-permute-done | bytes 16416 | tf_op jit(solution)/shard_map/while/body/eval_jaxpr/ppermute | solution.py:13
  106.6 0.6 dynamic_slice.60
  108.5 0.7 compare_and_fusion.3
  109.3 0.4 convolution_bitcast_fusion.3
  109.7 11.8 %psum.16 = f32[128]{0:T(128)S(1)} all-reduce(f32[128]{0:T(128)S(1)} %convolution_bitcast_fusion.3), channel_id=1, replica_groups=mesh['samp'=8,'feat'=4] {'samp'}, use_global_device_ids=true, to_apply=%region_2.2 | all-reduce | flops 128 | bytes 1024 | tf_op jit(solution)/shard_map/while/body/eval_jaxpr/psum | solution.py:58
  122.2 1.0 maximum_multiply_fusion.2
  123.2 0.7 fusion.60
  123.9 0.3 fusion.61
  124.2 1.4 %collective-permute-start = (f32[32,128]{1,0:T(8,128)S(1)}, f32[32,128]{1,0:T(8,128)S(1)}, u32[]{:S(2)}, u32[]{:S(2)}) collective-permute-start(f32[32,128]{1,0:T(8,128)S(1)} %fusion.61), channel_id=1, source_target_pairs={{0,1},{1,2},{2,3},{3,0},{4,5},{5,6},{6,7},{7,4},{8,9},{9,10},{10,1... | collective-permute-start | bytes 49160 | tf_op jit(solution)/shard_map/while/body/eval_jaxpr/ppermute | solution.py:13
  125.6 4.2 %collective-permute-done = f32[32,128]{1,0:T(8,128)S(1)} collective-permute-done((f32[32,128]{1,0:T(8,128)S(1)}, f32[32,128]{1,0:T(8,128)S(1)}, u32[]{:S(2)}, u32[]{:S(2)}) %collective-permute-start) | collective-permute-done | bytes 16416 | tf_op jit(solution)/shard_map/while/body/eval_jaxpr/ppermute | solution.py:13
  129.8 0.6 copy.35
  (33 shorter events, 0.8 us)
Async XLA Ops:
  7.2 6.0 %copy-start.2 = (s32[1,1,64]{2,1,0:T(1,128)S(1)}, s32[1,1,64]{2,1,0:T(1,128)}, u32[]{:S(2)}) copy-start(s32[1,1,64]{2,1,0:T(1,128)} %param.11) | copy-start | bytes 772
  7.2 29.6 %copy-start.3 = (s32[1,1,64]{2,1,0:T(1,128)S(1)}, s32[1,1,64]{2,1,0:T(1,128)}, u32[]{:S(2)}) copy-start(s32[1,1,64]{2,1,0:T(1,128)} %param.12) | copy-start | bytes 772
  7.2 29.6 %copy-start = (bf16[1,1,64,128,128]{4,3,2,1,0:T(8,128)(2,1)S(1)}, bf16[1,1,64,128,128]{4,3,2,1,0:T(8,128)(2,1)}, u32[]{:S(2)}) copy-start(bf16[1,1,64,128,128]{4,3,2,1,0:T(8,128)(2,1)} %param.13) | copy-start | bytes 6291460
  7.2 29.6 %copy-start.4 = (s32[1,4]{1,0:T(1,128)S(1)}, s32[1,4]{1,0:T(1,128)}, u32[]{:S(2)}) copy-start(s32[1,4]{1,0:T(1,128)} %param.14) | copy-start | bytes 52
  7.2 28.8 %reduce-scatter.2.cloned.1.call-start = ((), (), s32[]{:S(2)}) async-start(), calls=%async_computation.1 | async-start | bytes 81920 | tf_op jit(solution)/shard_map/reduce_scatter | solution.py:32
  36.9 18.9 %collective-permute-start.1 = (f32[32,128]{1,0:T(8,128)S(1)}, f32[32,128]{1,0:T(8,128)S(1)}, u32[]{:S(2)}, u32[]{:S(2)}) collective-permute-start(f32[32,128]{1,0:T(8,128)S(1)} %copy.27), channel_id=1, source_target_pairs={{0,1},{1,2},{2,3},{3,0},{4,5},{5,6},{6,7},{7,4},{8,9},{9,10},{10,1... | collective-permute-start | bytes 49160 | tf_op jit(solution)/shard_map/while/body/eval_jaxpr/ppermute | solution.py:13
  54.6 5.6 %collective-permute-start = (f32[32,128]{1,0:T(8,128)S(1)}, f32[32,128]{1,0:T(8,128)S(1)}, u32[]{:S(2)}, u32[]{:S(2)}) collective-permute-start(f32[32,128]{1,0:T(8,128)S(1)} %fusion.61), channel_id=1, source_target_pairs={{0,1},{1,2},{2,3},{3,0},{4,5},{5,6},{6,7},{7,4},{8,9},{9,10},{10,1... | collective-permute-start | bytes 49160 | tf_op jit(solution)/shard_map/while/body/eval_jaxpr/ppermute | solution.py:13
  60.2 18.5 %collective-permute-start.1 = (f32[32,128]{1,0:T(8,128)S(1)}, f32[32,128]{1,0:T(8,128)S(1)}, u32[]{:S(2)}, u32[]{:S(2)}) collective-permute-start(f32[32,128]{1,0:T(8,128)S(1)} %copy.27), channel_id=1, source_target_pairs={{0,1},{1,2},{2,3},{3,0},{4,5},{5,6},{6,7},{7,4},{8,9},{9,10},{10,1... | collective-permute-start | bytes 49160 | tf_op jit(solution)/shard_map/while/body/eval_jaxpr/ppermute | solution.py:13
  77.8 5.6 %collective-permute-start = (f32[32,128]{1,0:T(8,128)S(1)}, f32[32,128]{1,0:T(8,128)S(1)}, u32[]{:S(2)}, u32[]{:S(2)}) collective-permute-start(f32[32,128]{1,0:T(8,128)S(1)} %fusion.61), channel_id=1, source_target_pairs={{0,1},{1,2},{2,3},{3,0},{4,5},{5,6},{6,7},{7,4},{8,9},{9,10},{10,1... | collective-permute-start | bytes 49160 | tf_op jit(solution)/shard_map/while/body/eval_jaxpr/ppermute | solution.py:13
  83.4 19.0 %collective-permute-start.1 = (f32[32,128]{1,0:T(8,128)S(1)}, f32[32,128]{1,0:T(8,128)S(1)}, u32[]{:S(2)}, u32[]{:S(2)}) collective-permute-start(f32[32,128]{1,0:T(8,128)S(1)} %copy.27), channel_id=1, source_target_pairs={{0,1},{1,2},{2,3},{3,0},{4,5},{5,6},{6,7},{7,4},{8,9},{9,10},{10,1... | collective-permute-start | bytes 49160 | tf_op jit(solution)/shard_map/while/body/eval_jaxpr/ppermute | solution.py:13
  101.0 5.6 %collective-permute-start = (f32[32,128]{1,0:T(8,128)S(1)}, f32[32,128]{1,0:T(8,128)S(1)}, u32[]{:S(2)}, u32[]{:S(2)}) collective-permute-start(f32[32,128]{1,0:T(8,128)S(1)} %fusion.61), channel_id=1, source_target_pairs={{0,1},{1,2},{2,3},{3,0},{4,5},{5,6},{6,7},{7,4},{8,9},{9,10},{10,1... | collective-permute-start | bytes 49160 | tf_op jit(solution)/shard_map/while/body/eval_jaxpr/ppermute | solution.py:13
  106.6 19.0 %collective-permute-start.1 = (f32[32,128]{1,0:T(8,128)S(1)}, f32[32,128]{1,0:T(8,128)S(1)}, u32[]{:S(2)}, u32[]{:S(2)}) collective-permute-start(f32[32,128]{1,0:T(8,128)S(1)} %copy.27), channel_id=1, source_target_pairs={{0,1},{1,2},{2,3},{3,0},{4,5},{5,6},{6,7},{7,4},{8,9},{9,10},{10,1... | collective-permute-start | bytes 49160 | tf_op jit(solution)/shard_map/while/body/eval_jaxpr/ppermute | solution.py:13
  124.2 5.6 %collective-permute-start = (f32[32,128]{1,0:T(8,128)S(1)}, f32[32,128]{1,0:T(8,128)S(1)}, u32[]{:S(2)}, u32[]{:S(2)}) collective-permute-start(f32[32,128]{1,0:T(8,128)S(1)} %fusion.61), channel_id=1, source_target_pairs={{0,1},{1,2},{2,3},{3,0},{4,5},{5,6},{6,7},{7,4},{8,9},{9,10},{10,1... | collective-permute-start | bytes 49160 | tf_op jit(solution)/shard_map/while/body/eval_jaxpr/ppermute | solution.py:13
  129.8 0.7 copy-start.1
Sparse Core Ops, SparseCore 0:
  14.3 21.6 reduce-scatter.1
where the time goes:
time: 138 us; the launch traced here: 137 us
  blocking collectives  47.2 us (34%)
  waiting for transfers between devices  39.3 us (28%)
  matrix products  14.1 us (10%)
  between operations  14.1 us (10%)
  loops' own time  7.97 us (6%)
  local copies, waits for them, and re-layouts  4.92 us (4%)
  starting transfers between devices  4.89 us (4%)
  other arithmetic  4.78 us (3%)
    psum x4, blocking collectives, run_section(): gradient = lax.psum(local_grad, 'samp')  47.2 us
    reduce_scatter x1, waiting for transfers between devices, per_device(): lax.psum_scatter(partial_sum, 'feat', scatter_dimension=0, tiled=True)  21.9 us
    ppermute x8, waiting for transfers between devices, from_behind(): return lax.ppermute(value, axis, pairs)  17.5 us
    another operation x1, loops' own time, per_device(): lax.fori_loop(0, cycle_size, run_section, (blocks, residual, weight))  7.97 us
    ppermute x8, starting transfers between devices, from_behind(): return lax.ppermute(value, axis, pairs)  4.86 us
    dot_general x4, matrix products, run_section(): moved_block = current + jnp.dot(inverse, gradient, precision=exact_prec)  4.12 us
  transfers between devices with their start and end apart: 9, of which 5 were waited for; matrix products, arithmetic and copies ran while one was open for 11% of the time, Pallas kernels for 0%

commit v1 on v0

v1 whole, which is shorter than its diff:
```python
import jax
import jax.numpy as jnp
from jax import lax
from jax.sharding import PartitionSpec as P

exact_prec = lax.Precision.HIGHEST
l1_penalty = 0.25


def from_behind(value, axis, steps):
    count = lax.axis_size(axis)
    pairs = [(source, (source + steps) % count) for source in range(count)]
    return lax.ppermute(value, axis, pairs)


def exchange(parts, axis):
    return lax.all_to_all(parts, axis, 0, 0)


def per_device(labels, beta, tile_rows, tile_cols, tile_values, block_order, hess_inv):
    cycle_size = lax.axis_size("feat")
    samp_count = lax.axis_size("samp")
    my_index = lax.axis_index("feat")
    row_ids = tile_rows[0, 0]
    col_ids = tile_cols[0, 0]
    values = tile_values[0, 0]
    tile_edge = values.shape[-1]
    row_blocks = labels.shape[0] // tile_edge
    group_blocks = row_blocks // cycle_size
    blocks = beta.reshape(-1, tile_edge)
    picked = jnp.take(blocks, col_ids, axis=0, mode="clip").astype(jnp.bfloat16)
    products = jnp.einsum("krc,kc->kr", values, picked, preferred_element_type=jnp.float32)
    placing = (row_ids[:, None] == jnp.arange(row_blocks, dtype=jnp.int32)[None, :]).astype(
        jnp.float32
    )
    partial_sum = jnp.dot(placing.T, products, precision=exact_prec)
    parts = exchange(partial_sum.reshape(cycle_size, group_blocks, tile_edge), "feat")
    margins = jnp.sum(parts, axis=0)
    probability = jax.nn.sigmoid(margins)
    weight = probability * (1.0 - probability)
    own_labels = lax.dynamic_slice_in_dim(
        labels.reshape(row_blocks, tile_edge), my_index * group_blocks, group_blocks, 0
    )
    residual = own_labels.astype(jnp.float32) - probability
    sub_ids = jnp.arange(group_blocks, dtype=jnp.int32)
    inverses = hess_inv[0]
    targets = block_order[0]
    old_blocks = jnp.take(blocks, targets, axis=0, mode="clip")
    state = jnp.stack([residual, weight])
    for section in range(cycle_size):
        group_index = (my_index - section) % cycle_size
        target = targets[section]
        offsets = row_ids - group_index * group_blocks
        matches = (col_ids == target) & (offsets >= 0) & (offsets < group_blocks)
        chosen = (offsets[:, None] == sub_ids[None, :]) & matches[:, None]
        residual, weight = state[0], state[1]
        rounded = residual.astype(jnp.bfloat16)
        resid_tiles = jnp.dot(
            chosen.astype(jnp.bfloat16), rounded, preferred_element_type=jnp.float32
        ).astype(jnp.bfloat16)
        local_grad = jnp.einsum(
            "krc,kr->c", values, resid_tiles, preferred_element_type=jnp.float32
        )
        spread = jnp.broadcast_to(local_grad[None], (samp_count, tile_edge))
        gradient = jnp.sum(exchange(spread, "samp"), axis=0)
        current = old_blocks[section]
        moved_block = current + jnp.dot(inverses[section], gradient, precision=exact_prec)
        shrunk = jnp.sign(moved_block) * jnp.maximum(jnp.abs(moved_block) - l1_penalty, 0.0)
        change = (shrunk - current).astype(jnp.bfloat16)
        image_rows = jnp.einsum("krc,c->kr", values, change, preferred_element_type=jnp.float32)
        landed = jnp.dot(chosen.astype(jnp.float32).T, image_rows, precision=exact_prec)
        residual = residual - weight * landed
        blocks = lax.dynamic_update_index_in_dim(blocks, shrunk, target, 0)
        if section + 1 < cycle_size:
            state = from_behind(jnp.stack([residual, weight]), "feat", 1)
        else:
            residual = from_behind(residual, "feat", 1)
    return (blocks.reshape(-1), residual.reshape(-1))


def solution(mesh):
    placed = (
        P("samp"),
        P("feat"),
        P("samp", "feat", None),
        P("samp", "feat", None),
        P("samp", "feat", None, None, None),
        P("feat", None),
        P("feat", None, None, None),
    )
    return jax.shard_map(
        per_device,
        mesh=mesh,
        in_specs=placed,
        out_specs=(P("feat"), P(("samp", "feat"))),
        check_vma=False,
    )
```

time: 138 us -> 83.8 us (0.61)
  blocking collectives: 47.2 us -> 7.03 us
  starting transfers between devices: 4.89 us -> 17.8 us
  loops' own time: 7.97 us -> 0 us
  waiting for transfers between devices: 39.3 us -> 31.7 us
  between operations: 14.1 us -> 8.53 us
  matrix products: 14.1 us -> 9.14 us
  other arithmetic: 4.78 us -> 3.33 us
    psum x4 -> x0, blocking collectives: 47.2 us -> none  [run_section(): gradient = lax.psum(local_grad, 'samp')]
    reduce_scatter x1 -> x0, waiting for transfers between devices: 21.9 us -> none  [per_device(): lax.psum_scatter(partial_sum, 'feat', scatter_dimension=0, tiled=True)]
    all_to_all x0 -> x4, starting transfers between devices: none -> 16.7 us  [exchange(): return lax.all_to_all(parts, axis, 0, 0)]
    all_to_all x0 -> x4, waiting for transfers between devices: none -> 15.5 us  [exchange(): return lax.all_to_all(parts, axis, 0, 0)]
    another operation x1 -> x0, loops' own time: 7.97 us -> none  [per_device(): lax.fori_loop(0, cycle_size, run_section, (blocks, residual, weight))]
    all_to_all x0 -> x1, blocking collectives: none -> 7.03 us  [exchange(): return lax.all_to_all(parts, axis, 0, 0)]
    ppermute x8 -> x4, starting transfers between devices: 4.86 us -> 1.14 us  [from_behind(): return lax.ppermute(value, axis, pairs)]
    dot_general x20, matrix products: 10.4 us -> 7 us  [the longest x4 2.75 us: per_device(): jnp.einsum('krc,c->kr', values, change, preferred_element_type=jnp.float32)]
  transfers between devices with their start and end apart: 9 -> 8, of which waited for: 5 -> 7; matrix products, arithmetic and copies ran while one was open for 11% -> 5% of each run, Pallas kernels for 0% -> 0%
where the time goes in v1:
time: 83.8 us; the launch traced here: 83.2 us
  waiting for transfers between devices  31.7 us (38%)
  starting transfers between devices  17.8 us (21%)
  matrix products  9.14 us (11%)
  between operations  8.53 us (10%)
  blocking collectives  7.03 us (8%)
  local copies, waits for them, and re-layouts  5.68 us (7%)
  other arithmetic  3.33 us (4%)
    all_to_all x4, starting transfers between devices, exchange(): return lax.all_to_all(parts, axis, 0, 0)  16.7 us
    ppermute x4, waiting for transfers between devices, from_behind(): return lax.ppermute(value, axis, pairs)  16.2 us
    all_to_all x4, waiting for transfers between devices, exchange(): return lax.all_to_all(parts, axis, 0, 0)  15.5 us
    all_to_all x1, blocking collectives, exchange(): return lax.all_to_all(parts, axis, 0, 0)  7.03 us
    dot_general x4, matrix products, per_device(): jnp.einsum('krc,c->kr', values, change, preferred_element_type=jnp.float32)  2.75 us
    and x1, other arithmetic, per_device(): matches = (col_ids == target) & (offsets >= 0) & (offsets < group_blocks)  2.56 us
    broadcast_in_dim x4, local copies, waits for them, and re-layouts, per_device(): spread = jnp.broadcast_to(local_grad[None], (samp_count, tile_edge))  1.85 us
    unnamed x16, local copies, waits for them, and re-layouts  1.85 us
  transfers between devices with their start and end apart: 8, of which 7 were waited for; matrix products, arithmetic and copies ran while one was open for 5% of the time, Pallas kernels for 0%

profile of v1, /device:TPU:0, one launch (start us, length us, event | category | flops | bytes accessed | tf_op | source)
XLA Modules:
  0.0 83.2 jit_solution(15895826549924265611)
XLA Ops:
  0.7 1.1 %copy.39 = f32[65536]{0:T(1024)S(1)} copy(f32[65536]{0:T(1024)} %param.8) | data formatting | bytes 524288
  1.8 0.7 pad_clamp_fusion
  2.5 0.6 gather_fusion.1
  3.1 1.2 %fusion.16 = f32[64,1,128]{2,1,0:T(1,128)S(1)} fusion(bf16[1,1,64,128,128]{4,3,2,1,0:T(8,128)(2,1)S(1)} %copy-done, bf16[64,128,1]{1,0,2:T(8,128)(2,1)S(1)} %bitcast.272), kind=kOutput, calls=%fused_computation.18 | convolution fusion | flops 2097152 | bytes 2146304 | tf_op jit(solution)/shard_map/krc,kc->kr/dot_general | solution.py:32
  4.3 1.0 %fusion.56 = f32[128,128]{1,0:T(8,128)} fusion(f32[64,128]{1,0:T(8,128)S(1)} %bitcast.273, s32[64]{0:T(128)S(1)} %bitcast.288), kind=kOutput, calls=%fused_computation.65 | convolution fusion | flops 12591104 | bytes 98560 | tf_op jit(solution)/shard_map/dot_general | solution.py:36
  5.2 6.3 %all-to-all-start = ((f32[4,32,128]{2,1,0:T(8,128)}), f32[4,32,128]{2,1,0:T(8,128)S(1)}, u32[]{:S(2)}, u32[]{:S(2)}) async-start(f32[4,32,128]{2,1,0:T(8,128)} %bitcast.12), calls=%async_computation | async-start | bytes 131072 | tf_op jit(solution)/shard_map/all_to_all | solution.py:17
  11.6 0.7 fusion.147
  12.2 2.6 %fusion.106 = (pred[64]{0:T(512)(128)(4,1)S(1)}, s32[64]{0:T(128)S(1)}, pred[64]{0:T(512)(128)(4,1)S(1)}, s32[64]{0:T(128)S(1)}, pred[64]{0:T(512)(128)(4,1)S(1)...) fusion(s32[1,1,64]{2,1,0:T(1,128)S(1)} %copy-done.5, s32[]{:T(128)} %bitcast.53, s32[]{:T(128)S(6)} %mul.62, ...), kind=kLoop, calls=%fused_computation.113 | loop fusion | flops 1536 | bytes 1824 | tf_op jit(solution)/shard_map/and | solution.py:54
  14.8 0.6 gather_fusion
  15.4 1.9 %all-to-all-done = f32[4,32,128]{2,1,0:T(8,128)S(1)} async-done(((f32[4,32,128]{2,1,0:T(8,128)}), f32[4,32,128]{2,1,0:T(8,128)S(1)}, u32[]{:S(2)}, u32[]{:S(2)}) %all-to-all-start) | async-done | bytes 65568 | tf_op jit(solution)/shard_map/all_to_all | solution.py:17
  17.3 0.2 fusion.18
  17.5 0.4 fusion.28
  17.9 0.6 broadcast_in_dim.28
  18.5 3.7 %all-to-all-start.1 = ((f32[8,1,128]{2,1,0:T(1,128)}), f32[8,1,128]{2,1,0:T(1,128)S(1)}, u32[]{:S(2)}, u32[]{:S(2)}) async-start(f32[8,1,128]{2,1,0:T(1,128)} %broadcast_in_dim.28), calls=%async_computation.1 | async-start | bytes 8192 | tf_op jit(solution)/shard_map/all_to_all | solution.py:17
  22.3 4.6 %all-to-all-done.1 = f32[8,1,128]{2,1,0:T(1,128)S(1)} async-done(((f32[8,1,128]{2,1,0:T(1,128)}), f32[8,1,128]{2,1,0:T(1,128)S(1)}, u32[]{:S(2)}, u32[]{:S(2)}) %all-to-all-start.1) | async-done | bytes 4128 | tf_op jit(solution)/shard_map/all_to_all | solution.py:17
  26.9 0.2 maximum_multiply_fusion.3
  27.0 0.7 fusion.12
  27.7 0.3 fusion.23
  28.0 1.0 %collective-permute-start = (f32[2,32,128]{2,1,0:T(8,128)S(1)}, f32[2,32,128]{2,1,0:T(8,128)S(1)}, u32[]{:S(2)}, u32[]{:S(2)}) collective-permute-start(f32[2,32,128]{2,1,0:T(8,128)S(1)} %pad_maximum_fusion), channel_id=1, source_target_pairs={{0,1},{1,2},{2,3},{3,0},{4,5},{5,6},{6,7},{7,4},{8,9},{9,10},{10,1... | collective-permute-start | bytes 98312 | tf_op jit(solution)/shard_map/ppermute | solution.py:13
  29.0 4.8 %collective-permute-done = f32[2,32,128]{2,1,0:T(8,128)S(1)} collective-permute-done((f32[2,32,128]{2,1,0:T(8,128)S(1)}, f32[2,32,128]{2,1,0:T(8,128)S(1)}, u32[]{:S(2)}, u32[]{:S(2)}) %collective-permute-start) | collective-permute-done | bytes 32800 | tf_op jit(solution)/shard_map/ppermute | solution.py:13
  33.8 0.2 fusion.19
  34.0 0.4 fusion.31
  34.4 0.6 broadcast_in_dim.30
  35.0 3.3 %all-to-all-start.2 = ((f32[8,1,128]{2,1,0:T(1,128)}), f32[8,1,128]{2,1,0:T(1,128)S(1)}, u32[]{:S(2)}, u32[]{:S(2)}) async-start(f32[8,1,128]{2,1,0:T(1,128)} %broadcast_in_dim.30), calls=%async_computation.2 | async-start | bytes 8192 | tf_op jit(solution)/shard_map/all_to_all | solution.py:17
  38.3 4.5 %all-to-all-done.2 = f32[8,1,128]{2,1,0:T(1,128)S(1)} async-done(((f32[8,1,128]{2,1,0:T(1,128)}), f32[8,1,128]{2,1,0:T(1,128)S(1)}, u32[]{:S(2)}, u32[]{:S(2)}) %all-to-all-start.2) | async-done | bytes 4128 | tf_op jit(solution)/shard_map/all_to_all | solution.py:17
  42.9 0.2 maximum_multiply_fusion.2
  43.0 0.7 fusion.8
  43.7 0.3 fusion.74
  44.0 0.1 collective-permute-start.1
  44.1 5.7 %collective-permute-done.1 = f32[2,32,128]{2,1,0:T(8,128)S(1)} collective-permute-done((f32[2,32,128]{2,1,0:T(8,128)S(1)}, f32[2,32,128]{2,1,0:T(8,128)S(1)}, u32[]{:S(2)}, u32[]{:S(2)}) %collective-permute-start.1) | collective-permute-done | bytes 32800 | tf_op jit(solution)/shard_map/ppermute | solution.py:13
  49.8 0.2 fusion.20
  50.0 0.4 fusion.34
  50.4 0.6 broadcast_in_dim.32
  51.0 3.3 %all-to-all-start.3 = ((f32[8,1,128]{2,1,0:T(1,128)}), f32[8,1,128]{2,1,0:T(1,128)S(1)}, u32[]{:S(2)}, u32[]{:S(2)}) async-start(f32[8,1,128]{2,1,0:T(1,128)} %broadcast_in_dim.32), calls=%async_computation.3 | async-start | bytes 8192 | tf_op jit(solution)/shard_map/all_to_all | solution.py:17
  54.3 4.5 %all-to-all-done.3 = f32[8,1,128]{2,1,0:T(1,128)S(1)} async-done(((f32[8,1,128]{2,1,0:T(1,128)}), f32[8,1,128]{2,1,0:T(1,128)S(1)}, u32[]{:S(2)}, u32[]{:S(2)}) %all-to-all-start.3) | async-done | bytes 4128 | tf_op jit(solution)/shard_map/all_to_all | solution.py:17
  58.9 0.2 maximum_multiply_fusion.1
  59.0 0.7 fusion.4
  59.7 0.3 fusion.72
  60.0 0.1 collective-permute-start.2
  60.1 5.7 %collective-permute-done.2 = f32[2,32,128]{2,1,0:T(8,128)S(1)} collective-permute-done((f32[2,32,128]{2,1,0:T(8,128)S(1)}, f32[2,32,128]{2,1,0:T(8,128)S(1)}, u32[]{:S(2)}, u32[]{:S(2)}) %collective-permute-start.2) | collective-permute-done | bytes 32800 | tf_op jit(solution)/shard_map/ppermute | solution.py:13
  65.8 0.2 fusion.21
  66.0 0.4 fusion.37
  66.4 7.0 %all_to_all.29 = f32[8,1,128]{2,1,0:T(1,128)S(1)} all-to-all(f32[8,1,128]{2,1,0:T(1,128)S(1)} %broadcast_in_dim.34), channel_id=1, replica_groups=mesh['samp'=8,'feat'=4] {'samp'}, dimensions={0} | all-to-all | bytes 8192 | tf_op jit(solution)/shard_map/all_to_all | solution.py:17
  73.4 0.2 maximum_multiply_fusion
  73.6 0.7 fusion
  74.3 0.3 fusion.70
  74.6 0.1 collective-permute-start.3
  82.5 0.7 copy.40
  (32 shorter events, 0.3 us)
Async XLA Ops:
  0.6 2.4 %copy-start = (bf16[1,1,64,128,128]{4,3,2,1,0:T(8,128)(2,1)S(1)}, bf16[1,1,64,128,128]{4,3,2,1,0:T(8,128)(2,1)}, u32[]{:S(2)}) copy-start(bf16[1,1,64,128,128]{4,3,2,1,0:T(8,128)(2,1)} %param.11) | copy-start | bytes 6291460
  0.6 16.7 %copy-start.6 = (s32[16384]{0:T(1024)S(1)}, s32[16384]{0:T(1024)}, u32[]{:S(2)}) copy-start(s32[16384]{0:T(1024)} %param.7) | copy-start | bytes 196612
  0.7 3.6 %copy-start.4 = (s32[1,1,64]{2,1,0:T(1,128)S(1)}, s32[1,1,64]{2,1,0:T(1,128)}, u32[]{:S(2)}) copy-start(s32[1,1,64]{2,1,0:T(1,128)} %param.9) | copy-start | bytes 772
  0.7 11.6 %copy-start.5 = (s32[1,1,64]{2,1,0:T(1,128)S(1)}, s32[1,1,64]{2,1,0:T(1,128)}, u32[]{:S(2)}) copy-start(s32[1,1,64]{2,1,0:T(1,128)} %param.10) | copy-start | bytes 772
  0.7 10.9 %copy-start.3 = (s32[1,4]{1,0:T(1,128)S(1)}, s32[1,4]{1,0:T(1,128)}, u32[]{:S(2)}) copy-start(s32[1,4]{1,0:T(1,128)} %param.12) | copy-start | bytes 52
  3.1 23.8 %copy-start.2 = (f32[1,4,128,128]{3,2,1,0:T(8,128)S(1)}, f32[1,4,128,128]{3,2,1,0:T(8,128)}, u32[]{:S(2)}) copy-start(f32[1,4,128,128]{3,2,1,0:T(8,128)} %param.13) | copy-start | bytes 786436
  5.2 12.1 %all-to-all-start = ((f32[4,32,128]{2,1,0:T(8,128)}), f32[4,32,128]{2,1,0:T(8,128)S(1)}, u32[]{:S(2)}, u32[]{:S(2)}) async-start(f32[4,32,128]{2,1,0:T(8,128)} %bitcast.12), calls=%async_computation | async-start | bytes 131072 | tf_op jit(solution)/shard_map/all_to_all | solution.py:17
  18.5 8.3 %all-to-all-start.1 = ((f32[8,1,128]{2,1,0:T(1,128)}), f32[8,1,128]{2,1,0:T(1,128)S(1)}, u32[]{:S(2)}, u32[]{:S(2)}) async-start(f32[8,1,128]{2,1,0:T(1,128)} %broadcast_in_dim.28), calls=%async_computation.1 | async-start | bytes 8192 | tf_op jit(solution)/shard_map/all_to_all | solution.py:17
  28.0 5.8 %collective-permute-start = (f32[2,32,128]{2,1,0:T(8,128)S(1)}, f32[2,32,128]{2,1,0:T(8,128)S(1)}, u32[]{:S(2)}, u32[]{:S(2)}) collective-permute-start(f32[2,32,128]{2,1,0:T(8,128)S(1)} %pad_maximum_fusion), channel_id=1, source_target_pairs={{0,1},{1,2},{2,3},{3,0},{4,5},{5,6},{6,7},{7,4},{8,9},{9,10},{10,1... | collective-permute-start | bytes 98312 | tf_op jit(solution)/shard_map/ppermute | solution.py:13
  35.0 7.8 %all-to-all-start.2 = ((f32[8,1,128]{2,1,0:T(1,128)}), f32[8,1,128]{2,1,0:T(1,128)S(1)}, u32[]{:S(2)}, u32[]{:S(2)}) async-start(f32[8,1,128]{2,1,0:T(1,128)} %broadcast_in_dim.30), calls=%async_computation.2 | async-start | bytes 8192 | tf_op jit(solution)/shard_map/all_to_all | solution.py:17
  44.0 5.8 %collective-permute-start.1 = (f32[2,32,128]{2,1,0:T(8,128)S(1)}, f32[2,32,128]{2,1,0:T(8,128)S(1)}, u32[]{:S(2)}, u32[]{:S(2)}) collective-permute-start(f32[2,32,128]{2,1,0:T(8,128)S(1)} %pad_maximum_fusion.1), channel_id=1, source_target_pairs={{0,1},{1,2},{2,3},{3,0},{4,5},{5,6},{6,7},{7,4},{8,9},{9,10},{10,1... | collective-permute-start | bytes 98312 | tf_op jit(solution)/shard_map/ppermute | solution.py:13
  51.0 7.8 %all-to-all-start.3 = ((f32[8,1,128]{2,1,0:T(1,128)}), f32[8,1,128]{2,1,0:T(1,128)S(1)}, u32[]{:S(2)}, u32[]{:S(2)}) async-start(f32[8,1,128]{2,1,0:T(1,128)} %broadcast_in_dim.32), calls=%async_computation.3 | async-start | bytes 8192 | tf_op jit(solution)/shard_map/all_to_all | solution.py:17
  60.0 5.8 %collective-permute-start.2 = (f32[2,32,128]{2,1,0:T(8,128)S(1)}, f32[2,32,128]{2,1,0:T(8,128)S(1)}, u32[]{:S(2)}, u32[]{:S(2)}) collective-permute-start(f32[2,32,128]{2,1,0:T(8,128)S(1)} %pad_maximum_fusion.2), channel_id=1, source_target_pairs={{0,1},{1,2},{2,3},{3,0},{4,5},{5,6},{6,7},{7,4},{8,9},{9,10},{10,1... | collective-permute-start | bytes 98312 | tf_op jit(solution)/shard_map/ppermute | solution.py:13
  74.6 7.9 %collective-permute-start.3 = (f32[32,128]{1,0:T(8,128)S(1)}, f32[32,128]{1,0:T(8,128)S(1)}, u32[]{:S(2)}, u32[]{:S(2)}) collective-permute-start(f32[32,128]{1,0:T(8,128)S(1)} %fusion.70), channel_id=1, source_target_pairs={{0,1},{1,2},{2,3},{3,0},{4,5},{5,6},{6,7},{7,4},{8,9},{9,10},{10,1... | collective-permute-start | bytes 49160 | tf_op jit(solution)/shard_map/ppermute | solution.py:13
  82.5 0.7 copy-start.1

commit v2 on v1

--- a/solution.py
+++ b/solution.py
@@ -17,9 +17,20 @@
     return lax.all_to_all(parts, axis, 0, 0)
 
 
+def summed(value, axis):
+    count = lax.axis_size(axis)
+    if count & (count - 1):
+        return lax.psum(value, axis)
+    distance = 1
+    while distance < count:
+        pairs = [(source, source ^ distance) for source in range(count)]
+        value = value + lax.ppermute(value, axis, pairs)
+        distance *= 2
+    return value
+
+
 def per_device(labels, beta, tile_rows, tile_cols, tile_values, block_order, hess_inv):
     cycle_size = lax.axis_size("feat")
-    samp_count = lax.axis_size("samp")
     my_index = lax.axis_index("feat")
     row_ids = tile_rows[0, 0]
     col_ids = tile_cols[0, 0]
@@ -61,8 +72,7 @@
         local_grad = jnp.einsum(
             "krc,kr->c", values, resid_tiles, preferred_element_type=jnp.float32
         )
-        spread = jnp.broadcast_to(local_grad[None], (samp_count, tile_edge))
-        gradient = jnp.sum(exchange(spread, "samp"), axis=0)
+        gradient = summed(local_grad, "samp")
         current = old_blocks[section]
         moved_block = current + jnp.dot(inverses[section], gradient, precision=exact_prec)
         shrunk = jnp.sign(moved_block) * jnp.maximum(jnp.abs(moved_block) - l1_penalty, 0.0)

time: 83.8 us -> 83.7 us (level)
  waiting for transfers between devices: 31.7 us -> 38.8 us
  blocking collectives: 7.03 us -> 0 us
  starting transfers between devices: 17.8 us -> 19.8 us
  local copies, waits for them, and re-layouts: 5.68 us -> 3.82 us
    ppermute x0 -> x12, waiting for transfers between devices: none -> 20.1 us  [summed(): value = value + lax.ppermute(value, axis, pairs)]
    all_to_all x4 -> x1, waiting for transfers between devices: 15.5 us -> 2.53 us  [exchange(): return lax.all_to_all(parts, axis, 0, 0)]
    ppermute x0 -> x12, starting transfers between devices: none -> 12.3 us  [summed(): value = value + lax.ppermute(value, axis, pairs)]
    all_to_all x4 -> x1, starting transfers between devices: 16.7 us -> 6.32 us  [exchange(): return lax.all_to_all(parts, axis, 0, 0)]
    all_to_all x1 -> x0, blocking collectives: 7.03 us -> none  [exchange(): return lax.all_to_all(parts, axis, 0, 0)]
    broadcast_in_dim x4 -> x0, local copies, waits for them, and re-layouts: 1.85 us -> none  [per_device(): spread = jnp.broadcast_to(local_grad[None], (samp_count, tile_edge))]
  transfers between devices with their start and end apart: 8 -> 17, of which waited for: 7 -> 16; matrix products, arithmetic and copies ran while one was open for 5% -> 5% of each run, Pallas kernels for 0% -> 0%
where the time goes in v2:
time: 83.7 us; the launch traced here: 83.3 us
  waiting for transfers between devices  38.8 us (46%)
  starting transfers between devices  19.8 us (24%)
  matrix products  9.15 us (11%)
  between operations  8.45 us (10%)
  local copies, waits for them, and re-layouts  3.82 us (5%)
  other arithmetic  3.26 us (4%)
    ppermute x12, waiting for transfers between devices, summed(): value = value + lax.ppermute(value, axis, pairs)  20.1 us
    ppermute x4, waiting for transfers between devices, from_behind(): return lax.ppermute(value, axis, pairs)  16.2 us
    ppermute x12, starting transfers between devices, summed(): value = value + lax.ppermute(value, axis, pairs)  12.3 us
    all_to_all x1, starting transfers between devices, exchange(): return lax.all_to_all(parts, axis, 0, 0)  6.32 us
    dot_general x4, matrix products, per_device(): jnp.einsum('krc,c->kr', values, change, preferred_element_type=jnp.float32)  2.75 us
    and x1, other arithmetic, per_device(): matches = (col_ids == target) & (offsets >= 0) & (offsets < group_blocks)  2.54 us
    all_to_all x1, waiting for transfers between devices, exchange(): return lax.all_to_all(parts, axis, 0, 0)  2.53 us
    unnamed x16, local copies, waits for them, and re-layouts  1.85 us
  transfers between devices with their start and end apart: 17, of which 16 were waited for; matrix products, arithmetic and copies ran while one was open for 5% of the time, Pallas kernels for 0%

profile of v2, /device:TPU:0, one launch (start us, length us, event | category | flops | bytes accessed | tf_op | source)
XLA Modules:
  0.0 83.3 jit_solution(15126217747652609875)
XLA Ops:
  0.7 1.1 %copy.35 = f32[65536]{0:T(1024)S(1)} copy(f32[65536]{0:T(1024)} %param.8) | data formatting | bytes 524288
  1.8 0.7 pad_clamp_fusion
  2.5 0.6 gather_fusion.1
  3.1 1.2 %fusion.16 = f32[64,1,128]{2,1,0:T(1,128)S(1)} fusion(bf16[1,1,64,128,128]{4,3,2,1,0:T(8,128)(2,1)S(1)} %copy-done, bf16[64,128,1]{1,0,2:T(8,128)(2,1)S(1)} %bitcast.268), kind=kOutput, calls=%fused_computation.18 | convolution fusion | flops 2097152 | bytes 2146304 | tf_op jit(solution)/shard_map/krc,kc->kr/dot_general | solution.py:43
  4.3 1.0 %fusion.56 = f32[128,128]{1,0:T(8,128)} fusion(f32[64,128]{1,0:T(8,128)S(1)} %bitcast.269, s32[64]{0:T(128)S(1)} %bitcast.280), kind=kOutput, calls=%fused_computation.65 | convolution fusion | flops 12591104 | bytes 98560 | tf_op jit(solution)/shard_map/dot_general | solution.py:47
  5.2 6.3 %all-to-all-start = ((f32[4,32,128]{2,1,0:T(8,128)}), f32[4,32,128]{2,1,0:T(8,128)S(1)}, u32[]{:S(2)}, u32[]{:S(2)}) async-start(f32[4,32,128]{2,1,0:T(8,128)} %bitcast.12), calls=%async_computation | async-start | bytes 131072 | tf_op jit(solution)/shard_map/all_to_all | solution.py:17
  11.6 0.7 fusion.151
  12.2 2.5 %fusion.106 = (pred[64]{0:T(512)(128)(4,1)S(1)}, s32[64]{0:T(128)S(1)}, pred[64]{0:T(512)(128)(4,1)S(1)}, s32[64]{0:T(128)S(1)}, pred[64]{0:T(512)(128)(4,1)S(1)...) fusion(s32[1,1,64]{2,1,0:T(1,128)S(1)} %copy-done.5, s32[]{:T(128)} %bitcast.50, s32[]{:T(128)S(6)} %mul.62, ...), kind=kLoop, calls=%fused_computation.113 | loop fusion | flops 1536 | bytes 1824 | tf_op jit(solution)/shard_map/and | solution.py:65
  14.8 2.5 %all-to-all-done = f32[4,32,128]{2,1,0:T(8,128)S(1)} async-done(((f32[4,32,128]{2,1,0:T(8,128)}), f32[4,32,128]{2,1,0:T(8,128)S(1)}, u32[]{:S(2)}, u32[]{:S(2)}) %all-to-all-start) | async-done | bytes 65568 | tf_op jit(solution)/shard_map/all_to_all | solution.py:17
  17.3 0.2 fusion.18
  17.5 0.4 fusion.28
  18.0 1.1 %collective-permute-done = f32[128]{0:T(128)S(1)} collective-permute-done((f32[128]{0:T(128)S(1)}, f32[128]{0:T(128)S(1)}, u32[]{:S(2)}, u32[]{:S(2)}) %collective-permute-start) | collective-permute-done | bytes 544 | tf_op jit(solution)/shard_map/ppermute | solution.py:27
  19.1 1.5 %collective-permute-start.1 = (f32[128]{0:T(128)S(1)}, f32[128]{0:T(128)S(1)}, u32[]{:S(2)}, u32[]{:S(2)}) collective-permute-start(f32[128]{0:T(128)S(1)} %add.98), channel_id=1, source_target_pairs={{0,8},{4,12},{8,0},{12,4},{16,24},{20,28},{24,16},{28,20},{1,9},{5... | collective-permute-start | bytes 1544 | tf_op jit(solution)/shard_map/ppermute | solution.py:27
  20.6 0.6 gather_fusion
  21.2 1.5 %collective-permute-done.1 = f32[128]{0:T(128)S(1)} collective-permute-done((f32[128]{0:T(128)S(1)}, f32[128]{0:T(128)S(1)}, u32[]{:S(2)}, u32[]{:S(2)}) %collective-permute-start.1) | collective-permute-done | bytes 544 | tf_op jit(solution)/shard_map/ppermute | solution.py:27
  22.6 1.5 %collective-permute-start.2 = (f32[128]{0:T(128)S(1)}, f32[128]{0:T(128)S(1)}, u32[]{:S(2)}, u32[]{:S(2)}) collective-permute-start(f32[128]{0:T(128)S(1)} %add.99), channel_id=1, source_target_pairs={{0,16},{4,20},{8,24},{12,28},{16,0},{20,4},{24,8},{28,12},{1,17},{... | collective-permute-start | bytes 1544 | tf_op jit(solution)/shard_map/ppermute | solution.py:27
  24.2 2.0 %collective-permute-done.2 = f32[128]{0:T(128)S(1)} collective-permute-done((f32[128]{0:T(128)S(1)}, f32[128]{0:T(128)S(1)}, u32[]{:S(2)}, u32[]{:S(2)}) %collective-permute-start.2) | collective-permute-done | bytes 544 | tf_op jit(solution)/shard_map/ppermute | solution.py:27
  26.4 0.7 fusion.12
  27.1 0.3 fusion.23
  27.4 1.0 %collective-permute-start.3 = (f32[2,32,128]{2,1,0:T(8,128)S(1)}, f32[2,32,128]{2,1,0:T(8,128)S(1)}, u32[]{:S(2)}, u32[]{:S(2)}) collective-permute-start(f32[2,32,128]{2,1,0:T(8,128)S(1)} %pad_maximum_fusion), channel_id=1, source_target_pairs={{0,1},{1,2},{2,3},{3,0},{4,5},{5,6},{6,7},{7,4},{8,9},{9,10},{10,1... | collective-permute-start | bytes 98312 | tf_op jit(solution)/shard_map/ppermute | solution.py:13
  28.3 4.8 %collective-permute-done.3 = f32[2,32,128]{2,1,0:T(8,128)S(1)} collective-permute-done((f32[2,32,128]{2,1,0:T(8,128)S(1)}, f32[2,32,128]{2,1,0:T(8,128)S(1)}, u32[]{:S(2)}, u32[]{:S(2)}) %collective-permute-start.3) | collective-permute-done | bytes 32800 | tf_op jit(solution)/shard_map/ppermute | solution.py:13
  33.3 0.4 fusion.31
  33.8 1.1 %collective-permute-done.4 = f32[128]{0:T(128)S(1)} collective-permute-done((f32[128]{0:T(128)S(1)}, f32[128]{0:T(128)S(1)}, u32[]{:S(2)}, u32[]{:S(2)}) %collective-permute-start.4) | collective-permute-done | bytes 544 | tf_op jit(solution)/shard_map/ppermute | solution.py:27
  34.9 1.5 %collective-permute-start.5 = (f32[128]{0:T(128)S(1)}, f32[128]{0:T(128)S(1)}, u32[]{:S(2)}, u32[]{:S(2)}) collective-permute-start(f32[128]{0:T(128)S(1)} %add.104), channel_id=1, source_target_pairs={{0,8},{4,12},{8,0},{12,4},{16,24},{20,28},{24,16},{28,20},{1,9},{5... | collective-permute-start | bytes 1544 | tf_op jit(solution)/shard_map/ppermute | solution.py:27
  36.4 2.0 %collective-permute-done.5 = f32[128]{0:T(128)S(1)} collective-permute-done((f32[128]{0:T(128)S(1)}, f32[128]{0:T(128)S(1)}, u32[]{:S(2)}, u32[]{:S(2)}) %collective-permute-start.5) | collective-permute-done | bytes 544 | tf_op jit(solution)/shard_map/ppermute | solution.py:27
  38.5 1.5 %collective-permute-start.6 = (f32[128]{0:T(128)S(1)}, f32[128]{0:T(128)S(1)}, u32[]{:S(2)}, u32[]{:S(2)}) collective-permute-start(f32[128]{0:T(128)S(1)} %add.105), channel_id=1, source_target_pairs={{0,16},{4,20},{8,24},{12,28},{16,0},{20,4},{24,8},{28,12},{1,17},{... | collective-permute-start | bytes 1544 | tf_op jit(solution)/shard_map/ppermute | solution.py:27
  40.0 2.0 %collective-permute-done.6 = f32[128]{0:T(128)S(1)} collective-permute-done((f32[128]{0:T(128)S(1)}, f32[128]{0:T(128)S(1)}, u32[]{:S(2)}, u32[]{:S(2)}) %collective-permute-start.6) | collective-permute-done | bytes 544 | tf_op jit(solution)/shard_map/ppermute | solution.py:27
  42.2 0.7 fusion.8
  42.9 0.3 fusion.74
  43.2 5.7 %collective-permute-done.7 = f32[2,32,128]{2,1,0:T(8,128)S(1)} collective-permute-done((f32[2,32,128]{2,1,0:T(8,128)S(1)}, f32[2,32,128]{2,1,0:T(8,128)S(1)}, u32[]{:S(2)}, u32[]{:S(2)}) %collective-permute-start.7) | collective-permute-done | bytes 32800 | tf_op jit(solution)/shard_map/ppermute | solution.py:13
  49.1 0.4 fusion.34
  49.6 1.1 %collective-permute-done.8 = f32[128]{0:T(128)S(1)} collective-permute-done((f32[128]{0:T(128)S(1)}, f32[128]{0:T(128)S(1)}, u32[]{:S(2)}, u32[]{:S(2)}) %collective-permute-start.8) | collective-permute-done | bytes 544 | tf_op jit(solution)/shard_map/ppermute | solution.py:27
  50.7 1.5 %collective-permute-start.9 = (f32[128]{0:T(128)S(1)}, f32[128]{0:T(128)S(1)}, u32[]{:S(2)}, u32[]{:S(2)}) collective-permute-start(f32[128]{0:T(128)S(1)} %add.110), channel_id=1, source_target_pairs={{0,8},{4,12},{8,0},{12,4},{16,24},{20,28},{24,16},{28,20},{1,9},{5... | collective-permute-start | bytes 1544 | tf_op jit(solution)/shard_map/ppermute | solution.py:27
  52.2 2.0 %collective-permute-done.9 = f32[128]{0:T(128)S(1)} collective-permute-done((f32[128]{0:T(128)S(1)}, f32[128]{0:T(128)S(1)}, u32[]{:S(2)}, u32[]{:S(2)}) %collective-permute-start.9) | collective-permute-done | bytes 544 | tf_op jit(solution)/shard_map/ppermute | solution.py:27
  54.3 1.5 %collective-permute-start.10 = (f32[128]{0:T(128)S(1)}, f32[128]{0:T(128)S(1)}, u32[]{:S(2)}, u32[]{:S(2)}) collective-permute-start(f32[128]{0:T(128)S(1)} %add.111), channel_id=1, source_target_pairs={{0,16},{4,20},{8,24},{12,28},{16,0},{20,4},{24,8},{28,12},{1,17},{... | collective-permute-start | bytes 1544 | tf_op jit(solution)/shard_map/ppermute | solution.py:27
  55.8 2.0 %collective-permute-done.10 = f32[128]{0:T(128)S(1)} collective-permute-done((f32[128]{0:T(128)S(1)}, f32[128]{0:T(128)S(1)}, u32[]{:S(2)}, u32[]{:S(2)}) %collective-permute-start.10) | collective-permute-done | bytes 544 | tf_op jit(solution)/shard_map/ppermute | solution.py:27
  58.0 0.7 fusion.4
  58.7 0.3 fusion.72
  59.0 5.7 %collective-permute-done.11 = f32[2,32,128]{2,1,0:T(8,128)S(1)} collective-permute-done((f32[2,32,128]{2,1,0:T(8,128)S(1)}, f32[2,32,128]{2,1,0:T(8,128)S(1)}, u32[]{:S(2)}, u32[]{:S(2)}) %collective-permute-start.11) | collective-permute-done | bytes 32800 | tf_op jit(solution)/shard_map/ppermute | solution.py:13
  64.9 0.4 fusion.37
  65.4 1.1 %collective-permute-done.12 = f32[128]{0:T(128)S(1)} collective-permute-done((f32[128]{0:T(128)S(1)}, f32[128]{0:T(128)S(1)}, u32[]{:S(2)}, u32[]{:S(2)}) %collective-permute-start.12) | collective-permute-done | bytes 544 | tf_op jit(solution)/shard_map/ppermute | solution.py:27
  66.5 1.5 %collective-permute-start.13 = (f32[128]{0:T(128)S(1)}, f32[128]{0:T(128)S(1)}, u32[]{:S(2)}, u32[]{:S(2)}) collective-permute-start(f32[128]{0:T(128)S(1)} %add.116), channel_id=1, source_target_pairs={{0,8},{4,12},{8,0},{12,4},{16,24},{20,28},{24,16},{28,20},{1,9},{5... | collective-permute-start | bytes 1544 | tf_op jit(solution)/shard_map/ppermute | solution.py:27
  68.0 2.0 %collective-permute-done.13 = f32[128]{0:T(128)S(1)} collective-permute-done((f32[128]{0:T(128)S(1)}, f32[128]{0:T(128)S(1)}, u32[]{:S(2)}, u32[]{:S(2)}) %collective-permute-start.13) | collective-permute-done | bytes 544 | tf_op jit(solution)/shard_map/ppermute | solution.py:27
  70.1 1.5 %collective-permute-start.14 = (f32[128]{0:T(128)S(1)}, f32[128]{0:T(128)S(1)}, u32[]{:S(2)}, u32[]{:S(2)}) collective-permute-start(f32[128]{0:T(128)S(1)} %add.117), channel_id=1, source_target_pairs={{0,16},{4,20},{8,24},{12,28},{16,0},{20,4},{24,8},{28,12},{1,17},{... | collective-permute-start | bytes 1544 | tf_op jit(solution)/shard_map/ppermute | solution.py:27
  71.6 2.0 %collective-permute-done.14 = f32[128]{0:T(128)S(1)} collective-permute-done((f32[128]{0:T(128)S(1)}, f32[128]{0:T(128)S(1)}, u32[]{:S(2)}, u32[]{:S(2)}) %collective-permute-start.14) | collective-permute-done | bytes 544 | tf_op jit(solution)/shard_map/ppermute | solution.py:27
  73.8 0.7 fusion
  74.5 0.3 fusion.70
  82.6 0.7 copy.36
  (49 shorter events, 2.0 us)
Async XLA Ops:
  0.6 2.4 %copy-start = (bf16[1,1,64,128,128]{4,3,2,1,0:T(8,128)(2,1)S(1)}, bf16[1,1,64,128,128]{4,3,2,1,0:T(8,128)(2,1)}, u32[]{:S(2)}) copy-start(bf16[1,1,64,128,128]{4,3,2,1,0:T(8,128)(2,1)} %param.11) | copy-start | bytes 6291460
  0.6 16.7 %copy-start.6 = (s32[16384]{0:T(1024)S(1)}, s32[16384]{0:T(1024)}, u32[]{:S(2)}) copy-start(s32[16384]{0:T(1024)} %param.7) | copy-start | bytes 196612
  0.7 3.6 %copy-start.4 = (s32[1,1,64]{2,1,0:T(1,128)S(1)}, s32[1,1,64]{2,1,0:T(1,128)}, u32[]{:S(2)}) copy-start(s32[1,1,64]{2,1,0:T(1,128)} %param.9) | copy-start | bytes 772
  0.7 11.6 %copy-start.5 = (s32[1,1,64]{2,1,0:T(1,128)S(1)}, s32[1,1,64]{2,1,0:T(1,128)}, u32[]{:S(2)}) copy-start(s32[1,1,64]{2,1,0:T(1,128)} %param.10) | copy-start | bytes 772
  0.7 10.9 %copy-start.3 = (s32[1,4]{1,0:T(1,128)S(1)}, s32[1,4]{1,0:T(1,128)}, u32[]{:S(2)}) copy-start(s32[1,4]{1,0:T(1,128)} %param.12) | copy-start | bytes 52
  3.1 23.1 %copy-start.2 = (f32[1,4,128,128]{3,2,1,0:T(8,128)S(1)}, f32[1,4,128,128]{3,2,1,0:T(8,128)}, u32[]{:S(2)}) copy-start(f32[1,4,128,128]{3,2,1,0:T(8,128)} %param.13) | copy-start | bytes 786436
  5.2 12.1 %all-to-all-start = ((f32[4,32,128]{2,1,0:T(8,128)}), f32[4,32,128]{2,1,0:T(8,128)S(1)}, u32[]{:S(2)}, u32[]{:S(2)}) async-start(f32[4,32,128]{2,1,0:T(8,128)} %bitcast.12), calls=%async_computation | async-start | bytes 131072 | tf_op jit(solution)/shard_map/all_to_all | solution.py:17
  17.9 1.2 %collective-permute-start = (f32[128]{0:T(128)S(1)}, f32[128]{0:T(128)S(1)}, u32[]{:S(2)}, u32[]{:S(2)}) collective-permute-start(f32[128]{0:T(128)S(1)} %fusion.28), channel_id=1, source_target_pairs={{0,4},{4,0},{8,12},{12,8},{16,20},{20,16},{24,28},{28,24},{1,5},{5... | collective-permute-start | bytes 1544 | tf_op jit(solution)/shard_map/ppermute | solution.py:27
  19.1 3.5 %collective-permute-start.1 = (f32[128]{0:T(128)S(1)}, f32[128]{0:T(128)S(1)}, u32[]{:S(2)}, u32[]{:S(2)}) collective-permute-start(f32[128]{0:T(128)S(1)} %add.98), channel_id=1, source_target_pairs={{0,8},{4,12},{8,0},{12,4},{16,24},{20,28},{24,16},{28,20},{1,9},{5... | collective-permute-start | bytes 1544 | tf_op jit(solution)/shard_map/ppermute | solution.py:27
  22.6 3.5 %collective-permute-start.2 = (f32[128]{0:T(128)S(1)}, f32[128]{0:T(128)S(1)}, u32[]{:S(2)}, u32[]{:S(2)}) collective-permute-start(f32[128]{0:T(128)S(1)} %add.99), channel_id=1, source_target_pairs={{0,16},{4,20},{8,24},{12,28},{16,0},{20,4},{24,8},{28,12},{1,17},{... | collective-permute-start | bytes 1544 | tf_op jit(solution)/shard_map/ppermute | solution.py:27
  27.4 5.8 %collective-permute-start.3 = (f32[2,32,128]{2,1,0:T(8,128)S(1)}, f32[2,32,128]{2,1,0:T(8,128)S(1)}, u32[]{:S(2)}, u32[]{:S(2)}) collective-permute-start(f32[2,32,128]{2,1,0:T(8,128)S(1)} %pad_maximum_fusion), channel_id=1, source_target_pairs={{0,1},{1,2},{2,3},{3,0},{4,5},{5,6},{6,7},{7,4},{8,9},{9,10},{10,1... | collective-permute-start | bytes 98312 | tf_op jit(solution)/shard_map/ppermute | solution.py:13
  33.7 1.2 %collective-permute-start.4 = (f32[128]{0:T(128)S(1)}, f32[128]{0:T(128)S(1)}, u32[]{:S(2)}, u32[]{:S(2)}) collective-permute-start(f32[128]{0:T(128)S(1)} %fusion.31), channel_id=1, source_target_pairs={{0,4},{4,0},{8,12},{12,8},{16,20},{20,16},{24,28},{28,24},{1,5},{5... | collective-permute-start | bytes 1544 | tf_op jit(solution)/shard_map/ppermute | solution.py:27
  34.9 3.5 %collective-permute-start.5 = (f32[128]{0:T(128)S(1)}, f32[128]{0:T(128)S(1)}, u32[]{:S(2)}, u32[]{:S(2)}) collective-permute-start(f32[128]{0:T(128)S(1)} %add.104), channel_id=1, source_target_pairs={{0,8},{4,12},{8,0},{12,4},{16,24},{20,28},{24,16},{28,20},{1,9},{5... | collective-permute-start | bytes 1544 | tf_op jit(solution)/shard_map/ppermute | solution.py:27
  38.5 3.5 %collective-permute-start.6 = (f32[128]{0:T(128)S(1)}, f32[128]{0:T(128)S(1)}, u32[]{:S(2)}, u32[]{:S(2)}) collective-permute-start(f32[128]{0:T(128)S(1)} %add.105), channel_id=1, source_target_pairs={{0,16},{4,20},{8,24},{12,28},{16,0},{20,4},{24,8},{28,12},{1,17},{... | collective-permute-start | bytes 1544 | tf_op jit(solution)/shard_map/ppermute | solution.py:27
  43.2 5.8 %collective-permute-start.7 = (f32[2,32,128]{2,1,0:T(8,128)S(1)}, f32[2,32,128]{2,1,0:T(8,128)S(1)}, u32[]{:S(2)}, u32[]{:S(2)}) collective-permute-start(f32[2,32,128]{2,1,0:T(8,128)S(1)} %pad_maximum_fusion.1), channel_id=1, source_target_pairs={{0,1},{1,2},{2,3},{3,0},{4,5},{5,6},{6,7},{7,4},{8,9},{9,10},{10,1... | collective-permute-start | bytes 98312 | tf_op jit(solution)/shard_map/ppermute | solution.py:13
  49.5 1.2 %collective-permute-start.8 = (f32[128]{0:T(128)S(1)}, f32[128]{0:T(128)S(1)}, u32[]{:S(2)}, u32[]{:S(2)}) collective-permute-start(f32[128]{0:T(128)S(1)} %fusion.34), channel_id=1, source_target_pairs={{0,4},{4,0},{8,12},{12,8},{16,20},{20,16},{24,28},{28,24},{1,5},{5... | collective-permute-start | bytes 1544 | tf_op jit(solution)/shard_map/ppermute | solution.py:27
  50.7 3.5 %collective-permute-start.9 = (f32[128]{0:T(128)S(1)}, f32[128]{0:T(128)S(1)}, u32[]{:S(2)}, u32[]{:S(2)}) collective-permute-start(f32[128]{0:T(128)S(1)} %add.110), channel_id=1, source_target_pairs={{0,8},{4,12},{8,0},{12,4},{16,24},{20,28},{24,16},{28,20},{1,9},{5... | collective-permute-start | bytes 1544 | tf_op jit(solution)/shard_map/ppermute | solution.py:27
  54.3 3.5 %collective-permute-start.10 = (f32[128]{0:T(128)S(1)}, f32[128]{0:T(128)S(1)}, u32[]{:S(2)}, u32[]{:S(2)}) collective-permute-start(f32[128]{0:T(128)S(1)} %add.111), channel_id=1, source_target_pairs={{0,16},{4,20},{8,24},{12,28},{16,0},{20,4},{24,8},{28,12},{1,17},{... | collective-permute-start | bytes 1544 | tf_op jit(solution)/shard_map/ppermute | solution.py:27
  59.0 5.8 %collective-permute-start.11 = (f32[2,32,128]{2,1,0:T(8,128)S(1)}, f32[2,32,128]{2,1,0:T(8,128)S(1)}, u32[]{:S(2)}, u32[]{:S(2)}) collective-permute-start(f32[2,32,128]{2,1,0:T(8,128)S(1)} %pad_maximum_fusion.2), channel_id=1, source_target_pairs={{0,1},{1,2},{2,3},{3,0},{4,5},{5,6},{6,7},{7,4},{8,9},{9,10},{10,1... | collective-permute-start | bytes 98312 | tf_op jit(solution)/shard_map/ppermute | solution.py:13
  65.3 1.2 %collective-permute-start.12 = (f32[128]{0:T(128)S(1)}, f32[128]{0:T(128)S(1)}, u32[]{:S(2)}, u32[]{:S(2)}) collective-permute-start(f32[128]{0:T(128)S(1)} %fusion.37), channel_id=1, source_target_pairs={{0,4},{4,0},{8,12},{12,8},{16,20},{20,16},{24,28},{28,24},{1,5},{5... | collective-permute-start | bytes 1544 | tf_op jit(solution)/shard_map/ppermute | solution.py:27
  66.5 3.5 %collective-permute-start.13 = (f32[128]{0:T(128)S(1)}, f32[128]{0:T(128)S(1)}, u32[]{:S(2)}, u32[]{:S(2)}) collective-permute-start(f32[128]{0:T(128)S(1)} %add.116), channel_id=1, source_target_pairs={{0,8},{4,12},{8,0},{12,4},{16,24},{20,28},{24,16},{28,20},{1,9},{5... | collective-permute-start | bytes 1544 | tf_op jit(solution)/shard_map/ppermute | solution.py:27
  70.1 3.5 %collective-permute-start.14 = (f32[128]{0:T(128)S(1)}, f32[128]{0:T(128)S(1)}, u32[]{:S(2)}, u32[]{:S(2)}) collective-permute-start(f32[128]{0:T(128)S(1)} %add.117), channel_id=1, source_target_pairs={{0,16},{4,20},{8,24},{12,28},{16,0},{20,4},{24,8},{28,12},{1,17},{... | collective-permute-start | bytes 1544 | tf_op jit(solution)/shard_map/ppermute | solution.py:27
  74.8 7.8 %collective-permute-start.15 = (f32[32,128]{1,0:T(8,128)S(1)}, f32[32,128]{1,0:T(8,128)S(1)}, u32[]{:S(2)}, u32[]{:S(2)}) collective-permute-start(f32[32,128]{1,0:T(8,128)S(1)} %fusion.70), channel_id=1, source_target_pairs={{0,1},{1,2},{2,3},{3,0},{4,5},{5,6},{6,7},{7,4},{8,9},{9,10},{10,1... | collective-permute-start | bytes 49160 | tf_op jit(solution)/shard_map/ppermute | solution.py:13
  82.6 0.7 copy-start.1

commit v3 on v1

v3 whole, which is shorter than its diff:
```python
import jax
import jax.numpy as jnp
from jax import lax
from jax.sharding import PartitionSpec as P

exact_prec = lax.Precision.HIGHEST
l1_penalty = 0.25
both_axes = ("samp", "feat")


def on_planes(samp_pairs, planes):
    count = lax.axis_size("feat")
    return [
        (source * count + plane, target * count + plane)
        for plane in planes
        for source, target in samp_pairs
    ]


def summed(value, planes):
    count = lax.axis_size("samp")
    if count < 2 or count & (count - 1):
        return lax.psum(value, "samp")
    inward = [(even, even + 1) for even in range(0, count, 2)]
    value = value + lax.ppermute(value, both_axes, on_planes(inward, planes))
    distance = 2
    while distance < count:
        across = [(odd, odd ^ distance) for odd in range(1, count, 2)]
        value = value + lax.ppermute(value, both_axes, on_planes(across, planes))
        distance *= 2
    outward = [(even + 1, even) for even in range(0, count, 2)]
    copied = lax.ppermute(value, both_axes, on_planes(outward, planes))
    return jnp.where(lax.axis_index("samp") % 2 == 1, value, copied)


def to_next(value, planes):
    samp_count, feat_count = lax.axis_size("samp"), lax.axis_size("feat")
    pairs = [
        (row * feat_count + plane, row * feat_count + (plane + 1) % feat_count)
        for row in range(samp_count)
        for plane in planes
    ]
    return lax.ppermute(value, both_axes, pairs)


def per_device(labels, beta, tile_rows, tile_cols, tile_values, block_order, hess_inv):
    cycle_size = lax.axis_size("feat")
    strand_count = 2 if cycle_size % 2 == 0 else 1
    my_index = lax.axis_index("feat")
    row_ids = tile_rows[0, 0]
    col_ids = tile_cols[0, 0]
    values = tile_values[0, 0]
    tile_edge = values.shape[-1]
    row_blocks = labels.shape[0] // tile_edge
    group_blocks = row_blocks // cycle_size
    blocks = beta.reshape(-1, tile_edge)
    picked = jnp.take(blocks, col_ids, axis=0, mode="clip").astype(jnp.bfloat16)
    products = jnp.einsum("krc,kc->kr", values, picked, preferred_element_type=jnp.float32)
    placing = (row_ids[:, None] == jnp.arange(row_blocks, dtype=jnp.int32)[None, :]).astype(
        jnp.float32
    )
    partial_sum = jnp.dot(placing.T, products, precision=exact_prec)
    parts = lax.all_to_all(
        partial_sum.reshape(cycle_size, group_blocks, tile_edge), "feat", 0, 0
    )
    margins = jnp.sum(parts, axis=0)
    probability = jax.nn.sigmoid(margins)
    first_weight = probability * (1.0 - probability)
    own_labels = lax.dynamic_slice_in_dim(
        labels.reshape(row_blocks, tile_edge), my_index * group_blocks, group_blocks, 0
    )
    first_residual = own_labels.astype(jnp.float32) - probability
    sub_ids = jnp.arange(group_blocks, dtype=jnp.int32)
    inverses = hess_inv[0]
    targets = block_order[0]
    old_blocks = jnp.take(blocks, targets, axis=0, mode="clip")
    chosen = []
    for section in range(cycle_size):
        offsets = row_ids - ((my_index - section) % cycle_size) * group_blocks
        matches = (col_ids == targets[section]) & (offsets >= 0) & (offsets < group_blocks)
        chosen.append((offsets[:, None] == sub_ids[None, :]) & matches[:, None])

    def update(section, residual, weight, planes):
        rounded = residual.astype(jnp.bfloat16)
        resid_tiles = jnp.dot(
            chosen[section].astype(jnp.bfloat16), rounded, preferred_element_type=jnp.float32
        ).astype(jnp.bfloat16)
        local_grad = jnp.einsum(
            "krc,kr->c", values, resid_tiles, preferred_element_type=jnp.float32
        )
        gradient = summed(local_grad, planes)
        current = old_blocks[section]
        moved_block = current + jnp.dot(inverses[section], gradient, precision=exact_prec)
        shrunk = jnp.sign(moved_block) * jnp.maximum(jnp.abs(moved_block) - l1_penalty, 0.0)
        change = (shrunk - current).astype(jnp.bfloat16)
        image_rows = jnp.einsum("krc,c->kr", values, change, preferred_element_type=jnp.float32)
        landed = jnp.dot(chosen[section].astype(jnp.float32).T, image_rows, precision=exact_prec)
        return shrunk, residual - weight * landed

    state = jnp.stack([first_residual, first_weight])
    states = [state] * strand_count
    for section in range(cycle_size):
        shrunk_block = None
        for strand in range(strand_count):
            planes = [
                plane
                for plane in range(cycle_size)
                if (plane - section - strand) % strand_count == 0
            ]
            active = (my_index - section - strand) % strand_count == 0

            def work(state, section=section, planes=planes):
                shrunk, residual = update(section, state[0], state[1], planes)
                if section + 1 < cycle_size:
                    return shrunk, jnp.stack([residual, state[1]])
                return shrunk, residual

            def rest(state, section=section):
                kept = state if section + 1 < cycle_size else state[0]
                return jnp.zeros((tile_edge,), jnp.float32), kept

            shrunk, moving = lax.cond(active, work, rest, states[strand])
            later = (strand + 1) % strand_count
            if later != strand and (section + 1 < cycle_size or strand + 1 < strand_count):
                moving, states[later] = lax.optimization_barrier((moving, states[later]))
            states[strand] = to_next(moving, planes)
            shrunk_block = shrunk if strand == 0 else jnp.where(active, shrunk, shrunk_block)
        blocks = lax.dynamic_update_index_in_dim(blocks, shrunk_block, targets[section], 0)
    results = states
    residual = results[0]
    if strand_count == 2:
        from_first = (my_index - cycle_size) % strand_count == 0
        residual = jnp.where(from_first, results[0], results[1])
    return (blocks.reshape(-1), residual.reshape(-1))


def solution(mesh):
    placed = (
        P("samp"),
        P("feat"),
        P("samp", "feat", None),
        P("samp", "feat", None),
        P("samp", "feat", None, None, None),
        P("feat", None),
        P("feat", None, None, None),
    )
    return jax.shard_map(
        per_device,
        mesh=mesh,
        in_specs=placed,
        out_specs=(P("feat"), P(("samp", "feat"))),
        check_vma=False,
    )
```

time: 83.8 us -> 125 us (1.49)
  waiting for transfers between devices: 31.7 us -> 54.9 us
  starting transfers between devices: 17.8 us -> 33 us
  blocking collectives: 7.03 us -> 0 us
  matrix products: 9.14 us -> 14.7 us
  other arithmetic: 3.33 us -> 7.42 us
    ppermute x4 -> x24, waiting for transfers between devices: 16.2 us -> 52.9 us  [the longest x4 32.2 us: summed(): copied = lax.ppermute(value, both_axes, on_planes(outward, planes))]
    ppermute x4 -> x24, starting transfers between devices: 1.14 us -> 26.7 us  [the longest x8 10.3 us: to_next(): return lax.ppermute(value, both_axes, pairs)]
    all_to_all x4 -> x1, waiting for transfers between devices: 15.5 us -> 2.01 us  [per_device(): lax.all_to_all(partial_sum.reshape(cycle_size, group_blocks, tile_edge),...]
    all_to_all x4 -> x1, starting transfers between devices: 16.7 us -> 6.32 us  [per_device(): lax.all_to_all(partial_sum.reshape(cycle_size, group_blocks, tile_edge),...]
    all_to_all x1 -> x0, blocking collectives: 7.03 us -> none  [exchange(): return lax.all_to_all(parts, axis, 0, 0)]
    dot_general x20, matrix products: 7 us -> 11 us  [the longest x4 5.07 us: update(): jnp.einsum('krc,c->kr', values, change, preferred_element_type=jnp.float32)]
    broadcast_in_dim x0 -> x4, other arithmetic: none -> 2.59 us  [per_device(): lax.dynamic_update_index_in_dim(blocks, shrunk_block, targets[section], 0)]
    another operation x0 -> x4, local copies, waits for them, and re-layouts: none -> 2.11 us
  transfers between devices with their start and end apart: 8 -> 25, of which waited for: 7 -> 14; matrix products, arithmetic and copies ran while one was open for 5% -> 12% of each run, Pallas kernels for 0% -> 0%
where the time goes in v3:
time: 125 us; the launch traced here: 124 us
  waiting for transfers between devices  54.9 us (44%)
  starting transfers between devices  33 us (26%)
  matrix products  14.7 us (12%)
  between operations  8.15 us (7%)
  other arithmetic  7.42 us (6%)
  local copies, waits for them, and re-layouts  5.18 us (4%)
    ppermute x4, waiting for transfers between devices, summed(): copied = lax.ppermute(value, both_axes, on_planes(outward, planes))  32.2 us
    ppermute x8, waiting for transfers between devices, to_next(): return lax.ppermute(value, both_axes, pairs)  17.5 us
    ppermute x8, starting transfers between devices, to_next(): return lax.ppermute(value, both_axes, pairs)  10.3 us
    all_to_all x1, starting transfers between devices, per_device(): lax.all_to_all(partial_sum.reshape(cycle_size, group_blocks, tile_edge),...  6.32 us
    ppermute x4, starting transfers between devices, summed(): value = value + lax.ppermute(value, both_axes, on_planes(inward, planes))  5.99 us
    ppermute x8, starting transfers between devices, summed(): value = value + lax.ppermute(value, both_axes, on_planes(across, planes))  5.24 us
    ppermute x4, starting transfers between devices, summed(): copied = lax.ppermute(value, both_axes, on_planes(outward, planes))  5.17 us
    dot_general x4, matrix products, update(): jnp.einsum('krc,c->kr', values, change, preferred_element_type=jnp.float32)  5.07 us
  transfers between devices with their start and end apart: 25, of which 14 were waited for; matrix products, arithmetic and copies ran while one was open for 12% of the time, Pallas kernels for 0%

profile of v3, /device:TPU:0, one launch (start us, length us, event | category | flops | bytes accessed | tf_op | source)
XLA Modules:
  0.0 123.9 jit_solution(9065634309737621923)
XLA Ops:
  0.7 1.1 copy.102
  3.1 2.8 %fusion.151 = f32[64,1,128]{2,1,0:T(1,128)S(1)} fusion(bf16[64,128,1]{1,0,2:T(8,128)(2,1)S(1)} %bitcast.517, bf16[1,1,64,128,128]{4,3,2,1,0:T(8,128)(2,1)} %param.27), kind=kOutput, calls=%fused_computation.178 | convolution fusion | flops 2097152 | bytes 2146304 | tf_op jit(solution)/shard_map/krc,kc->kr/dot_general | solution.py:58
  5.8 1.0 fusion.153
  6.8 6.3 %all-to-all-start = ((f32[4,32,128]{2,1,0:T(8,128)}), f32[4,32,128]{2,1,0:T(8,128)S(1)}, u32[]{:S(2)}, u32[]{:S(2)}) async-start(f32[4,32,128]{2,1,0:T(8,128)} %bitcast.110), calls=%async_computation | async-start | bytes 131072 | tf_op jit(solution)/shard_map/all_to_all | solution.py:63
  13.8 2.4 %fusion.159 = (pred[64]{0:T(512)(128)(4,1)S(1)}, s32[64]{0:T(128)S(1)}, pred[64]{0:T(512)(128)(4,1)S(1)}, s32[64]{0:T(128)S(1)}, pred[64]{0:T(512)(128)(4,1)S(1)...) fusion(s32[1,1,64]{2,1,0:T(1,128)S(1)} %copy-done.5, s32[]{:T(128)} %bitcast.124, s32[]{:T(128)S(6)} %mul.81, ...), kind=kLoop, calls=%fused_computation.199 | loop fusion | flops 1536 | bytes 1824 | tf_op jit(solution)/shard_map/and | solution.py:80
  16.9 2.0 %all-to-all-done = f32[4,32,128]{2,1,0:T(8,128)S(1)} async-done(((f32[4,32,128]{2,1,0:T(8,128)}), f32[4,32,128]{2,1,0:T(8,128)S(1)}, u32[]{:S(2)}, u32[]{:S(2)}) %all-to-all-start) | async-done | bytes 65568 | tf_op jit(solution)/shard_map/all_to_all | solution.py:63
  18.9 0.7 add_divide_fusion
  19.7 15.6 %conditional.8 = (f32[128]{0:T(128)}, f32[2,32,128]{2,1,0:T(8,128)S(1)}) conditional(s32[]{:T(128)} %convert_element_type.114, f32[2,32,128]{2,1,0:T(8,128)S(1)} %pad_maximum_fusion.6, (f32[4,128]{1,0:T(4,128)S(1)}, f32[32,128]{1,0:T(8,128)S(1)}, pred[64,32]{1,0:T(32,128)(4,1)S(1)}, bf16[64,128,128]{2,1,0:T(8,128)(2,1)S(1)}, ...), branch_computations={%region_1.2_spmd, %region_2.3_spmd} | conditional | flops 8099343 | bytes 4510023 | solution.py:122
  20.2 1.3 %collective-permute-start = (f32[128]{0:T(128)S(1)}, f32[128]{0:T(128)S(1)}, u32[]{:S(2)}, u32[]{:S(2)}) collective-permute-start(f32[128]{0:T(128)S(1)} %convolution_bitcast_fusion.2), channel_id=1, source_target_pairs={{0,4},{8,12},{16,20},{24,28},{2,6},{10,14},{18,22},{26,30}} | collective-permute-start | bytes 1544 | tf_op jit(solution)/shard_map/cond/branch_1_fun/ppermute | solution.py:25
  21.5 0.8 collective-permute-done
  23.7 1.3 %collective-permute-start.3 = (f32[128]{0:T(128)S(1)}, f32[128]{0:T(128)S(1)}, u32[]{:S(2)}, u32[]{:S(2)}) collective-permute-start(f32[128]{0:T(128)S(1)} %add.148), channel_id=1, source_target_pairs={{4,0},{12,8},{20,16},{28,24},{6,2},{14,10},{22,18},{30,26}} | collective-permute-start | bytes 1544 | tf_op jit(solution)/shard_map/cond/branch_1_fun/ppermute | solution.py:32
  25.0 8.0 %collective-permute-done.3 = f32[128]{0:T(128)S(1)} collective-permute-done((f32[128]{0:T(128)S(1)}, f32[128]{0:T(128)S(1)}, u32[]{:S(2)}, u32[]{:S(2)}) %collective-permute-start.3) | collective-permute-done | bytes 544 | tf_op jit(solution)/shard_map/cond/branch_1_fun/ppermute | solution.py:32
  33.1 0.8 maximum_multiply_fusion
  33.8 1.3 %fusion.11 = f32[1,64,128]{2,0,1:T(1,128)S(1)} fusion(bf16[64,128,128]{2,1,0:T(8,128)(2,1)S(1)} %get-tuple-element.100, f32[128]{0:T(128)} %maximum_multiply_fusion, f32[4,128]{1,0:T(4,128)S(1)} %get-tuple-element.97), kind=kOutput, calls=%fused_computation.19 | convolution fusion | flops 2097408 | bytes 2130944 | tf_op jit(solution)/shard_map/cond/branch_1_fun/krc,c->kr/dot_general | solution.py:96
  35.3 1.3 %collective-permute-start.32 = (f32[2,32,128]{2,1,0:T(8,128)S(1)}, f32[2,32,128]{2,1,0:T(8,128)S(1)}, u32[]{:S(2)}, u32[]{:S(2)}) collective-permute-start(f32[2,32,128]{2,1,0:T(8,128)S(1)} %get-tuple-element.176), channel_id=1, source_target_pairs={{0,1},{2,3},{4,5},{6,7},{8,9},{10,11},{12,13},{14,15},{16,17},{18,... | collective-permute-start | bytes 98312 | tf_op jit(solution)/shard_map/ppermute | solution.py:43
  37.2 0.9 collective-permute-done.32
  38.2 1.3 %collective-permute-start.33 = (f32[2,32,128]{2,1,0:T(8,128)S(1)}, f32[2,32,128]{2,1,0:T(8,128)S(1)}, u32[]{:S(2)}, u32[]{:S(2)}) collective-permute-start(f32[2,32,128]{2,1,0:T(8,128)S(1)} %get-tuple-element.179), channel_id=1, source_target_pairs={{1,2},{3,0},{5,6},{7,4},{9,10},{11,8},{13,14},{15,12},{17,18},{19,... | collective-permute-start | bytes 98312 | tf_op jit(solution)/shard_map/ppermute | solution.py:43
  40.2 5.6 %collective-permute-done.33 = f32[2,32,128]{2,1,0:T(8,128)S(1)} collective-permute-done((f32[2,32,128]{2,1,0:T(8,128)S(1)}, f32[2,32,128]{2,1,0:T(8,128)S(1)}, u32[]{:S(2)}, u32[]{:S(2)}) %collective-permute-start.33) | collective-permute-done | bytes 32800 | tf_op jit(solution)/shard_map/ppermute | solution.py:43
  45.8 1.3 %collective-permute-start.34 = (f32[2,32,128]{2,1,0:T(8,128)S(1)}, f32[2,32,128]{2,1,0:T(8,128)S(1)}, u32[]{:S(2)}, u32[]{:S(2)}) collective-permute-start(f32[2,32,128]{2,1,0:T(8,128)S(1)} %get-tuple-element.184), channel_id=1, source_target_pairs={{1,2},{3,0},{5,6},{7,4},{9,10},{11,8},{13,14},{15,12},{17,18},{19,... | collective-permute-start | bytes 98312 | tf_op jit(solution)/shard_map/ppermute | solution.py:43
  54.4 15.6 %conditional.11 = (f32[128]{0:T(128)}, f32[2,32,128]{2,1,0:T(8,128)S(1)}) conditional(s32[]{:T(128)} %convert_element_type.117, f32[2,32,128]{2,1,0:T(8,128)S(1)} %collective-permute-done.33, (f32[4,128]{1,0:T(4,128)S(1)}, f32[2,32,128]{2,1,0:T(8,128)S(1)}, pred[64,32]{1,0:T(32,128)(4,1)S(1)}, bf16[64,128,128]{2,1,0:T(8,128)(2,1)S(1)}, ...), branch_computations={%region_7.8_spmd, %region_8.9_spmd} | conditional | flops 8087055 | bytes 4540743 | solution.py:122
  54.9 1.3 %collective-permute-start.12 = (f32[128]{0:T(128)S(1)}, f32[128]{0:T(128)S(1)}, u32[]{:S(2)}, u32[]{:S(2)}) collective-permute-start(f32[128]{0:T(128)S(1)} %convolution_bitcast_fusion.11), channel_id=1, source_target_pairs={{0,4},{8,12},{16,20},{24,28},{2,6},{10,14},{18,22},{26,30}} | collective-permute-start | bytes 1544 | tf_op jit(solution)/shard_map/cond/branch_1_fun/ppermute | solution.py:25
  56.2 0.8 collective-permute-done.12
  58.4 1.3 %collective-permute-start.15 = (f32[128]{0:T(128)S(1)}, f32[128]{0:T(128)S(1)}, u32[]{:S(2)}, u32[]{:S(2)}) collective-permute-start(f32[128]{0:T(128)S(1)} %add.163), channel_id=1, source_target_pairs={{4,0},{12,8},{20,16},{28,24},{6,2},{14,10},{22,18},{30,26}} | collective-permute-start | bytes 1544 | tf_op jit(solution)/shard_map/cond/branch_1_fun/ppermute | solution.py:32
  59.8 8.0 %collective-permute-done.15 = f32[128]{0:T(128)S(1)} collective-permute-done((f32[128]{0:T(128)S(1)}, f32[128]{0:T(128)S(1)}, u32[]{:S(2)}, u32[]{:S(2)}) %collective-permute-start.15) | collective-permute-done | bytes 544 | tf_op jit(solution)/shard_map/cond/branch_1_fun/ppermute | solution.py:32
  67.8 0.7 maximum_multiply_fusion.3
  68.5 1.2 fusion.68
  70.0 1.3 %collective-permute-start.35 = (f32[2,32,128]{2,1,0:T(8,128)S(1)}, f32[2,32,128]{2,1,0:T(8,128)S(1)}, u32[]{:S(2)}, u32[]{:S(2)}) collective-permute-start(f32[2,32,128]{2,1,0:T(8,128)S(1)} %get-tuple-element.187), channel_id=1, source_target_pairs={{0,1},{2,3},{4,5},{6,7},{8,9},{10,11},{12,13},{14,15},{16,17},{18,... | collective-permute-start | bytes 98312 | tf_op jit(solution)/shard_map/ppermute | solution.py:43
  72.0 16.5 %conditional.12 = (f32[128]{0:T(128)}, f32[2,32,128]{2,1,0:T(8,128)S(1)}) conditional(s32[]{:T(128)} %convert_element_type.117, f32[2,32,128]{2,1,0:T(8,128)S(1)} %collective-permute-done.34, (f32[4,128]{1,0:T(4,128)S(1)}, f32[2,32,128]{2,1,0:T(8,128)S(1)}, pred[64,32]{1,0:T(32,128)(4,1)S(1)}, bf16[64,128,128]{2,1,0:T(8,128)(2,1)S(1)}, ...), branch_computations={%region_9.10_spmd, %region_10.11_spmd} | conditional | flops 8087055 | bytes 4540743 | solution.py:122
  72.5 2.1 %collective-permute-start.16 = (f32[128]{0:T(128)S(1)}, f32[128]{0:T(128)S(1)}, u32[]{:S(2)}, u32[]{:S(2)}) collective-permute-start(f32[128]{0:T(128)S(1)} %convolution_bitcast_fusion.14), channel_id=1, source_target_pairs={{0,4},{8,12},{16,20},{24,28},{2,6},{10,14},{18,22},{26,30}} | collective-permute-start | bytes 1544 | tf_op jit(solution)/shard_map/cond/branch_1_fun/ppermute | solution.py:25
  74.6 0.8 collective-permute-done.16
  76.8 1.3 %collective-permute-start.19 = (f32[128]{0:T(128)S(1)}, f32[128]{0:T(128)S(1)}, u32[]{:S(2)}, u32[]{:S(2)}) collective-permute-start(f32[128]{0:T(128)S(1)} %add.168), channel_id=1, source_target_pairs={{4,0},{12,8},{20,16},{28,24},{6,2},{14,10},{22,18},{30,26}} | collective-permute-start | bytes 1544 | tf_op jit(solution)/shard_map/cond/branch_1_fun/ppermute | solution.py:32
  78.1 8.0 %collective-permute-done.19 = f32[128]{0:T(128)S(1)} collective-permute-done((f32[128]{0:T(128)S(1)}, f32[128]{0:T(128)S(1)}, u32[]{:S(2)}, u32[]{:S(2)}) %collective-permute-start.19) | collective-permute-done | bytes 544 | tf_op jit(solution)/shard_map/cond/branch_1_fun/ppermute | solution.py:32
  86.2 0.7 maximum_multiply_fusion.4
  86.9 1.3 %fusion.87 = f32[1,64,128]{2,0,1:T(1,128)S(1)} fusion(bf16[64,128,128]{2,1,0:T(8,128)(2,1)S(1)} %get-tuple-element.122, f32[128]{0:T(128)} %maximum_multiply_fusion.4, f32[4,128]{1,0:T(4,128)S(1)} %get-tuple-element.119), kind=kOutput, calls=%fused_computation.107 | convolution fusion | flops 2097408 | bytes 2130944 | tf_op jit(solution)/shard_map/cond/branch_1_fun/krc,c->kr/dot_general | solution.py:96
  88.5 1.3 %collective-permute-start.36 = (f32[2,32,128]{2,1,0:T(8,128)S(1)}, f32[2,32,128]{2,1,0:T(8,128)S(1)}, u32[]{:S(2)}, u32[]{:S(2)}) collective-permute-start(f32[2,32,128]{2,1,0:T(8,128)S(1)} %get-tuple-element.192), channel_id=1, source_target_pairs={{0,1},{2,3},{4,5},{6,7},{8,9},{10,11},{12,13},{14,15},{16,17},{18,... | collective-permute-start | bytes 98312 | tf_op jit(solution)/shard_map/ppermute | solution.py:43
  91.3 1.3 %collective-permute-start.37 = (f32[2,32,128]{2,1,0:T(8,128)S(1)}, f32[2,32,128]{2,1,0:T(8,128)S(1)}, u32[]{:S(2)}, u32[]{:S(2)}) collective-permute-start(f32[2,32,128]{2,1,0:T(8,128)S(1)} %get-tuple-element.195), channel_id=1, source_target_pairs={{1,2},{3,0},{5,6},{7,4},{9,10},{11,8},{13,14},{15,12},{17,18},{19,... | collective-permute-start | bytes 98312 | tf_op jit(solution)/shard_map/ppermute | solution.py:43
  92.6 0.7 fusion.165
  93.8 5.1 %collective-permute-done.37 = f32[2,32,128]{2,1,0:T(8,128)S(1)} collective-permute-done((f32[2,32,128]{2,1,0:T(8,128)S(1)}, f32[2,32,128]{2,1,0:T(8,128)S(1)}, u32[]{:S(2)}, u32[]{:S(2)}) %collective-permute-start.37) | collective-permute-done | bytes 32800 | tf_op jit(solution)/shard_map/ppermute | solution.py:43
  98.9 15.6 %conditional.15 = (f32[128]{0:T(128)}, f32[32,128]{1,0:T(8,128)S(1)}) conditional(s32[]{:T(128)} %convert_element_type.119, f32[2,32,128]{2,1,0:T(8,128)S(1)} %collective-permute-done.37, (f32[4,128]{1,0:T(4,128)S(1)}, f32[2,32,128]{2,1,0:T(8,128)S(1)}, pred[64,32]{1,0:T(32,128)(4,1)S(1)}, bf16[64,128,128]{2,1,0:T(8,128)(2,1)S(1)}, ...), branch_computations={%region_15.16_spmd, %region_16.17_spmd} | conditional | flops 8078863 | bytes 4442439 | solution.py:122
  99.4 1.3 %collective-permute-start.28 = (f32[128]{0:T(128)S(1)}, f32[128]{0:T(128)S(1)}, u32[]{:S(2)}, u32[]{:S(2)}) collective-permute-start(f32[128]{0:T(128)S(1)} %convolution_bitcast_fusion.23), channel_id=1, source_target_pairs={{0,4},{8,12},{16,20},{24,28},{2,6},{10,14},{18,22},{26,30}} | collective-permute-start | bytes 1544 | tf_op jit(solution)/shard_map/cond/branch_1_fun/ppermute | solution.py:25
  100.7 0.8 collective-permute-done.28
  102.9 1.3 %collective-permute-start.31 = (f32[128]{0:T(128)S(1)}, f32[128]{0:T(128)S(1)}, u32[]{:S(2)}, u32[]{:S(2)}) collective-permute-start(f32[128]{0:T(128)S(1)} %add.183), channel_id=1, source_target_pairs={{4,0},{12,8},{20,16},{28,24},{6,2},{14,10},{22,18},{30,26}} | collective-permute-start | bytes 1544 | tf_op jit(solution)/shard_map/cond/branch_1_fun/ppermute | solution.py:32
  104.2 8.0 %collective-permute-done.31 = f32[128]{0:T(128)S(1)} collective-permute-done((f32[128]{0:T(128)S(1)}, f32[128]{0:T(128)S(1)}, u32[]{:S(2)}, u32[]{:S(2)}) %collective-permute-start.31) | collective-permute-done | bytes 544 | tf_op jit(solution)/shard_map/cond/branch_1_fun/ppermute | solution.py:32
  112.3 0.7 maximum_multiply_fusion.7
  113.0 1.3 %fusion.142 = f32[1,64,128]{2,0,1:T(1,128)S(1)} fusion(bf16[64,128,128]{2,1,0:T(8,128)(2,1)S(1)} %get-tuple-element.137, f32[128]{0:T(128)} %maximum_multiply_fusion.7, f32[4,128]{1,0:T(4,128)S(1)} %get-tuple-element.134), kind=kOutput, calls=%fused_computation.171 | convolution fusion | flops 2097408 | bytes 2130944 | tf_op jit(solution)/shard_map/cond/branch_1_fun/krc,c->kr/dot_general | solution.py:96
  114.5 1.3 %collective-permute-start.39 = (f32[32,128]{1,0:T(8,128)S(1)}, f32[32,128]{1,0:T(8,128)S(1)}, u32[]{:S(2)}, u32[]{:S(2)}) collective-permute-start(f32[32,128]{1,0:T(8,128)S(1)} %get-tuple-element.200), channel_id=1, source_target_pairs={{0,1},{2,3},{4,5},{6,7},{8,9},{10,11},{12,13},{14,15},{16,17},{18,... | collective-permute-start | bytes 49160 | tf_op jit(solution)/shard_map/ppermute | solution.py:43
  115.8 1.3 %collective-permute-start.38 = (f32[32,128]{1,0:T(8,128)S(1)}, f32[32,128]{1,0:T(8,128)S(1)}, u32[]{:S(2)}, u32[]{:S(2)}) collective-permute-start(f32[32,128]{1,0:T(8,128)S(1)} %get-tuple-element.199), channel_id=1, source_target_pairs={{1,2},{3,0},{5,6},{7,4},{9,10},{11,8},{13,14},{15,12},{17,18},{19,... | collective-permute-start | bytes 49160 | tf_op jit(solution)/shard_map/ppermute | solution.py:43
  117.9 5.4 %collective-permute-done.38 = f32[32,128]{1,0:T(8,128)S(1)} collective-permute-done((f32[32,128]{1,0:T(8,128)S(1)}, f32[32,128]{1,0:T(8,128)S(1)}, u32[]{:S(2)}, u32[]{:S(2)}) %collective-permute-start.38) | collective-permute-done | bytes 16416 | tf_op jit(solution)/shard_map/ppermute | solution.py:43
  (90 shorter events, 18.5 us)
Async XLA Ops:
  0.6 5.2 %copy-start.4 = (s32[1,1,64]{2,1,0:T(1,128)S(1)}, s32[1,1,64]{2,1,0:T(1,128)}, u32[]{:S(2)}) copy-start(s32[1,1,64]{2,1,0:T(1,128)} %param.25) | copy-start | bytes 772
  0.6 13.1 %copy-start.5 = (s32[1,1,64]{2,1,0:T(1,128)S(1)}, s32[1,1,64]{2,1,0:T(1,128)}, u32[]{:S(2)}) copy-start(s32[1,1,64]{2,1,0:T(1,128)} %param.26) | copy-start | bytes 772
  0.7 19.0 %copy-start = (bf16[1,1,64,128,128]{4,3,2,1,0:T(8,128)(2,1)S(1)}, bf16[1,1,64,128,128]{4,3,2,1,0:T(8,128)(2,1)}, u32[]{:S(2)}) copy-start(bf16[1,1,64,128,128]{4,3,2,1,0:T(8,128)(2,1)} %param.27) | copy-start | bytes 6291460
  0.7 12.5 %copy-start.3 = (s32[1,4]{1,0:T(1,128)S(1)}, s32[1,4]{1,0:T(1,128)}, u32[]{:S(2)}) copy-start(s32[1,4]{1,0:T(1,128)} %param.28) | copy-start | bytes 52
  0.7 19.0 %copy-start.1 = (f32[1,4,128,128]{3,2,1,0:T(8,128)S(1)}, f32[1,4,128,128]{3,2,1,0:T(8,128)}, u32[]{:S(2)}) copy-start(f32[1,4,128,128]{3,2,1,0:T(8,128)} %param.29) | copy-start | bytes 786436
  6.8 12.1 %all-to-all-start = ((f32[4,32,128]{2,1,0:T(8,128)}), f32[4,32,128]{2,1,0:T(8,128)S(1)}, u32[]{:S(2)}, u32[]{:S(2)}) async-start(f32[4,32,128]{2,1,0:T(8,128)} %bitcast.110), calls=%async_computation | async-start | bytes 131072 | tf_op jit(solution)/shard_map/all_to_all | solution.py:63
  20.2 2.1 %collective-permute-start = (f32[128]{0:T(128)S(1)}, f32[128]{0:T(128)S(1)}, u32[]{:S(2)}, u32[]{:S(2)}) collective-permute-start(f32[128]{0:T(128)S(1)} %convolution_bitcast_fusion.2), channel_id=1, source_target_pairs={{0,4},{8,12},{16,20},{24,28},{2,6},{10,14},{18,22},{26,30}} | collective-permute-start | bytes 1544 | tf_op jit(solution)/shard_map/cond/branch_1_fun/ppermute | solution.py:25
  22.3 0.7 collective-permute-start.1
  23.0 0.7 collective-permute-start.2
  23.7 9.4 %collective-permute-start.3 = (f32[128]{0:T(128)S(1)}, f32[128]{0:T(128)S(1)}, u32[]{:S(2)}, u32[]{:S(2)}) collective-permute-start(f32[128]{0:T(128)S(1)} %add.148), channel_id=1, source_target_pairs={{4,0},{12,8},{20,16},{28,24},{6,2},{14,10},{22,18},{30,26}} | collective-permute-start | bytes 1544 | tf_op jit(solution)/shard_map/cond/branch_1_fun/ppermute | solution.py:32
  35.3 2.9 %collective-permute-start.32 = (f32[2,32,128]{2,1,0:T(8,128)S(1)}, f32[2,32,128]{2,1,0:T(8,128)S(1)}, u32[]{:S(2)}, u32[]{:S(2)}) collective-permute-start(f32[2,32,128]{2,1,0:T(8,128)S(1)} %get-tuple-element.176), channel_id=1, source_target_pairs={{0,1},{2,3},{4,5},{6,7},{8,9},{10,11},{12,13},{14,15},{16,17},{18,... | collective-permute-start | bytes 98312 | tf_op jit(solution)/shard_map/ppermute | solution.py:43
  38.2 7.6 %collective-permute-start.33 = (f32[2,32,128]{2,1,0:T(8,128)S(1)}, f32[2,32,128]{2,1,0:T(8,128)S(1)}, u32[]{:S(2)}, u32[]{:S(2)}) collective-permute-start(f32[2,32,128]{2,1,0:T(8,128)S(1)} %get-tuple-element.179), channel_id=1, source_target_pairs={{1,2},{3,0},{5,6},{7,4},{9,10},{11,8},{13,14},{15,12},{17,18},{19,... | collective-permute-start | bytes 98312 | tf_op jit(solution)/shard_map/ppermute | solution.py:43
  45.8 24.2 %collective-permute-start.34 = (f32[2,32,128]{2,1,0:T(8,128)S(1)}, f32[2,32,128]{2,1,0:T(8,128)S(1)}, u32[]{:S(2)}, u32[]{:S(2)}) collective-permute-start(f32[2,32,128]{2,1,0:T(8,128)S(1)} %get-tuple-element.184), channel_id=1, source_target_pairs={{1,2},{3,0},{5,6},{7,4},{9,10},{11,8},{13,14},{15,12},{17,18},{19,... | collective-permute-start | bytes 98312 | tf_op jit(solution)/shard_map/ppermute | solution.py:43
  54.9 2.1 %collective-permute-start.12 = (f32[128]{0:T(128)S(1)}, f32[128]{0:T(128)S(1)}, u32[]{:S(2)}, u32[]{:S(2)}) collective-permute-start(f32[128]{0:T(128)S(1)} %convolution_bitcast_fusion.11), channel_id=1, source_target_pairs={{0,4},{8,12},{16,20},{24,28},{2,6},{10,14},{18,22},{26,30}} | collective-permute-start | bytes 1544 | tf_op jit(solution)/shard_map/cond/branch_1_fun/ppermute | solution.py:25
  57.0 0.7 collective-permute-start.13
  57.7 0.7 collective-permute-start.14
  58.4 9.4 %collective-permute-start.15 = (f32[128]{0:T(128)S(1)}, f32[128]{0:T(128)S(1)}, u32[]{:S(2)}, u32[]{:S(2)}) collective-permute-start(f32[128]{0:T(128)S(1)} %add.163), channel_id=1, source_target_pairs={{4,0},{12,8},{20,16},{28,24},{6,2},{14,10},{22,18},{30,26}} | collective-permute-start | bytes 1544 | tf_op jit(solution)/shard_map/cond/branch_1_fun/ppermute | solution.py:32
  70.0 18.4 %collective-permute-start.35 = (f32[2,32,128]{2,1,0:T(8,128)S(1)}, f32[2,32,128]{2,1,0:T(8,128)S(1)}, u32[]{:S(2)}, u32[]{:S(2)}) collective-permute-start(f32[2,32,128]{2,1,0:T(8,128)S(1)} %get-tuple-element.187), channel_id=1, source_target_pairs={{0,1},{2,3},{4,5},{6,7},{8,9},{10,11},{12,13},{14,15},{16,17},{18,... | collective-permute-start | bytes 98312 | tf_op jit(solution)/shard_map/ppermute | solution.py:43
  72.5 2.9 %collective-permute-start.16 = (f32[128]{0:T(128)S(1)}, f32[128]{0:T(128)S(1)}, u32[]{:S(2)}, u32[]{:S(2)}) collective-permute-start(f32[128]{0:T(128)S(1)} %convolution_bitcast_fusion.14), channel_id=1, source_target_pairs={{0,4},{8,12},{16,20},{24,28},{2,6},{10,14},{18,22},{26,30}} | collective-permute-start | bytes 1544 | tf_op jit(solution)/shard_map/cond/branch_1_fun/ppermute | solution.py:25
  75.4 0.7 collective-permute-start.17
  76.1 0.7 collective-permute-start.18
  76.8 9.4 %collective-permute-start.19 = (f32[128]{0:T(128)S(1)}, f32[128]{0:T(128)S(1)}, u32[]{:S(2)}, u32[]{:S(2)}) collective-permute-start(f32[128]{0:T(128)S(1)} %add.168), channel_id=1, source_target_pairs={{4,0},{12,8},{20,16},{28,24},{6,2},{14,10},{22,18},{30,26}} | collective-permute-start | bytes 1544 | tf_op jit(solution)/shard_map/cond/branch_1_fun/ppermute | solution.py:32
  88.5 2.9 %collective-permute-start.36 = (f32[2,32,128]{2,1,0:T(8,128)S(1)}, f32[2,32,128]{2,1,0:T(8,128)S(1)}, u32[]{:S(2)}, u32[]{:S(2)}) collective-permute-start(f32[2,32,128]{2,1,0:T(8,128)S(1)} %get-tuple-element.192), channel_id=1, source_target_pairs={{0,1},{2,3},{4,5},{6,7},{8,9},{10,11},{12,13},{14,15},{16,17},{18,... | collective-permute-start | bytes 98312 | tf_op jit(solution)/shard_map/ppermute | solution.py:43
  91.3 7.6 %collective-permute-start.37 = (f32[2,32,128]{2,1,0:T(8,128)S(1)}, f32[2,32,128]{2,1,0:T(8,128)S(1)}, u32[]{:S(2)}, u32[]{:S(2)}) collective-permute-start(f32[2,32,128]{2,1,0:T(8,128)S(1)} %get-tuple-element.195), channel_id=1, source_target_pairs={{1,2},{3,0},{5,6},{7,4},{9,10},{11,8},{13,14},{15,12},{17,18},{19,... | collective-permute-start | bytes 98312 | tf_op jit(solution)/shard_map/ppermute | solution.py:43
  99.4 2.1 %collective-permute-start.28 = (f32[128]{0:T(128)S(1)}, f32[128]{0:T(128)S(1)}, u32[]{:S(2)}, u32[]{:S(2)}) collective-permute-start(f32[128]{0:T(128)S(1)} %convolution_bitcast_fusion.23), channel_id=1, source_target_pairs={{0,4},{8,12},{16,20},{24,28},{2,6},{10,14},{18,22},{26,30}} | collective-permute-start | bytes 1544 | tf_op jit(solution)/shard_map/cond/branch_1_fun/ppermute | solution.py:25
  101.5 0.7 collective-permute-start.29
  102.2 0.7 collective-permute-start.30
  102.9 9.4 %collective-permute-start.31 = (f32[128]{0:T(128)S(1)}, f32[128]{0:T(128)S(1)}, u32[]{:S(2)}, u32[]{:S(2)}) collective-permute-start(f32[128]{0:T(128)S(1)} %add.183), channel_id=1, source_target_pairs={{4,0},{12,8},{20,16},{28,24},{6,2},{14,10},{22,18},{30,26}} | collective-permute-start | bytes 1544 | tf_op jit(solution)/shard_map/cond/branch_1_fun/ppermute | solution.py:32
  114.5 3.3 %collective-permute-start.39 = (f32[32,128]{1,0:T(8,128)S(1)}, f32[32,128]{1,0:T(8,128)S(1)}, u32[]{:S(2)}, u32[]{:S(2)}) collective-permute-start(f32[32,128]{1,0:T(8,128)S(1)} %get-tuple-element.200), channel_id=1, source_target_pairs={{0,1},{2,3},{4,5},{6,7},{8,9},{10,11},{12,13},{14,15},{16,17},{18,... | collective-permute-start | bytes 49160 | tf_op jit(solution)/shard_map/ppermute | solution.py:43
  115.8 7.4 %collective-permute-start.38 = (f32[32,128]{1,0:T(8,128)S(1)}, f32[32,128]{1,0:T(8,128)S(1)}, u32[]{:S(2)}, u32[]{:S(2)}) collective-permute-start(f32[32,128]{1,0:T(8,128)S(1)} %get-tuple-element.199), channel_id=1, source_target_pairs={{1,2},{3,0},{5,6},{7,4},{9,10},{11,8},{13,14},{15,12},{17,18},{19,... | collective-permute-start | bytes 49160 | tf_op jit(solution)/shard_map/ppermute | solution.py:43
  117.8 6.0 %copy-start.2 = (f32[512,128]{1,0:T(8,128)}, f32[512,128]{1,0:T(8,128)S(1)}, u32[]{:S(2)}) copy-start(f32[512,128]{1,0:T(8,128)S(1)} %dynamic_update_slice.16) | copy-start | bytes 786436

commit v4 on v0

v4 whole, which is shorter than its diff:
```python
import functools

import jax
import jax.numpy as jnp
from jax import lax
from jax.experimental import pallas as pl
from jax.experimental.pallas import tpu as pltpu
from jax.sharding import PartitionSpec as P

exact_prec = lax.Precision.HIGHEST
l1_penalty = 0.25
chunk = 16

VMEM = pl.BlockSpec(memory_space=pltpu.VMEM)
SMEM = pl.BlockSpec(memory_space=pltpu.SMEM)


def float_of(shape):
    return jax.ShapeDtypeStruct(shape, jnp.float32)


def call(kernel, out_shape, in_specs):
    single = not isinstance(out_shape, tuple)
    return pl.pallas_call(
        kernel,
        out_shape=out_shape,
        in_specs=in_specs,
        out_specs=VMEM if single else tuple(VMEM for _ in out_shape),
        compiler_params=pltpu.CompilerParams(vmem_limit_bytes=24 << 20),
    )


def tile_products(vectors_of, values_ref):
    tiles, edge, _ = values_ref.shape
    sub = lax.broadcasted_iota(jnp.int32, (chunk, edge), 0)
    pieces = []
    for first in range(0, tiles, chunk):
        vectors = vectors_of(first)
        piece = jnp.zeros((chunk, edge), jnp.float32)
        for inner in range(chunk):
            product = lax.dot_general(
                vectors,
                values_ref[first + inner],
                (((1,), (1,)), ((), ())),
                preferred_element_type=jnp.float32,
            )
            piece = jnp.where(sub == inner, product, piece)
        pieces.append(piece)
    return jnp.concatenate(pieces, axis=0)


def margins_kernel(
    cols_smem, targets_smem, rows_ref, cols_ref, beta_ref, values_ref,
    partial_ref, chosen_ref, old_ref, picked_ref,
):
    tiles = cols_smem.shape[0]
    sections = targets_smem.shape[0]
    row_blocks = partial_ref.shape[0]
    group_blocks = chosen_ref.shape[1]
    for tile in range(tiles):
        picked_ref[pl.ds(tile, 1), :] = beta_ref[pl.ds(cols_smem[tile], 1), :]

    def vectors_of(first):
        return picked_ref[pl.ds(first, chunk), :].astype(jnp.bfloat16)

    products = tile_products(vectors_of, values_ref)
    rows = rows_ref[...]
    block_ids = lax.broadcasted_iota(jnp.int32, (row_blocks, tiles), 0)
    placing = (block_ids == rows).astype(jnp.float32)
    partial_ref[...] = jnp.dot(
        placing, products, precision=exact_prec, preferred_element_type=jnp.float32
    )
    my_index = lax.axis_index("feat")
    sub_ids = lax.broadcasted_iota(jnp.int32, (group_blocks, tiles), 0)
    for section in range(sections):
        group = lax.rem(my_index - section + sections, sections)
        hit = (sub_ids + group * group_blocks == rows) & (cols_ref[...] == targets_smem[section])
        chosen_ref[section] = hit.astype(jnp.float32)
        old_ref[pl.ds(section, 1), :] = beta_ref[pl.ds(targets_smem[section], 1), :]


def gradient_part(residual, chosen, values_ref):
    tiles, edge, _ = values_ref.shape
    picked = lax.dot_general(
        chosen.astype(jnp.bfloat16),
        residual.astype(jnp.bfloat16),
        (((0,), (0,)), ((), ())),
        preferred_element_type=jnp.float32,
    )
    sub = lax.broadcasted_iota(jnp.int32, (chunk, edge), 0)
    spread = []
    for tile in range(tiles):
        first = tile - tile % chunk
        kept = jnp.where(sub == tile - first, picked[first : first + chunk], 0.0)
        spread.append(kept.astype(jnp.bfloat16))
    summed = jnp.dot(
        jnp.concatenate(spread, axis=1),
        values_ref[...].reshape(tiles * edge, edge),
        preferred_element_type=jnp.float32,
    )
    return jnp.sum(summed, axis=0, keepdims=True)


def first_kernel(parts_ref, labels_ref, chosen_ref, values_ref, state_ref, grad_ref):
    group_blocks = parts_ref.shape[1]
    start = pl.multiple_of(lax.axis_index("feat") * group_blocks, 8)
    margins = parts_ref[0]
    for part in range(1, parts_ref.shape[0]):
        margins = margins + parts_ref[part]
    probability = 1.0 / (1.0 + jnp.exp(-margins))
    residual = labels_ref[pl.ds(start, group_blocks), :].astype(jnp.float32) - probability
    state_ref[0] = residual
    state_ref[1] = probability * (1.0 - probability)
    grad = gradient_part(residual, chosen_ref[0], values_ref)
    grad_ref[...] = jnp.broadcast_to(grad, grad_ref.shape)


def gradient_kernel(section, state_ref, chosen_ref, values_ref, grad_ref):
    grad = gradient_part(state_ref[0], chosen_ref[section], values_ref)
    grad_ref[...] = jnp.broadcast_to(grad, grad_ref.shape)


def update_kernel(
    section, grads_ref, state_ref, chosen_ref, old_ref, inverses_ref, values_ref,
    moved_ref, shrunk_ref,
):
    edge = grads_ref.shape[1]
    gradient = jnp.sum(grads_ref[...], axis=0, keepdims=True)
    step = lax.dot_general(
        jnp.broadcast_to(gradient, (8, edge)),
        inverses_ref[section],
        (((1,), (1,)), ((), ())),
        precision=exact_prec,
        preferred_element_type=jnp.float32,
    )
    old = old_ref[pl.ds(section, 1), :]
    raised = old + step
    size = jnp.maximum(jnp.abs(raised) - l1_penalty, 0.0)
    shrunk = jnp.where(raised < 0.0, -size, size)
    shrunk_ref[...] = shrunk[0:1]
    change = jnp.broadcast_to((shrunk - old)[0:1], (chunk, edge)).astype(jnp.bfloat16)
    image = tile_products(lambda first: change, values_ref)
    landed = jnp.dot(
        chosen_ref[section], image, precision=exact_prec, preferred_element_type=jnp.float32
    )
    weight = state_ref[1]
    residual = state_ref[0] - weight * landed
    if len(moved_ref.shape) == 3:
        moved_ref[0] = residual
        moved_ref[1] = weight
    else:
        moved_ref[...] = residual


def from_behind(value, axis, steps):
    count = lax.axis_size(axis)
    pairs = [(source, (source + steps) % count) for source in range(count)]
    return lax.ppermute(value, axis, pairs)


def gathered(parts, axis):
    count, edge = parts.shape
    return lax.all_to_all(parts.reshape(count, 1, edge), axis, 0, 0).reshape(count, edge)


def per_device(labels, beta, tile_rows, tile_cols, tile_values, block_order, hess_inv):
    sections = lax.axis_size("feat")
    samp_count = lax.axis_size("samp")
    values = tile_values[0, 0]
    tiles, edge, _ = values.shape
    row_blocks = labels.shape[0] // edge
    group_blocks = row_blocks // sections
    blocks = beta.reshape(-1, edge)
    inverses = hess_inv[0]
    targets = block_order[0]
    partial_sum, chosen, old_blocks = pl.pallas_call(
        margins_kernel,
        out_shape=(
            float_of((row_blocks, edge)),
            float_of((sections, group_blocks, tiles)),
            float_of((sections, edge)),
        ),
        in_specs=[SMEM, SMEM, VMEM, VMEM, VMEM, VMEM],
        out_specs=(VMEM, VMEM, VMEM),
        scratch_shapes=[pltpu.VMEM((tiles, edge), jnp.float32)],
        compiler_params=pltpu.CompilerParams(vmem_limit_bytes=24 << 20),
    )(tile_cols[0, 0], targets, tile_rows[0], tile_cols[0], blocks, values)
    parts = lax.all_to_all(partial_sum.reshape(sections, group_blocks, edge), "feat", 0, 0)
    state, grads = call(
        first_kernel,
        (float_of((2, group_blocks, edge)), float_of((samp_count, edge))),
        [VMEM] * 4,
    )(parts, labels.reshape(row_blocks, edge), chosen, values)
    shrunk_blocks = []
    for section in range(sections):
        final = section + 1 == sections
        moved_shape = (group_blocks, edge) if final else (2, group_blocks, edge)
        moving, shrunk = call(
            functools.partial(update_kernel, section),
            (float_of(moved_shape), float_of((1, edge))),
            [VMEM] * 6,
        )(gathered(grads, "samp"), state, chosen, old_blocks, inverses, values)
        shrunk_blocks.append(shrunk)
        state = from_behind(moving, "feat", 1)
        if not final:
            grads = call(
                functools.partial(gradient_kernel, section + 1),
                float_of((samp_count, edge)),
                [VMEM] * 3,
            )(state, chosen, values)
    block_ids = jnp.arange(blocks.shape[0], dtype=jnp.int32)[:, None]
    for section in range(sections):
        blocks = jnp.where(block_ids == targets[section], shrunk_blocks[section], blocks)
    return (blocks.reshape(-1), state.reshape(-1))


def solution(mesh):
    placed = (
        P("samp"),
        P("feat"),
        P("samp", "feat", None),
        P("samp", "feat", None),
        P("samp", "feat", None, None, None),
        P("feat", None),
        P("feat", None, None, None),
    )
    return jax.shard_map(
        per_device,
        mesh=mesh,
        in_specs=placed,
        out_specs=(P("feat"), P(("samp", "feat"))),
        check_vma=False,
    )
```

time: 138 us -> 83.4 us (0.60)
  blocking collectives: 47.2 us -> 27.1 us
  matrix products: 14.1 us -> 0 us
  between operations: 14.1 us -> 0.72 us
  waiting for transfers between devices: 39.3 us -> 26.4 us
  Pallas kernels: 0 us -> 11.7 us
  loops' own time: 7.97 us -> 0 us
  starting transfers between devices: 4.89 us -> 7.55 us
    psum x4 -> x0, blocking collectives: 47.2 us -> none  [run_section(): gradient = lax.psum(local_grad, 'samp')]
    all_to_all x0 -> x3, blocking collectives: none -> 27.1 us  [the longest x2 15.2 us: gathered(): lax.all_to_all(parts.reshape(count, 1, edge), axis, 0, 0)]
    reduce_scatter x1 -> x0, waiting for transfers between devices: 21.9 us -> none  [per_device(): lax.psum_scatter(partial_sum, 'feat', scatter_dimension=0, tiled=True)]
    dot_general x22 -> x0, matrix products: 14.1 us -> none  [the longest x4 4.12 us: run_section(): moved_block = current + jnp.dot(inverse, gradient, precision=exact_prec)]
    pallas_call x0 -> x9, Pallas kernels: none -> 11.7 us  [the longest x4 6.33 us: per_device(): call(functools.partial(update_kernel, section), (float_of(moved_shape), f...]
    another operation x1 -> x0, loops' own time: 7.97 us -> none  [per_device(): lax.fori_loop(0, cycle_size, run_section, (blocks, residual, weight))]
    all_to_all x0 -> x2, waiting for transfers between devices: none -> 6.98 us  [gathered(): lax.all_to_all(parts.reshape(count, 1, edge), axis, 0, 0)]
    all_to_all x0 -> x2, starting transfers between devices: none -> 6.62 us  [gathered(): lax.all_to_all(parts.reshape(count, 1, edge), axis, 0, 0)]
  transfers between devices with their start and end apart: 9 -> 6, of which waited for: 5 -> 6; matrix products, arithmetic and copies ran while one was open for 11% -> 5% of each run, Pallas kernels for 0% -> 0%
where the time goes in v4:
time: 83.4 us; the launch traced here: 82.9 us
  blocking collectives  27.1 us (32%)
  waiting for transfers between devices  26.4 us (32%)
  Pallas kernels  11.7 us (14%)
  starting transfers between devices  7.55 us (9%)
  local copies, waits for them, and re-layouts  5.8 us (7%)
  other arithmetic  3.64 us (4%)
    ppermute x4, waiting for transfers between devices, from_behind(): return lax.ppermute(value, axis, pairs)  19.5 us
    all_to_all x2, blocking collectives, gathered(): lax.all_to_all(parts.reshape(count, 1, edge), axis, 0, 0)  15.2 us
    all_to_all x1, blocking collectives, per_device(): lax.all_to_all(partial_sum.reshape(sections, group_blocks, edge), 'feat',...  11.9 us
    all_to_all x2, waiting for transfers between devices, gathered(): lax.all_to_all(parts.reshape(count, 1, edge), axis, 0, 0)  6.98 us
    all_to_all x2, starting transfers between devices, gathered(): lax.all_to_all(parts.reshape(count, 1, edge), axis, 0, 0)  6.62 us
    pallas_call x4, Pallas kernels, per_device(): call(functools.partial(update_kernel, section), (float_of(moved_shape), f...  6.33 us
    unnamed x21, local copies, waits for them, and re-layouts  5.13 us
    pallas_call x3, Pallas kernels, per_device(): call(functools.partial(gradient_kernel, section + 1), float_of((samp_coun...  2.84 us
  transfers between devices with their start and end apart: 6, of which 6 were waited for; matrix products, arithmetic and copies ran while one was open for 5% of the time, Pallas kernels for 0%

profile of v4, /device:TPU:0, one launch (start us, length us, event | category | flops | bytes accessed | tf_op | source)
XLA Modules:
  0.0 82.9 jit_solution(15563064716508289970)
XLA Ops:
  0.6 0.0 copy-start
  0.6 1.6 %copy-done = bf16[1,1,64,128,128]{4,3,2,1,0:T(8,128)(2,1)S(1)} copy-done((bf16[1,1,64,128,128]{4,3,2,1,0:T(8,128)(2,1)S(1)}, bf16[1,1,64,128,128]{4,3,2,1,0:T(8,128)(2,1)}, u32[]{:S(2)}) %copy-start) | copy-done | bytes 2097176
  2.2 0.0 copy-start.3
  2.2 0.9 %copy-done.3 = f32[65536]{0:T(1024)S(1)} copy-done((f32[65536]{0:T(1024)S(1)}, f32[65536]{0:T(1024)}, u32[]{:S(2)}) %copy-start.3) | copy-done | bytes 262168
  3.2 0.0 copy-start.6
  3.2 0.7 copy-done.6
  3.8 0.0 copy-start.8
  3.8 0.7 copy-done.8
  4.5 0.0 copy-start.9
  4.5 0.7 copy-done.9
  5.1 0.0 copy-start.1
  5.1 0.0 copy-start.5
  5.1 0.0 copy-start.2
  5.1 2.0 %shard_map.86 = (f32[128,128]{1,0:T(8,128)S(1)}, f32[4,32,64]{2,1,0:T(8,128)S(1)}, f32[4,128]{1,0:T(4,128)S(1)}) custom-call(s32[64]{0:T(128)S(1)} %bitcast.79, s32[4]{0:T(128)S(1)} %bitcast.77, s32[1,64]{1,0:T(1,128)S(1)} %bitcast.85, s32[1,64]{1,0:T(1,128)S(1)} %bitcast.80, f32[512,128]{1,0:T(8,128)S(1)} %bitcast.69, bf16[64,128,128]{2,1,0:T(8,128)(2,1)S(1)} %bitcast.56), custom_call_target="tpu_custom_call" | custom-call | tf_op jit(solution)/shard_map/pallas_call | solution.py:176
  7.2 11.9 %all_to_all.25.parts_ref = f32[4,32,128]{2,1,0:T(8,128)S(1)} all-to-all(f32[4,32,128]{2,1,0:T(8,128)S(1)} %bitcast.71), channel_id=1, replica_groups=mesh['samp'=8,'feat'=4] {'feat'}, dimensions={0} | all-to-all | bytes 131072 | tf_op jit(solution)/shard_map/all_to_all | solution.py:188
  19.0 0.0 copy-done.1
  19.0 0.0 copy-done.5
  19.0 0.5 shard_map.87
  19.6 8.2 %all_to_all.26 = f32[8,1,128]{2,1,0:T(1,128)S(1)} all-to-all(f32[8,1,128]{2,1,0:T(1,128)S(1)} %bitcast.78), channel_id=1, replica_groups=mesh['samp'=8,'feat'=4] {'samp'}, dimensions={0} | all-to-all | bytes 8192 | tf_op jit(solution)/shard_map/all_to_all | solution.py:163
  27.7 0.0 copy-done.2
  27.7 1.6 %shard_map.88 = (f32[2,32,128]{2,1,0:T(8,128)S(1)}, f32[1,128]{1,0:T(1,128)S(1)}) custom-call(f32[8,128]{1,0:T(8,128)S(1)} %bitcast.74, f32[2,32,128]{2,1,0:T(8,128)S(1)} %get-tuple-element.18.state_ref, f32[4,32,64]{2,1,0:T(8,128)S(1)} %get-tuple-element.16.chosen_ref, f32[4,128]{1,0:T(4,128)S(1)} %get-tuple-element.19.old_ref, ...), custom_call_target="tpu_custom_call" | custom-call | tf_op jit(solution)/shard_map/pallas_call | solution.py:198
  29.3 0.9 %collective-permute-start = (f32[2,32,128]{2,1,0:T(8,128)S(1)}, f32[2,32,128]{2,1,0:T(8,128)S(1)}, u32[]{:S(2)}, u32[]{:S(2)}) collective-permute-start(f32[2,32,128]{2,1,0:T(8,128)S(1)} %get-tuple-element.20), channel_id=1, source_target_pairs={{0,1},{1,2},{2,3},{3,0},{4,5},{5,6},{6,7},{7,4},{8,9},{9,10},{10,1... | collective-permute-start | bytes 98312 | tf_op jit(solution)/shard_map/ppermute | solution.py:158
  30.3 4.8 %collective-permute-done.state_ref = f32[2,32,128]{2,1,0:T(8,128)S(1)} collective-permute-done((f32[2,32,128]{2,1,0:T(8,128)S(1)}, f32[2,32,128]{2,1,0:T(8,128)S(1)}, u32[]{:S(2)}, u32[]{:S(2)}) %collective-permute-start) | collective-permute-done | bytes 32800 | tf_op jit(solution)/shard_map/ppermute | solution.py:158
  35.1 0.5 shard_map.89
  35.6 7.0 %all_to_all.27 = f32[8,1,128]{2,1,0:T(1,128)S(1)} all-to-all(f32[8,1,128]{2,1,0:T(1,128)S(1)} %bitcast.76), channel_id=1, replica_groups=mesh['samp'=8,'feat'=4] {'samp'}, dimensions={0} | all-to-all | bytes 8192 | tf_op jit(solution)/shard_map/all_to_all | solution.py:163
  42.6 1.6 %shard_map.90 = (f32[2,32,128]{2,1,0:T(8,128)S(1)}, f32[1,128]{1,0:T(1,128)S(1)}) custom-call(f32[8,128]{1,0:T(8,128)S(1)} %bitcast.75, f32[2,32,128]{2,1,0:T(8,128)S(1)} %collective-permute-done.state_ref, f32[4,32,64]{2,1,0:T(8,128)S(1)} %get-tuple-element.16.chosen_ref, f32[4,128]{1,0:T(4,128)S(1)} %get-tuple-element.19.old_ref, ...), custom_call_target="tpu_custom_call" | custom-call | tf_op jit(solution)/shard_map/pallas_call | solution.py:198
  44.2 0.0 collective-permute-start.1
  44.2 5.7 %collective-permute-done.1.state_ref = f32[2,32,128]{2,1,0:T(8,128)S(1)} collective-permute-done((f32[2,32,128]{2,1,0:T(8,128)S(1)}, f32[2,32,128]{2,1,0:T(8,128)S(1)}, u32[]{:S(2)}, u32[]{:S(2)}) %collective-permute-start.1) | collective-permute-done | bytes 32800 | tf_op jit(solution)/shard_map/ppermute | solution.py:158
  49.9 1.1 %shard_map.91 = f32[8,128]{1,0:T(8,128)} custom-call(f32[2,32,128]{2,1,0:T(8,128)S(1)} %collective-permute-done.1.state_ref, f32[4,32,64]{2,1,0:T(8,128)S(1)} %get-tuple-element.16.chosen_ref, bf16[64,128,128]{2,1,0:T(8,128)(2,1)S(1)} %bitcast.61), custom_call_target="tpu_custom_call" | custom-call | tf_op jit(solution)/shard_map/pallas_call | solution.py:206
  51.1 3.3 %all-to-all-start.3 = ((f32[8,1,128]{2,1,0:T(1,128)}), f32[8,1,128]{2,1,0:T(1,128)S(1)}, u32[]{:S(2)}, u32[]{:S(2)}) async-start(f32[8,1,128]{2,1,0:T(1,128)} %bitcast.18), calls=%async_computation.3 | async-start | bytes 8192 | tf_op jit(solution)/shard_map/all_to_all | solution.py:163
  54.4 0.0 copy-done.7
  54.4 0.7 fusion.3
  55.1 3.8 %all-to-all-done.3 = f32[8,1,128]{2,1,0:T(1,128)S(1)} async-done(((f32[8,1,128]{2,1,0:T(1,128)}), f32[8,1,128]{2,1,0:T(1,128)S(1)}, u32[]{:S(2)}, u32[]{:S(2)}) %all-to-all-start.3) | async-done | bytes 4128 | tf_op jit(solution)/shard_map/all_to_all | solution.py:163
  58.9 1.6 %shard_map.92 = (f32[2,32,128]{2,1,0:T(8,128)S(1)}, f32[1,128]{1,0:T(1,128)S(1)}) custom-call(f32[8,128]{1,0:T(8,128)S(1)} %bitcast.73, f32[2,32,128]{2,1,0:T(8,128)S(1)} %collective-permute-done.1.state_ref, f32[4,32,64]{2,1,0:T(8,128)S(1)} %get-tuple-element.16.chosen_ref, f32[4,128]{1,0:T(4,128)S(1)} %get-tuple-element.19.old_ref, ...), custom_call_target="tpu_custom_call" | custom-call | tf_op jit(solution)/shard_map/pallas_call | solution.py:198
  60.5 0.0 collective-permute-start.2
  60.5 1.2 %iota_compare_fusion.2 = (pred[512]{0:T(512)(128)(4,1)S(1)}, pred[512]{0:T(512)(128)(4,1)S(1)}) fusion(s32[]{:T(128)} %bitcast.25, s32[]{:T(128)} %bitcast), kind=kLoop, calls=%fused_computation.6 | loop fusion | flops 1024 | bytes 1032 | tf_op jit(solution)/shard_map/eq | solution.py:213
  61.7 0.0 copy-start.4
  61.8 4.5 %collective-permute-done.2.state_ref = f32[2,32,128]{2,1,0:T(8,128)S(1)} collective-permute-done((f32[2,32,128]{2,1,0:T(8,128)S(1)}, f32[2,32,128]{2,1,0:T(8,128)S(1)}, u32[]{:S(2)}, u32[]{:S(2)}) %collective-permute-start.2) | collective-permute-done | bytes 32800 | tf_op jit(solution)/shard_map/ppermute | solution.py:158
  66.2 1.1 %shard_map.93 = f32[8,128]{1,0:T(8,128)} custom-call(f32[2,32,128]{2,1,0:T(8,128)S(1)} %collective-permute-done.2.state_ref, f32[4,32,64]{2,1,0:T(8,128)S(1)} %get-tuple-element.16.chosen_ref, bf16[64,128,128]{2,1,0:T(8,128)(2,1)S(1)} %bitcast.63), custom_call_target="tpu_custom_call" | custom-call | tf_op jit(solution)/shard_map/pallas_call | solution.py:206
  67.4 3.3 %all-to-all-start.4 = ((f32[8,1,128]{2,1,0:T(1,128)}), f32[8,1,128]{2,1,0:T(1,128)S(1)}, u32[]{:S(2)}, u32[]{:S(2)}) async-start(f32[8,1,128]{2,1,0:T(1,128)} %bitcast.21), calls=%async_computation.4 | async-start | bytes 8192 | tf_op jit(solution)/shard_map/all_to_all | solution.py:163
  70.7 1.4 %iota_compare_fusion = (pred[512]{0:T(512)(128)(4,1)S(1)}, pred[512]{0:T(512)(128)(4,1)S(1)}) fusion(s32[]{:T(128)} %bitcast.33, s32[]{:T(128)} %bitcast.29), kind=kLoop, calls=%fused_computation.4 | loop fusion | flops 1024 | bytes 1032 | tf_op jit(solution)/shard_map/eq | solution.py:213
  72.1 3.1 %all-to-all-done.4 = f32[8,1,128]{2,1,0:T(1,128)S(1)} async-done(((f32[8,1,128]{2,1,0:T(1,128)}), f32[8,1,128]{2,1,0:T(1,128)S(1)}, u32[]{:S(2)}, u32[]{:S(2)}) %all-to-all-start.4) | async-done | bytes 4128 | tf_op jit(solution)/shard_map/all_to_all | solution.py:163
  75.2 1.6 %shard_map.94 = (f32[32,128]{1,0:T(8,128)S(1)}, f32[1,128]{1,0:T(1,128)S(1)}) custom-call(f32[8,128]{1,0:T(8,128)S(1)} %bitcast.72, f32[2,32,128]{2,1,0:T(8,128)S(1)} %collective-permute-done.2.state_ref, f32[4,32,64]{2,1,0:T(8,128)S(1)} %get-tuple-element.16.chosen_ref, f32[4,128]{1,0:T(4,128)S(1)} %get-tuple-element.19.old_ref, ...), custom_call_target="tpu_custom_call" | custom-call | tf_op jit(solution)/shard_map/pallas_call | solution.py:198
  76.8 0.0 collective-permute-start.3
  76.8 0.0 copy-done.4
  76.8 1.0 %fusion.2 = f32[65536]{0:T(1024)} fusion(f32[65536]{0:T(1024)S(1)} %copy-done.4, f32[128]{0:T(128)S(1)} %bitcast.81, f32[128]{0:T(128)S(1)} %bitcast.82, f32[128]{0:T(128)S(1)} %bitcast.83, f32[128]{0:T(128)S(1)} %bitcast.84, pred[512]{0:T(512)(128)(4,1)S(1)} %get-tuple-element.32, pred[512]{0:T(512)(128)(4,1)S(1)} %get-tuple-element.33, ...), kind=kLoop, calls=%fused_computation.3 | loop fusion | flops 262144 | bytes 528384 | tf_op jit(solution)/shard_map/jit(_where)/select_n | solution.py:213
  77.8 4.5 %collective-permute-done.3 = f32[32,128]{1,0:T(8,128)S(1)} collective-permute-done((f32[32,128]{1,0:T(8,128)S(1)}, f32[32,128]{1,0:T(8,128)S(1)}, u32[]{:S(2)}, u32[]{:S(2)}) %collective-permute-start.3) | collective-permute-done | bytes 16416 | tf_op jit(solution)/shard_map/ppermute | solution.py:158
  82.3 0.6 copy.14
  (1 shorter events, 0.0 us)
Async XLA Ops:
  0.6 1.6 %copy-start = (bf16[1,1,64,128,128]{4,3,2,1,0:T(8,128)(2,1)S(1)}, bf16[1,1,64,128,128]{4,3,2,1,0:T(8,128)(2,1)}, u32[]{:S(2)}) copy-start(bf16[1,1,64,128,128]{4,3,2,1,0:T(8,128)(2,1)} %param.11) | copy-start | bytes 6291460
  2.2 0.9 %copy-start.3 = (f32[65536]{0:T(1024)S(1)}, f32[65536]{0:T(1024)}, u32[]{:S(2)}) copy-start(f32[65536]{0:T(1024)} %param.8) | copy-start | bytes 786436
  3.2 0.7 copy-start.6
  3.8 0.7 copy-start.8
  4.5 0.7 copy-start.9
  5.1 13.9 %copy-start.1 = (bf16[1,1,64,128,128]{4,3,2,1,0:T(8,128)(2,1)S(1)}, bf16[1,1,64,128,128]{4,3,2,1,0:T(8,128)(2,1)}, u32[]{:S(2)}) copy-start(bf16[1,1,64,128,128]{4,3,2,1,0:T(8,128)(2,1)} %param.11) | copy-start | bytes 6291460
  5.1 13.9 %copy-start.5 = (s32[16384]{0:T(1024)S(1)}, s32[16384]{0:T(1024)}, u32[]{:S(2)}) copy-start(s32[16384]{0:T(1024)} %param.7) | copy-start | bytes 196612
  5.1 22.6 %copy-start.2 = (f32[1,4,128,128]{3,2,1,0:T(8,128)S(1)}, f32[1,4,128,128]{3,2,1,0:T(8,128)}, u32[]{:S(2)}) copy-start(f32[1,4,128,128]{3,2,1,0:T(8,128)} %param.13) | copy-start | bytes 786436
  29.3 5.7 %collective-permute-start = (f32[2,32,128]{2,1,0:T(8,128)S(1)}, f32[2,32,128]{2,1,0:T(8,128)S(1)}, u32[]{:S(2)}, u32[]{:S(2)}) collective-permute-start(f32[2,32,128]{2,1,0:T(8,128)S(1)} %get-tuple-element.20), channel_id=1, source_target_pairs={{0,1},{1,2},{2,3},{3,0},{4,5},{5,6},{6,7},{7,4},{8,9},{9,10},{10,1... | collective-permute-start | bytes 98312 | tf_op jit(solution)/shard_map/ppermute | solution.py:158
  42.6 11.8 %copy-start.7 = (s32[1,4]{1,0:T(1,128)S(1)}, s32[1,4]{1,0:T(1,128)}, u32[]{:S(2)}) copy-start(s32[1,4]{1,0:T(1,128)} %param.12) | copy-start | bytes 52
  44.2 5.7 %collective-permute-start.1 = (f32[2,32,128]{2,1,0:T(8,128)S(1)}, f32[2,32,128]{2,1,0:T(8,128)S(1)}, u32[]{:S(2)}, u32[]{:S(2)}) collective-permute-start(f32[2,32,128]{2,1,0:T(8,128)S(1)} %get-tuple-element.21), channel_id=1, source_target_pairs={{0,1},{1,2},{2,3},{3,0},{4,5},{5,6},{6,7},{7,4},{8,9},{9,10},{10,1... | collective-permute-start | bytes 98312 | tf_op jit(solution)/shard_map/ppermute | solution.py:158
  51.1 7.8 %all-to-all-start.3 = ((f32[8,1,128]{2,1,0:T(1,128)}), f32[8,1,128]{2,1,0:T(1,128)S(1)}, u32[]{:S(2)}, u32[]{:S(2)}) async-start(f32[8,1,128]{2,1,0:T(1,128)} %bitcast.18), calls=%async_computation.3 | async-start | bytes 8192 | tf_op jit(solution)/shard_map/all_to_all | solution.py:163
  60.5 5.7 %collective-permute-start.2 = (f32[2,32,128]{2,1,0:T(8,128)S(1)}, f32[2,32,128]{2,1,0:T(8,128)S(1)}, u32[]{:S(2)}, u32[]{:S(2)}) collective-permute-start(f32[2,32,128]{2,1,0:T(8,128)S(1)} %get-tuple-element.22), channel_id=1, source_target_pairs={{0,1},{1,2},{2,3},{3,0},{4,5},{5,6},{6,7},{7,4},{8,9},{9,10},{10,1... | collective-permute-start | bytes 98312 | tf_op jit(solution)/shard_map/ppermute | solution.py:158
  61.7 15.1 %copy-start.4 = (f32[65536]{0:T(1024)S(1)}, f32[65536]{0:T(1024)}, u32[]{:S(2)}) copy-start(f32[65536]{0:T(1024)} %param.8) | copy-start | bytes 786436
  67.4 7.8 %all-to-all-start.4 = ((f32[8,1,128]{2,1,0:T(1,128)}), f32[8,1,128]{2,1,0:T(1,128)S(1)}, u32[]{:S(2)}, u32[]{:S(2)}) async-start(f32[8,1,128]{2,1,0:T(1,128)} %bitcast.21), calls=%async_computation.4 | async-start | bytes 8192 | tf_op jit(solution)/shard_map/all_to_all | solution.py:163
  76.8 5.5 %collective-permute-start.3 = (f32[32,128]{1,0:T(8,128)S(1)}, f32[32,128]{1,0:T(8,128)S(1)}, u32[]{:S(2)}, u32[]{:S(2)}) collective-permute-start(f32[32,128]{1,0:T(8,128)S(1)} %get-tuple-element.27), channel_id=1, source_target_pairs={{0,1},{1,2},{2,3},{3,0},{4,5},{5,6},{6,7},{7,4},{8,9},{9,10},{10,1... | collective-permute-start | bytes 49160 | tf_op jit(solution)/shard_map/ppermute | solution.py:158

commit v5 on v4

v5 whole, which is shorter than its diff:
```python
import functools

import jax
import jax.numpy as jnp
from jax import lax
from jax.experimental import pallas as pl
from jax.experimental.pallas import tpu as pltpu
from jax.sharding import PartitionSpec as P

exact_prec = lax.Precision.HIGHEST
l1_penalty = 0.25
chunk = 16

VMEM = pl.BlockSpec(memory_space=pltpu.VMEM)
SMEM = pl.BlockSpec(memory_space=pltpu.SMEM)
HBM = pl.BlockSpec(memory_space=pltpu.HBM)


def float_of(shape):
    return jax.ShapeDtypeStruct(shape, jnp.float32)


def call(kernel, out_shape, in_specs):
    single = not isinstance(out_shape, tuple)
    return pl.pallas_call(
        kernel,
        out_shape=out_shape,
        in_specs=in_specs,
        out_specs=VMEM if single else tuple(VMEM for _ in out_shape),
        compiler_params=pltpu.CompilerParams(vmem_limit_bytes=24 << 20),
    )


def tile_products(vectors_of, tiles_of, tiles):
    pieces = []
    for first in range(0, tiles, chunk):
        vectors = vectors_of(first)
        edge = vectors.shape[1]
        products = lax.dot_general(
            vectors,
            tiles_of(first).reshape(chunk * edge, edge),
            (((1,), (1,)), ((), ())),
            preferred_element_type=jnp.float32,
        )
        sub = lax.broadcasted_iota(jnp.int32, (chunk, edge), 0)
        piece = products[:, :edge]
        for inner in range(1, chunk):
            piece = jnp.where(sub == inner, products[:, inner * edge : (inner + 1) * edge], piece)
        pieces.append(piece)
    return jnp.concatenate(pieces, axis=0)


def placed_sum(chosen, rows):
    high = rows.astype(jnp.bfloat16)
    rest = rows - high.astype(jnp.float32)
    middle = rest.astype(jnp.bfloat16)
    low = (rest - middle.astype(jnp.float32)).astype(jnp.bfloat16)
    ones = chosen.astype(jnp.bfloat16)
    return sum(
        jnp.dot(ones, part, preferred_element_type=jnp.float32) for part in (low, middle, high)
    )


def margins_kernel(
    cols_hbm, targets_hbm, rows_hbm, beta_hbm, values_hbm, partial_ref, old_ref,
    picked_ref, beta_ref, rows_ref, values_ref, cols_smem, targets_smem, small_sem, tile_sem,
):
    tiles = cols_smem.shape[1]
    sections = targets_smem.shape[1]
    row_blocks = partial_ref.shape[0]
    small = [
        pltpu.make_async_copy(cols_hbm, cols_smem, small_sem.at[0]),
        pltpu.make_async_copy(beta_hbm, beta_ref, small_sem.at[1]),
        pltpu.make_async_copy(targets_hbm, targets_smem, small_sem.at[2]),
        pltpu.make_async_copy(rows_hbm, rows_ref, small_sem.at[3]),
    ]
    large = [
        pltpu.make_async_copy(
            values_hbm.at[pl.ds(first, chunk)],
            values_ref.at[pl.ds(first, chunk)],
            tile_sem.at[first // chunk],
        )
        for first in range(0, tiles, chunk)
    ]
    for copy in small + large:
        copy.start()
    for copy in small:
        copy.wait()
    for tile in range(tiles):
        picked_ref[pl.ds(tile, 1), :] = beta_ref[pl.ds(cols_smem[0, tile], 1), :]
    for section in range(sections):
        old_ref[pl.ds(section, 1), :] = beta_ref[pl.ds(targets_smem[0, section], 1), :]

    def tiles_of(first):
        large[first // chunk].wait()
        return values_ref[pl.ds(first, chunk)]

    products = tile_products(
        lambda first: picked_ref[pl.ds(first, chunk), :].astype(jnp.bfloat16), tiles_of, tiles
    )
    block_ids = lax.broadcasted_iota(jnp.int32, (row_blocks, tiles), 0)
    placing = (block_ids == rows_ref[...]).astype(jnp.float32)
    partial_ref[...] = placed_sum(placing, products)


def gradient_part(residual, chosen, values_ref):
    tiles, edge, _ = values_ref.shape
    picked = lax.dot_general(
        chosen.astype(jnp.bfloat16),
        residual.astype(jnp.bfloat16),
        (((0,), (0,)), ((), ())),
        preferred_element_type=jnp.float32,
    )
    sub = lax.broadcasted_iota(jnp.int32, (chunk, edge), 0)
    spread = []
    for tile in range(tiles):
        first = tile - tile % chunk
        kept = jnp.where(sub == tile - first, picked[first : first + chunk], 0.0)
        spread.append(kept.astype(jnp.bfloat16))
    summed = jnp.dot(
        jnp.concatenate(spread, axis=1),
        values_ref[...].reshape(tiles * edge, edge),
        preferred_element_type=jnp.float32,
    )
    return jnp.sum(summed, axis=0, keepdims=True)


def first_kernel(
    parts_ref, labels_ref, rows_ref, cols_ref, targets_ref, values_ref,
    state_ref, grad_ref, chosen_ref,
):
    sections, group_blocks, _ = parts_ref.shape
    my_index = lax.axis_index("feat")
    sub_ids = lax.broadcasted_iota(jnp.int32, chosen_ref.shape[1:], 0)
    for section in range(sections):
        group = lax.rem(my_index - section + sections, sections)
        same_row = sub_ids + group * group_blocks == rows_ref[...]
        same_col = cols_ref[...] == targets_ref[:, section : section + 1]
        chosen_ref[section] = (same_row & same_col).astype(jnp.float32)
    start = pl.multiple_of(my_index * group_blocks, 8)
    margins = parts_ref[0]
    for part in range(1, parts_ref.shape[0]):
        margins = margins + parts_ref[part]
    probability = 1.0 / (1.0 + jnp.exp(-margins))
    residual = labels_ref[pl.ds(start, group_blocks), :].astype(jnp.float32) - probability
    state_ref[0] = residual
    state_ref[1] = probability * (1.0 - probability)
    grad = gradient_part(residual, chosen_ref[0], values_ref)
    grad_ref[...] = jnp.broadcast_to(grad, grad_ref.shape)


def gradient_kernel(section, state_ref, chosen_ref, values_ref, grad_ref):
    grad = gradient_part(state_ref[0], chosen_ref[section], values_ref)
    grad_ref[...] = jnp.broadcast_to(grad, grad_ref.shape)


def update_kernel(
    section, grads_ref, state_ref, chosen_ref, old_ref, inverses_ref, values_ref,
    moved_ref, shrunk_ref,
):
    tiles, edge, _ = values_ref.shape
    gradient = jnp.sum(grads_ref[...], axis=0, keepdims=True)
    step = jnp.sum(inverses_ref[section] * gradient, axis=1, keepdims=True)
    square = (edge, edge)
    on_diagonal = lax.broadcasted_iota(jnp.int32, square, 0) == lax.broadcasted_iota(
        jnp.int32, square, 1
    )
    step = jnp.sum(jnp.where(on_diagonal, step, 0.0), axis=0, keepdims=True)
    old = old_ref[pl.ds(section, 1), :]
    raised = old + step
    size = jnp.maximum(jnp.abs(raised) - l1_penalty, 0.0)
    shrunk = jnp.where(raised < 0.0, -size, size)
    shrunk_ref[...] = shrunk
    change = jnp.broadcast_to(shrunk - old, (chunk, edge)).astype(jnp.bfloat16)
    image = tile_products(
        lambda first: change, lambda first: values_ref[pl.ds(first, chunk)], tiles
    )
    landed = placed_sum(chosen_ref[section], image)
    weight = state_ref[1]
    residual = state_ref[0] - weight * landed
    if len(moved_ref.shape) == 3:
        moved_ref[0] = residual
        moved_ref[1] = weight
    else:
        moved_ref[...] = residual


def blocks_kernel(sections, targets_smem, beta_ref, *refs):
    blocks_ref = refs[sections]
    blocks_ref[...] = beta_ref[...]
    for section in range(sections):
        blocks_ref[pl.ds(targets_smem[0, section], 1), :] = refs[section][...]


def from_behind(value, axis, steps):
    count = lax.axis_size(axis)
    pairs = [(source, (source + steps) % count) for source in range(count)]
    return lax.ppermute(value, axis, pairs)


def gathered(parts, axis):
    count, edge = parts.shape
    return lax.all_to_all(parts.reshape(count, 1, edge), axis, 0, 0).reshape(count, edge)


def per_device(labels, beta, tile_rows, tile_cols, tile_values, block_order, hess_inv):
    sections = lax.axis_size("feat")
    samp_count = lax.axis_size("samp")
    tiles, edge = tile_values.shape[2], tile_values.shape[4]
    row_blocks = labels.shape[0] // edge
    group_blocks = row_blocks // sections
    blocks = beta.reshape(-1, edge)
    inverses = hess_inv[0]
    values = tile_values[0, 0]
    partial_sum, old_blocks = pl.pallas_call(
        margins_kernel,
        out_shape=(float_of((row_blocks, edge)), float_of((sections, edge))),
        in_specs=[HBM] * 5,
        out_specs=(VMEM, VMEM),
        scratch_shapes=[
            pltpu.VMEM((tiles, edge), jnp.float32),
            pltpu.VMEM(blocks.shape, jnp.float32),
            pltpu.VMEM((1, tiles), jnp.int32),
            pltpu.VMEM(values.shape, jnp.bfloat16),
            pltpu.SMEM((1, tiles), jnp.int32),
            pltpu.SMEM((1, sections), jnp.int32),
            pltpu.SemaphoreType.DMA((4,)),
            pltpu.SemaphoreType.DMA((tiles // chunk,)),
        ],
        compiler_params=pltpu.CompilerParams(vmem_limit_bytes=58 << 20),
    )(tile_cols[0], block_order, tile_rows[0], blocks, values)
    parts = lax.all_to_all(partial_sum.reshape(sections, group_blocks, edge), "feat", 0, 0)
    state, grads, chosen = call(
        first_kernel,
        (
            float_of((2, group_blocks, edge)),
            float_of((samp_count, edge)),
            float_of((sections, group_blocks, tiles)),
        ),
        [VMEM] * 6,
    )(parts, labels.reshape(row_blocks, edge), tile_rows[0], tile_cols[0], block_order, values)
    shrunk_blocks = []
    for section in range(sections):
        final = section + 1 == sections
        moved_shape = (group_blocks, edge) if final else (2, group_blocks, edge)
        moving, shrunk = call(
            functools.partial(update_kernel, section),
            (float_of(moved_shape), float_of((1, edge))),
            [VMEM] * 6,
        )(gathered(grads, "samp"), state, chosen, old_blocks, inverses, values)
        shrunk_blocks.append(shrunk)
        state = from_behind(moving, "feat", 1)
        if not final:
            grads = call(
                functools.partial(gradient_kernel, section + 1),
                float_of((samp_count, edge)),
                [VMEM] * 3,
            )(state, chosen, values)
    blocks = call(
        functools.partial(blocks_kernel, sections),
        float_of(blocks.shape),
        [SMEM] + [VMEM] * (1 + sections),
    )(block_order, blocks, *shrunk_blocks)
    return (blocks.reshape(-1), state.reshape(-1))


def solution(mesh):
    placed = (
        P("samp"),
        P("feat"),
        P("samp", "feat", None),
        P("samp", "feat", None),
        P("samp", "feat", None, None, None),
        P("feat", None),
        P("feat", None, None, None),
    )
    return jax.shard_map(
        per_device,
        mesh=mesh,
        in_specs=placed,
        out_specs=(P("feat"), P(("samp", "feat"))),
        check_vma=False,
    )
```

time: 83.4 us -> 74.9 us (0.90)
  blocking collectives: 27.1 us -> 41.3 us
  starting transfers between devices: 7.55 us -> 1.02 us
  waiting for transfers between devices: 26.4 us -> 20.5 us
  local copies, waits for them, and re-layouts: 5.8 us -> 0.65 us
  other arithmetic: 3.64 us -> 0 us
  Pallas kernels: 11.7 us -> 10.3 us
    all_to_all x2 -> x4, blocking collectives: 15.2 us -> 29.3 us  [gathered(): lax.all_to_all(parts.reshape(count, 1, edge), axis, 0, 0)]
    all_to_all x2 -> x0, waiting for transfers between devices: 6.98 us -> none  [gathered(): lax.all_to_all(parts.reshape(count, 1, edge), axis, 0, 0)]
    all_to_all x2 -> x0, starting transfers between devices: 6.62 us -> none  [gathered(): lax.all_to_all(parts.reshape(count, 1, edge), axis, 0, 0)]
    unnamed x21 -> x17, local copies, waits for them, and re-layouts: 5.13 us -> 0.65 us
    pallas_call x4, Pallas kernels: 6.33 us -> 3.43 us  [per_device(): call(functools.partial(update_kernel, section), (float_of(moved_shape), f...]
    eq x2 -> x0, other arithmetic: 2.6 us -> none  [per_device(): block_ids == targets[section]]
    pallas_call x1, Pallas kernels: 1.99 us -> 3.32 us  [per_device(): pl.pallas_call(margins_kernel, out_shape=(float_of((row_blocks, edge)), f...]
    pallas_call x0 -> x1, Pallas kernels: none -> 1.26 us  [per_device(): call(functools.partial(blocks_kernel, sections), float_of(blocks.shape),...]
  transfers between devices with their start and end apart: 6 -> 4, of which waited for: 6 -> 4; matrix products, arithmetic and copies ran while one was open for 5% -> 0% of each run, Pallas kernels for 0% -> 2%
where the time goes in v5:
time: 74.9 us; the launch traced here: 74.5 us
  blocking collectives  41.3 us (55%)
  waiting for transfers between devices  20.5 us (27%)
  Pallas kernels  10.3 us (14%)
  starting transfers between devices  1.02 us (1%)
  between operations  0.77 us (1%)
    all_to_all x4, blocking collectives, gathered(): lax.all_to_all(parts.reshape(count, 1, edge), axis, 0, 0)  29.3 us
    ppermute x4, waiting for transfers between devices, from_behind(): return lax.ppermute(value, axis, pairs)  20.5 us
    all_to_all x1, blocking collectives, per_device(): lax.all_to_all(partial_sum.reshape(sections, group_blocks, edge), 'feat',...  12.1 us
    pallas_call x4, Pallas kernels, per_device(): call(functools.partial(update_kernel, section), (float_of(moved_shape), f...  3.43 us
    pallas_call x1, Pallas kernels, per_device(): pl.pallas_call(margins_kernel, out_shape=(float_of((row_blocks, edge)), f...  3.32 us
    pallas_call x3, Pallas kernels, per_device(): call(functools.partial(gradient_kernel, section + 1), float_of((samp_coun...  1.63 us
  transfers between devices with their start and end apart: 4, of which 4 were waited for; matrix products, arithmetic and copies ran while one was open for 0% of the time, Pallas kernels for 2%

profile of v5, /device:TPU:0, one launch (start us, length us, event | category | flops | bytes accessed | tf_op | source)
XLA Modules:
  0.0 74.5 jit_solution(9741022795264634897)
XLA Ops:
  0.6 0.0 copy-start.5
  0.6 0.0 copy-start
  0.7 0.0 copy-start.6
  0.7 0.0 copy-start.7
  0.7 0.0 copy-start.3
  0.7 0.0 copy-start.1
  0.7 3.3 %shard_map.86 = (f32[128,128]{1,0:T(8,128)}, f32[4,128]{1,0:T(4,128)}) custom-call(s32[1,64]{1,0:T(1,128)} %bitcast.49, s32[1,4]{1,0:T(1,128)} %targets_smem.1, s32[1,64]{1,0:T(1,128)} %bitcast.51, f32[512,128]{1,0:T(8,128)} %bitcast.38, bf16[64,128,128]{2,1,0:T(8,128)(2,1)} %bitcast.25), custom_call_target="tpu_custom_call" | custom-call | tf_op jit(solution)/shard_map/pallas_call | solution.py:215
  4.0 0.0 copy-start.4
  4.0 12.1 %all_to_all.25.parts_ref = f32[4,32,128]{2,1,0:T(8,128)S(1)} all-to-all(f32[4,32,128]{2,1,0:T(8,128)} %bitcast.54), channel_id=1, replica_groups=mesh['samp'=8,'feat'=4] {'feat'}, dimensions={0} | all-to-all | bytes 131072 | tf_op jit(solution)/shard_map/all_to_all | solution.py:232
  16.1 0.0 copy-done.5
  16.1 0.0 copy-done
  16.1 0.0 copy-done.6
  16.1 0.0 copy-done.7
  16.1 0.0 copy-done.3
  16.1 0.6 shard_map.87
  16.8 8.2 %all_to_all.26 = f32[8,1,128]{2,1,0:T(1,128)S(1)} all-to-all(f32[8,1,128]{2,1,0:T(1,128)S(1)} %bitcast.48), channel_id=1, replica_groups=mesh['samp'=8,'feat'=4] {'samp'}, dimensions={0} | all-to-all | bytes 8192 | tf_op jit(solution)/shard_map/all_to_all | solution.py:203
  24.9 0.0 copy-done.1
  24.9 0.0 copy-done.4
  24.9 0.9 %shard_map.88 = (f32[2,32,128]{2,1,0:T(8,128)S(1)}, f32[1,128]{1,0:T(1,128)S(1)}) custom-call(f32[8,128]{1,0:T(8,128)S(1)} %bitcast.41, f32[2,32,128]{2,1,0:T(8,128)S(1)} %get-tuple-element.17.state_ref, f32[4,32,64]{2,1,0:T(8,128)S(1)} %get-tuple-element.18.chosen_ref, f32[4,128]{1,0:T(4,128)S(1)} %copy-done.4, f32[4,128,128]{2,1,0:T(8,128)S(1)} %bitcast.34, ...), custom_call_target="tpu_custom_call" | custom-call | tf_op jit(solution)/shard_map/pallas_call | solution.py:246
  25.8 0.9 %collective-permute-start = (f32[2,32,128]{2,1,0:T(8,128)S(1)}, f32[2,32,128]{2,1,0:T(8,128)S(1)}, u32[]{:S(2)}, u32[]{:S(2)}) collective-permute-start(f32[2,32,128]{2,1,0:T(8,128)S(1)} %get-tuple-element.21), channel_id=1, source_target_pairs={{0,1},{1,2},{2,3},{3,0},{4,5},{5,6},{6,7},{7,4},{8,9},{9,10},{10,1... | collective-permute-start | bytes 98312 | tf_op jit(solution)/shard_map/ppermute | solution.py:198
  26.7 4.8 %collective-permute-done.state_ref = f32[2,32,128]{2,1,0:T(8,128)S(1)} collective-permute-done((f32[2,32,128]{2,1,0:T(8,128)S(1)}, f32[2,32,128]{2,1,0:T(8,128)S(1)}, u32[]{:S(2)}, u32[]{:S(2)}) %collective-permute-start) | collective-permute-done | bytes 32800 | tf_op jit(solution)/shard_map/ppermute | solution.py:198
  31.5 0.5 shard_map.89
  32.1 7.0 %all_to_all.27 = f32[8,1,128]{2,1,0:T(1,128)S(1)} all-to-all(f32[8,1,128]{2,1,0:T(1,128)S(1)} %bitcast.45), channel_id=1, replica_groups=mesh['samp'=8,'feat'=4] {'samp'}, dimensions={0} | all-to-all | bytes 8192 | tf_op jit(solution)/shard_map/all_to_all | solution.py:203
  39.1 0.9 %shard_map.90 = (f32[2,32,128]{2,1,0:T(8,128)S(1)}, f32[1,128]{1,0:T(1,128)S(1)}) custom-call(f32[8,128]{1,0:T(8,128)S(1)} %bitcast.43, f32[2,32,128]{2,1,0:T(8,128)S(1)} %collective-permute-done.state_ref, f32[4,32,64]{2,1,0:T(8,128)S(1)} %get-tuple-element.18.chosen_ref, f32[4,128]{1,0:T(4,128)S(1)} %copy-done.4, f32[4,128,128]{2,1,0:T(8,128)S(1)} %bitcast.35, ...), custom_call_target="tpu_custom_call" | custom-call | tf_op jit(solution)/shard_map/pallas_call | solution.py:246
  40.0 0.0 collective-permute-start.1
  40.0 5.7 %collective-permute-done.1.state_ref = f32[2,32,128]{2,1,0:T(8,128)S(1)} collective-permute-done((f32[2,32,128]{2,1,0:T(8,128)S(1)}, f32[2,32,128]{2,1,0:T(8,128)S(1)}, u32[]{:S(2)}, u32[]{:S(2)}) %collective-permute-start.1) | collective-permute-done | bytes 32800 | tf_op jit(solution)/shard_map/ppermute | solution.py:198
  45.7 0.5 shard_map.91
  46.2 7.0 %all_to_all.28 = f32[8,1,128]{2,1,0:T(1,128)S(1)} all-to-all(f32[8,1,128]{2,1,0:T(1,128)S(1)} %bitcast.46), channel_id=1, replica_groups=mesh['samp'=8,'feat'=4] {'samp'}, dimensions={0} | all-to-all | bytes 8192 | tf_op jit(solution)/shard_map/all_to_all | solution.py:203
  53.3 0.9 %shard_map.92 = (f32[2,32,128]{2,1,0:T(8,128)S(1)}, f32[1,128]{1,0:T(1,128)S(1)}) custom-call(f32[8,128]{1,0:T(8,128)S(1)} %bitcast.44, f32[2,32,128]{2,1,0:T(8,128)S(1)} %collective-permute-done.1.state_ref, f32[4,32,64]{2,1,0:T(8,128)S(1)} %get-tuple-element.18.chosen_ref, f32[4,128]{1,0:T(4,128)S(1)} %copy-done.4, f32[4,128,128]{2,1,0:T(8,128)S(1)} %bitcast.36, ...), custom_call_target="tpu_custom_call" | custom-call | tf_op jit(solution)/shard_map/pallas_call | solution.py:246
  54.1 0.0 copy-start.2
  54.1 0.1 collective-permute-start.2
  54.2 5.7 %collective-permute-done.2.state_ref = f32[2,32,128]{2,1,0:T(8,128)S(1)} collective-permute-done((f32[2,32,128]{2,1,0:T(8,128)S(1)}, f32[2,32,128]{2,1,0:T(8,128)S(1)}, u32[]{:S(2)}, u32[]{:S(2)}) %collective-permute-start.2) | collective-permute-done | bytes 32800 | tf_op jit(solution)/shard_map/ppermute | solution.py:198
  59.9 0.5 shard_map.93
  60.5 7.0 %all_to_all.29 = f32[8,1,128]{2,1,0:T(1,128)S(1)} all-to-all(f32[8,1,128]{2,1,0:T(1,128)S(1)} %bitcast.47), channel_id=1, replica_groups=mesh['samp'=8,'feat'=4] {'samp'}, dimensions={0} | all-to-all | bytes 8192 | tf_op jit(solution)/shard_map/all_to_all | solution.py:203
  67.5 0.9 %shard_map.94 = (f32[32,128]{1,0:T(8,128)S(1)}, f32[1,128]{1,0:T(1,128)S(1)}) custom-call(f32[8,128]{1,0:T(8,128)S(1)} %bitcast.42, f32[2,32,128]{2,1,0:T(8,128)S(1)} %collective-permute-done.2.state_ref, f32[4,32,64]{2,1,0:T(8,128)S(1)} %get-tuple-element.18.chosen_ref, f32[4,128]{1,0:T(4,128)S(1)} %copy-done.4, f32[4,128,128]{2,1,0:T(8,128)S(1)} %bitcast.37, ...), custom_call_target="tpu_custom_call" | custom-call | tf_op jit(solution)/shard_map/pallas_call | solution.py:246
  68.3 0.0 collective-permute-start.3
  68.4 0.0 copy-done.2
  68.4 1.3 %shard_map.95 = f32[512,128]{1,0:T(8,128)} custom-call(s32[1,4]{1,0:T(1,128)S(1)} %copy-done.5, f32[512,128]{1,0:T(8,128)S(1)} %bitcast.39, f32[1,128]{1,0:T(1,128)S(1)} %get-tuple-element.20.refs_0_, f32[1,128]{1,0:T(1,128)S(1)} %get-tuple-element.22.refs_1_, f32[1,128]{1,0:T(1,128)S(1)} %get-tuple-element.24.refs_2_, f32[1,128]{1,0:T(1,128)S(1)} %get-tuple-element.26.refs_3_), custom_call_target="tpu_custom_call" | custom-call | tf_op jit(solution)/shard_map/pallas_call | solution.py:259
  69.6 4.3 %collective-permute-done.3 = f32[32,128]{1,0:T(8,128)S(1)} collective-permute-done((f32[32,128]{1,0:T(8,128)S(1)}, f32[32,128]{1,0:T(8,128)S(1)}, u32[]{:S(2)}, u32[]{:S(2)}) %collective-permute-start.3) | collective-permute-done | bytes 16416 | tf_op jit(solution)/shard_map/ppermute | solution.py:198
  73.9 0.6 copy.14
Async XLA Ops:
  0.6 15.5 %copy-start.5 = (s32[1,4]{1,0:T(1,128)S(1)}, s32[1,4]{1,0:T(1,128)}, u32[]{:S(2)}) copy-start(s32[1,4]{1,0:T(1,128)} %targets_smem.1) | copy-start | bytes 52
  0.6 15.5 %copy-start = (bf16[1,1,64,128,128]{4,3,2,1,0:T(8,128)(2,1)S(1)}, bf16[1,1,64,128,128]{4,3,2,1,0:T(8,128)(2,1)}, u32[]{:S(2)}) copy-start(bf16[1,1,64,128,128]{4,3,2,1,0:T(8,128)(2,1)} %param.11) | copy-start | bytes 6291460
  0.7 15.5 %copy-start.6 = (s32[1,1,64]{2,1,0:T(1,128)S(1)}, s32[1,1,64]{2,1,0:T(1,128)}, u32[]{:S(2)}) copy-start(s32[1,1,64]{2,1,0:T(1,128)} %param.10) | copy-start | bytes 772
  0.7 15.5 %copy-start.7 = (s32[1,1,64]{2,1,0:T(1,128)S(1)}, s32[1,1,64]{2,1,0:T(1,128)}, u32[]{:S(2)}) copy-start(s32[1,1,64]{2,1,0:T(1,128)} %param.9) | copy-start | bytes 772
  0.7 15.5 %copy-start.3 = (s32[16384]{0:T(1024)S(1)}, s32[16384]{0:T(1024)}, u32[]{:S(2)}) copy-start(s32[16384]{0:T(1024)} %param.7) | copy-start | bytes 196612
  0.7 24.3 %copy-start.1 = (f32[1,4,128,128]{3,2,1,0:T(8,128)S(1)}, f32[1,4,128,128]{3,2,1,0:T(8,128)}, u32[]{:S(2)}) copy-start(f32[1,4,128,128]{3,2,1,0:T(8,128)} %param.13) | copy-start | bytes 786436
  4.0 20.9 %copy-start.4 = (f32[4,128]{1,0:T(4,128)S(1)}, f32[4,128]{1,0:T(4,128)}, u32[]{:S(2)}) copy-start(f32[4,128]{1,0:T(4,128)} %get-tuple-element.19.old_ref) | copy-start | bytes 6148
  25.8 5.7 %collective-permute-start = (f32[2,32,128]{2,1,0:T(8,128)S(1)}, f32[2,32,128]{2,1,0:T(8,128)S(1)}, u32[]{:S(2)}, u32[]{:S(2)}) collective-permute-start(f32[2,32,128]{2,1,0:T(8,128)S(1)} %get-tuple-element.21), channel_id=1, source_target_pairs={{0,1},{1,2},{2,3},{3,0},{4,5},{5,6},{6,7},{7,4},{8,9},{9,10},{10,1... | collective-permute-start | bytes 98312 | tf_op jit(solution)/shard_map/ppermute | solution.py:198
  40.0 5.7 %collective-permute-start.1 = (f32[2,32,128]{2,1,0:T(8,128)S(1)}, f32[2,32,128]{2,1,0:T(8,128)S(1)}, u32[]{:S(2)}, u32[]{:S(2)}) collective-permute-start(f32[2,32,128]{2,1,0:T(8,128)S(1)} %get-tuple-element.23), channel_id=1, source_target_pairs={{0,1},{1,2},{2,3},{3,0},{4,5},{5,6},{6,7},{7,4},{8,9},{9,10},{10,1... | collective-permute-start | bytes 98312 | tf_op jit(solution)/shard_map/ppermute | solution.py:198
  54.1 14.2 %copy-start.2 = (f32[65536]{0:T(1024)S(1)}, f32[65536]{0:T(1024)}, u32[]{:S(2)}) copy-start(f32[65536]{0:T(1024)} %param.8) | copy-start | bytes 786436
  54.1 5.8 %collective-permute-start.2 = (f32[2,32,128]{2,1,0:T(8,128)S(1)}, f32[2,32,128]{2,1,0:T(8,128)S(1)}, u32[]{:S(2)}, u32[]{:S(2)}) collective-permute-start(f32[2,32,128]{2,1,0:T(8,128)S(1)} %get-tuple-element.25), channel_id=1, source_target_pairs={{0,1},{1,2},{2,3},{3,0},{4,5},{5,6},{6,7},{7,4},{8,9},{9,10},{10,1... | collective-permute-start | bytes 98312 | tf_op jit(solution)/shard_map/ppermute | solution.py:198
  68.3 5.6 %collective-permute-start.3 = (f32[32,128]{1,0:T(8,128)S(1)}, f32[32,128]{1,0:T(8,128)S(1)}, u32[]{:S(2)}, u32[]{:S(2)}) collective-permute-start(f32[32,128]{1,0:T(8,128)S(1)} %get-tuple-element.27), channel_id=1, source_target_pairs={{0,1},{1,2},{2,3},{3,0},{4,5},{5,6},{6,7},{7,4},{8,9},{9,10},{10,1... | collective-permute-start | bytes 49160 | tf_op jit(solution)/shard_map/ppermute | solution.py:198

commit v6 on v5

--- a/solution.py
+++ b/solution.py
@@ -200,7 +200,11 @@
 
 def gathered(parts, axis):
     count, edge = parts.shape
-    return lax.all_to_all(parts.reshape(count, 1, edge), axis, 0, 0).reshape(count, edge)
+    order = [index ^ 1 for index in range(count)] if count % 2 == 0 else list(range(count))
+    received = lax.all_to_all(
+        parts.reshape(count, 1, edge), axis, 0, 0, axis_index_groups=[order]
+    )
+    return received.reshape(count, edge)
 
 
 def per_device(labels, beta, tile_rows, tile_cols, tile_values, block_order, hess_inv):
@@ -249,7 +253,7 @@
             [VMEM] * 6,
         )(gathered(grads, "samp"), state, chosen, old_blocks, inverses, values)
         shrunk_blocks.append(shrunk)
-        state = from_behind(moving, "feat", 1)
+        state = from_behind(moving.reshape(-1) if final else moving, "feat", 1)
         if not final:
             grads = call(
                 functools.partial(gradient_kernel, section + 1),
@@ -261,7 +265,7 @@
         float_of(blocks.shape),
         [SMEM] + [VMEM] * (1 + sections),
     )(block_order, blocks, *shrunk_blocks)
-    return (blocks.reshape(-1), state.reshape(-1))
+    return (blocks.reshape(-1), state)
 
 
 def solution(mesh):

time: 74.9 us -> 72.1 us (0.963)
  blocking collectives: 41.3 us -> 38.5 us
    all_to_all x4, blocking collectives: 29.3 us -> 26.5 us  [gathered(): lax.all_to_all(parts.reshape(count, 1, edge), axis, 0, 0, axis_index_grou...]
where the time goes in v6:
time: 72.1 us; the launch traced here: 71.7 us
  blocking collectives  38.5 us (53%)
  waiting for transfers between devices  20.5 us (28%)
  Pallas kernels  10.3 us (14%)
  starting transfers between devices  1.02 us (1%)
  between operations  0.77 us (1%)
    all_to_all x4, blocking collectives, gathered(): lax.all_to_all(parts.reshape(count, 1, edge), axis, 0, 0, axis_index_grou...  26.5 us
    ppermute x4, waiting for transfers between devices, from_behind(): return lax.ppermute(value, axis, pairs)  20.5 us
    all_to_all x1, blocking collectives, per_device(): lax.all_to_all(partial_sum.reshape(sections, group_blocks, edge), 'feat',...  12.1 us
    pallas_call x4, Pallas kernels, per_device(): call(functools.partial(update_kernel, section), (float_of(moved_shape), f...  3.43 us
    pallas_call x1, Pallas kernels, per_device(): pl.pallas_call(margins_kernel, out_shape=(float_of((row_blocks, edge)), f...  3.32 us
    pallas_call x3, Pallas kernels, per_device(): call(functools.partial(gradient_kernel, section + 1), float_of((samp_coun...  1.63 us
  transfers between devices with their start and end apart: 4, of which 4 were waited for; matrix products, arithmetic and copies ran while one was open for 0% of the time, Pallas kernels for 2%

profile of v6, /device:TPU:0, one launch (start us, length us, event | category | flops | bytes accessed | tf_op | source)
XLA Modules:
  0.0 71.7 jit_solution(16786401216796171437)
XLA Ops:
  0.6 0.0 copy-start.5
  0.6 0.0 copy-start
  0.7 0.0 copy-start.6
  0.7 0.0 copy-start.7
  0.7 0.0 copy-start.3
  0.7 0.0 copy-start.1
  0.7 3.3 %shard_map.86 = (f32[128,128]{1,0:T(8,128)}, f32[4,128]{1,0:T(4,128)}) custom-call(s32[1,64]{1,0:T(1,128)} %bitcast.49, s32[1,4]{1,0:T(1,128)} %targets_smem.1, s32[1,64]{1,0:T(1,128)} %bitcast.51, f32[512,128]{1,0:T(8,128)} %bitcast.38, bf16[64,128,128]{2,1,0:T(8,128)(2,1)} %bitcast.25), custom_call_target="tpu_custom_call" | custom-call | tf_op jit(solution)/shard_map/pallas_call | solution.py:219
  4.0 0.0 copy-start.4
  4.0 12.1 %all_to_all.25.parts_ref = f32[4,32,128]{2,1,0:T(8,128)S(1)} all-to-all(f32[4,32,128]{2,1,0:T(8,128)} %bitcast.55), channel_id=1, replica_groups=mesh['samp'=8,'feat'=4] {'feat'}, dimensions={0} | all-to-all | bytes 131072 | tf_op jit(solution)/shard_map/all_to_all | solution.py:236
  16.1 0.0 copy-done.5
  16.1 0.0 copy-done
  16.1 0.0 copy-done.6
  16.1 0.0 copy-done.7
  16.1 0.0 copy-done.3
  16.1 0.6 shard_map.87
  16.8 7.9 %all_to_all.26 = f32[8,1,128]{2,1,0:T(1,128)S(1)} all-to-all(f32[8,1,128]{2,1,0:T(1,128)S(1)} %bitcast.48), channel_id=1, replica_groups={{4,0,12,8,20,16,28,24},{5,1,13,9,21,17,29,25},{6,2,14,10,22,18,30,26},{..., dimensions={0} | all-to-all | bytes 8192 | tf_op jit(solution)/shard_map/all_to_all | solution.py:204
  24.7 0.0 copy-done.1
  24.7 0.0 copy-done.4
  24.7 0.9 %shard_map.88 = (f32[2,32,128]{2,1,0:T(8,128)S(1)}, f32[1,128]{1,0:T(1,128)S(1)}) custom-call(f32[8,128]{1,0:T(8,128)S(1)} %bitcast.41, f32[2,32,128]{2,1,0:T(8,128)S(1)} %get-tuple-element.17.state_ref, f32[4,32,64]{2,1,0:T(8,128)S(1)} %get-tuple-element.18.chosen_ref, f32[4,128]{1,0:T(4,128)S(1)} %copy-done.4, f32[4,128,128]{2,1,0:T(8,128)S(1)} %bitcast.34, ...), custom_call_target="tpu_custom_call" | custom-call | tf_op jit(solution)/shard_map/pallas_call | solution.py:250
  25.5 0.9 %collective-permute-start = (f32[2,32,128]{2,1,0:T(8,128)S(1)}, f32[2,32,128]{2,1,0:T(8,128)S(1)}, u32[]{:S(2)}, u32[]{:S(2)}) collective-permute-start(f32[2,32,128]{2,1,0:T(8,128)S(1)} %get-tuple-element.21), channel_id=1, source_target_pairs={{0,1},{1,2},{2,3},{3,0},{4,5},{5,6},{6,7},{7,4},{8,9},{9,10},{10,1... | collective-permute-start | bytes 98312 | tf_op jit(solution)/shard_map/ppermute | solution.py:198
  26.5 4.8 %collective-permute-done.state_ref = f32[2,32,128]{2,1,0:T(8,128)S(1)} collective-permute-done((f32[2,32,128]{2,1,0:T(8,128)S(1)}, f32[2,32,128]{2,1,0:T(8,128)S(1)}, u32[]{:S(2)}, u32[]{:S(2)}) %collective-permute-start) | collective-permute-done | bytes 32800 | tf_op jit(solution)/shard_map/ppermute | solution.py:198
  31.3 0.5 shard_map.89
  31.8 6.1 %all_to_all.27 = f32[8,1,128]{2,1,0:T(1,128)S(1)} all-to-all(f32[8,1,128]{2,1,0:T(1,128)S(1)} %bitcast.45), channel_id=1, replica_groups={{4,0,12,8,20,16,28,24},{5,1,13,9,21,17,29,25},{6,2,14,10,22,18,30,26},{..., dimensions={0} | all-to-all | bytes 8192 | tf_op jit(solution)/shard_map/all_to_all | solution.py:204
  37.9 0.9 %shard_map.90 = (f32[2,32,128]{2,1,0:T(8,128)S(1)}, f32[1,128]{1,0:T(1,128)S(1)}) custom-call(f32[8,128]{1,0:T(8,128)S(1)} %bitcast.43, f32[2,32,128]{2,1,0:T(8,128)S(1)} %collective-permute-done.state_ref, f32[4,32,64]{2,1,0:T(8,128)S(1)} %get-tuple-element.18.chosen_ref, f32[4,128]{1,0:T(4,128)S(1)} %copy-done.4, f32[4,128,128]{2,1,0:T(8,128)S(1)} %bitcast.35, ...), custom_call_target="tpu_custom_call" | custom-call | tf_op jit(solution)/shard_map/pallas_call | solution.py:250
  38.7 0.0 collective-permute-start.1
  38.8 5.7 %collective-permute-done.1.state_ref = f32[2,32,128]{2,1,0:T(8,128)S(1)} collective-permute-done((f32[2,32,128]{2,1,0:T(8,128)S(1)}, f32[2,32,128]{2,1,0:T(8,128)S(1)}, u32[]{:S(2)}, u32[]{:S(2)}) %collective-permute-start.1) | collective-permute-done | bytes 32800 | tf_op jit(solution)/shard_map/ppermute | solution.py:198
  44.5 0.5 shard_map.91
  45.0 6.4 %all_to_all.28 = f32[8,1,128]{2,1,0:T(1,128)S(1)} all-to-all(f32[8,1,128]{2,1,0:T(1,128)S(1)} %bitcast.46), channel_id=1, replica_groups={{4,0,12,8,20,16,28,24},{5,1,13,9,21,17,29,25},{6,2,14,10,22,18,30,26},{..., dimensions={0} | all-to-all | bytes 8192 | tf_op jit(solution)/shard_map/all_to_all | solution.py:204
  51.5 0.9 %shard_map.92 = (f32[2,32,128]{2,1,0:T(8,128)S(1)}, f32[1,128]{1,0:T(1,128)S(1)}) custom-call(f32[8,128]{1,0:T(8,128)S(1)} %bitcast.44, f32[2,32,128]{2,1,0:T(8,128)S(1)} %collective-permute-done.1.state_ref, f32[4,32,64]{2,1,0:T(8,128)S(1)} %get-tuple-element.18.chosen_ref, f32[4,128]{1,0:T(4,128)S(1)} %copy-done.4, f32[4,128,128]{2,1,0:T(8,128)S(1)} %bitcast.36, ...), custom_call_target="tpu_custom_call" | custom-call | tf_op jit(solution)/shard_map/pallas_call | solution.py:250
  52.3 0.0 copy-start.2
  52.3 0.1 collective-permute-start.2
  52.4 5.7 %collective-permute-done.2.state_ref = f32[2,32,128]{2,1,0:T(8,128)S(1)} collective-permute-done((f32[2,32,128]{2,1,0:T(8,128)S(1)}, f32[2,32,128]{2,1,0:T(8,128)S(1)}, u32[]{:S(2)}, u32[]{:S(2)}) %collective-permute-start.2) | collective-permute-done | bytes 32800 | tf_op jit(solution)/shard_map/ppermute | solution.py:198
  58.1 0.5 shard_map.93
  58.6 6.1 %all_to_all.29 = f32[8,1,128]{2,1,0:T(1,128)S(1)} all-to-all(f32[8,1,128]{2,1,0:T(1,128)S(1)} %bitcast.47), channel_id=1, replica_groups={{4,0,12,8,20,16,28,24},{5,1,13,9,21,17,29,25},{6,2,14,10,22,18,30,26},{..., dimensions={0} | all-to-all | bytes 8192 | tf_op jit(solution)/shard_map/all_to_all | solution.py:204
  64.7 0.9 %shard_map.94 = (f32[32,128]{1,0:T(8,128)S(1)}, f32[1,128]{1,0:T(1,128)S(1)}) custom-call(f32[8,128]{1,0:T(8,128)S(1)} %bitcast.42, f32[2,32,128]{2,1,0:T(8,128)S(1)} %collective-permute-done.2.state_ref, f32[4,32,64]{2,1,0:T(8,128)S(1)} %get-tuple-element.18.chosen_ref, f32[4,128]{1,0:T(4,128)S(1)} %copy-done.4, f32[4,128,128]{2,1,0:T(8,128)S(1)} %bitcast.37, ...), custom_call_target="tpu_custom_call" | custom-call | tf_op jit(solution)/shard_map/pallas_call | solution.py:250
  65.6 0.0 collective-permute-start.3
  65.6 0.0 copy-done.2
  65.6 1.3 %shard_map.95 = f32[512,128]{1,0:T(8,128)} custom-call(s32[1,4]{1,0:T(1,128)S(1)} %copy-done.5, f32[512,128]{1,0:T(8,128)S(1)} %bitcast.39, f32[1,128]{1,0:T(1,128)S(1)} %get-tuple-element.20.refs_0_, f32[1,128]{1,0:T(1,128)S(1)} %get-tuple-element.22.refs_1_, f32[1,128]{1,0:T(1,128)S(1)} %get-tuple-element.24.refs_2_, f32[1,128]{1,0:T(1,128)S(1)} %get-tuple-element.26.refs_3_), custom_call_target="tpu_custom_call" | custom-call | tf_op jit(solution)/shard_map/pallas_call | solution.py:263
  66.9 4.3 %collective-permute-done.3 = f32[4096]{0:T(1024)S(1)} collective-permute-done((f32[4096]{0:T(1024)S(1)}, f32[4096]{0:T(1024)S(1)}, u32[]{:S(2)}, u32[]{:S(2)}) %collective-permute-start.3) | collective-permute-done | bytes 16416 | tf_op jit(solution)/shard_map/ppermute | solution.py:198
  71.1 0.6 copy.14
Async XLA Ops:
  0.6 15.5 %copy-start.5 = (s32[1,4]{1,0:T(1,128)S(1)}, s32[1,4]{1,0:T(1,128)}, u32[]{:S(2)}) copy-start(s32[1,4]{1,0:T(1,128)} %targets_smem.1) | copy-start | bytes 52
  0.6 15.5 %copy-start = (bf16[1,1,64,128,128]{4,3,2,1,0:T(8,128)(2,1)S(1)}, bf16[1,1,64,128,128]{4,3,2,1,0:T(8,128)(2,1)}, u32[]{:S(2)}) copy-start(bf16[1,1,64,128,128]{4,3,2,1,0:T(8,128)(2,1)} %param.11) | copy-start | bytes 6291460
  0.7 15.5 %copy-start.6 = (s32[1,1,64]{2,1,0:T(1,128)S(1)}, s32[1,1,64]{2,1,0:T(1,128)}, u32[]{:S(2)}) copy-start(s32[1,1,64]{2,1,0:T(1,128)} %param.10) | copy-start | bytes 772
  0.7 15.5 %copy-start.7 = (s32[1,1,64]{2,1,0:T(1,128)S(1)}, s32[1,1,64]{2,1,0:T(1,128)}, u32[]{:S(2)}) copy-start(s32[1,1,64]{2,1,0:T(1,128)} %param.9) | copy-start | bytes 772
  0.7 15.5 %copy-start.3 = (s32[16384]{0:T(1024)S(1)}, s32[16384]{0:T(1024)}, u32[]{:S(2)}) copy-start(s32[16384]{0:T(1024)} %param.7) | copy-start | bytes 196612
  0.7 24.0 %copy-start.1 = (f32[1,4,128,128]{3,2,1,0:T(8,128)S(1)}, f32[1,4,128,128]{3,2,1,0:T(8,128)}, u32[]{:S(2)}) copy-start(f32[1,4,128,128]{3,2,1,0:T(8,128)} %param.13) | copy-start | bytes 786436
  4.0 20.7 %copy-start.4 = (f32[4,128]{1,0:T(4,128)S(1)}, f32[4,128]{1,0:T(4,128)}, u32[]{:S(2)}) copy-start(f32[4,128]{1,0:T(4,128)} %get-tuple-element.19.old_ref) | copy-start | bytes 6148
  25.5 5.7 %collective-permute-start = (f32[2,32,128]{2,1,0:T(8,128)S(1)}, f32[2,32,128]{2,1,0:T(8,128)S(1)}, u32[]{:S(2)}, u32[]{:S(2)}) collective-permute-start(f32[2,32,128]{2,1,0:T(8,128)S(1)} %get-tuple-element.21), channel_id=1, source_target_pairs={{0,1},{1,2},{2,3},{3,0},{4,5},{5,6},{6,7},{7,4},{8,9},{9,10},{10,1... | collective-permute-start | bytes 98312 | tf_op jit(solution)/shard_map/ppermute | solution.py:198
  38.7 5.7 %collective-permute-start.1 = (f32[2,32,128]{2,1,0:T(8,128)S(1)}, f32[2,32,128]{2,1,0:T(8,128)S(1)}, u32[]{:S(2)}, u32[]{:S(2)}) collective-permute-start(f32[2,32,128]{2,1,0:T(8,128)S(1)} %get-tuple-element.23), channel_id=1, source_target_pairs={{0,1},{1,2},{2,3},{3,0},{4,5},{5,6},{6,7},{7,4},{8,9},{9,10},{10,1... | collective-permute-start | bytes 98312 | tf_op jit(solution)/shard_map/ppermute | solution.py:198
  52.3 13.3 %copy-start.2 = (f32[65536]{0:T(1024)S(1)}, f32[65536]{0:T(1024)}, u32[]{:S(2)}) copy-start(f32[65536]{0:T(1024)} %param.8) | copy-start | bytes 786436
  52.3 5.8 %collective-permute-start.2 = (f32[2,32,128]{2,1,0:T(8,128)S(1)}, f32[2,32,128]{2,1,0:T(8,128)S(1)}, u32[]{:S(2)}, u32[]{:S(2)}) collective-permute-start(f32[2,32,128]{2,1,0:T(8,128)S(1)} %get-tuple-element.25), channel_id=1, source_target_pairs={{0,1},{1,2},{2,3},{3,0},{4,5},{5,6},{6,7},{7,4},{8,9},{9,10},{10,1... | collective-permute-start | bytes 98312 | tf_op jit(solution)/shard_map/ppermute | solution.py:198
  65.6 5.6 %collective-permute-start.3 = (f32[4096]{0:T(1024)S(1)}, f32[4096]{0:T(1024)S(1)}, u32[]{:S(2)}, u32[]{:S(2)}) collective-permute-start(f32[4096]{0:T(1024)S(1)} %bitcast.53), channel_id=1, source_target_pairs={{0,1},{1,2},{2,3},{3,0},{4,5},{5,6},{6,7},{7,4},{8,9},{9,10},{10,1... | collective-permute-start | bytes 49160 | tf_op jit(solution)/shard_map/ppermute | solution.py:198

commit v7 on v6

--- a/solution.py
+++ b/solution.py
@@ -29,6 +29,10 @@
         out_specs=VMEM if single else tuple(VMEM for _ in out_shape),
         compiler_params=pltpu.CompilerParams(vmem_limit_bytes=24 << 20),
     )
+
+
+def middle_first(count):
+    return sorted(range(count), key=lambda index: (abs(index - count // 2), index))
 
 
 def tile_products(vectors_of, tiles_of, tiles):
@@ -100,7 +104,12 @@
     )
     block_ids = lax.broadcasted_iota(jnp.int32, (row_blocks, tiles), 0)
     placing = (block_ids == rows_ref[...]).astype(jnp.float32)
-    partial_ref[...] = placed_sum(placing, products)
+    partial = placed_sum(placing, products)
+    group_blocks = row_blocks // sections
+    for place, group in enumerate(middle_first(sections)):
+        partial_ref[pl.ds(place * group_blocks, group_blocks), :] = partial[
+            group * group_blocks : (group + 1) * group_blocks
+        ]
 
 
 def gradient_part(residual, chosen, values_ref):
@@ -127,7 +136,7 @@
 
 def first_kernel(
     parts_ref, labels_ref, rows_ref, cols_ref, targets_ref, values_ref,
-    state_ref, grad_ref, chosen_ref,
+    residual_ref, weight_ref, grad_ref, chosen_ref,
 ):
     sections, group_blocks, _ = parts_ref.shape
     my_index = lax.axis_index("feat")
@@ -143,19 +152,19 @@
         margins = margins + parts_ref[part]
     probability = 1.0 / (1.0 + jnp.exp(-margins))
     residual = labels_ref[pl.ds(start, group_blocks), :].astype(jnp.float32) - probability
-    state_ref[0] = residual
-    state_ref[1] = probability * (1.0 - probability)
+    residual_ref[...] = residual
+    weight_ref[...] = probability * (1.0 - probability)
     grad = gradient_part(residual, chosen_ref[0], values_ref)
     grad_ref[...] = jnp.broadcast_to(grad, grad_ref.shape)
 
 
-def gradient_kernel(section, state_ref, chosen_ref, values_ref, grad_ref):
-    grad = gradient_part(state_ref[0], chosen_ref[section], values_ref)
+def gradient_kernel(section, residual_ref, chosen_ref, values_ref, grad_ref):
+    grad = gradient_part(residual_ref[...], chosen_ref[section], values_ref)
     grad_ref[...] = jnp.broadcast_to(grad, grad_ref.shape)
 
 
 def update_kernel(
-    section, grads_ref, state_ref, chosen_ref, old_ref, inverses_ref, values_ref,
+    section, grads_ref, residual_ref, weight_ref, chosen_ref, old_ref, inverses_ref, values_ref,
     moved_ref, shrunk_ref,
 ):
     tiles, edge, _ = values_ref.shape
@@ -176,13 +185,7 @@
         lambda first: change, lambda first: values_ref[pl.ds(first, chunk)], tiles
     )
     landed = placed_sum(chosen_ref[section], image)
-    weight = state_ref[1]
-    residual = state_ref[0] - weight * landed
-    if len(moved_ref.shape) == 3:
-        moved_ref[0] = residual
-        moved_ref[1] = weight
-    else:
-        moved_ref[...] = residual
+    moved_ref[...] = residual_ref[...] - weight_ref[...] * landed
 
 
 def blocks_kernel(sections, targets_smem, beta_ref, *refs):
@@ -233,11 +236,19 @@
         ],
         compiler_params=pltpu.CompilerParams(vmem_limit_bytes=58 << 20),
     )(tile_cols[0], block_order, tile_rows[0], blocks, values)
-    parts = lax.all_to_all(partial_sum.reshape(sections, group_blocks, edge), "feat", 0, 0)
-    state, grads, chosen = call(
+    parts = lax.all_to_all(
+        partial_sum.reshape(sections, group_blocks, edge),
+        "feat",
+        0,
+        0,
+        axis_index_groups=[middle_first(sections)],
+    )
+    group_shape = (group_blocks, edge)
+    residual, weight, grads, chosen = call(
         first_kernel,
         (
-            float_of((2, group_blocks, edge)),
+            float_of(group_shape),
+            float_of(group_shape),
             float_of((samp_count, edge)),
             float_of((sections, group_blocks, tiles)),
         ),
@@ -245,27 +256,26 @@
     )(parts, labels.reshape(row_blocks, edge), tile_rows[0], tile_cols[0], block_order, values)
     shrunk_blocks = []
     for section in range(sections):
-        final = section + 1 == sections
-        moved_shape = (group_blocks, edge) if final else (2, group_blocks, edge)
         moving, shrunk = call(
             functools.partial(update_kernel, section),
-            (float_of(moved_shape), float_of((1, edge))),
-            [VMEM] * 6,
-        )(gathered(grads, "samp"), state, chosen, old_blocks, inverses, values)
+            (float_of(group_shape), float_of((1, edge))),
+            [VMEM] * 7,
+        )(gathered(grads, "samp"), residual, weight, chosen, old_blocks, inverses, values)
         shrunk_blocks.append(shrunk)
-        state = from_behind(moving.reshape(-1) if final else moving, "feat", 1)
-        if not final:
+        residual = from_behind(moving, "feat", 1)
+        if section + 1 < sections:
+            weight = from_behind(weight, "feat", 1)
             grads = call(
                 functools.partial(gradient_kernel, section + 1),
                 float_of((samp_count, edge)),
                 [VMEM] * 3,
-            )(state, chosen, values)
+            )(residual, chosen, values)
     blocks = call(
         functools.partial(blocks_kernel, sections),
         float_of(blocks.shape),
         [SMEM] + [VMEM] * (1 + sections),
     )(block_order, blocks, *shrunk_blocks)
-    return (blocks.reshape(-1), state)
+    return (blocks.reshape(-1), residual.reshape(-1))
 
 
 def solution(mesh):

time: 72.1 us -> 73.1 us (1.014)
  blocking collectives: 38.5 us -> 18.6 us
  starting transfers between devices: 1.02 us -> 12.2 us
  waiting for transfers between devices: 20.5 us -> 28.3 us
  Pallas kernels: 10.3 us -> 12.1 us
    all_to_all x4 -> x1, blocking collectives: 26.5 us -> 7.92 us  [gathered(): lax.all_to_all(parts.reshape(count, 1, edge), axis, 0, 0, axis_index_grou...]
    all_to_all x0 -> x3, starting transfers between devices: none -> 9.78 us  [gathered(): lax.all_to_all(parts.reshape(count, 1, edge), axis, 0, 0, axis_index_grou...]
    all_to_all x0 -> x3, waiting for transfers between devices: none -> 9.75 us  [gathered(): lax.all_to_all(parts.reshape(count, 1, edge), axis, 0, 0, axis_index_grou...]
    ppermute x4 -> x7, waiting for transfers between devices: 20.5 us -> 18.5 us  [from_behind(): return lax.ppermute(value, axis, pairs)]
    pallas_call x3, Pallas kernels: 1.63 us -> 3.44 us  [per_device(): call(functools.partial(gradient_kernel, section + 1), float_of((samp_coun...]
    ppermute x4 -> x7, starting transfers between devices: 1.02 us -> 2.43 us  [from_behind(): return lax.ppermute(value, axis, pairs)]
    all_to_all x1, blocking collectives: 12.1 us -> 10.7 us  [per_device(): lax.all_to_all(partial_sum.reshape(sections, group_blocks, edge), 'feat',...]
  transfers between devices with their start and end apart: 4 -> 10, of which waited for: 4 -> 7; matrix products, arithmetic and copies ran while one was open for 0% -> 0% of each run, Pallas kernels for 2% -> 6%
where the time goes in v7:
time: 73.1 us; the launch traced here: 72.7 us
  waiting for transfers between devices  28.3 us (39%)
  blocking collectives  18.6 us (25%)
  starting transfers between devices  12.2 us (17%)
  Pallas kernels  12.1 us (17%)
  between operations  0.82 us (1%)
    ppermute x7, waiting for transfers between devices, from_behind(): return lax.ppermute(value, axis, pairs)  18.5 us
    all_to_all x1, blocking collectives, per_device(): lax.all_to_all(partial_sum.reshape(sections, group_blocks, edge), 'feat',...  10.7 us
    all_to_all x3, starting transfers between devices, gathered(): lax.all_to_all(parts.reshape(count, 1, edge), axis, 0, 0, axis_index_grou...  9.78 us
    all_to_all x3, waiting for transfers between devices, gathered(): lax.all_to_all(parts.reshape(count, 1, edge), axis, 0, 0, axis_index_grou...  9.75 us
    all_to_all x1, blocking collectives, gathered(): lax.all_to_all(parts.reshape(count, 1, edge), axis, 0, 0, axis_index_grou...  7.92 us
    pallas_call x3, Pallas kernels, per_device(): call(functools.partial(gradient_kernel, section + 1), float_of((samp_coun...  3.44 us
    pallas_call x4, Pallas kernels, per_device(): call(functools.partial(update_kernel, section), (float_of(group_shape), f...  3.43 us
    pallas_call x1, Pallas kernels, per_device(): pl.pallas_call(margins_kernel, out_shape=(float_of((row_blocks, edge)), f...  3.32 us
  transfers between devices with their start and end apart: 10, of which 7 were waited for; matrix products, arithmetic and copies ran while one was open for 0% of the time, Pallas kernels for 6%

profile of v7, /device:TPU:0, one launch (start us, length us, event | category | flops | bytes accessed | tf_op | source)
XLA Modules:
  0.0 72.7 jit_solution(11807663502429912561)
XLA Ops:
  0.6 0.0 copy-start.5
  0.6 0.0 copy-start
  0.7 0.0 copy-start.6
  0.7 0.0 copy-start.7
  0.7 0.0 copy-start.3
  0.7 0.0 copy-start.1
  0.7 3.3 %shard_map.86 = (f32[128,128]{1,0:T(8,128)}, f32[4,128]{1,0:T(4,128)}) custom-call(s32[1,64]{1,0:T(1,128)} %bitcast.46, s32[1,4]{1,0:T(1,128)} %targets_smem.1, s32[1,64]{1,0:T(1,128)} %bitcast.48, f32[512,128]{1,0:T(8,128)} %bitcast.38, bf16[64,128,128]{2,1,0:T(8,128)(2,1)} %bitcast.25), custom_call_target="tpu_custom_call" | custom-call | tf_op jit(solution)/shard_map/pallas_call | solution.py:222
  4.0 0.0 copy-start.4
  4.0 10.7 %all_to_all.25.parts_ref = f32[4,32,128]{2,1,0:T(8,128)S(1)} all-to-all(f32[4,32,128]{2,1,0:T(8,128)} %bitcast.51), channel_id=1, replica_groups={{2,1,3,0},{6,5,7,4},{10,9,11,8},{14,13,15,12},{18,17,19,16},{22,21,23,2..., dimensions={0} | all-to-all | bytes 131072 | tf_op jit(solution)/shard_map/all_to_all | solution.py:239
  14.7 0.0 copy-done.5
  14.7 0.0 copy-done
  14.7 0.0 copy-done.6
  14.7 0.0 copy-done.7
  14.7 0.0 copy-done.3
  14.7 0.6 shard_map.87
  15.4 7.9 %all_to_all.26 = f32[8,1,128]{2,1,0:T(1,128)S(1)} all-to-all(f32[8,1,128]{2,1,0:T(1,128)S(1)} %bitcast.45), channel_id=1, replica_groups={{4,0,12,8,20,16,28,24},{5,1,13,9,21,17,29,25},{6,2,14,10,22,18,30,26},{..., dimensions={0} | all-to-all | bytes 8192 | tf_op jit(solution)/shard_map/all_to_all | solution.py:207
  23.3 0.0 copy-done.1
  23.3 0.0 copy-done.4
  23.3 0.9 %shard_map.88 = (f32[32,128]{1,0:T(8,128)S(1)}, f32[1,128]{1,0:T(1,128)S(1)}) custom-call(f32[8,128]{1,0:T(8,128)S(1)} %bitcast.44, f32[32,128]{1,0:T(8,128)S(1)} %get-tuple-element.18.residual_ref, f32[32,128]{1,0:T(8,128)S(1)} %get-tuple-element.19.weight_ref, f32[4,32,64]{2,1,0:T(8,128)S(1)} %get-tuple-element.20.chosen_ref, f32[4,128]{1,0:T(4,128)S(1)} %copy-done.4, ...), custom_call_target="tpu_custom_call" | custom-call | tf_op jit(solution)/shard_map/pallas_call | solution.py:259
  24.2 0.9 %collective-permute-start = (f32[32,128]{1,0:T(8,128)S(1)}, f32[32,128]{1,0:T(8,128)S(1)}, u32[]{:S(2)}, u32[]{:S(2)}) collective-permute-start(f32[32,128]{1,0:T(8,128)S(1)} %get-tuple-element.23), channel_id=1, source_target_pairs={{0,1},{1,2},{2,3},{3,0},{4,5},{5,6},{6,7},{7,4},{8,9},{9,10},{10,1... | collective-permute-start | bytes 49160 | tf_op jit(solution)/shard_map/ppermute | solution.py:201
  25.1 1.1 %collective-permute-start.1 = (f32[32,128]{1,0:T(8,128)S(1)}, f32[32,128]{1,0:T(8,128)S(1)}, u32[]{:S(2)}, u32[]{:S(2)}) collective-permute-start(f32[32,128]{1,0:T(8,128)S(1)} %get-tuple-element.19.weight_ref), channel_id=1, source_target_pairs={{0,1},{1,2},{2,3},{3,0},{4,5},{5,6},{6,7},{7,4},{8,9},{9,10},{10,1... | collective-permute-start | bytes 49160 | tf_op jit(solution)/shard_map/ppermute | solution.py:201
  26.2 3.5 %collective-permute-done.residual_ref = f32[32,128]{1,0:T(8,128)S(1)} collective-permute-done((f32[32,128]{1,0:T(8,128)S(1)}, f32[32,128]{1,0:T(8,128)S(1)}, u32[]{:S(2)}, u32[]{:S(2)}) %collective-permute-start) | collective-permute-done | bytes 16416 | tf_op jit(solution)/shard_map/ppermute | solution.py:201
  29.7 1.1 %shard_map.89 = f32[8,128]{1,0:T(8,128)} custom-call(f32[32,128]{1,0:T(8,128)S(1)} %collective-permute-done.residual_ref, f32[4,32,64]{2,1,0:T(8,128)S(1)} %get-tuple-element.20.chosen_ref, bf16[64,128,128]{2,1,0:T(8,128)(2,1)S(1)} %bitcast.28), custom_call_target="tpu_custom_call" | custom-call | tf_op jit(solution)/shard_map/pallas_call | solution.py:268
  30.9 3.3 %all-to-all-start.2 = ((f32[8,1,128]{2,1,0:T(1,128)}), f32[8,1,128]{2,1,0:T(1,128)S(1)}, u32[]{:S(2)}, u32[]{:S(2)}) async-start(f32[8,1,128]{2,1,0:T(1,128)} %bitcast.11), calls=%async_computation.2 | async-start | bytes 8192 | tf_op jit(solution)/shard_map/all_to_all | solution.py:207
  34.1 0.0 collective-permute-done.1.weight_ref
  34.1 2.9 %all-to-all-done.2 = f32[8,1,128]{2,1,0:T(1,128)S(1)} async-done(((f32[8,1,128]{2,1,0:T(1,128)}), f32[8,1,128]{2,1,0:T(1,128)S(1)}, u32[]{:S(2)}, u32[]{:S(2)}) %all-to-all-start.2) | async-done | bytes 4128 | tf_op jit(solution)/shard_map/all_to_all | solution.py:207
  37.0 0.9 %shard_map.90 = (f32[32,128]{1,0:T(8,128)S(1)}, f32[1,128]{1,0:T(1,128)S(1)}) custom-call(f32[8,128]{1,0:T(8,128)S(1)} %bitcast.42, f32[32,128]{1,0:T(8,128)S(1)} %collective-permute-done.residual_ref, f32[32,128]{1,0:T(8,128)S(1)} %collective-permute-done.1.weight_ref, f32[4,32,64]{2,1,0:T(8,128)S(1)} %get-tuple-element.20.chosen_ref, ...), custom_call_target="tpu_custom_call" | custom-call | tf_op jit(solution)/shard_map/pallas_call | solution.py:259
  37.9 0.0 collective-permute-start.2
  37.9 0.2 collective-permute-start.3
  38.2 5.3 %collective-permute-done.2.residual_ref = f32[32,128]{1,0:T(8,128)S(1)} collective-permute-done((f32[32,128]{1,0:T(8,128)S(1)}, f32[32,128]{1,0:T(8,128)S(1)}, u32[]{:S(2)}, u32[]{:S(2)}) %collective-permute-start.2) | collective-permute-done | bytes 16416 | tf_op jit(solution)/shard_map/ppermute | solution.py:201
  43.5 1.1 %shard_map.91 = f32[8,128]{1,0:T(8,128)} custom-call(f32[32,128]{1,0:T(8,128)S(1)} %collective-permute-done.2.residual_ref, f32[4,32,64]{2,1,0:T(8,128)S(1)} %get-tuple-element.20.chosen_ref, bf16[64,128,128]{2,1,0:T(8,128)(2,1)S(1)} %bitcast.30), custom_call_target="tpu_custom_call" | custom-call | tf_op jit(solution)/shard_map/pallas_call | solution.py:268
  44.6 3.3 %all-to-all-start.3 = ((f32[8,1,128]{2,1,0:T(1,128)}), f32[8,1,128]{2,1,0:T(1,128)S(1)}, u32[]{:S(2)}, u32[]{:S(2)}) async-start(f32[8,1,128]{2,1,0:T(1,128)} %bitcast.14), calls=%async_computation.3 | async-start | bytes 8192 | tf_op jit(solution)/shard_map/all_to_all | solution.py:207
  47.9 0.0 collective-permute-done.3.weight_ref
  47.9 4.0 %all-to-all-done.3 = f32[8,1,128]{2,1,0:T(1,128)S(1)} async-done(((f32[8,1,128]{2,1,0:T(1,128)}), f32[8,1,128]{2,1,0:T(1,128)S(1)}, u32[]{:S(2)}, u32[]{:S(2)}) %all-to-all-start.3) | async-done | bytes 4128 | tf_op jit(solution)/shard_map/all_to_all | solution.py:207
  51.8 0.9 %shard_map.92 = (f32[32,128]{1,0:T(8,128)S(1)}, f32[1,128]{1,0:T(1,128)S(1)}) custom-call(f32[8,128]{1,0:T(8,128)S(1)} %bitcast.43, f32[32,128]{1,0:T(8,128)S(1)} %collective-permute-done.2.residual_ref, f32[32,128]{1,0:T(8,128)S(1)} %collective-permute-done.3.weight_ref, f32[4,32,64]{2,1,0:T(8,128)S(1)} %get-tuple-element.20.chosen_ref, ...), custom_call_target="tpu_custom_call" | custom-call | tf_op jit(solution)/shard_map/pallas_call | solution.py:259
  52.7 0.0 copy-start.2
  52.7 0.1 collective-permute-start.4
  52.8 0.1 collective-permute-start.5
  52.8 5.5 %collective-permute-done.4.residual_ref = f32[32,128]{1,0:T(8,128)S(1)} collective-permute-done((f32[32,128]{1,0:T(8,128)S(1)}, f32[32,128]{1,0:T(8,128)S(1)}, u32[]{:S(2)}, u32[]{:S(2)}) %collective-permute-start.4) | collective-permute-done | bytes 16416 | tf_op jit(solution)/shard_map/ppermute | solution.py:201
  58.3 1.1 %shard_map.93 = f32[8,128]{1,0:T(8,128)} custom-call(f32[32,128]{1,0:T(8,128)S(1)} %collective-permute-done.4.residual_ref, f32[4,32,64]{2,1,0:T(8,128)S(1)} %get-tuple-element.20.chosen_ref, bf16[64,128,128]{2,1,0:T(8,128)(2,1)S(1)} %bitcast.32), custom_call_target="tpu_custom_call" | custom-call | tf_op jit(solution)/shard_map/pallas_call | solution.py:268
  59.4 3.3 %all-to-all-start.4 = ((f32[8,1,128]{2,1,0:T(1,128)}), f32[8,1,128]{2,1,0:T(1,128)S(1)}, u32[]{:S(2)}, u32[]{:S(2)}) async-start(f32[8,1,128]{2,1,0:T(1,128)} %bitcast.17), calls=%async_computation.4 | async-start | bytes 8192 | tf_op jit(solution)/shard_map/all_to_all | solution.py:207
  62.7 0.0 collective-permute-done.5.weight_ref
  62.7 2.9 %all-to-all-done.4 = f32[8,1,128]{2,1,0:T(1,128)S(1)} async-done(((f32[8,1,128]{2,1,0:T(1,128)}), f32[8,1,128]{2,1,0:T(1,128)S(1)}, u32[]{:S(2)}, u32[]{:S(2)}) %all-to-all-start.4) | async-done | bytes 4128 | tf_op jit(solution)/shard_map/all_to_all | solution.py:207
  65.6 0.9 %shard_map.94 = (f32[32,128]{1,0:T(8,128)S(1)}, f32[1,128]{1,0:T(1,128)S(1)}) custom-call(f32[8,128]{1,0:T(8,128)S(1)} %bitcast.41, f32[32,128]{1,0:T(8,128)S(1)} %collective-permute-done.4.residual_ref, f32[32,128]{1,0:T(8,128)S(1)} %collective-permute-done.5.weight_ref, f32[4,32,64]{2,1,0:T(8,128)S(1)} %get-tuple-element.20.chosen_ref, ...), custom_call_target="tpu_custom_call" | custom-call | tf_op jit(solution)/shard_map/pallas_call | solution.py:259
  66.5 0.0 collective-permute-start.6
  66.5 1.3 %shard_map.95 = f32[512,128]{1,0:T(8,128)} custom-call(s32[1,4]{1,0:T(1,128)S(1)} %copy-done.5, f32[512,128]{1,0:T(8,128)S(1)} %bitcast.39, f32[1,128]{1,0:T(1,128)S(1)} %get-tuple-element.22.refs_0_, f32[1,128]{1,0:T(1,128)S(1)} %get-tuple-element.24.refs_1_, f32[1,128]{1,0:T(1,128)S(1)} %get-tuple-element.26.refs_2_, f32[1,128]{1,0:T(1,128)S(1)} %get-tuple-element.28.refs_3_), custom_call_target="tpu_custom_call" | custom-call | tf_op jit(solution)/shard_map/pallas_call | solution.py:273
  67.8 4.3 %collective-permute-done.6 = f32[32,128]{1,0:T(8,128)S(1)} collective-permute-done((f32[32,128]{1,0:T(8,128)S(1)}, f32[32,128]{1,0:T(8,128)S(1)}, u32[]{:S(2)}, u32[]{:S(2)}) %collective-permute-start.6) | collective-permute-done | bytes 16416 | tf_op jit(solution)/shard_map/ppermute | solution.py:201
  72.0 0.6 copy.14
  (1 shorter events, 0.0 us)
Async XLA Ops:
  0.6 14.1 %copy-start.5 = (s32[1,4]{1,0:T(1,128)S(1)}, s32[1,4]{1,0:T(1,128)}, u32[]{:S(2)}) copy-start(s32[1,4]{1,0:T(1,128)} %targets_smem.1) | copy-start | bytes 52
  0.6 14.1 %copy-start = (bf16[1,1,64,128,128]{4,3,2,1,0:T(8,128)(2,1)S(1)}, bf16[1,1,64,128,128]{4,3,2,1,0:T(8,128)(2,1)}, u32[]{:S(2)}) copy-start(bf16[1,1,64,128,128]{4,3,2,1,0:T(8,128)(2,1)} %param.11) | copy-start | bytes 6291460
  0.7 14.1 %copy-start.6 = (s32[1,1,64]{2,1,0:T(1,128)S(1)}, s32[1,1,64]{2,1,0:T(1,128)}, u32[]{:S(2)}) copy-start(s32[1,1,64]{2,1,0:T(1,128)} %param.10) | copy-start | bytes 772
  0.7 14.1 %copy-start.7 = (s32[1,1,64]{2,1,0:T(1,128)S(1)}, s32[1,1,64]{2,1,0:T(1,128)}, u32[]{:S(2)}) copy-start(s32[1,1,64]{2,1,0:T(1,128)} %param.9) | copy-start | bytes 772
  0.7 14.1 %copy-start.3 = (s32[16384]{0:T(1024)S(1)}, s32[16384]{0:T(1024)}, u32[]{:S(2)}) copy-start(s32[16384]{0:T(1024)} %param.7) | copy-start | bytes 196612
  0.7 22.6 %copy-start.1 = (f32[1,4,128,128]{3,2,1,0:T(8,128)S(1)}, f32[1,4,128,128]{3,2,1,0:T(8,128)}, u32[]{:S(2)}) copy-start(f32[1,4,128,128]{3,2,1,0:T(8,128)} %param.13) | copy-start | bytes 786436
  4.0 19.3 %copy-start.4 = (f32[4,128]{1,0:T(4,128)S(1)}, f32[4,128]{1,0:T(4,128)}, u32[]{:S(2)}) copy-start(f32[4,128]{1,0:T(4,128)} %get-tuple-element.21.old_ref) | copy-start | bytes 6148
  24.2 5.6 %collective-permute-start = (f32[32,128]{1,0:T(8,128)S(1)}, f32[32,128]{1,0:T(8,128)S(1)}, u32[]{:S(2)}, u32[]{:S(2)}) collective-permute-start(f32[32,128]{1,0:T(8,128)S(1)} %get-tuple-element.23), channel_id=1, source_target_pairs={{0,1},{1,2},{2,3},{3,0},{4,5},{5,6},{6,7},{7,4},{8,9},{9,10},{10,1... | collective-permute-start | bytes 49160 | tf_op jit(solution)/shard_map/ppermute | solution.py:201
  25.1 9.0 %collective-permute-start.1 = (f32[32,128]{1,0:T(8,128)S(1)}, f32[32,128]{1,0:T(8,128)S(1)}, u32[]{:S(2)}, u32[]{:S(2)}) collective-permute-start(f32[32,128]{1,0:T(8,128)S(1)} %get-tuple-element.19.weight_ref), channel_id=1, source_target_pairs={{0,1},{1,2},{2,3},{3,0},{4,5},{5,6},{6,7},{7,4},{8,9},{9,10},{10,1... | collective-permute-start | bytes 49160 | tf_op jit(solution)/shard_map/ppermute | solution.py:201
  30.9 6.2 %all-to-all-start.2 = ((f32[8,1,128]{2,1,0:T(1,128)}), f32[8,1,128]{2,1,0:T(1,128)S(1)}, u32[]{:S(2)}, u32[]{:S(2)}) async-start(f32[8,1,128]{2,1,0:T(1,128)} %bitcast.11), calls=%async_computation.2 | async-start | bytes 8192 | tf_op jit(solution)/shard_map/all_to_all | solution.py:207
  37.9 5.6 %collective-permute-start.2 = (f32[32,128]{1,0:T(8,128)S(1)}, f32[32,128]{1,0:T(8,128)S(1)}, u32[]{:S(2)}, u32[]{:S(2)}) collective-permute-start(f32[32,128]{1,0:T(8,128)S(1)} %get-tuple-element.25), channel_id=1, source_target_pairs={{0,1},{1,2},{2,3},{3,0},{4,5},{5,6},{6,7},{7,4},{8,9},{9,10},{10,1... | collective-permute-start | bytes 49160 | tf_op jit(solution)/shard_map/ppermute | solution.py:201
  37.9 10.0 %collective-permute-start.3 = (f32[32,128]{1,0:T(8,128)S(1)}, f32[32,128]{1,0:T(8,128)S(1)}, u32[]{:S(2)}, u32[]{:S(2)}) collective-permute-start(f32[32,128]{1,0:T(8,128)S(1)} %collective-permute-done.1.weight_ref), channel_id=1, source_target_pairs={{0,1},{1,2},{2,3},{3,0},{4,5},{5,6},{6,7},{7,4},{8,9},{9,10},{10,1... | collective-permute-start | bytes 49160 | tf_op jit(solution)/shard_map/ppermute | solution.py:201
  44.6 7.2 %all-to-all-start.3 = ((f32[8,1,128]{2,1,0:T(1,128)}), f32[8,1,128]{2,1,0:T(1,128)S(1)}, u32[]{:S(2)}, u32[]{:S(2)}) async-start(f32[8,1,128]{2,1,0:T(1,128)} %bitcast.14), calls=%async_computation.3 | async-start | bytes 8192 | tf_op jit(solution)/shard_map/all_to_all | solution.py:207
  52.7 13.8 %copy-start.2 = (f32[65536]{0:T(1024)S(1)}, f32[65536]{0:T(1024)}, u32[]{:S(2)}) copy-start(f32[65536]{0:T(1024)} %param.8) | copy-start | bytes 786436
  52.7 5.6 %collective-permute-start.4 = (f32[32,128]{1,0:T(8,128)S(1)}, f32[32,128]{1,0:T(8,128)S(1)}, u32[]{:S(2)}, u32[]{:S(2)}) collective-permute-start(f32[32,128]{1,0:T(8,128)S(1)} %get-tuple-element.27), channel_id=1, source_target_pairs={{0,1},{1,2},{2,3},{3,0},{4,5},{5,6},{6,7},{7,4},{8,9},{9,10},{10,1... | collective-permute-start | bytes 49160 | tf_op jit(solution)/shard_map/ppermute | solution.py:201
  52.8 9.9 %collective-permute-start.5 = (f32[32,128]{1,0:T(8,128)S(1)}, f32[32,128]{1,0:T(8,128)S(1)}, u32[]{:S(2)}, u32[]{:S(2)}) collective-permute-start(f32[32,128]{1,0:T(8,128)S(1)} %collective-permute-done.3.weight_ref), channel_id=1, source_target_pairs={{0,1},{1,2},{2,3},{3,0},{4,5},{5,6},{6,7},{7,4},{8,9},{9,10},{10,1... | collective-permute-start | bytes 49160 | tf_op jit(solution)/shard_map/ppermute | solution.py:201
  59.4 6.2 %all-to-all-start.4 = ((f32[8,1,128]{2,1,0:T(1,128)}), f32[8,1,128]{2,1,0:T(1,128)S(1)}, u32[]{:S(2)}, u32[]{:S(2)}) async-start(f32[8,1,128]{2,1,0:T(1,128)} %bitcast.17), calls=%async_computation.4 | async-start | bytes 8192 | tf_op jit(solution)/shard_map/all_to_all | solution.py:207
  66.5 5.6 %collective-permute-start.6 = (f32[32,128]{1,0:T(8,128)S(1)}, f32[32,128]{1,0:T(8,128)S(1)}, u32[]{:S(2)}, u32[]{:S(2)}) collective-permute-start(f32[32,128]{1,0:T(8,128)S(1)} %get-tuple-element.29), channel_id=1, source_target_pairs={{0,1},{1,2},{2,3},{3,0},{4,5},{5,6},{6,7},{7,4},{8,9},{9,10},{10,1... | collective-permute-start | bytes 49160 | tf_op jit(solution)/shard_map/ppermute | solution.py:201

commit v8 on v6

--- a/solution.py
+++ b/solution.py
@@ -29,6 +29,10 @@
         out_specs=VMEM if single else tuple(VMEM for _ in out_shape),
         compiler_params=pltpu.CompilerParams(vmem_limit_bytes=24 << 20),
     )
+
+
+def middle_first(count):
+    return sorted(range(count), key=lambda index: (abs(index - count // 2), index))
 
 
 def tile_products(vectors_of, tiles_of, tiles):
@@ -100,7 +104,12 @@
     )
     block_ids = lax.broadcasted_iota(jnp.int32, (row_blocks, tiles), 0)
     placing = (block_ids == rows_ref[...]).astype(jnp.float32)
-    partial_ref[...] = placed_sum(placing, products)
+    partial = placed_sum(placing, products)
+    group_blocks = row_blocks // sections
+    for place, group in enumerate(middle_first(sections)):
+        partial_ref[pl.ds(place * group_blocks, group_blocks), :] = partial[
+            group * group_blocks : (group + 1) * group_blocks
+        ]
 
 
 def gradient_part(residual, chosen, values_ref):
@@ -200,7 +209,11 @@
 
 def gathered(parts, axis):
     count, edge = parts.shape
-    order = [index ^ 1 for index in range(count)] if count % 2 == 0 else list(range(count))
+    order = list(range(count))
+    if count % 2 == 0:
+        half = count // 2
+        far_apart = [pair // 2 if pair % 2 == 0 else half - 1 - pair // 2 for pair in range(half)]
+        order = [2 * chip + 1 for chip in far_apart] + [2 * chip for chip in far_apart]
     received = lax.all_to_all(
         parts.reshape(count, 1, edge), axis, 0, 0, axis_index_groups=[order]
     )
@@ -233,7 +246,13 @@
         ],
         compiler_params=pltpu.CompilerParams(vmem_limit_bytes=58 << 20),
     )(tile_cols[0], block_order, tile_rows[0], blocks, values)
-    parts = lax.all_to_all(partial_sum.reshape(sections, group_blocks, edge), "feat", 0, 0)
+    parts = lax.all_to_all(
+        partial_sum.reshape(sections, group_blocks, edge),
+        "feat",
+        0,
+        0,
+        axis_index_groups=[middle_first(sections)],
+    )
     state, grads, chosen = call(
         first_kernel,
         (
@@ -253,7 +272,7 @@
             [VMEM] * 6,
         )(gathered(grads, "samp"), state, chosen, old_blocks, inverses, values)
         shrunk_blocks.append(shrunk)
-        state = from_behind(moving.reshape(-1) if final else moving, "feat", 1)
+        state = from_behind(moving, "feat", 1)
         if not final:
             grads = call(
                 functools.partial(gradient_kernel, section + 1),
@@ -265,7 +284,7 @@
         float_of(blocks.shape),
         [SMEM] + [VMEM] * (1 + sections),
     )(block_order, blocks, *shrunk_blocks)
-    return (blocks.reshape(-1), state)
+    return (blocks.reshape(-1), state.reshape(-1))
 
 
 def solution(mesh):

time: 72.1 us -> 70.8 us (0.982)
  blocking collectives: 38.5 us -> 37.2 us
    all_to_all x1, blocking collectives: 12.1 us -> 10.7 us  [per_device(): lax.all_to_all(partial_sum.reshape(sections, group_blocks, edge), 'feat',...]
where the time goes in v8:
time: 70.8 us; the launch traced here: 70.3 us
  blocking collectives  37.2 us (53%)
  waiting for transfers between devices  20.5 us (29%)
  Pallas kernels  10.3 us (15%)
  starting transfers between devices  1.03 us (1%)
  between operations  0.77 us (1%)
    all_to_all x4, blocking collectives, gathered(): lax.all_to_all(parts.reshape(count, 1, edge), axis, 0, 0, axis_index_grou...  26.5 us
    ppermute x4, waiting for transfers between devices, from_behind(): return lax.ppermute(value, axis, pairs)  20.5 us
    all_to_all x1, blocking collectives, per_device(): lax.all_to_all(partial_sum.reshape(sections, group_blocks, edge), 'feat',...  10.7 us
    pallas_call x4, Pallas kernels, per_device(): call(functools.partial(update_kernel, section), (float_of(moved_shape), f...  3.43 us
    pallas_call x1, Pallas kernels, per_device(): pl.pallas_call(margins_kernel, out_shape=(float_of((row_blocks, edge)), f...  3.32 us
    pallas_call x3, Pallas kernels, per_device(): call(functools.partial(gradient_kernel, section + 1), float_of((samp_coun...  1.63 us
  transfers between devices with their start and end apart: 4, of which 4 were waited for; matrix products, arithmetic and copies ran while one was open for 0% of the time, Pallas kernels for 2%

profile of v8, /device:TPU:0, one launch (start us, length us, event | category | flops | bytes accessed | tf_op | source)
XLA Modules:
  0.0 70.3 jit_solution(6744581564479375859)
XLA Ops:
  0.6 0.0 copy-start.5
  0.6 0.0 copy-start
  0.7 0.0 copy-start.6
  0.7 0.0 copy-start.7
  0.7 0.0 copy-start.3
  0.7 0.0 copy-start.1
  0.7 3.3 %shard_map.86 = (f32[128,128]{1,0:T(8,128)}, f32[4,128]{1,0:T(4,128)}) custom-call(s32[1,64]{1,0:T(1,128)} %bitcast.49, s32[1,4]{1,0:T(1,128)} %targets_smem.1, s32[1,64]{1,0:T(1,128)} %bitcast.51, f32[512,128]{1,0:T(8,128)} %bitcast.38, bf16[64,128,128]{2,1,0:T(8,128)(2,1)} %bitcast.25), custom_call_target="tpu_custom_call" | custom-call | tf_op jit(solution)/shard_map/pallas_call | solution.py:232
  4.0 0.0 copy-start.4
  4.0 10.7 %all_to_all.25.parts_ref = f32[4,32,128]{2,1,0:T(8,128)S(1)} all-to-all(f32[4,32,128]{2,1,0:T(8,128)} %bitcast.54), channel_id=1, replica_groups={{2,1,3,0},{6,5,7,4},{10,9,11,8},{14,13,15,12},{18,17,19,16},{22,21,23,2..., dimensions={0} | all-to-all | bytes 131072 | tf_op jit(solution)/shard_map/all_to_all | solution.py:249
  14.7 0.0 copy-done.5
  14.7 0.0 copy-done
  14.7 0.0 copy-done.6
  14.7 0.0 copy-done.7
  14.7 0.0 copy-done.3
  14.7 0.6 shard_map.87
  15.4 7.9 %all_to_all.26 = f32[8,1,128]{2,1,0:T(1,128)S(1)} all-to-all(f32[8,1,128]{2,1,0:T(1,128)S(1)} %bitcast.48), channel_id=1, replica_groups={{4,28,12,20,0,24,8,16},{5,29,13,21,1,25,9,17},{6,30,14,22,2,26,10,18},{..., dimensions={0} | all-to-all | bytes 8192 | tf_op jit(solution)/shard_map/all_to_all | solution.py:217
  23.3 0.0 copy-done.1
  23.3 0.0 copy-done.4
  23.3 0.9 %shard_map.88 = (f32[2,32,128]{2,1,0:T(8,128)S(1)}, f32[1,128]{1,0:T(1,128)S(1)}) custom-call(f32[8,128]{1,0:T(8,128)S(1)} %bitcast.41, f32[2,32,128]{2,1,0:T(8,128)S(1)} %get-tuple-element.17.state_ref, f32[4,32,64]{2,1,0:T(8,128)S(1)} %get-tuple-element.18.chosen_ref, f32[4,128]{1,0:T(4,128)S(1)} %copy-done.4, f32[4,128,128]{2,1,0:T(8,128)S(1)} %bitcast.34, ...), custom_call_target="tpu_custom_call" | custom-call | tf_op jit(solution)/shard_map/pallas_call | solution.py:269
  24.1 0.9 %collective-permute-start = (f32[2,32,128]{2,1,0:T(8,128)S(1)}, f32[2,32,128]{2,1,0:T(8,128)S(1)}, u32[]{:S(2)}, u32[]{:S(2)}) collective-permute-start(f32[2,32,128]{2,1,0:T(8,128)S(1)} %get-tuple-element.21), channel_id=1, source_target_pairs={{0,1},{1,2},{2,3},{3,0},{4,5},{5,6},{6,7},{7,4},{8,9},{9,10},{10,1... | collective-permute-start | bytes 98312 | tf_op jit(solution)/shard_map/ppermute | solution.py:207
  25.1 4.8 %collective-permute-done.state_ref = f32[2,32,128]{2,1,0:T(8,128)S(1)} collective-permute-done((f32[2,32,128]{2,1,0:T(8,128)S(1)}, f32[2,32,128]{2,1,0:T(8,128)S(1)}, u32[]{:S(2)}, u32[]{:S(2)}) %collective-permute-start) | collective-permute-done | bytes 32800 | tf_op jit(solution)/shard_map/ppermute | solution.py:207
  29.9 0.5 shard_map.89
  30.4 6.1 %all_to_all.27 = f32[8,1,128]{2,1,0:T(1,128)S(1)} all-to-all(f32[8,1,128]{2,1,0:T(1,128)S(1)} %bitcast.45), channel_id=1, replica_groups={{4,28,12,20,0,24,8,16},{5,29,13,21,1,25,9,17},{6,30,14,22,2,26,10,18},{..., dimensions={0} | all-to-all | bytes 8192 | tf_op jit(solution)/shard_map/all_to_all | solution.py:217
  36.5 0.9 %shard_map.90 = (f32[2,32,128]{2,1,0:T(8,128)S(1)}, f32[1,128]{1,0:T(1,128)S(1)}) custom-call(f32[8,128]{1,0:T(8,128)S(1)} %bitcast.43, f32[2,32,128]{2,1,0:T(8,128)S(1)} %collective-permute-done.state_ref, f32[4,32,64]{2,1,0:T(8,128)S(1)} %get-tuple-element.18.chosen_ref, f32[4,128]{1,0:T(4,128)S(1)} %copy-done.4, f32[4,128,128]{2,1,0:T(8,128)S(1)} %bitcast.35, ...), custom_call_target="tpu_custom_call" | custom-call | tf_op jit(solution)/shard_map/pallas_call | solution.py:269
  37.3 0.0 collective-permute-start.1
  37.4 5.7 %collective-permute-done.1.state_ref = f32[2,32,128]{2,1,0:T(8,128)S(1)} collective-permute-done((f32[2,32,128]{2,1,0:T(8,128)S(1)}, f32[2,32,128]{2,1,0:T(8,128)S(1)}, u32[]{:S(2)}, u32[]{:S(2)}) %collective-permute-start.1) | collective-permute-done | bytes 32800 | tf_op jit(solution)/shard_map/ppermute | solution.py:207
  43.1 0.5 shard_map.91
  43.6 6.5 %all_to_all.28 = f32[8,1,128]{2,1,0:T(1,128)S(1)} all-to-all(f32[8,1,128]{2,1,0:T(1,128)S(1)} %bitcast.46), channel_id=1, replica_groups={{4,28,12,20,0,24,8,16},{5,29,13,21,1,25,9,17},{6,30,14,22,2,26,10,18},{..., dimensions={0} | all-to-all | bytes 8192 | tf_op jit(solution)/shard_map/all_to_all | solution.py:217
  50.1 0.9 %shard_map.92 = (f32[2,32,128]{2,1,0:T(8,128)S(1)}, f32[1,128]{1,0:T(1,128)S(1)}) custom-call(f32[8,128]{1,0:T(8,128)S(1)} %bitcast.44, f32[2,32,128]{2,1,0:T(8,128)S(1)} %collective-permute-done.1.state_ref, f32[4,32,64]{2,1,0:T(8,128)S(1)} %get-tuple-element.18.chosen_ref, f32[4,128]{1,0:T(4,128)S(1)} %copy-done.4, f32[4,128,128]{2,1,0:T(8,128)S(1)} %bitcast.36, ...), custom_call_target="tpu_custom_call" | custom-call | tf_op jit(solution)/shard_map/pallas_call | solution.py:269
  50.9 0.0 copy-start.2
  50.9 0.1 collective-permute-start.2
  51.0 5.7 %collective-permute-done.2.state_ref = f32[2,32,128]{2,1,0:T(8,128)S(1)} collective-permute-done((f32[2,32,128]{2,1,0:T(8,128)S(1)}, f32[2,32,128]{2,1,0:T(8,128)S(1)}, u32[]{:S(2)}, u32[]{:S(2)}) %collective-permute-start.2) | collective-permute-done | bytes 32800 | tf_op jit(solution)/shard_map/ppermute | solution.py:207
  56.7 0.5 shard_map.93
  57.3 6.1 %all_to_all.29 = f32[8,1,128]{2,1,0:T(1,128)S(1)} all-to-all(f32[8,1,128]{2,1,0:T(1,128)S(1)} %bitcast.47), channel_id=1, replica_groups={{4,28,12,20,0,24,8,16},{5,29,13,21,1,25,9,17},{6,30,14,22,2,26,10,18},{..., dimensions={0} | all-to-all | bytes 8192 | tf_op jit(solution)/shard_map/all_to_all | solution.py:217
  63.3 0.9 %shard_map.94 = (f32[32,128]{1,0:T(8,128)S(1)}, f32[1,128]{1,0:T(1,128)S(1)}) custom-call(f32[8,128]{1,0:T(8,128)S(1)} %bitcast.42, f32[2,32,128]{2,1,0:T(8,128)S(1)} %collective-permute-done.2.state_ref, f32[4,32,64]{2,1,0:T(8,128)S(1)} %get-tuple-element.18.chosen_ref, f32[4,128]{1,0:T(4,128)S(1)} %copy-done.4, f32[4,128,128]{2,1,0:T(8,128)S(1)} %bitcast.37, ...), custom_call_target="tpu_custom_call" | custom-call | tf_op jit(solution)/shard_map/pallas_call | solution.py:269
  64.2 0.0 collective-permute-start.3
  64.2 0.0 copy-done.2
  64.2 1.3 %shard_map.95 = f32[512,128]{1,0:T(8,128)} custom-call(s32[1,4]{1,0:T(1,128)S(1)} %copy-done.5, f32[512,128]{1,0:T(8,128)S(1)} %bitcast.39, f32[1,128]{1,0:T(1,128)S(1)} %get-tuple-element.20.refs_0_, f32[1,128]{1,0:T(1,128)S(1)} %get-tuple-element.22.refs_1_, f32[1,128]{1,0:T(1,128)S(1)} %get-tuple-element.24.refs_2_, f32[1,128]{1,0:T(1,128)S(1)} %get-tuple-element.26.refs_3_), custom_call_target="tpu_custom_call" | custom-call | tf_op jit(solution)/shard_map/pallas_call | solution.py:282
  65.5 4.3 %collective-permute-done.3 = f32[32,128]{1,0:T(8,128)S(1)} collective-permute-done((f32[32,128]{1,0:T(8,128)S(1)}, f32[32,128]{1,0:T(8,128)S(1)}, u32[]{:S(2)}, u32[]{:S(2)}) %collective-permute-start.3) | collective-permute-done | bytes 16416 | tf_op jit(solution)/shard_map/ppermute | solution.py:207
  69.7 0.6 copy.14
Async XLA Ops:
  0.6 14.1 %copy-start.5 = (s32[1,4]{1,0:T(1,128)S(1)}, s32[1,4]{1,0:T(1,128)}, u32[]{:S(2)}) copy-start(s32[1,4]{1,0:T(1,128)} %targets_smem.1) | copy-start | bytes 52
  0.6 14.1 %copy-start = (bf16[1,1,64,128,128]{4,3,2,1,0:T(8,128)(2,1)S(1)}, bf16[1,1,64,128,128]{4,3,2,1,0:T(8,128)(2,1)}, u32[]{:S(2)}) copy-start(bf16[1,1,64,128,128]{4,3,2,1,0:T(8,128)(2,1)} %param.11) | copy-start | bytes 6291460
  0.7 14.1 %copy-start.6 = (s32[1,1,64]{2,1,0:T(1,128)S(1)}, s32[1,1,64]{2,1,0:T(1,128)}, u32[]{:S(2)}) copy-start(s32[1,1,64]{2,1,0:T(1,128)} %param.10) | copy-start | bytes 772
  0.7 14.1 %copy-start.7 = (s32[1,1,64]{2,1,0:T(1,128)S(1)}, s32[1,1,64]{2,1,0:T(1,128)}, u32[]{:S(2)}) copy-start(s32[1,1,64]{2,1,0:T(1,128)} %param.9) | copy-start | bytes 772
  0.7 14.1 %copy-start.3 = (s32[16384]{0:T(1024)S(1)}, s32[16384]{0:T(1024)}, u32[]{:S(2)}) copy-start(s32[16384]{0:T(1024)} %param.7) | copy-start | bytes 196612
  0.7 22.6 %copy-start.1 = (f32[1,4,128,128]{3,2,1,0:T(8,128)S(1)}, f32[1,4,128,128]{3,2,1,0:T(8,128)}, u32[]{:S(2)}) copy-start(f32[1,4,128,128]{3,2,1,0:T(8,128)} %param.13) | copy-start | bytes 786436
  4.0 19.3 %copy-start.4 = (f32[4,128]{1,0:T(4,128)S(1)}, f32[4,128]{1,0:T(4,128)}, u32[]{:S(2)}) copy-start(f32[4,128]{1,0:T(4,128)} %get-tuple-element.19.old_ref) | copy-start | bytes 6148
  24.1 5.7 %collective-permute-start = (f32[2,32,128]{2,1,0:T(8,128)S(1)}, f32[2,32,128]{2,1,0:T(8,128)S(1)}, u32[]{:S(2)}, u32[]{:S(2)}) collective-permute-start(f32[2,32,128]{2,1,0:T(8,128)S(1)} %get-tuple-element.21), channel_id=1, source_target_pairs={{0,1},{1,2},{2,3},{3,0},{4,5},{5,6},{6,7},{7,4},{8,9},{9,10},{10,1... | collective-permute-start | bytes 98312 | tf_op jit(solution)/shard_map/ppermute | solution.py:207
  37.3 5.7 %collective-permute-start.1 = (f32[2,32,128]{2,1,0:T(8,128)S(1)}, f32[2,32,128]{2,1,0:T(8,128)S(1)}, u32[]{:S(2)}, u32[]{:S(2)}) collective-permute-start(f32[2,32,128]{2,1,0:T(8,128)S(1)} %get-tuple-element.23), channel_id=1, source_target_pairs={{0,1},{1,2},{2,3},{3,0},{4,5},{5,6},{6,7},{7,4},{8,9},{9,10},{10,1... | collective-permute-start | bytes 98312 | tf_op jit(solution)/shard_map/ppermute | solution.py:207
  50.9 13.3 %copy-start.2 = (f32[65536]{0:T(1024)S(1)}, f32[65536]{0:T(1024)}, u32[]{:S(2)}) copy-start(f32[65536]{0:T(1024)} %param.8) | copy-start | bytes 786436
  50.9 5.8 %collective-permute-start.2 = (f32[2,32,128]{2,1,0:T(8,128)S(1)}, f32[2,32,128]{2,1,0:T(8,128)S(1)}, u32[]{:S(2)}, u32[]{:S(2)}) collective-permute-start(f32[2,32,128]{2,1,0:T(8,128)S(1)} %get-tuple-element.25), channel_id=1, source_target_pairs={{0,1},{1,2},{2,3},{3,0},{4,5},{5,6},{6,7},{7,4},{8,9},{9,10},{10,1... | collective-permute-start | bytes 98312 | tf_op jit(solution)/shard_map/ppermute | solution.py:207
  64.2 5.6 %collective-permute-start.3 = (f32[32,128]{1,0:T(8,128)S(1)}, f32[32,128]{1,0:T(8,128)S(1)}, u32[]{:S(2)}, u32[]{:S(2)}) collective-permute-start(f32[32,128]{1,0:T(8,128)S(1)} %get-tuple-element.27), channel_id=1, source_target_pairs={{0,1},{1,2},{2,3},{3,0},{4,5},{5,6},{6,7},{7,4},{8,9},{9,10},{10,1... | collective-permute-start | bytes 49160 | tf_op jit(solution)/shard_map/ppermute | solution.py:207

commit v9 on v8

--- a/solution.py
+++ b/solution.py
@@ -20,13 +20,14 @@
     return jax.ShapeDtypeStruct(shape, jnp.float32)
 
 
-def call(kernel, out_shape, in_specs):
+def call(kernel, out_shape, in_specs, scratch_shapes=()):
     single = not isinstance(out_shape, tuple)
     return pl.pallas_call(
         kernel,
         out_shape=out_shape,
         in_specs=in_specs,
         out_specs=VMEM if single else tuple(VMEM for _ in out_shape),
+        scratch_shapes=scratch_shapes,
         compiler_params=pltpu.CompilerParams(vmem_limit_bytes=24 << 20),
     )
 
@@ -158,12 +159,22 @@
     grad_ref[...] = jnp.broadcast_to(grad, grad_ref.shape)
 
 
-def gradient_kernel(section, state_ref, chosen_ref, values_ref, grad_ref):
+def gradient_kernel(
+    section, ahead_ref, aside_any, chosen_ref, values_ref, state_ref, grad_ref, aside_sem
+):
+    state_ref[...] = ahead_ref[...]
+
+    @pl.when(lax.axis_index("feat") == 1)
+    def _():
+        copy = pltpu.make_async_copy(aside_any, state_ref, aside_sem)
+        copy.start()
+        copy.wait()
+
     grad = gradient_part(state_ref[0], chosen_ref[section], values_ref)
     grad_ref[...] = jnp.broadcast_to(grad, grad_ref.shape)
 
 
-def update_kernel(
+def update(
     section, grads_ref, state_ref, chosen_ref, old_ref, inverses_ref, values_ref,
     moved_ref, shrunk_ref,
 ):
@@ -194,6 +205,24 @@
         moved_ref[...] = residual
 
 
+def update_kernel(section, *refs):
+    update(section, *refs)
+
+
+def update_where_kernel(section, on_first, *refs):
+    state_ref, moved_ref, shrunk_ref = refs[1], refs[-2], refs[-1]
+    mine = (lax.axis_index("feat") == 0) == on_first
+
+    @pl.when(mine)
+    def _():
+        update(section, *refs)
+
+    @pl.when(jnp.logical_not(mine))
+    def _():
+        moved_ref[...] = state_ref[...] if len(moved_ref.shape) == 3 else state_ref[0]
+        shrunk_ref[...] = jnp.zeros_like(shrunk_ref)
+
+
 def blocks_kernel(sections, targets_smem, beta_ref, *refs):
     blocks_ref = refs[sections]
     blocks_ref[...] = beta_ref[...]
@@ -204,6 +233,11 @@
 def from_behind(value, axis, steps):
     count = lax.axis_size(axis)
     pairs = [(source, (source + steps) % count) for source in range(count)]
+    return lax.ppermute(value, axis, pairs)
+
+
+def swapped_in_pairs(value, axis):
+    pairs = [(index, index ^ 1) for index in range(lax.axis_size(axis))]
     return lax.ppermute(value, axis, pairs)
 
 
@@ -262,29 +296,55 @@
         ),
         [VMEM] * 6,
     )(parts, labels.reshape(row_blocks, edge), tile_rows[0], tile_cols[0], block_order, values)
+    my_index = lax.axis_index("feat")
+    first_apart = sections % 2 == 0
     shrunk_blocks = []
     for section in range(sections):
         final = section + 1 == sections
         moved_shape = (group_blocks, edge) if final else (2, group_blocks, edge)
-        moving, shrunk = call(
-            functools.partial(update_kernel, section),
-            (float_of(moved_shape), float_of((1, edge))),
-            [VMEM] * 6,
-        )(gathered(grads, "samp"), state, chosen, old_blocks, inverses, values)
+        out_shape = (float_of(moved_shape), float_of((1, edge)))
+        operands = (gathered(grads, "samp"), state, chosen, old_blocks, inverses, values)
+        if first_apart:
+            moving, shrunk = call(
+                functools.partial(update_where_kernel, section, False), out_shape, [VMEM] * 6
+            )(*operands)
+            ahead = from_behind(moving, "feat", 1)
+
+            def in_first_pair(*operands, section=section, out_shape=out_shape):
+                moving, shrunk = call(
+                    functools.partial(update_where_kernel, section, True), out_shape, [VMEM] * 6
+                )(*operands)
+                return swapped_in_pairs(moving, "feat"), shrunk
+
+            def elsewhere(*operands, out_shape=out_shape):
+                return tuple(jnp.zeros(part.shape, part.dtype) for part in out_shape)
+
+            aside, shrunk_on_first = lax.cond(
+                my_index <= 1, in_first_pair, elsewhere, *operands
+            )
+            shrunk = jnp.where(my_index == 0, shrunk_on_first, shrunk)
+        else:
+            moving, shrunk = call(
+                functools.partial(update_kernel, section), out_shape, [VMEM] * 6
+            )(*operands)
+            ahead = from_behind(moving, "feat", 1)
+            aside = ahead
         shrunk_blocks.append(shrunk)
-        state = from_behind(moving, "feat", 1)
-        if not final:
-            grads = call(
+        if final:
+            residual = jnp.where(my_index == 1, aside, ahead)
+        else:
+            state, grads = call(
                 functools.partial(gradient_kernel, section + 1),
-                float_of((samp_count, edge)),
-                [VMEM] * 3,
-            )(state, chosen, values)
+                (float_of(moved_shape), float_of((samp_count, edge))),
+                [VMEM, pl.BlockSpec(memory_space=pl.ANY), VMEM, VMEM],
+                [pltpu.SemaphoreType.DMA],
+            )(ahead, aside, chosen, values)
     blocks = call(
         functools.partial(blocks_kernel, sections),
         float_of(blocks.shape),
         [SMEM] + [VMEM] * (1 + sections),
     )(block_order, blocks, *shrunk_blocks)
-    return (blocks.reshape(-1), state.reshape(-1))
+    return (blocks.reshape(-1), residual.reshape(-1))
 
 
 def solution(mesh):

time: 70.8 us -> 74.5 us (1.052)
  starting transfers between devices: 1.03 us -> 13.8 us
  blocking collectives: 37.2 us -> 24.6 us
  waiting for transfers between devices: 20.5 us -> 22.5 us
  Pallas kernels: 10.3 us -> 11.5 us
    ppermute x4, waiting for transfers between devices: 20.5 us -> 0.01 us  [from_behind(): return lax.ppermute(value, axis, pairs)]
    ppermute x0 -> x4, waiting for transfers between devices: none -> 15.7 us  [swapped_in_pairs(): return lax.ppermute(value, axis, pairs)]
    all_to_all x4 -> x2, blocking collectives: 26.5 us -> 14 us  [gathered(): lax.all_to_all(parts.reshape(count, 1, edge), axis, 0, 0, axis_index_grou...]
    all_to_all x0 -> x2, waiting for transfers between devices: none -> 6.86 us  [gathered(): lax.all_to_all(parts.reshape(count, 1, edge), axis, 0, 0, axis_index_grou...]
    all_to_all x0 -> x2, starting transfers between devices: none -> 6.55 us  [gathered(): lax.all_to_all(parts.reshape(count, 1, edge), axis, 0, 0, axis_index_grou...]
    ppermute x4, starting transfers between devices: 1.03 us -> 6.93 us  [from_behind(): return lax.ppermute(value, axis, pairs)]
    pallas_call x7 -> x11, Pallas kernels: 5.06 us -> 6.34 us  [the longest x4 3.43 us: in_first_pair(): call(functools.partial(update_where_kernel, section, True), out_shape, [V...]
  transfers between devices with their start and end apart: 4 -> 10, of which waited for: 4 -> 6; matrix products, arithmetic and copies ran while one was open for 0% -> 0% of each run, Pallas kernels for 2% -> 6%
where the time goes in v9:
time: 74.5 us; the launch traced here: 74 us
  blocking collectives  24.6 us (33%)
  waiting for transfers between devices  22.5 us (30%)
  starting transfers between devices  13.8 us (19%)
  Pallas kernels  11.5 us (15%)
  between operations  0.78 us (1%)
    ppermute x4, waiting for transfers between devices, swapped_in_pairs(): return lax.ppermute(value, axis, pairs)  15.7 us
    all_to_all x2, blocking collectives, gathered(): lax.all_to_all(parts.reshape(count, 1, edge), axis, 0, 0, axis_index_grou...  14 us
    all_to_all x1, blocking collectives, per_device(): lax.all_to_all(partial_sum.reshape(sections, group_blocks, edge), 'feat',...  10.7 us
    ppermute x4, starting transfers between devices, from_behind(): return lax.ppermute(value, axis, pairs)  6.93 us
    all_to_all x2, waiting for transfers between devices, gathered(): lax.all_to_all(parts.reshape(count, 1, edge), axis, 0, 0, axis_index_grou...  6.86 us
    all_to_all x2, starting transfers between devices, gathered(): lax.all_to_all(parts.reshape(count, 1, edge), axis, 0, 0, axis_index_grou...  6.55 us
    pallas_call x4, Pallas kernels, in_first_pair(): call(functools.partial(update_where_kernel, section, True), out_shape, [V...  3.43 us
    pallas_call x1, Pallas kernels, per_device(): pl.pallas_call(margins_kernel, out_shape=(float_of((row_blocks, edge)), f...  3.32 us
  transfers between devices with their start and end apart: 10, of which 6 were waited for; matrix products, arithmetic and copies ran while one was open for 0% of the time, Pallas kernels for 6%

profile of v9, /device:TPU:0, one launch (start us, length us, event | category | flops | bytes accessed | tf_op | source)
XLA Modules:
  0.0 74.0 jit_solution(7234963447693927268)
XLA Ops:
  0.6 0.0 copy-start.2
  0.6 0.0 copy-start.5
  0.7 0.0 copy-start.3
  0.7 0.0 copy-start.4
  0.7 0.0 copy-start.1
  0.7 0.0 copy-start.6
  0.7 3.3 %shard_map.86 = (f32[128,128]{1,0:T(8,128)}, f32[4,128]{1,0:T(4,128)S(1)}) custom-call(s32[1,64]{1,0:T(1,128)} %bitcast.31, s32[1,4]{1,0:T(1,128)} %targets_smem.1, s32[1,64]{1,0:T(1,128)} %bitcast.33, f32[512,128]{1,0:T(8,128)} %bitcast.26, bf16[64,128,128]{2,1,0:T(8,128)(2,1)} %bitcast.35), custom_call_target="tpu_custom_call" | custom-call | tf_op jit(solution)/shard_map/pallas_call | solution.py:266
  4.0 10.7 %all_to_all.25.parts_ref = f32[4,32,128]{2,1,0:T(8,128)S(1)} all-to-all(f32[4,32,128]{2,1,0:T(8,128)} %bitcast.57), channel_id=1, replica_groups={{2,1,3,0},{6,5,7,4},{10,9,11,8},{14,13,15,12},{18,17,19,16},{22,21,23,2..., dimensions={0} | all-to-all | bytes 131072 | tf_op jit(solution)/shard_map/all_to_all | solution.py:283
  14.7 0.0 copy-done.2
  14.7 0.0 copy-done.5
  14.7 0.0 copy-done.3
  14.7 0.0 copy-done.4
  14.7 0.6 shard_map.87
  15.4 7.9 %all_to_all.26 = f32[8,1,128]{2,1,0:T(1,128)S(1)} all-to-all(f32[8,1,128]{2,1,0:T(1,128)S(1)} %bitcast.29), channel_id=1, replica_groups={{4,28,12,20,0,24,8,16},{5,29,13,21,1,25,9,17},{6,30,14,22,2,26,10,18},{..., dimensions={0} | all-to-all | bytes 8192 | tf_op jit(solution)/shard_map/all_to_all | solution.py:251
  23.3 1.8 %collective-permute-start.4 = (f32[2,32,128]{2,1,0:T(8,128)S(1)}, f32[2,32,128]{2,1,0:T(8,128)S(1)}, u32[]{:S(2)}, u32[]{:S(2)}) collective-permute-start(f32[2,32,128]{2,1,0:T(8,128)S(1)} %get-tuple-element.116), channel_id=1, source_target_pairs={{0,1},{1,2},{2,3},{3,0},{4,5},{5,6},{6,7},{7,4},{8,9},{9,10},{10,1... | collective-permute-start | bytes 98312 | tf_op jit(solution)/shard_map/ppermute | solution.py:236
  25.1 4.9 %conditional.4 = (f32[2,32,128]{2,1,0:T(8,128)}, f32[1,128]{1,0:T(1,128)S(1)}) conditional(s32[]{:T(128)} %convert_element_type.2, () %tuple.40, (f32[8,128]{1,0:T(8,128)S(1)}, f32[2,32,128]{2,1,0:T(8,128)S(1)}, f32[4,32,64]{2,1,0:T(8,128)S(1)}, f32[4,128]{1,0:T(4,128)S(1)}, f32[4,128,128]{2,1,0:T(8,128)S(1)}, ...), branch_computations={%region_0.0_spmd, %region_1.0_spmd} | conditional | bytes 131128 | solution.py:322
  25.1 0.9 %branch_1_fun.4 = (f32[2,32,128]{2,1,0:T(8,128)S(1)}, f32[1,128]{1,0:T(1,128)S(1)}) custom-call(f32[8,128]{1,0:T(8,128)S(1)} %get-tuple-element.48.refs_0_, f32[2,32,128]{2,1,0:T(8,128)S(1)} %get-tuple-element.49.refs_1_, f32[4,32,64]{2,1,0:T(8,128)S(1)} %get-tuple-element.50.refs_2_, f32[4,128]{1,0:T(4,128)S(1)} %get-tuple-element.51.refs_3_, ...), custom_call_target="tpu_custom_call" | custom-call | tf_op jit(solution)/shard_map/cond/branch_1_fun/pallas_call | solution.py:314
  25.9 0.3 collective-permute-start
  26.2 3.8 %collective-permute-done = f32[2,32,128]{2,1,0:T(8,128)} collective-permute-done((f32[2,32,128]{2,1,0:T(8,128)S(1)}, f32[2,32,128]{2,1,0:T(8,128)}, u32[]{:S(2)}, u32[]{:S(2)}) %collective-permute-start) | collective-permute-done | bytes 32800 | tf_op jit(solution)/shard_map/cond/branch_1_fun/ppermute | solution.py:241
  30.0 0.0 collective-permute-done.4.ahead_ref
  30.0 0.6 shard_map.89
  30.6 6.0 %all_to_all.27 = f32[8,1,128]{2,1,0:T(1,128)S(1)} all-to-all(f32[8,1,128]{2,1,0:T(1,128)S(1)} %bitcast.30), channel_id=1, replica_groups={{4,28,12,20,0,24,8,16},{5,29,13,21,1,25,9,17},{6,30,14,22,2,26,10,18},{..., dimensions={0} | all-to-all | bytes 8192 | tf_op jit(solution)/shard_map/all_to_all | solution.py:251
  36.6 1.9 %collective-permute-start.5 = (f32[2,32,128]{2,1,0:T(8,128)S(1)}, f32[2,32,128]{2,1,0:T(8,128)S(1)}, u32[]{:S(2)}, u32[]{:S(2)}) collective-permute-start(f32[2,32,128]{2,1,0:T(8,128)S(1)} %get-tuple-element.122), channel_id=1, source_target_pairs={{0,1},{1,2},{2,3},{3,0},{4,5},{5,6},{6,7},{7,4},{8,9},{9,10},{10,1... | collective-permute-start | bytes 98312 | tf_op jit(solution)/shard_map/ppermute | solution.py:236
  38.5 4.9 %conditional.5 = (f32[2,32,128]{2,1,0:T(8,128)}, f32[1,128]{1,0:T(1,128)S(1)}) conditional(s32[]{:T(128)} %convert_element_type.2, () %tuple.42, (f32[8,128]{1,0:T(8,128)S(1)}, f32[2,32,128]{2,1,0:T(8,128)S(1)}, f32[4,32,64]{2,1,0:T(8,128)S(1)}, f32[4,128]{1,0:T(4,128)S(1)}, f32[4,128,128]{2,1,0:T(8,128)S(1)}, ...), branch_computations={%region_2.3_spmd, %region_3.4_spmd} | conditional | bytes 131128 | solution.py:322
  38.5 0.9 %branch_1_fun.5 = (f32[2,32,128]{2,1,0:T(8,128)S(1)}, f32[1,128]{1,0:T(1,128)S(1)}) custom-call(f32[8,128]{1,0:T(8,128)S(1)} %get-tuple-element.56.refs_0_, f32[2,32,128]{2,1,0:T(8,128)S(1)} %get-tuple-element.57.refs_1_, f32[4,32,64]{2,1,0:T(8,128)S(1)} %get-tuple-element.58.refs_2_, f32[4,128]{1,0:T(4,128)S(1)} %get-tuple-element.59.refs_3_, ...), custom_call_target="tpu_custom_call" | custom-call | tf_op jit(solution)/shard_map/cond/branch_1_fun/pallas_call | solution.py:314
  39.3 0.0 collective-permute-start.1
  39.4 4.0 %collective-permute-done.1 = f32[2,32,128]{2,1,0:T(8,128)} collective-permute-done((f32[2,32,128]{2,1,0:T(8,128)S(1)}, f32[2,32,128]{2,1,0:T(8,128)}, u32[]{:S(2)}, u32[]{:S(2)}) %collective-permute-start.1) | collective-permute-done | bytes 32800 | tf_op jit(solution)/shard_map/cond/branch_1_fun/ppermute | solution.py:241
  43.4 0.0 collective-permute-done.5.ahead_ref
  43.4 1.2 %shard_map.91 = (f32[2,32,128]{2,1,0:T(8,128)S(1)}, f32[8,128]{1,0:T(8,128)}) custom-call(f32[2,32,128]{2,1,0:T(8,128)S(1)} %collective-permute-done.5.ahead_ref, f32[2,32,128]{2,1,0:T(8,128)} %get-tuple-element.123.aside_any, f32[4,32,64]{2,1,0:T(8,128)S(1)} %get-tuple-element.112.refs_2_.chosen_ref, bf16[64,128,128]{2,1,0:T(8,128)(2,1)S(1)} %bitcast.42), custom_call_target="tpu_custom_call" | custom-call | tf_op jit(solution)/shard_map/pallas_call | solution.py:336
  44.5 3.3 %all-to-all-start.3 = ((f32[8,1,128]{2,1,0:T(1,128)}), f32[8,1,128]{2,1,0:T(1,128)S(1)}, u32[]{:S(2)}, u32[]{:S(2)}) async-start(f32[8,1,128]{2,1,0:T(1,128)} %bitcast.14), calls=%async_computation.3 | async-start | bytes 8192 | tf_op jit(solution)/shard_map/all_to_all | solution.py:251
  47.8 3.3 %all-to-all-done.3 = f32[8,1,128]{2,1,0:T(1,128)S(1)} async-done(((f32[8,1,128]{2,1,0:T(1,128)}), f32[8,1,128]{2,1,0:T(1,128)S(1)}, u32[]{:S(2)}, u32[]{:S(2)}) %all-to-all-start.3) | async-done | bytes 4128 | tf_op jit(solution)/shard_map/all_to_all | solution.py:251
  51.1 1.6 %collective-permute-start.6 = (f32[2,32,128]{2,1,0:T(8,128)S(1)}, f32[2,32,128]{2,1,0:T(8,128)S(1)}, u32[]{:S(2)}, u32[]{:S(2)}) collective-permute-start(f32[2,32,128]{2,1,0:T(8,128)S(1)} %get-tuple-element.128), channel_id=1, source_target_pairs={{0,1},{1,2},{2,3},{3,0},{4,5},{5,6},{6,7},{7,4},{8,9},{9,10},{10,1... | collective-permute-start | bytes 98312 | tf_op jit(solution)/shard_map/ppermute | solution.py:236
  52.8 4.9 %conditional.6 = (f32[2,32,128]{2,1,0:T(8,128)}, f32[1,128]{1,0:T(1,128)S(1)}) conditional(s32[]{:T(128)} %convert_element_type.2, () %tuple.44, (f32[8,128]{1,0:T(8,128)S(1)}, f32[2,32,128]{2,1,0:T(8,128)S(1)}, f32[4,32,64]{2,1,0:T(8,128)S(1)}, f32[4,128]{1,0:T(4,128)S(1)}, f32[4,128,128]{2,1,0:T(8,128)S(1)}, ...), branch_computations={%region_4.5_spmd, %region_5.6_spmd} | conditional | bytes 131128 | solution.py:322
  52.8 0.9 %branch_1_fun.6 = (f32[2,32,128]{2,1,0:T(8,128)S(1)}, f32[1,128]{1,0:T(1,128)S(1)}) custom-call(f32[8,128]{1,0:T(8,128)S(1)} %get-tuple-element.64.refs_0_, f32[2,32,128]{2,1,0:T(8,128)S(1)} %get-tuple-element.65.refs_1_, f32[4,32,64]{2,1,0:T(8,128)S(1)} %get-tuple-element.66.refs_2_, f32[4,128]{1,0:T(4,128)S(1)} %get-tuple-element.67.refs_3_, ...), custom_call_target="tpu_custom_call" | custom-call | tf_op jit(solution)/shard_map/cond/branch_1_fun/pallas_call | solution.py:314
  53.6 0.0 collective-permute-start.2
  53.7 4.0 %collective-permute-done.2 = f32[2,32,128]{2,1,0:T(8,128)} collective-permute-done((f32[2,32,128]{2,1,0:T(8,128)S(1)}, f32[2,32,128]{2,1,0:T(8,128)}, u32[]{:S(2)}, u32[]{:S(2)}) %collective-permute-start.2) | collective-permute-done | bytes 32800 | tf_op jit(solution)/shard_map/cond/branch_1_fun/ppermute | solution.py:241
  57.7 0.0 collective-permute-done.6.ahead_ref
  57.7 1.2 %shard_map.93 = (f32[2,32,128]{2,1,0:T(8,128)S(1)}, f32[8,128]{1,0:T(8,128)}) custom-call(f32[2,32,128]{2,1,0:T(8,128)S(1)} %collective-permute-done.6.ahead_ref, f32[2,32,128]{2,1,0:T(8,128)} %get-tuple-element.129.aside_any, f32[4,32,64]{2,1,0:T(8,128)S(1)} %get-tuple-element.112.refs_2_.chosen_ref, bf16[64,128,128]{2,1,0:T(8,128)(2,1)S(1)} %bitcast.45), custom_call_target="tpu_custom_call" | custom-call | tf_op jit(solution)/shard_map/pallas_call | solution.py:336
  58.9 3.3 %all-to-all-start.4 = ((f32[8,1,128]{2,1,0:T(1,128)}), f32[8,1,128]{2,1,0:T(1,128)S(1)}, u32[]{:S(2)}, u32[]{:S(2)}) async-start(f32[8,1,128]{2,1,0:T(1,128)} %bitcast.17), calls=%async_computation.4 | async-start | bytes 8192 | tf_op jit(solution)/shard_map/all_to_all | solution.py:251
  62.2 3.6 %all-to-all-done.4 = f32[8,1,128]{2,1,0:T(1,128)S(1)} async-done(((f32[8,1,128]{2,1,0:T(1,128)}), f32[8,1,128]{2,1,0:T(1,128)S(1)}, u32[]{:S(2)}, u32[]{:S(2)}) %all-to-all-start.4) | async-done | bytes 4128 | tf_op jit(solution)/shard_map/all_to_all | solution.py:251
  65.7 1.6 %collective-permute-start.7 = (f32[32,128]{1,0:T(8,128)S(1)}, f32[32,128]{1,0:T(8,128)S(1)}, u32[]{:S(2)}, u32[]{:S(2)}) collective-permute-start(f32[32,128]{1,0:T(8,128)S(1)} %get-tuple-element.135), channel_id=1, source_target_pairs={{0,1},{1,2},{2,3},{3,0},{4,5},{5,6},{6,7},{7,4},{8,9},{9,10},{10,1... | collective-permute-start | bytes 49160 | tf_op jit(solution)/shard_map/ppermute | solution.py:236
  67.3 4.7 %conditional.7 = (f32[32,128]{1,0:T(8,128)}, f32[1,128]{1,0:T(1,128)S(1)}) conditional(s32[]{:T(128)} %convert_element_type.2, () %tuple.46, (f32[8,128]{1,0:T(8,128)S(1)}, f32[2,32,128]{2,1,0:T(8,128)S(1)}, f32[4,32,64]{2,1,0:T(8,128)S(1)}, f32[4,128]{1,0:T(4,128)S(1)}, f32[4,128,128]{2,1,0:T(8,128)S(1)}, ...), branch_computations={%region_6.7_spmd, %region_7.8_spmd} | conditional | bytes 65592 | solution.py:322
  67.3 0.9 %branch_1_fun.7 = (f32[32,128]{1,0:T(8,128)S(1)}, f32[1,128]{1,0:T(1,128)S(1)}) custom-call(f32[8,128]{1,0:T(8,128)S(1)} %get-tuple-element.72.refs_0_, f32[2,32,128]{2,1,0:T(8,128)S(1)} %get-tuple-element.73.refs_1_, f32[4,32,64]{2,1,0:T(8,128)S(1)} %get-tuple-element.74.refs_2_, f32[4,128]{1,0:T(4,128)S(1)} %get-tuple-element.75.refs_3_, ...), custom_call_target="tpu_custom_call" | custom-call | tf_op jit(solution)/shard_map/cond/branch_1_fun/pallas_call | solution.py:314
  68.2 0.0 collective-permute-start.3
  68.2 3.8 %collective-permute-done.3 = f32[32,128]{1,0:T(8,128)} collective-permute-done((f32[32,128]{1,0:T(8,128)S(1)}, f32[32,128]{1,0:T(8,128)}, u32[]{:S(2)}, u32[]{:S(2)}) %collective-permute-start.3) | collective-permute-done | bytes 16416 | tf_op jit(solution)/shard_map/cond/branch_1_fun/ppermute | solution.py:241
  72.1 1.3 %shard_map.95 = f32[512,128]{1,0:T(8,128)} custom-call(s32[1,4]{1,0:T(1,128)S(1)} %copy-done.2, f32[512,128]{1,0:T(8,128)S(1)} %bitcast.27, f32[1,128]{1,0:T(1,128)S(1)} %broadcast_select_fusion.3.refs_0_, f32[1,128]{1,0:T(1,128)S(1)} %broadcast_select_fusion.2.refs_1_, f32[1,128]{1,0:T(1,128)S(1)} %broadcast_select_fusion.1.refs_2_, ...), custom_call_target="tpu_custom_call" | custom-call | tf_op jit(solution)/shard_map/pallas_call | solution.py:342
  73.3 0.0 collective-permute-done.7
  73.3 0.6 select_bitcast_fusion
  (12 shorter events, 0.0 us)
Async XLA Ops:
  0.6 14.1 %copy-start.2 = (s32[1,4]{1,0:T(1,128)S(1)}, s32[1,4]{1,0:T(1,128)}, u32[]{:S(2)}) copy-start(s32[1,4]{1,0:T(1,128)} %targets_smem.1) | copy-start | bytes 52
  0.6 14.1 %copy-start.5 = (bf16[1,1,64,128,128]{4,3,2,1,0:T(8,128)(2,1)S(1)}, bf16[1,1,64,128,128]{4,3,2,1,0:T(8,128)(2,1)}, u32[]{:S(2)}) copy-start(bf16[1,1,64,128,128]{4,3,2,1,0:T(8,128)(2,1)} %param.19) | copy-start | bytes 6291460
  0.7 14.1 %copy-start.3 = (s32[1,1,64]{2,1,0:T(1,128)S(1)}, s32[1,1,64]{2,1,0:T(1,128)}, u32[]{:S(2)}) copy-start(s32[1,1,64]{2,1,0:T(1,128)} %param.18) | copy-start | bytes 772
  0.7 14.0 %copy-start.4 = (s32[1,1,64]{2,1,0:T(1,128)S(1)}, s32[1,1,64]{2,1,0:T(1,128)}, u32[]{:S(2)}) copy-start(s32[1,1,64]{2,1,0:T(1,128)} %param.17) | copy-start | bytes 772
  0.7 14.0 %copy-start.1 = (s32[16384]{0:T(1024)S(1)}, s32[16384]{0:T(1024)}, u32[]{:S(2)}) copy-start(s32[16384]{0:T(1024)} %param.15) | copy-start | bytes 196612
  0.7 22.6 %copy-start.6 = (f32[1,4,128,128]{3,2,1,0:T(8,128)S(1)}, f32[1,4,128,128]{3,2,1,0:T(8,128)}, u32[]{:S(2)}) copy-start(f32[1,4,128,128]{3,2,1,0:T(8,128)} %param.21) | copy-start | bytes 786436
  23.3 6.7 %collective-permute-start.4 = (f32[2,32,128]{2,1,0:T(8,128)S(1)}, f32[2,32,128]{2,1,0:T(8,128)S(1)}, u32[]{:S(2)}, u32[]{:S(2)}) collective-permute-start(f32[2,32,128]{2,1,0:T(8,128)S(1)} %get-tuple-element.116), channel_id=1, source_target_pairs={{0,1},{1,2},{2,3},{3,0},{4,5},{5,6},{6,7},{7,4},{8,9},{9,10},{10,1... | collective-permute-start | bytes 98312 | tf_op jit(solution)/shard_map/ppermute | solution.py:236
  25.9 4.0 %collective-permute-start = (f32[2,32,128]{2,1,0:T(8,128)S(1)}, f32[2,32,128]{2,1,0:T(8,128)}, u32[]{:S(2)}, u32[]{:S(2)}) collective-permute-start(f32[2,32,128]{2,1,0:T(8,128)S(1)} %get-tuple-element.54), channel_id=1, source_target_pairs={{0,1},{1,0},{2,3},{3,2},{4,5},{5,4},{6,7},{7,6},{8,9},{9,8},{10,11... | collective-permute-start | bytes 98312 | tf_op jit(solution)/shard_map/cond/branch_1_fun/ppermute | solution.py:241
  36.6 6.8 %collective-permute-start.5 = (f32[2,32,128]{2,1,0:T(8,128)S(1)}, f32[2,32,128]{2,1,0:T(8,128)S(1)}, u32[]{:S(2)}, u32[]{:S(2)}) collective-permute-start(f32[2,32,128]{2,1,0:T(8,128)S(1)} %get-tuple-element.122), channel_id=1, source_target_pairs={{0,1},{1,2},{2,3},{3,0},{4,5},{5,6},{6,7},{7,4},{8,9},{9,10},{10,1... | collective-permute-start | bytes 98312 | tf_op jit(solution)/shard_map/ppermute | solution.py:236
  39.3 4.0 %collective-permute-start.1 = (f32[2,32,128]{2,1,0:T(8,128)S(1)}, f32[2,32,128]{2,1,0:T(8,128)}, u32[]{:S(2)}, u32[]{:S(2)}) collective-permute-start(f32[2,32,128]{2,1,0:T(8,128)S(1)} %get-tuple-element.62), channel_id=1, source_target_pairs={{0,1},{1,0},{2,3},{3,2},{4,5},{5,4},{6,7},{7,6},{8,9},{9,8},{10,11... | collective-permute-start | bytes 98312 | tf_op jit(solution)/shard_map/cond/branch_1_fun/ppermute | solution.py:241
  44.5 6.6 %all-to-all-start.3 = ((f32[8,1,128]{2,1,0:T(1,128)}), f32[8,1,128]{2,1,0:T(1,128)S(1)}, u32[]{:S(2)}, u32[]{:S(2)}) async-start(f32[8,1,128]{2,1,0:T(1,128)} %bitcast.14), calls=%async_computation.3 | async-start | bytes 8192 | tf_op jit(solution)/shard_map/all_to_all | solution.py:251
  51.1 6.5 %collective-permute-start.6 = (f32[2,32,128]{2,1,0:T(8,128)S(1)}, f32[2,32,128]{2,1,0:T(8,128)S(1)}, u32[]{:S(2)}, u32[]{:S(2)}) collective-permute-start(f32[2,32,128]{2,1,0:T(8,128)S(1)} %get-tuple-element.128), channel_id=1, source_target_pairs={{0,1},{1,2},{2,3},{3,0},{4,5},{5,6},{6,7},{7,4},{8,9},{9,10},{10,1... | collective-permute-start | bytes 98312 | tf_op jit(solution)/shard_map/ppermute | solution.py:236
  53.6 4.0 %collective-permute-start.2 = (f32[2,32,128]{2,1,0:T(8,128)S(1)}, f32[2,32,128]{2,1,0:T(8,128)}, u32[]{:S(2)}, u32[]{:S(2)}) collective-permute-start(f32[2,32,128]{2,1,0:T(8,128)S(1)} %get-tuple-element.70), channel_id=1, source_target_pairs={{0,1},{1,0},{2,3},{3,2},{4,5},{5,4},{6,7},{7,6},{8,9},{9,8},{10,11... | collective-permute-start | bytes 98312 | tf_op jit(solution)/shard_map/cond/branch_1_fun/ppermute | solution.py:241
  58.9 6.8 %all-to-all-start.4 = ((f32[8,1,128]{2,1,0:T(1,128)}), f32[8,1,128]{2,1,0:T(1,128)S(1)}, u32[]{:S(2)}, u32[]{:S(2)}) async-start(f32[8,1,128]{2,1,0:T(1,128)} %bitcast.17), calls=%async_computation.4 | async-start | bytes 8192 | tf_op jit(solution)/shard_map/all_to_all | solution.py:251
  65.7 6.4 %copy-start = (f32[65536]{0:T(1024)S(1)}, f32[65536]{0:T(1024)}, u32[]{:S(2)}) copy-start(f32[65536]{0:T(1024)} %param.16) | copy-start | bytes 786436
  65.7 7.6 %collective-permute-start.7 = (f32[32,128]{1,0:T(8,128)S(1)}, f32[32,128]{1,0:T(8,128)S(1)}, u32[]{:S(2)}, u32[]{:S(2)}) collective-permute-start(f32[32,128]{1,0:T(8,128)S(1)} %get-tuple-element.135), channel_id=1, source_target_pairs={{0,1},{1,2},{2,3},{3,0},{4,5},{5,6},{6,7},{7,4},{8,9},{9,10},{10,1... | collective-permute-start | bytes 49160 | tf_op jit(solution)/shard_map/ppermute | solution.py:236
  68.2 3.9 %collective-permute-start.3 = (f32[32,128]{1,0:T(8,128)S(1)}, f32[32,128]{1,0:T(8,128)}, u32[]{:S(2)}, u32[]{:S(2)}) collective-permute-start(f32[32,128]{1,0:T(8,128)S(1)} %get-tuple-element.78), channel_id=1, source_target_pairs={{0,1},{1,0},{2,3},{3,2},{4,5},{5,4},{6,7},{7,6},{8,9},{9,8},{10,11... | collective-permute-start | bytes 49160 | tf_op jit(solution)/shard_map/cond/branch_1_fun/ppermute | solution.py:241

commit v10 on v8

--- a/solution.py
+++ b/solution.py
@@ -20,13 +20,14 @@
     return jax.ShapeDtypeStruct(shape, jnp.float32)
 
 
-def call(kernel, out_shape, in_specs):
+def call(kernel, out_shape, in_specs, scratch_shapes):
     single = not isinstance(out_shape, tuple)
     return pl.pallas_call(
         kernel,
         out_shape=out_shape,
         in_specs=in_specs,
         out_specs=VMEM if single else tuple(VMEM for _ in out_shape),
+        scratch_shapes=scratch_shapes,
         compiler_params=pltpu.CompilerParams(vmem_limit_bytes=24 << 20),
     )
 
@@ -65,8 +66,32 @@
     )
 
 
+def over_lanes(left, right):
+    return lax.dot_general(
+        left.astype(jnp.bfloat16),
+        right.astype(jnp.bfloat16),
+        (((1,), (1,)), ((), ())),
+        preferred_element_type=jnp.float32,
+    )
+
+
+def listed(chosen):
+    tiles = chosen.shape[1]
+    square = (tiles, tiles)
+    sub = lax.broadcasted_iota(jnp.int32, square, 0)
+    lane = lax.broadcasted_iota(jnp.int32, square, 1)
+    taken = jnp.sum(chosen, axis=0, keepdims=True)
+    before = over_lanes(jnp.broadcast_to(taken, (8, tiles)), (lane < sub).astype(jnp.float32))
+    in_slot = (sub == before[0:1].astype(jnp.int32)) & (taken > 0.0)
+    in_slot = in_slot.astype(jnp.float32)
+    numbers = lax.broadcasted_iota(jnp.int32, (8, tiles), 1) + 1
+    ids = over_lanes(numbers.astype(jnp.float32), in_slot)[0:1].astype(jnp.int32) - 1
+    return ids, over_lanes(in_slot, chosen), over_lanes(chosen, in_slot)
+
+
 def margins_kernel(
-    cols_hbm, targets_hbm, rows_hbm, beta_hbm, values_hbm, partial_ref, old_ref,
+    cols_hbm, targets_hbm, rows_hbm, beta_hbm, values_hbm,
+    partial_ref, old_ref,
     picked_ref, beta_ref, rows_ref, values_ref, cols_smem, targets_smem, small_sem, tile_sem,
 ):
     tiles = cols_smem.shape[1]
@@ -112,40 +137,62 @@
         ]
 
 
-def gradient_part(residual, chosen, values_ref):
-    tiles, edge, _ = values_ref.shape
-    picked = lax.dot_general(
-        chosen.astype(jnp.bfloat16),
+def listed_tiles(section, part, ids_ref, values_ref):
+    return jnp.concatenate(
+        [
+            values_ref[jnp.maximum(ids_ref[section, part * chunk + inner], 0)]
+            for inner in range(chunk)
+        ],
+        axis=0,
+    )
+
+
+def for_parts(section, ids_ref, run):
+    run(0)
+    for part in range(1, ids_ref.shape[1] // chunk):
+        pl.when(ids_ref[section, part * chunk] >= 0)(functools.partial(run, part))
+
+
+def gradient_part(section, residual, ids_ref, picking_ref, values_ref, total_ref):
+    edge = values_ref.shape[2]
+    picked = jnp.dot(
+        picking_ref[section].astype(jnp.bfloat16),
         residual.astype(jnp.bfloat16),
-        (((0,), (0,)), ((), ())),
         preferred_element_type=jnp.float32,
     )
     sub = lax.broadcasted_iota(jnp.int32, (chunk, edge), 0)
-    spread = []
-    for tile in range(tiles):
-        first = tile - tile % chunk
-        kept = jnp.where(sub == tile - first, picked[first : first + chunk], 0.0)
-        spread.append(kept.astype(jnp.bfloat16))
-    summed = jnp.dot(
-        jnp.concatenate(spread, axis=1),
-        values_ref[...].reshape(tiles * edge, edge),
-        preferred_element_type=jnp.float32,
-    )
-    return jnp.sum(summed, axis=0, keepdims=True)
+
+    def run(part):
+        rows = picked[part * chunk : (part + 1) * chunk]
+        spread = [
+            jnp.where(sub == inner, rows, 0.0).astype(jnp.bfloat16) for inner in range(chunk)
+        ]
+        total = jnp.dot(
+            jnp.concatenate(spread, axis=1),
+            listed_tiles(section, part, ids_ref, values_ref),
+            preferred_element_type=jnp.float32,
+        )
+        total_ref[...] = total if part == 0 else total_ref[...] + total
+
+    for_parts(section, ids_ref, run)
+    return jnp.sum(total_ref[...], axis=0, keepdims=True)
 
 
 def first_kernel(
     parts_ref, labels_ref, rows_ref, cols_ref, targets_ref, values_ref,
-    state_ref, grad_ref, chosen_ref,
+    state_ref, grad_ref, ids_ref, picking_ref, placing_ref, total_ref,
 ):
     sections, group_blocks, _ = parts_ref.shape
     my_index = lax.axis_index("feat")
-    sub_ids = lax.broadcasted_iota(jnp.int32, chosen_ref.shape[1:], 0)
+    sub_ids = lax.broadcasted_iota(jnp.int32, placing_ref.shape[1:], 0)
     for section in range(sections):
         group = lax.rem(my_index - section + sections, sections)
         same_row = sub_ids + group * group_blocks == rows_ref[...]
         same_col = cols_ref[...] == targets_ref[:, section : section + 1]
-        chosen_ref[section] = (same_row & same_col).astype(jnp.float32)
+        ids, picking, placing = listed((same_row & same_col).astype(jnp.float32))
+        ids_ref[pl.ds(section, 1), :] = ids
+        picking_ref[section] = picking
+        placing_ref[section] = placing
     start = pl.multiple_of(my_index * group_blocks, 8)
     margins = parts_ref[0]
     for part in range(1, parts_ref.shape[0]):
@@ -154,18 +201,18 @@
     residual = labels_ref[pl.ds(start, group_blocks), :].astype(jnp.float32) - probability
     state_ref[0] = residual
     state_ref[1] = probability * (1.0 - probability)
-    grad = gradient_part(residual, chosen_ref[0], values_ref)
+    grad = gradient_part(0, residual, ids_ref, picking_ref, values_ref, total_ref)
     grad_ref[...] = jnp.broadcast_to(grad, grad_ref.shape)
 
 
-def gradient_kernel(section, state_ref, chosen_ref, values_ref, grad_ref):
-    grad = gradient_part(state_ref[0], chosen_ref[section], values_ref)
+def gradient_kernel(section, state_ref, ids_ref, picking_ref, values_ref, grad_ref, total_ref):
+    grad = gradient_part(section, state_ref[0], ids_ref, picking_ref, values_ref, total_ref)
     grad_ref[...] = jnp.broadcast_to(grad, grad_ref.shape)
 
 
 def update_kernel(
-    section, grads_ref, state_ref, chosen_ref, old_ref, inverses_ref, values_ref,
-    moved_ref, shrunk_ref,
+    section, grads_ref, state_ref, ids_ref, placing_ref, old_ref, inverses_ref, values_ref,
+    moved_ref, shrunk_ref, image_ref,
 ):
     tiles, edge, _ = values_ref.shape
     gradient = jnp.sum(grads_ref[...], axis=0, keepdims=True)
@@ -181,10 +228,15 @@
     shrunk = jnp.where(raised < 0.0, -size, size)
     shrunk_ref[...] = shrunk
     change = jnp.broadcast_to(shrunk - old, (chunk, edge)).astype(jnp.bfloat16)
-    image = tile_products(
-        lambda first: change, lambda first: values_ref[pl.ds(first, chunk)], tiles
-    )
-    landed = placed_sum(chosen_ref[section], image)
+    image_ref[...] = jnp.zeros_like(image_ref)
+
+    def run(part):
+        image_ref[pl.ds(part * chunk, chunk), :] = tile_products(
+            lambda first: change, lambda first: listed_tiles(section, part, ids_ref, values_ref), chunk
+        )
+
+    for_parts(section, ids_ref, run)
+    landed = placed_sum(placing_ref[section], image_ref[...])
     weight = state_ref[1]
     residual = state_ref[0] - weight * landed
     if len(moved_ref.shape) == 3:
@@ -253,36 +305,43 @@
         0,
         axis_index_groups=[middle_first(sections)],
     )
-    state, grads, chosen = call(
+    group_shape = (group_blocks, edge)
+    total = pltpu.VMEM((chunk, edge), jnp.float32)
+    state, grads, ids, picking, placing = call(
         first_kernel,
         (
-            float_of((2, group_blocks, edge)),
+            float_of((2, *group_shape)),
             float_of((samp_count, edge)),
+            jax.ShapeDtypeStruct((sections, tiles), jnp.int32),
+            float_of((sections, tiles, group_blocks)),
             float_of((sections, group_blocks, tiles)),
         ),
         [VMEM] * 6,
+        [total],
     )(parts, labels.reshape(row_blocks, edge), tile_rows[0], tile_cols[0], block_order, values)
     shrunk_blocks = []
     for section in range(sections):
         final = section + 1 == sections
-        moved_shape = (group_blocks, edge) if final else (2, group_blocks, edge)
         moving, shrunk = call(
             functools.partial(update_kernel, section),
-            (float_of(moved_shape), float_of((1, edge))),
-            [VMEM] * 6,
-        )(gathered(grads, "samp"), state, chosen, old_blocks, inverses, values)
+            (float_of(group_shape if final else (2, *group_shape)), float_of((1, edge))),
+            [VMEM] * 7,
+            [pltpu.VMEM((tiles, edge), jnp.float32)],
+        )(gathered(grads, "samp"), state, ids, placing, old_blocks, inverses, values)
         shrunk_blocks.append(shrunk)
         state = from_behind(moving, "feat", 1)
         if not final:
             grads = call(
                 functools.partial(gradient_kernel, section + 1),
                 float_of((samp_count, edge)),
-                [VMEM] * 3,
-            )(state, chosen, values)
+                [VMEM] * 4,
+                [total],
+            )(state, ids, picking, values)
     blocks = call(
         functools.partial(blocks_kernel, sections),
         float_of(blocks.shape),
         [SMEM] + [VMEM] * (1 + sections),
+        [],
     )(block_order, blocks, *shrunk_blocks)
     return (blocks.reshape(-1), state.reshape(-1))
 

time: 70.8 us -> 70.6 us (level)
  no operation moved by 1% of the time
where the time goes in v10:
time: 70.6 us; the launch traced here: 70.2 us
  blocking collectives  37.2 us (53%)
  waiting for transfers between devices  20.5 us (29%)
  Pallas kernels  10.2 us (14%)
  starting transfers between devices  1.01 us (1%)
  between operations  0.78 us (1%)
    all_to_all x4, blocking collectives, gathered(): lax.all_to_all(parts.reshape(count, 1, edge), axis, 0, 0, axis_index_grou...  26.5 us
    ppermute x4, waiting for transfers between devices, from_behind(): return lax.ppermute(value, axis, pairs)  20.5 us
    all_to_all x1, blocking collectives, per_device(): lax.all_to_all(partial_sum.reshape(sections, group_blocks, edge), 'feat',...  10.7 us
    pallas_call x1, Pallas kernels, per_device(): pl.pallas_call(margins_kernel, out_shape=(float_of((row_blocks, edge)), f...  3.32 us
    pallas_call x4, Pallas kernels, per_device(): call(functools.partial(update_kernel, section), (float_of(group_shape if...  2.94 us
    pallas_call x3, Pallas kernels, per_device(): call(functools.partial(gradient_kernel, section + 1), float_of((samp_coun...  1.56 us
  transfers between devices with their start and end apart: 4, of which 4 were waited for; matrix products, arithmetic and copies ran while one was open for 0% of the time, Pallas kernels for 2%

profile of v10, /device:TPU:0, one launch (start us, length us, event | category | flops | bytes accessed | tf_op | source)
XLA Modules:
  0.0 70.2 jit_solution(17291041708225638614)
XLA Ops:
  0.6 0.0 copy-start.5
  0.6 0.0 copy-start
  0.7 0.0 copy-start.6
  0.7 0.0 copy-start.7
  0.7 0.0 copy-start.3
  0.7 0.0 copy-start.1
  0.7 3.3 %shard_map.86 = (f32[128,128]{1,0:T(8,128)}, f32[4,128]{1,0:T(4,128)}) custom-call(s32[1,64]{1,0:T(1,128)} %bitcast.49, s32[1,4]{1,0:T(1,128)} %targets_smem.1, s32[1,64]{1,0:T(1,128)} %bitcast.51, f32[512,128]{1,0:T(8,128)} %bitcast.38, bf16[64,128,128]{2,1,0:T(8,128)(2,1)} %bitcast.25), custom_call_target="tpu_custom_call" | custom-call | tf_op jit(solution)/shard_map/pallas_call | solution.py:284
  4.0 0.0 copy-start.4
  4.0 10.7 %all_to_all.25.parts_ref = f32[4,32,128]{2,1,0:T(8,128)S(1)} all-to-all(f32[4,32,128]{2,1,0:T(8,128)} %bitcast.54), channel_id=1, replica_groups={{2,1,3,0},{6,5,7,4},{10,9,11,8},{14,13,15,12},{18,17,19,16},{22,21,23,2..., dimensions={0} | all-to-all | bytes 131072 | tf_op jit(solution)/shard_map/all_to_all | solution.py:301
  14.7 0.0 copy-done.5
  14.7 0.0 copy-done
  14.7 0.0 copy-done.6
  14.7 0.0 copy-done.7
  14.7 0.0 copy-done.3
  14.7 1.1 %shard_map.87 = (f32[2,32,128]{2,1,0:T(8,128)S(1)}, f32[8,128]{1,0:T(8,128)S(1)}, s32[4,64]{1,0:T(4,128)S(1)}, f32[4,64,32]{2,1,0:T(8,128)S(1)}, f32[4,32,64]{2,1,0:T(8,128)S(1)}) custom-call(f32[4,32,128]{2,1,0:T(8,128)S(1)} %all_to_all.25.parts_ref, s32[128,128]{1,0:T(8,128)S(1)} %bitcast.40, s32[1,64]{1,0:T(1,128)S(1)} %bitcast.52, s32[1,64]{1,0:T(1,128)S(1)} %bitcast.50, ...), custom_call_target="tpu_custom_call" | custom-call | tf_op jit(solution)/shard_map/pallas_call | solution.py:310
  15.8 7.9 %all_to_all.26 = f32[8,1,128]{2,1,0:T(1,128)S(1)} all-to-all(f32[8,1,128]{2,1,0:T(1,128)S(1)} %bitcast.48), channel_id=1, replica_groups={{4,28,12,20,0,24,8,16},{5,29,13,21,1,25,9,17},{6,30,14,22,2,26,10,18},{..., dimensions={0} | all-to-all | bytes 8192 | tf_op jit(solution)/shard_map/all_to_all | solution.py:269
  23.7 0.0 copy-done.1
  23.8 0.0 copy-done.4
  23.8 0.7 %shard_map.88 = (f32[2,32,128]{2,1,0:T(8,128)S(1)}, f32[1,128]{1,0:T(1,128)S(1)}) custom-call(f32[8,128]{1,0:T(8,128)S(1)} %bitcast.42, f32[2,32,128]{2,1,0:T(8,128)S(1)} %get-tuple-element.19.state_ref, s32[4,64]{1,0:T(4,128)S(1)} %get-tuple-element.20.ids_ref, f32[4,32,64]{2,1,0:T(8,128)S(1)} %get-tuple-element.21.placing_ref, f32[4,128]{1,0:T(4,128)S(1)} %copy-done.4, ...), custom_call_target="tpu_custom_call" | custom-call | tf_op jit(solution)/shard_map/pallas_call | solution.py:325
  24.5 0.9 %collective-permute-start = (f32[2,32,128]{2,1,0:T(8,128)S(1)}, f32[2,32,128]{2,1,0:T(8,128)S(1)}, u32[]{:S(2)}, u32[]{:S(2)}) collective-permute-start(f32[2,32,128]{2,1,0:T(8,128)S(1)} %get-tuple-element.24), channel_id=1, source_target_pairs={{0,1},{1,2},{2,3},{3,0},{4,5},{5,6},{6,7},{7,4},{8,9},{9,10},{10,1... | collective-permute-start | bytes 98312 | tf_op jit(solution)/shard_map/ppermute | solution.py:259
  25.4 4.8 %collective-permute-done.state_ref = f32[2,32,128]{2,1,0:T(8,128)S(1)} collective-permute-done((f32[2,32,128]{2,1,0:T(8,128)S(1)}, f32[2,32,128]{2,1,0:T(8,128)S(1)}, u32[]{:S(2)}, u32[]{:S(2)}) %collective-permute-start) | collective-permute-done | bytes 32800 | tf_op jit(solution)/shard_map/ppermute | solution.py:259
  30.2 0.5 shard_map.89
  30.7 6.0 %all_to_all.27 = f32[8,1,128]{2,1,0:T(1,128)S(1)} all-to-all(f32[8,1,128]{2,1,0:T(1,128)S(1)} %bitcast.46), channel_id=1, replica_groups={{4,28,12,20,0,24,8,16},{5,29,13,21,1,25,9,17},{6,30,14,22,2,26,10,18},{..., dimensions={0} | all-to-all | bytes 8192 | tf_op jit(solution)/shard_map/all_to_all | solution.py:269
  36.8 0.7 %shard_map.90 = (f32[2,32,128]{2,1,0:T(8,128)S(1)}, f32[1,128]{1,0:T(1,128)S(1)}) custom-call(f32[8,128]{1,0:T(8,128)S(1)} %bitcast.43, f32[2,32,128]{2,1,0:T(8,128)S(1)} %collective-permute-done.state_ref, s32[4,64]{1,0:T(4,128)S(1)} %get-tuple-element.20.ids_ref, f32[4,32,64]{2,1,0:T(8,128)S(1)} %get-tuple-element.21.placing_ref, f32[4,128]{1,0:T(4,128)S(1)} %copy-done.4, ...), custom_call_target="tpu_custom_call" | custom-call | tf_op jit(solution)/shard_map/pallas_call | solution.py:325
  37.5 0.0 collective-permute-start.1
  37.5 5.7 %collective-permute-done.1.state_ref = f32[2,32,128]{2,1,0:T(8,128)S(1)} collective-permute-done((f32[2,32,128]{2,1,0:T(8,128)S(1)}, f32[2,32,128]{2,1,0:T(8,128)S(1)}, u32[]{:S(2)}, u32[]{:S(2)}) %collective-permute-start.1) | collective-permute-done | bytes 32800 | tf_op jit(solution)/shard_map/ppermute | solution.py:259
  43.3 0.5 shard_map.91
  43.8 6.5 %all_to_all.28 = f32[8,1,128]{2,1,0:T(1,128)S(1)} all-to-all(f32[8,1,128]{2,1,0:T(1,128)S(1)} %bitcast.47), channel_id=1, replica_groups={{4,28,12,20,0,24,8,16},{5,29,13,21,1,25,9,17},{6,30,14,22,2,26,10,18},{..., dimensions={0} | all-to-all | bytes 8192 | tf_op jit(solution)/shard_map/all_to_all | solution.py:269
  50.2 0.7 %shard_map.92 = (f32[2,32,128]{2,1,0:T(8,128)S(1)}, f32[1,128]{1,0:T(1,128)S(1)}) custom-call(f32[8,128]{1,0:T(8,128)S(1)} %bitcast.44, f32[2,32,128]{2,1,0:T(8,128)S(1)} %collective-permute-done.1.state_ref, s32[4,64]{1,0:T(4,128)S(1)} %get-tuple-element.20.ids_ref, f32[4,32,64]{2,1,0:T(8,128)S(1)} %get-tuple-element.21.placing_ref, ...), custom_call_target="tpu_custom_call" | custom-call | tf_op jit(solution)/shard_map/pallas_call | solution.py:325
  51.0 0.0 copy-start.2
  51.0 0.1 collective-permute-start.2
  51.1 5.7 %collective-permute-done.2.state_ref = f32[2,32,128]{2,1,0:T(8,128)S(1)} collective-permute-done((f32[2,32,128]{2,1,0:T(8,128)S(1)}, f32[2,32,128]{2,1,0:T(8,128)S(1)}, u32[]{:S(2)}, u32[]{:S(2)}) %collective-permute-start.2) | collective-permute-done | bytes 32800 | tf_op jit(solution)/shard_map/ppermute | solution.py:259
  56.8 0.5 shard_map.93
  57.3 6.0 %all_to_all.29 = f32[8,1,128]{2,1,0:T(1,128)S(1)} all-to-all(f32[8,1,128]{2,1,0:T(1,128)S(1)} %bitcast.45), channel_id=1, replica_groups={{4,28,12,20,0,24,8,16},{5,29,13,21,1,25,9,17},{6,30,14,22,2,26,10,18},{..., dimensions={0} | all-to-all | bytes 8192 | tf_op jit(solution)/shard_map/all_to_all | solution.py:269
  63.3 0.7 %shard_map.94 = (f32[32,128]{1,0:T(8,128)S(1)}, f32[1,128]{1,0:T(1,128)S(1)}) custom-call(f32[8,128]{1,0:T(8,128)S(1)} %bitcast.41, f32[2,32,128]{2,1,0:T(8,128)S(1)} %collective-permute-done.2.state_ref, s32[4,64]{1,0:T(4,128)S(1)} %get-tuple-element.20.ids_ref, f32[4,32,64]{2,1,0:T(8,128)S(1)} %get-tuple-element.21.placing_ref, f32[4,128]{1,0:T(4,128)S(1)} %copy-done.4, ...), custom_call_target="tpu_custom_call" | custom-call | tf_op jit(solution)/shard_map/pallas_call | solution.py:325
  64.1 0.0 collective-permute-start.3
  64.1 0.0 copy-done.2
  64.1 1.3 %shard_map.95 = f32[512,128]{1,0:T(8,128)} custom-call(s32[1,4]{1,0:T(1,128)S(1)} %copy-done.5, f32[512,128]{1,0:T(8,128)S(1)} %bitcast.39, f32[1,128]{1,0:T(1,128)S(1)} %get-tuple-element.23.refs_0_, f32[1,128]{1,0:T(1,128)S(1)} %get-tuple-element.26.refs_1_, f32[1,128]{1,0:T(1,128)S(1)} %get-tuple-element.28.refs_2_, f32[1,128]{1,0:T(1,128)S(1)} %get-tuple-element.30.refs_3_), custom_call_target="tpu_custom_call" | custom-call | tf_op jit(solution)/shard_map/pallas_call | solution.py:340
  65.4 4.3 %collective-permute-done.3 = f32[32,128]{1,0:T(8,128)S(1)} collective-permute-done((f32[32,128]{1,0:T(8,128)S(1)}, f32[32,128]{1,0:T(8,128)S(1)}, u32[]{:S(2)}, u32[]{:S(2)}) %collective-permute-start.3) | collective-permute-done | bytes 16416 | tf_op jit(solution)/shard_map/ppermute | solution.py:259
  69.6 0.6 copy.14
Async XLA Ops:
  0.6 14.1 %copy-start.5 = (s32[1,4]{1,0:T(1,128)S(1)}, s32[1,4]{1,0:T(1,128)}, u32[]{:S(2)}) copy-start(s32[1,4]{1,0:T(1,128)} %targets_smem.1) | copy-start | bytes 52
  0.6 14.1 %copy-start = (bf16[1,1,64,128,128]{4,3,2,1,0:T(8,128)(2,1)S(1)}, bf16[1,1,64,128,128]{4,3,2,1,0:T(8,128)(2,1)}, u32[]{:S(2)}) copy-start(bf16[1,1,64,128,128]{4,3,2,1,0:T(8,128)(2,1)} %param.11) | copy-start | bytes 6291460
  0.7 14.1 %copy-start.6 = (s32[1,1,64]{2,1,0:T(1,128)S(1)}, s32[1,1,64]{2,1,0:T(1,128)}, u32[]{:S(2)}) copy-start(s32[1,1,64]{2,1,0:T(1,128)} %param.10) | copy-start | bytes 772
  0.7 14.1 %copy-start.7 = (s32[1,1,64]{2,1,0:T(1,128)S(1)}, s32[1,1,64]{2,1,0:T(1,128)}, u32[]{:S(2)}) copy-start(s32[1,1,64]{2,1,0:T(1,128)} %param.9) | copy-start | bytes 772
  0.7 14.1 %copy-start.3 = (s32[16384]{0:T(1024)S(1)}, s32[16384]{0:T(1024)}, u32[]{:S(2)}) copy-start(s32[16384]{0:T(1024)} %param.7) | copy-start | bytes 196612
  0.7 23.1 %copy-start.1 = (f32[1,4,128,128]{3,2,1,0:T(8,128)S(1)}, f32[1,4,128,128]{3,2,1,0:T(8,128)}, u32[]{:S(2)}) copy-start(f32[1,4,128,128]{3,2,1,0:T(8,128)} %param.13) | copy-start | bytes 786436
  4.0 19.7 %copy-start.4 = (f32[4,128]{1,0:T(4,128)S(1)}, f32[4,128]{1,0:T(4,128)}, u32[]{:S(2)}) copy-start(f32[4,128]{1,0:T(4,128)} %get-tuple-element.22.old_ref) | copy-start | bytes 6148
  24.5 5.7 %collective-permute-start = (f32[2,32,128]{2,1,0:T(8,128)S(1)}, f32[2,32,128]{2,1,0:T(8,128)S(1)}, u32[]{:S(2)}, u32[]{:S(2)}) collective-permute-start(f32[2,32,128]{2,1,0:T(8,128)S(1)} %get-tuple-element.24), channel_id=1, source_target_pairs={{0,1},{1,2},{2,3},{3,0},{4,5},{5,6},{6,7},{7,4},{8,9},{9,10},{10,1... | collective-permute-start | bytes 98312 | tf_op jit(solution)/shard_map/ppermute | solution.py:259
  37.5 5.7 %collective-permute-start.1 = (f32[2,32,128]{2,1,0:T(8,128)S(1)}, f32[2,32,128]{2,1,0:T(8,128)S(1)}, u32[]{:S(2)}, u32[]{:S(2)}) collective-permute-start(f32[2,32,128]{2,1,0:T(8,128)S(1)} %get-tuple-element.27), channel_id=1, source_target_pairs={{0,1},{1,2},{2,3},{3,0},{4,5},{5,6},{6,7},{7,4},{8,9},{9,10},{10,1... | collective-permute-start | bytes 98312 | tf_op jit(solution)/shard_map/ppermute | solution.py:259
  51.0 13.1 %copy-start.2 = (f32[65536]{0:T(1024)S(1)}, f32[65536]{0:T(1024)}, u32[]{:S(2)}) copy-start(f32[65536]{0:T(1024)} %param.8) | copy-start | bytes 786436
  51.0 5.8 %collective-permute-start.2 = (f32[2,32,128]{2,1,0:T(8,128)S(1)}, f32[2,32,128]{2,1,0:T(8,128)S(1)}, u32[]{:S(2)}, u32[]{:S(2)}) collective-permute-start(f32[2,32,128]{2,1,0:T(8,128)S(1)} %get-tuple-element.29), channel_id=1, source_target_pairs={{0,1},{1,2},{2,3},{3,0},{4,5},{5,6},{6,7},{7,4},{8,9},{9,10},{10,1... | collective-permute-start | bytes 98312 | tf_op jit(solution)/shard_map/ppermute | solution.py:259
  64.1 5.6 %collective-permute-start.3 = (f32[32,128]{1,0:T(8,128)S(1)}, f32[32,128]{1,0:T(8,128)S(1)}, u32[]{:S(2)}, u32[]{:S(2)}) collective-permute-start(f32[32,128]{1,0:T(8,128)S(1)} %get-tuple-element.31), channel_id=1, source_target_pairs={{0,1},{1,2},{2,3},{3,0},{4,5},{5,6},{6,7},{7,4},{8,9},{9,10},{10,1... | collective-permute-start | bytes 49160 | tf_op jit(solution)/shard_map/ppermute | solution.py:259

commit v11 on v8

--- a/solution.py
+++ b/solution.py
@@ -20,13 +20,14 @@
     return jax.ShapeDtypeStruct(shape, jnp.float32)
 
 
-def call(kernel, out_shape, in_specs):
+def call(kernel, out_shape, in_specs, scratch_shapes):
     single = not isinstance(out_shape, tuple)
     return pl.pallas_call(
         kernel,
         out_shape=out_shape,
         in_specs=in_specs,
         out_specs=VMEM if single else tuple(VMEM for _ in out_shape),
+        scratch_shapes=scratch_shapes,
         compiler_params=pltpu.CompilerParams(vmem_limit_bytes=24 << 20),
     )
 
@@ -65,9 +66,35 @@
     )
 
 
+def over_lanes(left, right):
+    return lax.dot_general(
+        left.astype(jnp.bfloat16),
+        right.astype(jnp.bfloat16),
+        (((1,), (1,)), ((), ())),
+        preferred_element_type=jnp.float32,
+    )
+
+
+def listed(row_in_group, taken, group_blocks):
+    tiles = taken.shape[1]
+    square = (tiles, tiles)
+    sub = lax.broadcasted_iota(jnp.int32, square, 0)
+    lane = lax.broadcasted_iota(jnp.int32, square, 1)
+    taken = jnp.broadcast_to(taken, (8, tiles)).astype(jnp.float32)
+    before = over_lanes(taken, (lane < sub).astype(jnp.float32))
+    in_slot = (sub == before[0:1].astype(jnp.int32)) & (taken[0:1] > 0.0)
+    numbers = lax.broadcasted_iota(jnp.int32, (8, tiles), 1) + 1
+    short = group_blocks - row_in_group
+    facts = jnp.where(lax.broadcasted_iota(jnp.int32, (8, tiles), 0) == 0, numbers, short)
+    found = over_lanes(facts.astype(jnp.float32), in_slot.astype(jnp.float32)).astype(jnp.int32)
+    return found[0:1] - 1, group_blocks - found[1:2]
+
+
 def margins_kernel(
-    cols_hbm, targets_hbm, rows_hbm, beta_hbm, values_hbm, partial_ref, old_ref,
-    picked_ref, beta_ref, rows_ref, values_ref, cols_smem, targets_smem, small_sem, tile_sem,
+    cols_hbm, targets_hbm, rows_hbm, beta_hbm, values_hbm,
+    partial_ref, old_ref, lists_ref,
+    picked_ref, beta_ref, rows_ref, cols_ref, values_ref,
+    cols_smem, targets_smem, small_sem, tile_sem,
 ):
     tiles = cols_smem.shape[1]
     sections = targets_smem.shape[1]
@@ -77,6 +104,7 @@
         pltpu.make_async_copy(beta_hbm, beta_ref, small_sem.at[1]),
         pltpu.make_async_copy(targets_hbm, targets_smem, small_sem.at[2]),
         pltpu.make_async_copy(rows_hbm, rows_ref, small_sem.at[3]),
+        pltpu.make_async_copy(cols_hbm, cols_ref, small_sem.at[4]),
     ]
     large = [
         pltpu.make_async_copy(
@@ -95,6 +123,20 @@
     for section in range(sections):
         old_ref[pl.ds(section, 1), :] = beta_ref[pl.ds(targets_smem[0, section], 1), :]
 
+    my_index = lax.axis_index("feat")
+    group_blocks = row_blocks // sections
+    for section in range(sections):
+        group = lax.rem(my_index - section + sections, sections)
+        row_in_group = rows_ref[...] - group * group_blocks
+        taken = (
+            (row_in_group >= 0)
+            & (row_in_group < group_blocks)
+            & (cols_ref[...] == targets_smem[0, section])
+        )
+        ids, places = listed(row_in_group, taken, group_blocks)
+        lists_ref[pl.ds(2 * section, 1), :] = ids
+        lists_ref[pl.ds(2 * section + 1, 1), :] = places
+
     def tiles_of(first):
         large[first // chunk].wait()
         return values_ref[pl.ds(first, chunk)]
@@ -105,14 +147,29 @@
     block_ids = lax.broadcasted_iota(jnp.int32, (row_blocks, tiles), 0)
     placing = (block_ids == rows_ref[...]).astype(jnp.float32)
     partial = placed_sum(placing, products)
-    group_blocks = row_blocks // sections
     for place, group in enumerate(middle_first(sections)):
         partial_ref[pl.ds(place * group_blocks, group_blocks), :] = partial[
             group * group_blocks : (group + 1) * group_blocks
         ]
 
 
-def gradient_part(residual, chosen, values_ref):
+def listed_tiles(section, part, lists_ref, values_ref):
+    return jnp.concatenate(
+        [
+            values_ref[jnp.maximum(lists_ref[2 * section, part * chunk + inner], 0)]
+            for inner in range(chunk)
+        ],
+        axis=0,
+    )
+
+
+def for_parts(section, lists_ref, run):
+    run(0)
+    for part in range(1, lists_ref.shape[1] // chunk):
+        pl.when(lists_ref[2 * section, part * chunk] >= 0)(functools.partial(run, part))
+
+
+def gradient_of_all(residual, chosen, values_ref):
     tiles, edge, _ = values_ref.shape
     picked = lax.dot_general(
         chosen.astype(jnp.bfloat16),
@@ -135,39 +192,52 @@
 
 
 def first_kernel(
-    parts_ref, labels_ref, rows_ref, cols_ref, targets_ref, values_ref,
-    state_ref, grad_ref, chosen_ref,
+    parts_ref, labels_ref, rows_ref, cols_ref, targets_ref, values_ref, state_ref, grad_ref
 ):
-    sections, group_blocks, _ = parts_ref.shape
-    my_index = lax.axis_index("feat")
-    sub_ids = lax.broadcasted_iota(jnp.int32, chosen_ref.shape[1:], 0)
-    for section in range(sections):
-        group = lax.rem(my_index - section + sections, sections)
-        same_row = sub_ids + group * group_blocks == rows_ref[...]
-        same_col = cols_ref[...] == targets_ref[:, section : section + 1]
-        chosen_ref[section] = (same_row & same_col).astype(jnp.float32)
-    start = pl.multiple_of(my_index * group_blocks, 8)
+    group_blocks = parts_ref.shape[1]
+    first_row = lax.axis_index("feat") * group_blocks
+    sub_ids = lax.broadcasted_iota(jnp.int32, (group_blocks, rows_ref.shape[1]), 0)
+    same_row = sub_ids + first_row == rows_ref[...]
+    chosen = (same_row & (cols_ref[...] == targets_ref[:, 0:1])).astype(jnp.float32)
     margins = parts_ref[0]
     for part in range(1, parts_ref.shape[0]):
         margins = margins + parts_ref[part]
     probability = 1.0 / (1.0 + jnp.exp(-margins))
-    residual = labels_ref[pl.ds(start, group_blocks), :].astype(jnp.float32) - probability
+    labels = labels_ref[pl.ds(pl.multiple_of(first_row, 8), group_blocks), :]
+    residual = labels.astype(jnp.float32) - probability
     state_ref[0] = residual
     state_ref[1] = probability * (1.0 - probability)
-    grad = gradient_part(residual, chosen_ref[0], values_ref)
+    grad = gradient_of_all(residual, chosen, values_ref)
     grad_ref[...] = jnp.broadcast_to(grad, grad_ref.shape)
 
 
-def gradient_kernel(section, state_ref, chosen_ref, values_ref, grad_ref):
-    grad = gradient_part(state_ref[0], chosen_ref[section], values_ref)
-    grad_ref[...] = jnp.broadcast_to(grad, grad_ref.shape)
+def gradient_kernel(section, state_ref, lists_ref, values_ref, grad_ref, rows_ref, total_ref):
+    _, group_blocks, edge = state_ref.shape
+    rows_ref[pl.ds(0, group_blocks), :] = state_ref[0]
+    rows_ref[pl.ds(group_blocks, 8), :] = jnp.zeros((8, edge), jnp.float32)
+
+    def run(part):
+        spread = []
+        for inner in range(chunk):
+            place = lists_ref[2 * section + 1, part * chunk + inner]
+            row = jnp.broadcast_to(rows_ref[pl.ds(place, 1), :], (chunk, edge))
+            spread.append(row.astype(jnp.bfloat16))
+        total = jnp.dot(
+            jnp.concatenate(spread, axis=1),
+            listed_tiles(section, part, lists_ref, values_ref),
+            preferred_element_type=jnp.float32,
+        )
+        total_ref[...] = total if part == 0 else total_ref[...] + total
+
+    for_parts(section, lists_ref, run)
+    grad_ref[...] = jnp.broadcast_to(total_ref[0:1, :], grad_ref.shape)
 
 
 def update_kernel(
-    section, grads_ref, state_ref, chosen_ref, old_ref, inverses_ref, values_ref,
-    moved_ref, shrunk_ref,
+    section, grads_ref, state_ref, lists_ref, old_ref, inverses_ref, values_ref,
+    moved_ref, shrunk_ref, landed_ref,
 ):
-    tiles, edge, _ = values_ref.shape
+    _, group_blocks, edge = state_ref.shape
     gradient = jnp.sum(grads_ref[...], axis=0, keepdims=True)
     step = jnp.sum(inverses_ref[section] * gradient, axis=1, keepdims=True)
     square = (edge, edge)
@@ -181,12 +251,23 @@
     shrunk = jnp.where(raised < 0.0, -size, size)
     shrunk_ref[...] = shrunk
     change = jnp.broadcast_to(shrunk - old, (chunk, edge)).astype(jnp.bfloat16)
-    image = tile_products(
-        lambda first: change, lambda first: values_ref[pl.ds(first, chunk)], tiles
-    )
-    landed = placed_sum(chosen_ref[section], image)
+    landed_ref[...] = jnp.zeros_like(landed_ref)
+
+    def run(part):
+        images = lax.dot_general(
+            change,
+            listed_tiles(section, part, lists_ref, values_ref),
+            (((1,), (1,)), ((), ())),
+            preferred_element_type=jnp.float32,
+        )
+        for inner in range(chunk):
+            place = lists_ref[2 * section + 1, part * chunk + inner]
+            image = images[0:1, inner * edge : (inner + 1) * edge]
+            landed_ref[pl.ds(place, 1), :] = landed_ref[pl.ds(place, 1), :] + image
+
+    for_parts(section, lists_ref, run)
     weight = state_ref[1]
-    residual = state_ref[0] - weight * landed
+    residual = state_ref[0] - weight * landed_ref[pl.ds(0, group_blocks), :]
     if len(moved_ref.shape) == 3:
         moved_ref[0] = residual
         moved_ref[1] = weight
@@ -229,19 +310,24 @@
     blocks = beta.reshape(-1, edge)
     inverses = hess_inv[0]
     values = tile_values[0, 0]
-    partial_sum, old_blocks = pl.pallas_call(
+    partial_sum, old_blocks, lists = pl.pallas_call(
         margins_kernel,
-        out_shape=(float_of((row_blocks, edge)), float_of((sections, edge))),
+        out_shape=(
+            float_of((row_blocks, edge)),
+            float_of((sections, edge)),
+            jax.ShapeDtypeStruct((2 * sections, tiles), jnp.int32),
+        ),
         in_specs=[HBM] * 5,
-        out_specs=(VMEM, VMEM),
+        out_specs=(VMEM, VMEM, VMEM),
         scratch_shapes=[
             pltpu.VMEM((tiles, edge), jnp.float32),
             pltpu.VMEM(blocks.shape, jnp.float32),
             pltpu.VMEM((1, tiles), jnp.int32),
+            pltpu.VMEM((1, tiles), jnp.int32),
             pltpu.VMEM(values.shape, jnp.bfloat16),
             pltpu.SMEM((1, tiles), jnp.int32),
             pltpu.SMEM((1, sections), jnp.int32),
-            pltpu.SemaphoreType.DMA((4,)),
+            pltpu.SemaphoreType.DMA((5,)),
             pltpu.SemaphoreType.DMA((tiles // chunk,)),
         ],
         compiler_params=pltpu.CompilerParams(vmem_limit_bytes=58 << 20),
@@ -253,24 +339,23 @@
         0,
         axis_index_groups=[middle_first(sections)],
     )
-    state, grads, chosen = call(
+    group_shape = (group_blocks, edge)
+    state, grads = call(
         first_kernel,
-        (
-            float_of((2, group_blocks, edge)),
-            float_of((samp_count, edge)),
-            float_of((sections, group_blocks, tiles)),
-        ),
+        (float_of((2, *group_shape)), float_of((samp_count, edge))),
         [VMEM] * 6,
+        [],
     )(parts, labels.reshape(row_blocks, edge), tile_rows[0], tile_cols[0], block_order, values)
+    padded = pltpu.VMEM((group_blocks + 8, edge), jnp.float32)
     shrunk_blocks = []
     for section in range(sections):
         final = section + 1 == sections
-        moved_shape = (group_blocks, edge) if final else (2, group_blocks, edge)
         moving, shrunk = call(
             functools.partial(update_kernel, section),
-            (float_of(moved_shape), float_of((1, edge))),
+            (float_of(group_shape if final else (2, *group_shape)), float_of((1, edge))),
             [VMEM] * 6,
-        )(gathered(grads, "samp"), state, chosen, old_blocks, inverses, values)
+            [padded],
+        )(gathered(grads, "samp"), state, lists, old_blocks, inverses, values)
         shrunk_blocks.append(shrunk)
         state = from_behind(moving, "feat", 1)
         if not final:
@@ -278,11 +363,13 @@
                 functools.partial(gradient_kernel, section + 1),
                 float_of((samp_count, edge)),
                 [VMEM] * 3,
-            )(state, chosen, values)
+                [padded, pltpu.VMEM((chunk, edge), jnp.float32)],
+            )(state, lists, values)
     blocks = call(
         functools.partial(blocks_kernel, sections),
         float_of(blocks.shape),
         [SMEM] + [VMEM] * (1 + sections),
+        [],
     )(block_order, blocks, *shrunk_blocks)
     return (blocks.reshape(-1), state.reshape(-1))
 

time: 70.8 us -> 70.3 us (level)
    pallas_call x5, Pallas kernels: 4.06 us -> 3.24 us  [the longest x4 2.62 us: per_device(): call(functools.partial(update_kernel, section), (float_of(group_shape if...]
where the time goes in v11:
time: 70.3 us; the launch traced here: 69.9 us
  blocking collectives  37.2 us (53%)
  waiting for transfers between devices  20.4 us (29%)
  Pallas kernels  9.73 us (14%)
  starting transfers between devices  1.15 us (2%)
  between operations  0.83 us (1%)
    all_to_all x4, blocking collectives, gathered(): lax.all_to_all(parts.reshape(count, 1, edge), axis, 0, 0, axis_index_grou...  26.5 us
    ppermute x4, waiting for transfers between devices, from_behind(): return lax.ppermute(value, axis, pairs)  20.4 us
    all_to_all x1, blocking collectives, per_device(): lax.all_to_all(partial_sum.reshape(sections, group_blocks, edge), 'feat',...  10.7 us
    pallas_call x1, Pallas kernels, per_device(): pl.pallas_call(margins_kernel, out_shape=(float_of((row_blocks, edge)), f...  3.64 us
    pallas_call x4, Pallas kernels, per_device(): call(functools.partial(update_kernel, section), (float_of(group_shape if...  2.62 us
    pallas_call x3, Pallas kernels, per_device(): call(functools.partial(gradient_kernel, section + 1), float_of((samp_coun...  1.58 us
  transfers between devices with their start and end apart: 4, of which 4 were waited for; matrix products, arithmetic and copies ran while one was open for 0% of the time, Pallas kernels for 2%

profile of v11, /device:TPU:0, one launch (start us, length us, event | category | flops | bytes accessed | tf_op | source)
XLA Modules:
  0.0 69.9 jit_solution(5899420611780517208)
XLA Ops:
  0.6 0.0 copy-start.6
  0.6 0.0 copy-start
  0.7 0.0 copy-start.7
  0.7 0.0 copy-start.8
  0.7 0.0 copy-start.4
  0.7 0.0 copy-start.1
  0.7 3.6 %shard_map.86 = (f32[128,128]{1,0:T(8,128)}, f32[4,128]{1,0:T(4,128)}, s32[8,64]{1,0:T(8,128)}) custom-call(s32[1,64]{1,0:T(1,128)} %bitcast.49, s32[1,4]{1,0:T(1,128)} %targets_smem.1, s32[1,64]{1,0:T(1,128)} %bitcast.51, f32[512,128]{1,0:T(8,128)} %bitcast.38, bf16[64,128,128]{2,1,0:T(8,128)(2,1)} %bitcast.25), custom_call_target="tpu_custom_call" | custom-call | tf_op jit(solution)/shard_map/pallas_call | solution.py:313
  4.3 0.0 copy-start.3
  4.4 0.0 copy-start.5
  4.4 10.7 %all_to_all.25.parts_ref = f32[4,32,128]{2,1,0:T(8,128)S(1)} all-to-all(f32[4,32,128]{2,1,0:T(8,128)} %bitcast.54), channel_id=1, replica_groups={{2,1,3,0},{6,5,7,4},{10,9,11,8},{14,13,15,12},{18,17,19,16},{22,21,23,2..., dimensions={0} | all-to-all | bytes 131072 | tf_op jit(solution)/shard_map/all_to_all | solution.py:335
  15.0 0.0 copy-done.6
  15.0 0.0 copy-done
  15.0 0.0 copy-done.7
  15.1 0.0 copy-done.8
  15.1 0.0 copy-done.4
  15.1 0.6 shard_map.87
  15.7 7.9 %all_to_all.26 = f32[8,1,128]{2,1,0:T(1,128)S(1)} all-to-all(f32[8,1,128]{2,1,0:T(1,128)S(1)} %bitcast.48), channel_id=1, replica_groups={{4,28,12,20,0,24,8,16},{5,29,13,21,1,25,9,17},{6,30,14,22,2,26,10,18},{..., dimensions={0} | all-to-all | bytes 8192 | tf_op jit(solution)/shard_map/all_to_all | solution.py:298
  23.6 0.0 copy-done.1
  23.6 0.0 copy-done.3
  23.6 0.0 copy-done.5
  23.6 0.7 shard_map.88
  24.3 1.0 %collective-permute-start = (f32[2,32,128]{2,1,0:T(8,128)S(1)}, f32[2,32,128]{2,1,0:T(8,128)S(1)}, u32[]{:S(2)}, u32[]{:S(2)}) collective-permute-start(f32[2,32,128]{2,1,0:T(8,128)S(1)} %get-tuple-element.21), channel_id=1, source_target_pairs={{0,1},{1,2},{2,3},{3,0},{4,5},{5,6},{6,7},{7,4},{8,9},{9,10},{10,1... | collective-permute-start | bytes 98312 | tf_op jit(solution)/shard_map/ppermute | solution.py:288
  25.3 4.8 %collective-permute-done.state_ref = f32[2,32,128]{2,1,0:T(8,128)S(1)} collective-permute-done((f32[2,32,128]{2,1,0:T(8,128)S(1)}, f32[2,32,128]{2,1,0:T(8,128)S(1)}, u32[]{:S(2)}, u32[]{:S(2)}) %collective-permute-start) | collective-permute-done | bytes 32800 | tf_op jit(solution)/shard_map/ppermute | solution.py:288
  30.1 0.5 shard_map.89
  30.6 6.1 %all_to_all.27 = f32[8,1,128]{2,1,0:T(1,128)S(1)} all-to-all(f32[8,1,128]{2,1,0:T(1,128)S(1)} %bitcast.45), channel_id=1, replica_groups={{4,28,12,20,0,24,8,16},{5,29,13,21,1,25,9,17},{6,30,14,22,2,26,10,18},{..., dimensions={0} | all-to-all | bytes 8192 | tf_op jit(solution)/shard_map/all_to_all | solution.py:298
  36.6 0.7 shard_map.90
  37.3 0.1 collective-permute-start.1
  37.4 5.7 %collective-permute-done.1.state_ref = f32[2,32,128]{2,1,0:T(8,128)S(1)} collective-permute-done((f32[2,32,128]{2,1,0:T(8,128)S(1)}, f32[2,32,128]{2,1,0:T(8,128)S(1)}, u32[]{:S(2)}, u32[]{:S(2)}) %collective-permute-start.1) | collective-permute-done | bytes 32800 | tf_op jit(solution)/shard_map/ppermute | solution.py:288
  43.1 0.5 shard_map.91
  43.6 6.5 %all_to_all.28 = f32[8,1,128]{2,1,0:T(1,128)S(1)} all-to-all(f32[8,1,128]{2,1,0:T(1,128)S(1)} %bitcast.46), channel_id=1, replica_groups={{4,28,12,20,0,24,8,16},{5,29,13,21,1,25,9,17},{6,30,14,22,2,26,10,18},{..., dimensions={0} | all-to-all | bytes 8192 | tf_op jit(solution)/shard_map/all_to_all | solution.py:298
  50.1 0.7 shard_map.92
  50.7 0.0 copy-start.2
  50.7 0.1 collective-permute-start.2
  50.8 5.7 %collective-permute-done.2.state_ref = f32[2,32,128]{2,1,0:T(8,128)S(1)} collective-permute-done((f32[2,32,128]{2,1,0:T(8,128)S(1)}, f32[2,32,128]{2,1,0:T(8,128)S(1)}, u32[]{:S(2)}, u32[]{:S(2)}) %collective-permute-start.2) | collective-permute-done | bytes 32800 | tf_op jit(solution)/shard_map/ppermute | solution.py:288
  56.5 0.5 shard_map.93
  57.0 6.0 %all_to_all.29 = f32[8,1,128]{2,1,0:T(1,128)S(1)} all-to-all(f32[8,1,128]{2,1,0:T(1,128)S(1)} %bitcast.47), channel_id=1, replica_groups={{4,28,12,20,0,24,8,16},{5,29,13,21,1,25,9,17},{6,30,14,22,2,26,10,18},{..., dimensions={0} | all-to-all | bytes 8192 | tf_op jit(solution)/shard_map/all_to_all | solution.py:298
  63.1 0.7 shard_map.94
  63.8 0.1 collective-permute-start.3
  63.8 0.0 copy-done.2
  63.8 1.3 %shard_map.95 = f32[512,128]{1,0:T(8,128)} custom-call(s32[1,4]{1,0:T(1,128)S(1)} %copy-done.6, f32[512,128]{1,0:T(8,128)S(1)} %bitcast.39, f32[1,128]{1,0:T(1,128)S(1)} %get-tuple-element.20.refs_0_, f32[1,128]{1,0:T(1,128)S(1)} %get-tuple-element.22.refs_1_, f32[1,128]{1,0:T(1,128)S(1)} %get-tuple-element.24.refs_2_, f32[1,128]{1,0:T(1,128)S(1)} %get-tuple-element.26.refs_3_), custom_call_target="tpu_custom_call" | custom-call | tf_op jit(solution)/shard_map/pallas_call | solution.py:368
  65.1 4.2 %collective-permute-done.3 = f32[32,128]{1,0:T(8,128)S(1)} collective-permute-done((f32[32,128]{1,0:T(8,128)S(1)}, f32[32,128]{1,0:T(8,128)S(1)}, u32[]{:S(2)}, u32[]{:S(2)}) %collective-permute-start.3) | collective-permute-done | bytes 16416 | tf_op jit(solution)/shard_map/ppermute | solution.py:288
  69.3 0.6 copy.14
Async XLA Ops:
  0.6 14.4 %copy-start.6 = (s32[1,4]{1,0:T(1,128)S(1)}, s32[1,4]{1,0:T(1,128)}, u32[]{:S(2)}) copy-start(s32[1,4]{1,0:T(1,128)} %targets_smem.1) | copy-start | bytes 52
  0.6 14.4 %copy-start = (bf16[1,1,64,128,128]{4,3,2,1,0:T(8,128)(2,1)S(1)}, bf16[1,1,64,128,128]{4,3,2,1,0:T(8,128)(2,1)}, u32[]{:S(2)}) copy-start(bf16[1,1,64,128,128]{4,3,2,1,0:T(8,128)(2,1)} %param.11) | copy-start | bytes 6291460
  0.7 14.4 %copy-start.7 = (s32[1,1,64]{2,1,0:T(1,128)S(1)}, s32[1,1,64]{2,1,0:T(1,128)}, u32[]{:S(2)}) copy-start(s32[1,1,64]{2,1,0:T(1,128)} %param.10) | copy-start | bytes 772
  0.7 14.4 %copy-start.8 = (s32[1,1,64]{2,1,0:T(1,128)S(1)}, s32[1,1,64]{2,1,0:T(1,128)}, u32[]{:S(2)}) copy-start(s32[1,1,64]{2,1,0:T(1,128)} %param.9) | copy-start | bytes 772
  0.7 14.4 %copy-start.4 = (s32[16384]{0:T(1024)S(1)}, s32[16384]{0:T(1024)}, u32[]{:S(2)}) copy-start(s32[16384]{0:T(1024)} %param.7) | copy-start | bytes 196612
  0.7 22.9 %copy-start.1 = (f32[1,4,128,128]{3,2,1,0:T(8,128)S(1)}, f32[1,4,128,128]{3,2,1,0:T(8,128)}, u32[]{:S(2)}) copy-start(f32[1,4,128,128]{3,2,1,0:T(8,128)} %param.13) | copy-start | bytes 786436
  4.3 19.3 %copy-start.3 = (s32[8,64]{1,0:T(8,128)S(1)}, s32[8,64]{1,0:T(8,128)}, u32[]{:S(2)}) copy-start(s32[8,64]{1,0:T(8,128)} %get-tuple-element.18.lists_ref) | copy-start | bytes 6148
  4.4 19.3 %copy-start.5 = (f32[4,128]{1,0:T(4,128)S(1)}, f32[4,128]{1,0:T(4,128)}, u32[]{:S(2)}) copy-start(f32[4,128]{1,0:T(4,128)} %get-tuple-element.19.old_ref) | copy-start | bytes 6148
  24.3 5.8 %collective-permute-start = (f32[2,32,128]{2,1,0:T(8,128)S(1)}, f32[2,32,128]{2,1,0:T(8,128)S(1)}, u32[]{:S(2)}, u32[]{:S(2)}) collective-permute-start(f32[2,32,128]{2,1,0:T(8,128)S(1)} %get-tuple-element.21), channel_id=1, source_target_pairs={{0,1},{1,2},{2,3},{3,0},{4,5},{5,6},{6,7},{7,4},{8,9},{9,10},{10,1... | collective-permute-start | bytes 98312 | tf_op jit(solution)/shard_map/ppermute | solution.py:288
  37.3 5.8 %collective-permute-start.1 = (f32[2,32,128]{2,1,0:T(8,128)S(1)}, f32[2,32,128]{2,1,0:T(8,128)S(1)}, u32[]{:S(2)}, u32[]{:S(2)}) collective-permute-start(f32[2,32,128]{2,1,0:T(8,128)S(1)} %get-tuple-element.23), channel_id=1, source_target_pairs={{0,1},{1,2},{2,3},{3,0},{4,5},{5,6},{6,7},{7,4},{8,9},{9,10},{10,1... | collective-permute-start | bytes 98312 | tf_op jit(solution)/shard_map/ppermute | solution.py:288
  50.7 13.1 %copy-start.2 = (f32[65536]{0:T(1024)S(1)}, f32[65536]{0:T(1024)}, u32[]{:S(2)}) copy-start(f32[65536]{0:T(1024)} %param.8) | copy-start | bytes 786436
  50.7 5.8 %collective-permute-start.2 = (f32[2,32,128]{2,1,0:T(8,128)S(1)}, f32[2,32,128]{2,1,0:T(8,128)S(1)}, u32[]{:S(2)}, u32[]{:S(2)}) collective-permute-start(f32[2,32,128]{2,1,0:T(8,128)S(1)} %get-tuple-element.25), channel_id=1, source_target_pairs={{0,1},{1,2},{2,3},{3,0},{4,5},{5,6},{6,7},{7,4},{8,9},{9,10},{10,1... | collective-permute-start | bytes 98312 | tf_op jit(solution)/shard_map/ppermute | solution.py:288
  63.8 5.6 %collective-permute-start.3 = (f32[32,128]{1,0:T(8,128)S(1)}, f32[32,128]{1,0:T(8,128)S(1)}, u32[]{:S(2)}, u32[]{:S(2)}) collective-permute-start(f32[32,128]{1,0:T(8,128)S(1)} %get-tuple-element.27), channel_id=1, source_target_pairs={{0,1},{1,2},{2,3},{3,0},{4,5},{5,6},{6,7},{7,4},{8,9},{9,10},{10,1... | collective-permute-start | bytes 49160 | tf_op jit(solution)/shard_map/ppermute | solution.py:288

commit v12 on v11

--- a/solution.py
+++ b/solution.py
@@ -10,6 +10,7 @@
 exact_prec = lax.Precision.HIGHEST
 l1_penalty = 0.25
 chunk = 16
+copied = 4
 
 VMEM = pl.BlockSpec(memory_space=pltpu.VMEM)
 SMEM = pl.BlockSpec(memory_space=pltpu.SMEM)
@@ -108,11 +109,11 @@
     ]
     large = [
         pltpu.make_async_copy(
-            values_hbm.at[pl.ds(first, chunk)],
-            values_ref.at[pl.ds(first, chunk)],
-            tile_sem.at[first // chunk],
-        )
-        for first in range(0, tiles, chunk)
+            values_hbm.at[pl.ds(first, copied)],
+            values_ref.at[pl.ds(first, copied)],
+            tile_sem.at[first // copied],
+        )
+        for first in range(0, tiles, copied)
     ]
     for copy in small + large:
         copy.start()
@@ -138,7 +139,8 @@
         lists_ref[pl.ds(2 * section + 1, 1), :] = places
 
     def tiles_of(first):
-        large[first // chunk].wait()
+        for copy in large[first // copied : (first + chunk) // copied]:
+            copy.wait()
         return values_ref[pl.ds(first, chunk)]
 
     products = tile_products(
@@ -163,10 +165,11 @@
     )
 
 
-def for_parts(section, lists_ref, run):
-    run(0)
-    for part in range(1, lists_ref.shape[1] // chunk):
-        pl.when(lists_ref[2 * section, part * chunk] >= 0)(functools.partial(run, part))
+def for_parts(section, lists_ref, run, part=0):
+    run(part)
+    if (part + 1) * chunk < lists_ref.shape[1]:
+        more = lists_ref[2 * section, (part + 1) * chunk] >= 0
+        pl.when(more)(functools.partial(for_parts, section, lists_ref, run, part + 1))
 
 
 def gradient_of_all(residual, chosen, values_ref):
@@ -328,7 +331,7 @@
             pltpu.SMEM((1, tiles), jnp.int32),
             pltpu.SMEM((1, sections), jnp.int32),
             pltpu.SemaphoreType.DMA((5,)),
-            pltpu.SemaphoreType.DMA((tiles // chunk,)),
+            pltpu.SemaphoreType.DMA((tiles // copied,)),
         ],
         compiler_params=pltpu.CompilerParams(vmem_limit_bytes=58 << 20),
     )(tile_cols[0], block_order, tile_rows[0], blocks, values)

time: 70.3 us -> 69.2 us (0.984)
  Pallas kernels: 9.73 us -> 8.66 us
    pallas_call x4, Pallas kernels: 2.62 us -> 1.76 us  [per_device(): call(functools.partial(update_kernel, section), (float_of(group_shape if...]
where the time goes in v12:
time: 69.2 us; the launch traced here: 68.8 us
  blocking collectives  37.1 us (54%)
  waiting for transfers between devices  20.4 us (29%)
  Pallas kernels  8.66 us (13%)
  starting transfers between devices  1.13 us (2%)
  between operations  0.77 us (1%)
    all_to_all x4, blocking collectives, gathered(): lax.all_to_all(parts.reshape(count, 1, edge), axis, 0, 0, axis_index_grou...  26.5 us
    ppermute x4, waiting for transfers between devices, from_behind(): return lax.ppermute(value, axis, pairs)  20.4 us
    all_to_all x1, blocking collectives, per_device(): lax.all_to_all(partial_sum.reshape(sections, group_blocks, edge), 'feat',...  10.7 us
    pallas_call x1, Pallas kernels, per_device(): pl.pallas_call(margins_kernel, out_shape=(float_of((row_blocks, edge)), f...  4.09 us
    pallas_call x4, Pallas kernels, per_device(): call(functools.partial(update_kernel, section), (float_of(group_shape if...  1.76 us
  transfers between devices with their start and end apart: 4, of which 4 were waited for; matrix products, arithmetic and copies ran while one was open for 0% of the time, Pallas kernels for 2%

profile of v12, /device:TPU:0, one launch (start us, length us, event | category | flops | bytes accessed | tf_op | source)
XLA Modules:
  0.0 68.8 jit_solution(15231243279917764800)
XLA Ops:
  0.6 0.0 copy-start.6
  0.6 0.0 copy-start
  0.7 0.0 copy-start.7
  0.7 0.0 copy-start.8
  0.7 0.0 copy-start.4
  0.7 0.0 copy-start.1
  0.7 4.1 %shard_map.86 = (f32[128,128]{1,0:T(8,128)}, f32[4,128]{1,0:T(4,128)}, s32[8,64]{1,0:T(8,128)}) custom-call(s32[1,64]{1,0:T(1,128)} %bitcast.49, s32[1,4]{1,0:T(1,128)} %targets_smem.1, s32[1,64]{1,0:T(1,128)} %bitcast.51, f32[512,128]{1,0:T(8,128)} %bitcast.38, bf16[64,128,128]{2,1,0:T(8,128)(2,1)} %bitcast.25), custom_call_target="tpu_custom_call" | custom-call | tf_op jit(solution)/shard_map/pallas_call | solution.py:316
  4.8 0.0 copy-start.3
  4.8 0.0 copy-start.5
  4.8 10.7 %all_to_all.25.parts_ref = f32[4,32,128]{2,1,0:T(8,128)S(1)} all-to-all(f32[4,32,128]{2,1,0:T(8,128)} %bitcast.54), channel_id=1, replica_groups={{2,1,3,0},{6,5,7,4},{10,9,11,8},{14,13,15,12},{18,17,19,16},{22,21,23,2..., dimensions={0} | all-to-all | bytes 131072 | tf_op jit(solution)/shard_map/all_to_all | solution.py:338
  15.5 0.0 copy-done.6
  15.5 0.0 copy-done
  15.5 0.0 copy-done.7
  15.5 0.0 copy-done.8
  15.5 0.0 copy-done.4
  15.5 0.6 shard_map.87
  16.1 7.9 %all_to_all.26 = f32[8,1,128]{2,1,0:T(1,128)S(1)} all-to-all(f32[8,1,128]{2,1,0:T(1,128)S(1)} %bitcast.48), channel_id=1, replica_groups={{4,28,12,20,0,24,8,16},{5,29,13,21,1,25,9,17},{6,30,14,22,2,26,10,18},{..., dimensions={0} | all-to-all | bytes 8192 | tf_op jit(solution)/shard_map/all_to_all | solution.py:301
  24.1 0.0 copy-done.1
  24.1 0.0 copy-done.3
  24.1 0.0 copy-done.5
  24.1 0.4 shard_map.88
  24.5 1.0 %collective-permute-start = (f32[2,32,128]{2,1,0:T(8,128)S(1)}, f32[2,32,128]{2,1,0:T(8,128)S(1)}, u32[]{:S(2)}, u32[]{:S(2)}) collective-permute-start(f32[2,32,128]{2,1,0:T(8,128)S(1)} %get-tuple-element.21), channel_id=1, source_target_pairs={{0,1},{1,2},{2,3},{3,0},{4,5},{5,6},{6,7},{7,4},{8,9},{9,10},{10,1... | collective-permute-start | bytes 98312 | tf_op jit(solution)/shard_map/ppermute | solution.py:291
  25.5 4.8 %collective-permute-done.state_ref = f32[2,32,128]{2,1,0:T(8,128)S(1)} collective-permute-done((f32[2,32,128]{2,1,0:T(8,128)S(1)}, f32[2,32,128]{2,1,0:T(8,128)S(1)}, u32[]{:S(2)}, u32[]{:S(2)}) %collective-permute-start) | collective-permute-done | bytes 32800 | tf_op jit(solution)/shard_map/ppermute | solution.py:291
  30.3 0.3 shard_map.89
  30.6 6.0 %all_to_all.27 = f32[8,1,128]{2,1,0:T(1,128)S(1)} all-to-all(f32[8,1,128]{2,1,0:T(1,128)S(1)} %bitcast.45), channel_id=1, replica_groups={{4,28,12,20,0,24,8,16},{5,29,13,21,1,25,9,17},{6,30,14,22,2,26,10,18},{..., dimensions={0} | all-to-all | bytes 8192 | tf_op jit(solution)/shard_map/all_to_all | solution.py:301
  36.6 0.4 shard_map.90
  37.1 0.1 collective-permute-start.1
  37.1 5.7 %collective-permute-done.1.state_ref = f32[2,32,128]{2,1,0:T(8,128)S(1)} collective-permute-done((f32[2,32,128]{2,1,0:T(8,128)S(1)}, f32[2,32,128]{2,1,0:T(8,128)S(1)}, u32[]{:S(2)}, u32[]{:S(2)}) %collective-permute-start.1) | collective-permute-done | bytes 32800 | tf_op jit(solution)/shard_map/ppermute | solution.py:291
  42.8 0.3 shard_map.91
  43.1 6.4 %all_to_all.28 = f32[8,1,128]{2,1,0:T(1,128)S(1)} all-to-all(f32[8,1,128]{2,1,0:T(1,128)S(1)} %bitcast.46), channel_id=1, replica_groups={{4,28,12,20,0,24,8,16},{5,29,13,21,1,25,9,17},{6,30,14,22,2,26,10,18},{..., dimensions={0} | all-to-all | bytes 8192 | tf_op jit(solution)/shard_map/all_to_all | solution.py:301
  49.6 0.4 shard_map.92
  50.0 0.0 copy-start.2
  50.0 0.1 collective-permute-start.2
  50.1 5.7 %collective-permute-done.2.state_ref = f32[2,32,128]{2,1,0:T(8,128)S(1)} collective-permute-done((f32[2,32,128]{2,1,0:T(8,128)S(1)}, f32[2,32,128]{2,1,0:T(8,128)S(1)}, u32[]{:S(2)}, u32[]{:S(2)}) %collective-permute-start.2) | collective-permute-done | bytes 32800 | tf_op jit(solution)/shard_map/ppermute | solution.py:291
  55.8 0.3 shard_map.93
  56.1 6.0 %all_to_all.29 = f32[8,1,128]{2,1,0:T(1,128)S(1)} all-to-all(f32[8,1,128]{2,1,0:T(1,128)S(1)} %bitcast.47), channel_id=1, replica_groups={{4,28,12,20,0,24,8,16},{5,29,13,21,1,25,9,17},{6,30,14,22,2,26,10,18},{..., dimensions={0} | all-to-all | bytes 8192 | tf_op jit(solution)/shard_map/all_to_all | solution.py:301
  62.2 0.4 shard_map.94
  62.6 0.1 collective-permute-start.3
  62.7 0.0 copy-done.2
  62.7 1.3 %shard_map.95 = f32[512,128]{1,0:T(8,128)} custom-call(s32[1,4]{1,0:T(1,128)S(1)} %copy-done.6, f32[512,128]{1,0:T(8,128)S(1)} %bitcast.39, f32[1,128]{1,0:T(1,128)S(1)} %get-tuple-element.20.refs_0_, f32[1,128]{1,0:T(1,128)S(1)} %get-tuple-element.22.refs_1_, f32[1,128]{1,0:T(1,128)S(1)} %get-tuple-element.24.refs_2_, f32[1,128]{1,0:T(1,128)S(1)} %get-tuple-element.26.refs_3_), custom_call_target="tpu_custom_call" | custom-call | tf_op jit(solution)/shard_map/pallas_call | solution.py:371
  63.9 4.2 %collective-permute-done.3 = f32[32,128]{1,0:T(8,128)S(1)} collective-permute-done((f32[32,128]{1,0:T(8,128)S(1)}, f32[32,128]{1,0:T(8,128)S(1)}, u32[]{:S(2)}, u32[]{:S(2)}) %collective-permute-start.3) | collective-permute-done | bytes 16416 | tf_op jit(solution)/shard_map/ppermute | solution.py:291
  68.2 0.6 copy.14
Async XLA Ops:
  0.6 14.9 %copy-start.6 = (s32[1,4]{1,0:T(1,128)S(1)}, s32[1,4]{1,0:T(1,128)}, u32[]{:S(2)}) copy-start(s32[1,4]{1,0:T(1,128)} %targets_smem.1) | copy-start | bytes 52
  0.6 14.9 %copy-start = (bf16[1,1,64,128,128]{4,3,2,1,0:T(8,128)(2,1)S(1)}, bf16[1,1,64,128,128]{4,3,2,1,0:T(8,128)(2,1)}, u32[]{:S(2)}) copy-start(bf16[1,1,64,128,128]{4,3,2,1,0:T(8,128)(2,1)} %param.11) | copy-start | bytes 6291460
  0.7 14.8 %copy-start.7 = (s32[1,1,64]{2,1,0:T(1,128)S(1)}, s32[1,1,64]{2,1,0:T(1,128)}, u32[]{:S(2)}) copy-start(s32[1,1,64]{2,1,0:T(1,128)} %param.10) | copy-start | bytes 772
  0.7 14.8 %copy-start.8 = (s32[1,1,64]{2,1,0:T(1,128)S(1)}, s32[1,1,64]{2,1,0:T(1,128)}, u32[]{:S(2)}) copy-start(s32[1,1,64]{2,1,0:T(1,128)} %param.9) | copy-start | bytes 772
  0.7 14.8 %copy-start.4 = (s32[16384]{0:T(1024)S(1)}, s32[16384]{0:T(1024)}, u32[]{:S(2)}) copy-start(s32[16384]{0:T(1024)} %param.7) | copy-start | bytes 196612
  0.7 23.4 %copy-start.1 = (f32[1,4,128,128]{3,2,1,0:T(8,128)S(1)}, f32[1,4,128,128]{3,2,1,0:T(8,128)}, u32[]{:S(2)}) copy-start(f32[1,4,128,128]{3,2,1,0:T(8,128)} %param.13) | copy-start | bytes 786436
  4.8 19.3 %copy-start.3 = (s32[8,64]{1,0:T(8,128)S(1)}, s32[8,64]{1,0:T(8,128)}, u32[]{:S(2)}) copy-start(s32[8,64]{1,0:T(8,128)} %get-tuple-element.18.lists_ref) | copy-start | bytes 6148
  4.8 19.3 %copy-start.5 = (f32[4,128]{1,0:T(4,128)S(1)}, f32[4,128]{1,0:T(4,128)}, u32[]{:S(2)}) copy-start(f32[4,128]{1,0:T(4,128)} %get-tuple-element.19.old_ref) | copy-start | bytes 6148
  24.5 5.8 %collective-permute-start = (f32[2,32,128]{2,1,0:T(8,128)S(1)}, f32[2,32,128]{2,1,0:T(8,128)S(1)}, u32[]{:S(2)}, u32[]{:S(2)}) collective-permute-start(f32[2,32,128]{2,1,0:T(8,128)S(1)} %get-tuple-element.21), channel_id=1, source_target_pairs={{0,1},{1,2},{2,3},{3,0},{4,5},{5,6},{6,7},{7,4},{8,9},{9,10},{10,1... | collective-permute-start | bytes 98312 | tf_op jit(solution)/shard_map/ppermute | solution.py:291
  37.1 5.8 %collective-permute-start.1 = (f32[2,32,128]{2,1,0:T(8,128)S(1)}, f32[2,32,128]{2,1,0:T(8,128)S(1)}, u32[]{:S(2)}, u32[]{:S(2)}) collective-permute-start(f32[2,32,128]{2,1,0:T(8,128)S(1)} %get-tuple-element.23), channel_id=1, source_target_pairs={{0,1},{1,2},{2,3},{3,0},{4,5},{5,6},{6,7},{7,4},{8,9},{9,10},{10,1... | collective-permute-start | bytes 98312 | tf_op jit(solution)/shard_map/ppermute | solution.py:291
  50.0 12.6 %copy-start.2 = (f32[65536]{0:T(1024)S(1)}, f32[65536]{0:T(1024)}, u32[]{:S(2)}) copy-start(f32[65536]{0:T(1024)} %param.8) | copy-start | bytes 786436
  50.0 5.8 %collective-permute-start.2 = (f32[2,32,128]{2,1,0:T(8,128)S(1)}, f32[2,32,128]{2,1,0:T(8,128)S(1)}, u32[]{:S(2)}, u32[]{:S(2)}) collective-permute-start(f32[2,32,128]{2,1,0:T(8,128)S(1)} %get-tuple-element.25), channel_id=1, source_target_pairs={{0,1},{1,2},{2,3},{3,0},{4,5},{5,6},{6,7},{7,4},{8,9},{9,10},{10,1... | collective-permute-start | bytes 98312 | tf_op jit(solution)/shard_map/ppermute | solution.py:291
  62.6 5.6 %collective-permute-start.3 = (f32[32,128]{1,0:T(8,128)S(1)}, f32[32,128]{1,0:T(8,128)S(1)}, u32[]{:S(2)}, u32[]{:S(2)}) collective-permute-start(f32[32,128]{1,0:T(8,128)S(1)} %get-tuple-element.27), channel_id=1, source_target_pairs={{0,1},{1,2},{2,3},{3,0},{4,5},{5,6},{6,7},{7,4},{8,9},{9,10},{10,1... | collective-permute-start | bytes 49160 | tf_op jit(solution)/shard_map/ppermute | solution.py:291

commit v13 on v12

--- a/solution.py
+++ b/solution.py
@@ -10,7 +10,7 @@
 exact_prec = lax.Precision.HIGHEST
 l1_penalty = 0.25
 chunk = 16
-copied = 4
+copied = 16
 
 VMEM = pl.BlockSpec(memory_space=pltpu.VMEM)
 SMEM = pl.BlockSpec(memory_space=pltpu.SMEM)
@@ -76,6 +76,10 @@
     )
 
 
+def bits_of(group_blocks):
+    return group_blocks.bit_length()
+
+
 def listed(row_in_group, taken, group_blocks):
     tiles = taken.shape[1]
     square = (tiles, tiles)
@@ -84,11 +88,11 @@
     taken = jnp.broadcast_to(taken, (8, tiles)).astype(jnp.float32)
     before = over_lanes(taken, (lane < sub).astype(jnp.float32))
     in_slot = (sub == before[0:1].astype(jnp.int32)) & (taken[0:1] > 0.0)
-    numbers = lax.broadcasted_iota(jnp.int32, (8, tiles), 1) + 1
+    numbers = lax.broadcasted_iota(jnp.int32, (8, tiles), 1)
     short = group_blocks - row_in_group
     facts = jnp.where(lax.broadcasted_iota(jnp.int32, (8, tiles), 0) == 0, numbers, short)
     found = over_lanes(facts.astype(jnp.float32), in_slot.astype(jnp.float32)).astype(jnp.int32)
-    return found[0:1] - 1, group_blocks - found[1:2]
+    return found[0:1] * 2 ** bits_of(group_blocks) + group_blocks - found[1:2]
 
 
 def margins_kernel(
@@ -124,6 +128,14 @@
     for section in range(sections):
         old_ref[pl.ds(section, 1), :] = beta_ref[pl.ds(targets_smem[0, section], 1), :]
 
+    def tiles_of(first):
+        for copy in large[first // copied : (first + chunk) // copied]:
+            copy.wait()
+        return values_ref[pl.ds(first, chunk)]
+
+    products = tile_products(
+        lambda first: picked_ref[pl.ds(first, chunk), :].astype(jnp.bfloat16), tiles_of, tiles
+    )
     my_index = lax.axis_index("feat")
     group_blocks = row_blocks // sections
     for section in range(sections):
@@ -134,18 +146,8 @@
             & (row_in_group < group_blocks)
             & (cols_ref[...] == targets_smem[0, section])
         )
-        ids, places = listed(row_in_group, taken, group_blocks)
-        lists_ref[pl.ds(2 * section, 1), :] = ids
-        lists_ref[pl.ds(2 * section + 1, 1), :] = places
-
-    def tiles_of(first):
-        for copy in large[first // copied : (first + chunk) // copied]:
-            copy.wait()
-        return values_ref[pl.ds(first, chunk)]
-
-    products = tile_products(
-        lambda first: picked_ref[pl.ds(first, chunk), :].astype(jnp.bfloat16), tiles_of, tiles
-    )
+        lists_ref[pl.ds(section, 1), :] = listed(row_in_group, taken, group_blocks)
+
     block_ids = lax.broadcasted_iota(jnp.int32, (row_blocks, tiles), 0)
     placing = (block_ids == rows_ref[...]).astype(jnp.float32)
     partial = placed_sum(placing, products)
@@ -155,21 +157,20 @@
         ]
 
 
-def listed_tiles(section, part, lists_ref, values_ref):
-    return jnp.concatenate(
-        [
-            values_ref[jnp.maximum(lists_ref[2 * section, part * chunk + inner], 0)]
-            for inner in range(chunk)
-        ],
-        axis=0,
-    )
-
-
-def for_parts(section, lists_ref, run, part=0):
+def listed_slots(section, part, group_blocks, lists_ref, values_ref):
+    bits = bits_of(group_blocks)
+    found = [lists_ref[section, part * chunk + inner] for inner in range(chunk)]
+    tiles = [values_ref[lax.shift_right_logical(number, bits)] for number in found]
+    return jnp.concatenate(tiles, axis=0), [number & (2**bits - 1) for number in found]
+
+
+def for_parts(section, group_blocks, lists_ref, run, part=0):
     run(part)
     if (part + 1) * chunk < lists_ref.shape[1]:
-        more = lists_ref[2 * section, (part + 1) * chunk] >= 0
-        pl.when(more)(functools.partial(for_parts, section, lists_ref, run, part + 1))
+        more = lists_ref[section, (part + 1) * chunk] != group_blocks
+        pl.when(more)(
+            functools.partial(for_parts, section, group_blocks, lists_ref, run, part + 1)
+        )
 
 
 def gradient_of_all(residual, chosen, values_ref):
@@ -220,19 +221,17 @@
     rows_ref[pl.ds(group_blocks, 8), :] = jnp.zeros((8, edge), jnp.float32)
 
     def run(part):
+        tiles, places = listed_slots(section, part, group_blocks, lists_ref, values_ref)
         spread = []
-        for inner in range(chunk):
-            place = lists_ref[2 * section + 1, part * chunk + inner]
+        for place in places:
             row = jnp.broadcast_to(rows_ref[pl.ds(place, 1), :], (chunk, edge))
             spread.append(row.astype(jnp.bfloat16))
         total = jnp.dot(
-            jnp.concatenate(spread, axis=1),
-            listed_tiles(section, part, lists_ref, values_ref),
-            preferred_element_type=jnp.float32,
+            jnp.concatenate(spread, axis=1), tiles, preferred_element_type=jnp.float32
         )
         total_ref[...] = total if part == 0 else total_ref[...] + total
 
-    for_parts(section, lists_ref, run)
+    for_parts(section, group_blocks, lists_ref, run)
     grad_ref[...] = jnp.broadcast_to(total_ref[0:1, :], grad_ref.shape)
 
 
@@ -257,18 +256,15 @@
     landed_ref[...] = jnp.zeros_like(landed_ref)
 
     def run(part):
+        tiles, places = listed_slots(section, part, group_blocks, lists_ref, values_ref)
         images = lax.dot_general(
-            change,
-            listed_tiles(section, part, lists_ref, values_ref),
-            (((1,), (1,)), ((), ())),
-            preferred_element_type=jnp.float32,
-        )
-        for inner in range(chunk):
-            place = lists_ref[2 * section + 1, part * chunk + inner]
+            change, tiles, (((1,), (1,)), ((), ())), preferred_element_type=jnp.float32
+        )
+        for inner, place in enumerate(places):
             image = images[0:1, inner * edge : (inner + 1) * edge]
             landed_ref[pl.ds(place, 1), :] = landed_ref[pl.ds(place, 1), :] + image
 
-    for_parts(section, lists_ref, run)
+    for_parts(section, group_blocks, lists_ref, run)
     weight = state_ref[1]
     residual = state_ref[0] - weight * landed_ref[pl.ds(0, group_blocks), :]
     if len(moved_ref.shape) == 3:
@@ -318,7 +314,7 @@
         out_shape=(
             float_of((row_blocks, edge)),
             float_of((sections, edge)),
-            jax.ShapeDtypeStruct((2 * sections, tiles), jnp.int32),
+            jax.ShapeDtypeStruct((sections, tiles), jnp.int32),
         ),
         in_specs=[HBM] * 5,
         out_specs=(VMEM, VMEM, VMEM),

time: 69.2 us -> 68.3 us (0.987)
  Pallas kernels: 8.66 us -> 7.77 us
    pallas_call x1, Pallas kernels: 4.09 us -> 3.33 us  [per_device(): pl.pallas_call(margins_kernel, out_shape=(float_of((row_blocks, edge)), f...]
where the time goes in v13:
time: 68.3 us; the launch traced here: 67.9 us
  blocking collectives  37.1 us (54%)
  waiting for transfers between devices  20.4 us (30%)
  Pallas kernels  7.77 us (11%)
  starting transfers between devices  1.14 us (2%)
  between operations  0.78 us (1%)
    all_to_all x4, blocking collectives, gathered(): lax.all_to_all(parts.reshape(count, 1, edge), axis, 0, 0, axis_index_grou...  26.4 us
    ppermute x4, waiting for transfers between devices, from_behind(): return lax.ppermute(value, axis, pairs)  20.4 us
    all_to_all x1, blocking collectives, per_device(): lax.all_to_all(partial_sum.reshape(sections, group_blocks, edge), 'feat',...  10.7 us
    pallas_call x1, Pallas kernels, per_device(): pl.pallas_call(margins_kernel, out_shape=(float_of((row_blocks, edge)), f...  3.33 us
    pallas_call x4, Pallas kernels, per_device(): call(functools.partial(update_kernel, section), (float_of(group_shape if...  1.67 us
  transfers between devices with their start and end apart: 4, of which 4 were waited for; matrix products, arithmetic and copies ran while one was open for 0% of the time, Pallas kernels for 2%

profile of v13, /device:TPU:0, one launch (start us, length us, event | category | flops | bytes accessed | tf_op | source)
XLA Modules:
  0.0 67.9 jit_solution(11086057366760678617)
XLA Ops:
  0.6 0.0 copy-start.6
  0.6 0.0 copy-start
  0.7 0.0 copy-start.7
  0.7 0.0 copy-start.8
  0.7 0.0 copy-start.4
  0.7 0.0 copy-start.1
  0.7 3.3 %shard_map.86 = (f32[128,128]{1,0:T(8,128)}, f32[4,128]{1,0:T(4,128)}, s32[4,64]{1,0:T(4,128)}) custom-call(s32[1,64]{1,0:T(1,128)} %bitcast.49, s32[1,4]{1,0:T(1,128)} %targets_smem.1, s32[1,64]{1,0:T(1,128)} %bitcast.51, f32[512,128]{1,0:T(8,128)} %bitcast.38, bf16[64,128,128]{2,1,0:T(8,128)(2,1)} %bitcast.25), custom_call_target="tpu_custom_call" | custom-call | tf_op jit(solution)/shard_map/pallas_call | solution.py:312
  4.0 0.0 copy-start.3
  4.0 0.0 copy-start.5
  4.0 10.7 %all_to_all.25.parts_ref = f32[4,32,128]{2,1,0:T(8,128)S(1)} all-to-all(f32[4,32,128]{2,1,0:T(8,128)} %bitcast.54), channel_id=1, replica_groups={{2,1,3,0},{6,5,7,4},{10,9,11,8},{14,13,15,12},{18,17,19,16},{22,21,23,2..., dimensions={0} | all-to-all | bytes 131072 | tf_op jit(solution)/shard_map/all_to_all | solution.py:334
  14.7 0.0 copy-done.6
  14.7 0.0 copy-done
  14.7 0.0 copy-done.7
  14.7 0.0 copy-done.8
  14.8 0.0 copy-done.4
  14.8 0.6 shard_map.87
  15.4 7.9 %all_to_all.26 = f32[8,1,128]{2,1,0:T(1,128)S(1)} all-to-all(f32[8,1,128]{2,1,0:T(1,128)S(1)} %bitcast.48), channel_id=1, replica_groups={{4,28,12,20,0,24,8,16},{5,29,13,21,1,25,9,17},{6,30,14,22,2,26,10,18},{..., dimensions={0} | all-to-all | bytes 8192 | tf_op jit(solution)/shard_map/all_to_all | solution.py:297
  23.3 0.0 copy-done.1
  23.3 0.0 copy-done.3
  23.3 0.0 copy-done.5
  23.3 0.4 shard_map.88
  23.7 1.0 %collective-permute-start = (f32[2,32,128]{2,1,0:T(8,128)S(1)}, f32[2,32,128]{2,1,0:T(8,128)S(1)}, u32[]{:S(2)}, u32[]{:S(2)}) collective-permute-start(f32[2,32,128]{2,1,0:T(8,128)S(1)} %get-tuple-element.21), channel_id=1, source_target_pairs={{0,1},{1,2},{2,3},{3,0},{4,5},{5,6},{6,7},{7,4},{8,9},{9,10},{10,1... | collective-permute-start | bytes 98312 | tf_op jit(solution)/shard_map/ppermute | solution.py:287
  24.7 4.8 %collective-permute-done.state_ref = f32[2,32,128]{2,1,0:T(8,128)S(1)} collective-permute-done((f32[2,32,128]{2,1,0:T(8,128)S(1)}, f32[2,32,128]{2,1,0:T(8,128)S(1)}, u32[]{:S(2)}, u32[]{:S(2)}) %collective-permute-start) | collective-permute-done | bytes 32800 | tf_op jit(solution)/shard_map/ppermute | solution.py:287
  29.5 0.3 shard_map.89
  29.8 6.0 %all_to_all.27 = f32[8,1,128]{2,1,0:T(1,128)S(1)} all-to-all(f32[8,1,128]{2,1,0:T(1,128)S(1)} %bitcast.45), channel_id=1, replica_groups={{4,28,12,20,0,24,8,16},{5,29,13,21,1,25,9,17},{6,30,14,22,2,26,10,18},{..., dimensions={0} | all-to-all | bytes 8192 | tf_op jit(solution)/shard_map/all_to_all | solution.py:297
  35.8 0.4 shard_map.90
  36.2 0.1 collective-permute-start.1
  36.3 5.7 %collective-permute-done.1.state_ref = f32[2,32,128]{2,1,0:T(8,128)S(1)} collective-permute-done((f32[2,32,128]{2,1,0:T(8,128)S(1)}, f32[2,32,128]{2,1,0:T(8,128)S(1)}, u32[]{:S(2)}, u32[]{:S(2)}) %collective-permute-start.1) | collective-permute-done | bytes 32800 | tf_op jit(solution)/shard_map/ppermute | solution.py:287
  42.0 0.3 shard_map.91
  42.3 6.5 %all_to_all.28 = f32[8,1,128]{2,1,0:T(1,128)S(1)} all-to-all(f32[8,1,128]{2,1,0:T(1,128)S(1)} %bitcast.46), channel_id=1, replica_groups={{4,28,12,20,0,24,8,16},{5,29,13,21,1,25,9,17},{6,30,14,22,2,26,10,18},{..., dimensions={0} | all-to-all | bytes 8192 | tf_op jit(solution)/shard_map/all_to_all | solution.py:297
  48.8 0.4 shard_map.92
  49.2 0.0 copy-start.2
  49.2 0.1 collective-permute-start.2
  49.2 5.7 %collective-permute-done.2.state_ref = f32[2,32,128]{2,1,0:T(8,128)S(1)} collective-permute-done((f32[2,32,128]{2,1,0:T(8,128)S(1)}, f32[2,32,128]{2,1,0:T(8,128)S(1)}, u32[]{:S(2)}, u32[]{:S(2)}) %collective-permute-start.2) | collective-permute-done | bytes 32800 | tf_op jit(solution)/shard_map/ppermute | solution.py:287
  54.9 0.3 shard_map.93
  55.2 6.0 %all_to_all.29 = f32[8,1,128]{2,1,0:T(1,128)S(1)} all-to-all(f32[8,1,128]{2,1,0:T(1,128)S(1)} %bitcast.47), channel_id=1, replica_groups={{4,28,12,20,0,24,8,16},{5,29,13,21,1,25,9,17},{6,30,14,22,2,26,10,18},{..., dimensions={0} | all-to-all | bytes 8192 | tf_op jit(solution)/shard_map/all_to_all | solution.py:297
  61.3 0.4 shard_map.94
  61.7 0.1 collective-permute-start.3
  61.8 0.0 copy-done.2
  61.8 1.3 %shard_map.95 = f32[512,128]{1,0:T(8,128)} custom-call(s32[1,4]{1,0:T(1,128)S(1)} %copy-done.6, f32[512,128]{1,0:T(8,128)S(1)} %bitcast.39, f32[1,128]{1,0:T(1,128)S(1)} %get-tuple-element.20.refs_0_, f32[1,128]{1,0:T(1,128)S(1)} %get-tuple-element.22.refs_1_, f32[1,128]{1,0:T(1,128)S(1)} %get-tuple-element.24.refs_2_, f32[1,128]{1,0:T(1,128)S(1)} %get-tuple-element.26.refs_3_), custom_call_target="tpu_custom_call" | custom-call | tf_op jit(solution)/shard_map/pallas_call | solution.py:367
  63.0 4.2 %collective-permute-done.3 = f32[32,128]{1,0:T(8,128)S(1)} collective-permute-done((f32[32,128]{1,0:T(8,128)S(1)}, f32[32,128]{1,0:T(8,128)S(1)}, u32[]{:S(2)}, u32[]{:S(2)}) %collective-permute-start.3) | collective-permute-done | bytes 16416 | tf_op jit(solution)/shard_map/ppermute | solution.py:287
  67.3 0.6 copy.14
Async XLA Ops:
  0.6 14.1 %copy-start.6 = (s32[1,4]{1,0:T(1,128)S(1)}, s32[1,4]{1,0:T(1,128)}, u32[]{:S(2)}) copy-start(s32[1,4]{1,0:T(1,128)} %targets_smem.1) | copy-start | bytes 52
  0.6 14.1 %copy-start = (bf16[1,1,64,128,128]{4,3,2,1,0:T(8,128)(2,1)S(1)}, bf16[1,1,64,128,128]{4,3,2,1,0:T(8,128)(2,1)}, u32[]{:S(2)}) copy-start(bf16[1,1,64,128,128]{4,3,2,1,0:T(8,128)(2,1)} %param.11) | copy-start | bytes 6291460
  0.7 14.1 %copy-start.7 = (s32[1,1,64]{2,1,0:T(1,128)S(1)}, s32[1,1,64]{2,1,0:T(1,128)}, u32[]{:S(2)}) copy-start(s32[1,1,64]{2,1,0:T(1,128)} %param.10) | copy-start | bytes 772
  0.7 14.1 %copy-start.8 = (s32[1,1,64]{2,1,0:T(1,128)S(1)}, s32[1,1,64]{2,1,0:T(1,128)}, u32[]{:S(2)}) copy-start(s32[1,1,64]{2,1,0:T(1,128)} %param.9) | copy-start | bytes 772
  0.7 14.1 %copy-start.4 = (s32[16384]{0:T(1024)S(1)}, s32[16384]{0:T(1024)}, u32[]{:S(2)}) copy-start(s32[16384]{0:T(1024)} %param.7) | copy-start | bytes 196612
  0.7 22.6 %copy-start.1 = (f32[1,4,128,128]{3,2,1,0:T(8,128)S(1)}, f32[1,4,128,128]{3,2,1,0:T(8,128)}, u32[]{:S(2)}) copy-start(f32[1,4,128,128]{3,2,1,0:T(8,128)} %param.13) | copy-start | bytes 786436
  4.0 19.3 %copy-start.3 = (s32[4,64]{1,0:T(4,128)S(1)}, s32[4,64]{1,0:T(4,128)}, u32[]{:S(2)}) copy-start(s32[4,64]{1,0:T(4,128)} %get-tuple-element.18.lists_ref) | copy-start | bytes 3076
  4.0 19.3 %copy-start.5 = (f32[4,128]{1,0:T(4,128)S(1)}, f32[4,128]{1,0:T(4,128)}, u32[]{:S(2)}) copy-start(f32[4,128]{1,0:T(4,128)} %get-tuple-element.19.old_ref) | copy-start | bytes 6148
  23.7 5.8 %collective-permute-start = (f32[2,32,128]{2,1,0:T(8,128)S(1)}, f32[2,32,128]{2,1,0:T(8,128)S(1)}, u32[]{:S(2)}, u32[]{:S(2)}) collective-permute-start(f32[2,32,128]{2,1,0:T(8,128)S(1)} %get-tuple-element.21), channel_id=1, source_target_pairs={{0,1},{1,2},{2,3},{3,0},{4,5},{5,6},{6,7},{7,4},{8,9},{9,10},{10,1... | collective-permute-start | bytes 98312 | tf_op jit(solution)/shard_map/ppermute | solution.py:287
  36.2 5.8 %collective-permute-start.1 = (f32[2,32,128]{2,1,0:T(8,128)S(1)}, f32[2,32,128]{2,1,0:T(8,128)S(1)}, u32[]{:S(2)}, u32[]{:S(2)}) collective-permute-start(f32[2,32,128]{2,1,0:T(8,128)S(1)} %get-tuple-element.23), channel_id=1, source_target_pairs={{0,1},{1,2},{2,3},{3,0},{4,5},{5,6},{6,7},{7,4},{8,9},{9,10},{10,1... | collective-permute-start | bytes 98312 | tf_op jit(solution)/shard_map/ppermute | solution.py:287
  49.2 12.6 %copy-start.2 = (f32[65536]{0:T(1024)S(1)}, f32[65536]{0:T(1024)}, u32[]{:S(2)}) copy-start(f32[65536]{0:T(1024)} %param.8) | copy-start | bytes 786436
  49.2 5.8 %collective-permute-start.2 = (f32[2,32,128]{2,1,0:T(8,128)S(1)}, f32[2,32,128]{2,1,0:T(8,128)S(1)}, u32[]{:S(2)}, u32[]{:S(2)}) collective-permute-start(f32[2,32,128]{2,1,0:T(8,128)S(1)} %get-tuple-element.25), channel_id=1, source_target_pairs={{0,1},{1,2},{2,3},{3,0},{4,5},{5,6},{6,7},{7,4},{8,9},{9,10},{10,1... | collective-permute-start | bytes 98312 | tf_op jit(solution)/shard_map/ppermute | solution.py:287
  61.7 5.6 %collective-permute-start.3 = (f32[32,128]{1,0:T(8,128)S(1)}, f32[32,128]{1,0:T(8,128)S(1)}, u32[]{:S(2)}, u32[]{:S(2)}) collective-permute-start(f32[32,128]{1,0:T(8,128)S(1)} %get-tuple-element.27), channel_id=1, source_target_pairs={{0,1},{1,2},{2,3},{3,0},{4,5},{5,6},{6,7},{7,4},{8,9},{9,10},{10,1... | collective-permute-start | bytes 49160 | tf_op jit(solution)/shard_map/ppermute | solution.py:287

commit v14 on v13

--- a/solution.py
+++ b/solution.py
@@ -33,8 +33,8 @@
     )
 
 
-def middle_first(count):
-    return sorted(range(count), key=lambda index: (abs(index - count // 2), index))
+def last_first(count):
+    return list(range(count))[::-1]
 
 
 def tile_products(vectors_of, tiles_of, tiles):
@@ -151,7 +151,7 @@
     block_ids = lax.broadcasted_iota(jnp.int32, (row_blocks, tiles), 0)
     placing = (block_ids == rows_ref[...]).astype(jnp.float32)
     partial = placed_sum(placing, products)
-    for place, group in enumerate(middle_first(sections)):
+    for place, group in enumerate(last_first(sections)):
         partial_ref[pl.ds(place * group_blocks, group_blocks), :] = partial[
             group * group_blocks : (group + 1) * group_blocks
         ]
@@ -292,7 +292,7 @@
     order = list(range(count))
     if count % 2 == 0:
         half = count // 2
-        far_apart = [pair // 2 if pair % 2 == 0 else half - 1 - pair // 2 for pair in range(half)]
+        far_apart = [half - 1 - pair // 2 if pair % 2 == 0 else pair // 2 for pair in range(half)]
         order = [2 * chip + 1 for chip in far_apart] + [2 * chip for chip in far_apart]
     received = lax.all_to_all(
         parts.reshape(count, 1, edge), axis, 0, 0, axis_index_groups=[order]
@@ -336,7 +336,7 @@
         "feat",
         0,
         0,
-        axis_index_groups=[middle_first(sections)],
+        axis_index_groups=[last_first(sections)],
     )
     group_shape = (group_blocks, edge)
     state, grads = call(

time: 68.3 us -> 67.2 us (0.984)
  blocking collectives: 37.1 us -> 36.1 us
    all_to_all x4, blocking collectives: 26.4 us -> 25.1 us  [gathered(): lax.all_to_all(parts.reshape(count, 1, edge), axis, 0, 0, axis_index_grou...]
where the time goes in v14:
time: 67.2 us; the launch traced here: 66.8 us
  blocking collectives  36.1 us (54%)
  waiting for transfers between devices  19.9 us (30%)
  Pallas kernels  7.77 us (12%)
  starting transfers between devices  1.69 us (3%)
  between operations  0.78 us (1%)
    all_to_all x4, blocking collectives, gathered(): lax.all_to_all(parts.reshape(count, 1, edge), axis, 0, 0, axis_index_grou...  25.1 us
    ppermute x4, waiting for transfers between devices, from_behind(): return lax.ppermute(value, axis, pairs)  19.9 us
    all_to_all x1, blocking collectives, per_device(): lax.all_to_all(partial_sum.reshape(sections, group_blocks, edge), 'feat',...  11 us
    pallas_call x1, Pallas kernels, per_device(): pl.pallas_call(margins_kernel, out_shape=(float_of((row_blocks, edge)), f...  3.33 us
    ppermute x4, starting transfers between devices, from_behind(): return lax.ppermute(value, axis, pairs)  1.69 us
    pallas_call x4, Pallas kernels, per_device(): call(functools.partial(update_kernel, section), (float_of(group_shape if...  1.67 us
  transfers between devices with their start and end apart: 4, of which 4 were waited for; matrix products, arithmetic and copies ran while one was open for 0% of the time, Pallas kernels for 2%

profile of v14, /device:TPU:0, one launch (start us, length us, event | category | flops | bytes accessed | tf_op | source)
XLA Modules:
  0.0 66.8 jit_solution(16524687492548774889)
XLA Ops:
  0.6 0.0 copy-start.6
  0.6 0.0 copy-start
  0.7 0.0 copy-start.7
  0.7 0.0 copy-start.8
  0.7 0.0 copy-start.4
  0.7 0.0 copy-start.1
  0.7 3.3 %shard_map.86 = (f32[128,128]{1,0:T(8,128)}, f32[4,128]{1,0:T(4,128)}, s32[4,64]{1,0:T(4,128)}) custom-call(s32[1,64]{1,0:T(1,128)} %bitcast.49, s32[1,4]{1,0:T(1,128)} %targets_smem.1, s32[1,64]{1,0:T(1,128)} %bitcast.51, f32[512,128]{1,0:T(8,128)} %bitcast.38, bf16[64,128,128]{2,1,0:T(8,128)(2,1)} %bitcast.25), custom_call_target="tpu_custom_call" | custom-call | tf_op jit(solution)/shard_map/pallas_call | solution.py:312
  4.0 0.0 copy-start.3
  4.0 0.0 copy-start.5
  4.0 11.0 %all_to_all.25.parts_ref = f32[4,32,128]{2,1,0:T(8,128)S(1)} all-to-all(f32[4,32,128]{2,1,0:T(8,128)} %bitcast.54), channel_id=1, replica_groups={{3,2,1,0},{7,6,5,4},{11,10,9,8},{15,14,13,12},{19,18,17,16},{23,22,21,2..., dimensions={0} | all-to-all | bytes 131072 | tf_op jit(solution)/shard_map/all_to_all | solution.py:334
  15.0 0.0 copy-done.6
  15.0 0.0 copy-done
  15.0 0.0 copy-done.7
  15.0 0.0 copy-done.8
  15.0 0.0 copy-done.4
  15.1 0.6 shard_map.87
  15.7 6.6 %all_to_all.26 = f32[8,1,128]{2,1,0:T(1,128)S(1)} all-to-all(f32[8,1,128]{2,1,0:T(1,128)S(1)} %bitcast.48), channel_id=1, replica_groups={{28,4,20,12,24,0,16,8},{29,5,21,13,25,1,17,9},{30,6,22,14,26,2,18,10},{..., dimensions={0} | all-to-all | bytes 8192 | tf_op jit(solution)/shard_map/all_to_all | solution.py:297
  22.2 0.0 copy-done.1
  22.2 0.0 copy-done.3
  22.2 0.0 copy-done.5
  22.2 0.4 shard_map.88
  22.7 1.5 %collective-permute-start = (f32[2,32,128]{2,1,0:T(8,128)S(1)}, f32[2,32,128]{2,1,0:T(8,128)S(1)}, u32[]{:S(2)}, u32[]{:S(2)}) collective-permute-start(f32[2,32,128]{2,1,0:T(8,128)S(1)} %get-tuple-element.21), channel_id=1, source_target_pairs={{0,1},{1,2},{2,3},{3,0},{4,5},{5,6},{6,7},{7,4},{8,9},{9,10},{10,1... | collective-permute-start | bytes 98312 | tf_op jit(solution)/shard_map/ppermute | solution.py:287
  24.2 4.2 %collective-permute-done.state_ref = f32[2,32,128]{2,1,0:T(8,128)S(1)} collective-permute-done((f32[2,32,128]{2,1,0:T(8,128)S(1)}, f32[2,32,128]{2,1,0:T(8,128)S(1)}, u32[]{:S(2)}, u32[]{:S(2)}) %collective-permute-start) | collective-permute-done | bytes 32800 | tf_op jit(solution)/shard_map/ppermute | solution.py:287
  28.4 0.3 shard_map.89
  28.7 6.0 %all_to_all.27 = f32[8,1,128]{2,1,0:T(1,128)S(1)} all-to-all(f32[8,1,128]{2,1,0:T(1,128)S(1)} %bitcast.45), channel_id=1, replica_groups={{28,4,20,12,24,0,16,8},{29,5,21,13,25,1,17,9},{30,6,22,14,26,2,18,10},{..., dimensions={0} | all-to-all | bytes 8192 | tf_op jit(solution)/shard_map/all_to_all | solution.py:297
  34.8 0.4 shard_map.90
  35.2 0.1 collective-permute-start.1
  35.2 5.7 %collective-permute-done.1.state_ref = f32[2,32,128]{2,1,0:T(8,128)S(1)} collective-permute-done((f32[2,32,128]{2,1,0:T(8,128)S(1)}, f32[2,32,128]{2,1,0:T(8,128)S(1)}, u32[]{:S(2)}, u32[]{:S(2)}) %collective-permute-start.1) | collective-permute-done | bytes 32800 | tf_op jit(solution)/shard_map/ppermute | solution.py:287
  40.9 0.3 shard_map.91
  41.2 6.5 %all_to_all.28 = f32[8,1,128]{2,1,0:T(1,128)S(1)} all-to-all(f32[8,1,128]{2,1,0:T(1,128)S(1)} %bitcast.46), channel_id=1, replica_groups={{28,4,20,12,24,0,16,8},{29,5,21,13,25,1,17,9},{30,6,22,14,26,2,18,10},{..., dimensions={0} | all-to-all | bytes 8192 | tf_op jit(solution)/shard_map/all_to_all | solution.py:297
  47.7 0.4 shard_map.92
  48.1 0.0 copy-start.2
  48.1 0.1 collective-permute-start.2
  48.2 5.7 %collective-permute-done.2.state_ref = f32[2,32,128]{2,1,0:T(8,128)S(1)} collective-permute-done((f32[2,32,128]{2,1,0:T(8,128)S(1)}, f32[2,32,128]{2,1,0:T(8,128)S(1)}, u32[]{:S(2)}, u32[]{:S(2)}) %collective-permute-start.2) | collective-permute-done | bytes 32800 | tf_op jit(solution)/shard_map/ppermute | solution.py:287
  53.9 0.3 shard_map.93
  54.2 6.0 %all_to_all.29 = f32[8,1,128]{2,1,0:T(1,128)S(1)} all-to-all(f32[8,1,128]{2,1,0:T(1,128)S(1)} %bitcast.47), channel_id=1, replica_groups={{28,4,20,12,24,0,16,8},{29,5,21,13,25,1,17,9},{30,6,22,14,26,2,18,10},{..., dimensions={0} | all-to-all | bytes 8192 | tf_op jit(solution)/shard_map/all_to_all | solution.py:297
  60.2 0.4 shard_map.94
  60.6 0.1 collective-permute-start.3
  60.7 0.0 copy-done.2
  60.7 1.3 %shard_map.95 = f32[512,128]{1,0:T(8,128)} custom-call(s32[1,4]{1,0:T(1,128)S(1)} %copy-done.6, f32[512,128]{1,0:T(8,128)S(1)} %bitcast.39, f32[1,128]{1,0:T(1,128)S(1)} %get-tuple-element.20.refs_0_, f32[1,128]{1,0:T(1,128)S(1)} %get-tuple-element.22.refs_1_, f32[1,128]{1,0:T(1,128)S(1)} %get-tuple-element.24.refs_2_, f32[1,128]{1,0:T(1,128)S(1)} %get-tuple-element.26.refs_3_), custom_call_target="tpu_custom_call" | custom-call | tf_op jit(solution)/shard_map/pallas_call | solution.py:367
  62.0 4.2 %collective-permute-done.3 = f32[32,128]{1,0:T(8,128)S(1)} collective-permute-done((f32[32,128]{1,0:T(8,128)S(1)}, f32[32,128]{1,0:T(8,128)S(1)}, u32[]{:S(2)}, u32[]{:S(2)}) %collective-permute-start.3) | collective-permute-done | bytes 16416 | tf_op jit(solution)/shard_map/ppermute | solution.py:287
  66.2 0.6 copy.14
Async XLA Ops:
  0.6 14.4 %copy-start.6 = (s32[1,4]{1,0:T(1,128)S(1)}, s32[1,4]{1,0:T(1,128)}, u32[]{:S(2)}) copy-start(s32[1,4]{1,0:T(1,128)} %targets_smem.1) | copy-start | bytes 52
  0.6 14.4 %copy-start = (bf16[1,1,64,128,128]{4,3,2,1,0:T(8,128)(2,1)S(1)}, bf16[1,1,64,128,128]{4,3,2,1,0:T(8,128)(2,1)}, u32[]{:S(2)}) copy-start(bf16[1,1,64,128,128]{4,3,2,1,0:T(8,128)(2,1)} %param.11) | copy-start | bytes 6291460
  0.7 14.4 %copy-start.7 = (s32[1,1,64]{2,1,0:T(1,128)S(1)}, s32[1,1,64]{2,1,0:T(1,128)}, u32[]{:S(2)}) copy-start(s32[1,1,64]{2,1,0:T(1,128)} %param.10) | copy-start | bytes 772
  0.7 14.4 %copy-start.8 = (s32[1,1,64]{2,1,0:T(1,128)S(1)}, s32[1,1,64]{2,1,0:T(1,128)}, u32[]{:S(2)}) copy-start(s32[1,1,64]{2,1,0:T(1,128)} %param.9) | copy-start | bytes 772
  0.7 14.4 %copy-start.4 = (s32[16384]{0:T(1024)S(1)}, s32[16384]{0:T(1024)}, u32[]{:S(2)}) copy-start(s32[16384]{0:T(1024)} %param.7) | copy-start | bytes 196612
  0.7 21.6 %copy-start.1 = (f32[1,4,128,128]{3,2,1,0:T(8,128)S(1)}, f32[1,4,128,128]{3,2,1,0:T(8,128)}, u32[]{:S(2)}) copy-start(f32[1,4,128,128]{3,2,1,0:T(8,128)} %param.13) | copy-start | bytes 786436
  4.0 18.2 %copy-start.3 = (s32[4,64]{1,0:T(4,128)S(1)}, s32[4,64]{1,0:T(4,128)}, u32[]{:S(2)}) copy-start(s32[4,64]{1,0:T(4,128)} %get-tuple-element.18.lists_ref) | copy-start | bytes 3076
  4.0 18.2 %copy-start.5 = (f32[4,128]{1,0:T(4,128)S(1)}, f32[4,128]{1,0:T(4,128)}, u32[]{:S(2)}) copy-start(f32[4,128]{1,0:T(4,128)} %get-tuple-element.19.old_ref) | copy-start | bytes 6148
  22.7 5.8 %collective-permute-start = (f32[2,32,128]{2,1,0:T(8,128)S(1)}, f32[2,32,128]{2,1,0:T(8,128)S(1)}, u32[]{:S(2)}, u32[]{:S(2)}) collective-permute-start(f32[2,32,128]{2,1,0:T(8,128)S(1)} %get-tuple-element.21), channel_id=1, source_target_pairs={{0,1},{1,2},{2,3},{3,0},{4,5},{5,6},{6,7},{7,4},{8,9},{9,10},{10,1... | collective-permute-start | bytes 98312 | tf_op jit(solution)/shard_map/ppermute | solution.py:287
  35.2 5.8 %collective-permute-start.1 = (f32[2,32,128]{2,1,0:T(8,128)S(1)}, f32[2,32,128]{2,1,0:T(8,128)S(1)}, u32[]{:S(2)}, u32[]{:S(2)}) collective-permute-start(f32[2,32,128]{2,1,0:T(8,128)S(1)} %get-tuple-element.23), channel_id=1, source_target_pairs={{0,1},{1,2},{2,3},{3,0},{4,5},{5,6},{6,7},{7,4},{8,9},{9,10},{10,1... | collective-permute-start | bytes 98312 | tf_op jit(solution)/shard_map/ppermute | solution.py:287
  48.1 12.6 %copy-start.2 = (f32[65536]{0:T(1024)S(1)}, f32[65536]{0:T(1024)}, u32[]{:S(2)}) copy-start(f32[65536]{0:T(1024)} %param.8) | copy-start | bytes 786436
  48.1 5.8 %collective-permute-start.2 = (f32[2,32,128]{2,1,0:T(8,128)S(1)}, f32[2,32,128]{2,1,0:T(8,128)S(1)}, u32[]{:S(2)}, u32[]{:S(2)}) collective-permute-start(f32[2,32,128]{2,1,0:T(8,128)S(1)} %get-tuple-element.25), channel_id=1, source_target_pairs={{0,1},{1,2},{2,3},{3,0},{4,5},{5,6},{6,7},{7,4},{8,9},{9,10},{10,1... | collective-permute-start | bytes 98312 | tf_op jit(solution)/shard_map/ppermute | solution.py:287
  60.6 5.6 %collective-permute-start.3 = (f32[32,128]{1,0:T(8,128)S(1)}, f32[32,128]{1,0:T(8,128)S(1)}, u32[]{:S(2)}, u32[]{:S(2)}) collective-permute-start(f32[32,128]{1,0:T(8,128)S(1)} %get-tuple-element.27), channel_id=1, source_target_pairs={{0,1},{1,2},{2,3},{3,0},{4,5},{5,6},{6,7},{7,4},{8,9},{9,10},{10,1... | collective-permute-start | bytes 49160 | tf_op jit(solution)/shard_map/ppermute | solution.py:287

commit v15 on v13

--- a/solution.py
+++ b/solution.py
@@ -10,7 +10,7 @@
 exact_prec = lax.Precision.HIGHEST
 l1_penalty = 0.25
 chunk = 16
-copied = 16
+copied = 32
 
 VMEM = pl.BlockSpec(memory_space=pltpu.VMEM)
 SMEM = pl.BlockSpec(memory_space=pltpu.SMEM)
@@ -129,8 +129,8 @@
         old_ref[pl.ds(section, 1), :] = beta_ref[pl.ds(targets_smem[0, section], 1), :]
 
     def tiles_of(first):
-        for copy in large[first // copied : (first + chunk) // copied]:
-            copy.wait()
+        if first % copied == 0:
+            large[first // copied].wait()
         return values_ref[pl.ds(first, chunk)]
 
     products = tile_products(
@@ -292,7 +292,7 @@
     order = list(range(count))
     if count % 2 == 0:
         half = count // 2
-        far_apart = [pair // 2 if pair % 2 == 0 else half - 1 - pair // 2 for pair in range(half)]
+        far_apart = [half - 1 - pair // 2 if pair % 2 == 0 else pair // 2 for pair in range(half)]
         order = [2 * chip + 1 for chip in far_apart] + [2 * chip for chip in far_apart]
     received = lax.all_to_all(
         parts.reshape(count, 1, edge), axis, 0, 0, axis_index_groups=[order]

time: 68.3 us -> 67.1 us (0.982)
  blocking collectives: 37.1 us -> 35.8 us
    all_to_all x4, blocking collectives: 26.4 us -> 25.1 us  [gathered(): lax.all_to_all(parts.reshape(count, 1, edge), axis, 0, 0, axis_index_grou...]
where the time goes in v15:
time: 67.1 us; the launch traced here: 67 us
  blocking collectives  35.8 us (53%)
  waiting for transfers between devices  20.4 us (30%)
  Pallas kernels  8.2 us (12%)
  starting transfers between devices  1.14 us (2%)
  between operations  0.78 us (1%)
    all_to_all x4, blocking collectives, gathered(): lax.all_to_all(parts.reshape(count, 1, edge), axis, 0, 0, axis_index_grou...  25.1 us
    ppermute x4, waiting for transfers between devices, from_behind(): return lax.ppermute(value, axis, pairs)  20.4 us
    all_to_all x1, blocking collectives, per_device(): lax.all_to_all(partial_sum.reshape(sections, group_blocks, edge), 'feat',...  10.7 us
    pallas_call x1, Pallas kernels, per_device(): pl.pallas_call(margins_kernel, out_shape=(float_of((row_blocks, edge)), f...  3.15 us
    pallas_call x4, Pallas kernels, per_device(): call(functools.partial(update_kernel, section), (float_of(group_shape if...  2.04 us
  transfers between devices with their start and end apart: 4, of which 4 were waited for; matrix products, arithmetic and copies ran while one was open for 0% of the time, Pallas kernels for 2%

profile of v15, /device:TPU:0, one launch (start us, length us, event | category | flops | bytes accessed | tf_op | source)
XLA Modules:
  0.0 67.0 jit_solution(14241438242693327637)
XLA Ops:
  0.6 0.0 copy-start.6
  0.6 0.0 copy-start
  0.7 0.0 copy-start.7
  0.7 0.0 copy-start.8
  0.7 0.0 copy-start.4
  0.7 0.0 copy-start.1
  0.7 3.1 %shard_map.86 = (f32[128,128]{1,0:T(8,128)}, f32[4,128]{1,0:T(4,128)}, s32[4,64]{1,0:T(4,128)}) custom-call(s32[1,64]{1,0:T(1,128)} %bitcast.49, s32[1,4]{1,0:T(1,128)} %targets_smem.1, s32[1,64]{1,0:T(1,128)} %bitcast.51, f32[512,128]{1,0:T(8,128)} %bitcast.38, bf16[64,128,128]{2,1,0:T(8,128)(2,1)} %bitcast.25), custom_call_target="tpu_custom_call" | custom-call | tf_op jit(solution)/shard_map/pallas_call | solution.py:312
  3.8 0.0 copy-start.3
  3.9 0.0 copy-start.5
  3.9 10.7 %all_to_all.25.parts_ref = f32[4,32,128]{2,1,0:T(8,128)S(1)} all-to-all(f32[4,32,128]{2,1,0:T(8,128)} %bitcast.54), channel_id=1, replica_groups={{2,1,3,0},{6,5,7,4},{10,9,11,8},{14,13,15,12},{18,17,19,16},{22,21,23,2..., dimensions={0} | all-to-all | bytes 131072 | tf_op jit(solution)/shard_map/all_to_all | solution.py:334
  14.5 0.0 copy-done.6
  14.6 0.0 copy-done
  14.6 0.0 copy-done.7
  14.6 0.0 copy-done.8
  14.6 0.0 copy-done.4
  14.6 0.6 shard_map.87
  15.2 6.6 %all_to_all.26 = f32[8,1,128]{2,1,0:T(1,128)S(1)} all-to-all(f32[8,1,128]{2,1,0:T(1,128)S(1)} %bitcast.48), channel_id=1, replica_groups={{28,4,20,12,24,0,16,8},{29,5,21,13,25,1,17,9},{30,6,22,14,26,2,18,10},{..., dimensions={0} | all-to-all | bytes 8192 | tf_op jit(solution)/shard_map/all_to_all | solution.py:297
  21.8 0.0 copy-done.1
  21.8 0.0 copy-done.3
  21.8 0.0 copy-done.5
  21.8 0.4 shard_map.88
  22.2 1.0 %collective-permute-start = (f32[2,32,128]{2,1,0:T(8,128)S(1)}, f32[2,32,128]{2,1,0:T(8,128)S(1)}, u32[]{:S(2)}, u32[]{:S(2)}) collective-permute-start(f32[2,32,128]{2,1,0:T(8,128)S(1)} %get-tuple-element.21), channel_id=1, source_target_pairs={{0,1},{1,2},{2,3},{3,0},{4,5},{5,6},{6,7},{7,4},{8,9},{9,10},{10,1... | collective-permute-start | bytes 98312 | tf_op jit(solution)/shard_map/ppermute | solution.py:287
  23.2 4.8 %collective-permute-done.state_ref = f32[2,32,128]{2,1,0:T(8,128)S(1)} collective-permute-done((f32[2,32,128]{2,1,0:T(8,128)S(1)}, f32[2,32,128]{2,1,0:T(8,128)S(1)}, u32[]{:S(2)}, u32[]{:S(2)}) %collective-permute-start) | collective-permute-done | bytes 32800 | tf_op jit(solution)/shard_map/ppermute | solution.py:287
  28.0 0.5 shard_map.89
  28.5 6.0 %all_to_all.27 = f32[8,1,128]{2,1,0:T(1,128)S(1)} all-to-all(f32[8,1,128]{2,1,0:T(1,128)S(1)} %bitcast.45), channel_id=1, replica_groups={{28,4,20,12,24,0,16,8},{29,5,21,13,25,1,17,9},{30,6,22,14,26,2,18,10},{..., dimensions={0} | all-to-all | bytes 8192 | tf_op jit(solution)/shard_map/all_to_all | solution.py:297
  34.5 0.8 %shard_map.90 = (f32[2,32,128]{2,1,0:T(8,128)S(1)}, f32[1,128]{1,0:T(1,128)S(1)}) custom-call(f32[8,128]{1,0:T(8,128)S(1)} %bitcast.43, f32[2,32,128]{2,1,0:T(8,128)S(1)} %collective-permute-done.state_ref, s32[4,64]{1,0:T(4,128)S(1)} %copy-done.3, f32[4,128]{1,0:T(4,128)S(1)} %copy-done.5, f32[4,128,128]{2,1,0:T(8,128)S(1)} %bitcast.35, ...), custom_call_target="tpu_custom_call" | custom-call | tf_op jit(solution)/shard_map/pallas_call | solution.py:352
  35.3 0.1 collective-permute-start.1
  35.4 5.7 %collective-permute-done.1.state_ref = f32[2,32,128]{2,1,0:T(8,128)S(1)} collective-permute-done((f32[2,32,128]{2,1,0:T(8,128)S(1)}, f32[2,32,128]{2,1,0:T(8,128)S(1)}, u32[]{:S(2)}, u32[]{:S(2)}) %collective-permute-start.1) | collective-permute-done | bytes 32800 | tf_op jit(solution)/shard_map/ppermute | solution.py:287
  41.1 0.3 shard_map.91
  41.4 6.1 %all_to_all.28 = f32[8,1,128]{2,1,0:T(1,128)S(1)} all-to-all(f32[8,1,128]{2,1,0:T(1,128)S(1)} %bitcast.46), channel_id=1, replica_groups={{28,4,20,12,24,0,16,8},{29,5,21,13,25,1,17,9},{30,6,22,14,26,2,18,10},{..., dimensions={0} | all-to-all | bytes 8192 | tf_op jit(solution)/shard_map/all_to_all | solution.py:297
  47.5 0.4 shard_map.92
  47.9 0.0 copy-start.2
  47.9 0.1 collective-permute-start.2
  48.0 5.7 %collective-permute-done.2.state_ref = f32[2,32,128]{2,1,0:T(8,128)S(1)} collective-permute-done((f32[2,32,128]{2,1,0:T(8,128)S(1)}, f32[2,32,128]{2,1,0:T(8,128)S(1)}, u32[]{:S(2)}, u32[]{:S(2)}) %collective-permute-start.2) | collective-permute-done | bytes 32800 | tf_op jit(solution)/shard_map/ppermute | solution.py:287
  53.7 0.3 shard_map.93
  54.0 6.4 %all_to_all.29 = f32[8,1,128]{2,1,0:T(1,128)S(1)} all-to-all(f32[8,1,128]{2,1,0:T(1,128)S(1)} %bitcast.47), channel_id=1, replica_groups={{28,4,20,12,24,0,16,8},{29,5,21,13,25,1,17,9},{30,6,22,14,26,2,18,10},{..., dimensions={0} | all-to-all | bytes 8192 | tf_op jit(solution)/shard_map/all_to_all | solution.py:297
  60.4 0.4 shard_map.94
  60.8 0.1 collective-permute-start.3
  60.8 0.0 copy-done.2
  60.9 1.3 %shard_map.95 = f32[512,128]{1,0:T(8,128)} custom-call(s32[1,4]{1,0:T(1,128)S(1)} %copy-done.6, f32[512,128]{1,0:T(8,128)S(1)} %bitcast.39, f32[1,128]{1,0:T(1,128)S(1)} %get-tuple-element.20.refs_0_, f32[1,128]{1,0:T(1,128)S(1)} %get-tuple-element.22.refs_1_, f32[1,128]{1,0:T(1,128)S(1)} %get-tuple-element.24.refs_2_, f32[1,128]{1,0:T(1,128)S(1)} %get-tuple-element.26.refs_3_), custom_call_target="tpu_custom_call" | custom-call | tf_op jit(solution)/shard_map/pallas_call | solution.py:367
  62.1 4.2 %collective-permute-done.3 = f32[32,128]{1,0:T(8,128)S(1)} collective-permute-done((f32[32,128]{1,0:T(8,128)S(1)}, f32[32,128]{1,0:T(8,128)S(1)}, u32[]{:S(2)}, u32[]{:S(2)}) %collective-permute-start.3) | collective-permute-done | bytes 16416 | tf_op jit(solution)/shard_map/ppermute | solution.py:287
  66.4 0.6 copy.14
Async XLA Ops:
  0.6 13.9 %copy-start.6 = (s32[1,4]{1,0:T(1,128)S(1)}, s32[1,4]{1,0:T(1,128)}, u32[]{:S(2)}) copy-start(s32[1,4]{1,0:T(1,128)} %targets_smem.1) | copy-start | bytes 52
  0.6 13.9 %copy-start = (bf16[1,1,64,128,128]{4,3,2,1,0:T(8,128)(2,1)S(1)}, bf16[1,1,64,128,128]{4,3,2,1,0:T(8,128)(2,1)}, u32[]{:S(2)}) copy-start(bf16[1,1,64,128,128]{4,3,2,1,0:T(8,128)(2,1)} %param.11) | copy-start | bytes 6291460
  0.7 13.9 %copy-start.7 = (s32[1,1,64]{2,1,0:T(1,128)S(1)}, s32[1,1,64]{2,1,0:T(1,128)}, u32[]{:S(2)}) copy-start(s32[1,1,64]{2,1,0:T(1,128)} %param.10) | copy-start | bytes 772
  0.7 13.9 %copy-start.8 = (s32[1,1,64]{2,1,0:T(1,128)S(1)}, s32[1,1,64]{2,1,0:T(1,128)}, u32[]{:S(2)}) copy-start(s32[1,1,64]{2,1,0:T(1,128)} %param.9) | copy-start | bytes 772
  0.7 13.9 %copy-start.4 = (s32[16384]{0:T(1024)S(1)}, s32[16384]{0:T(1024)}, u32[]{:S(2)}) copy-start(s32[16384]{0:T(1024)} %param.7) | copy-start | bytes 196612
  0.7 21.1 %copy-start.1 = (f32[1,4,128,128]{3,2,1,0:T(8,128)S(1)}, f32[1,4,128,128]{3,2,1,0:T(8,128)}, u32[]{:S(2)}) copy-start(f32[1,4,128,128]{3,2,1,0:T(8,128)} %param.13) | copy-start | bytes 786436
  3.8 17.9 %copy-start.3 = (s32[4,64]{1,0:T(4,128)S(1)}, s32[4,64]{1,0:T(4,128)}, u32[]{:S(2)}) copy-start(s32[4,64]{1,0:T(4,128)} %get-tuple-element.18.lists_ref) | copy-start | bytes 3076
  3.9 17.9 %copy-start.5 = (f32[4,128]{1,0:T(4,128)S(1)}, f32[4,128]{1,0:T(4,128)}, u32[]{:S(2)}) copy-start(f32[4,128]{1,0:T(4,128)} %get-tuple-element.19.old_ref) | copy-start | bytes 6148
  22.2 5.8 %collective-permute-start = (f32[2,32,128]{2,1,0:T(8,128)S(1)}, f32[2,32,128]{2,1,0:T(8,128)S(1)}, u32[]{:S(2)}, u32[]{:S(2)}) collective-permute-start(f32[2,32,128]{2,1,0:T(8,128)S(1)} %get-tuple-element.21), channel_id=1, source_target_pairs={{0,1},{1,2},{2,3},{3,0},{4,5},{5,6},{6,7},{7,4},{8,9},{9,10},{10,1... | collective-permute-start | bytes 98312 | tf_op jit(solution)/shard_map/ppermute | solution.py:287
  35.3 5.8 %collective-permute-start.1 = (f32[2,32,128]{2,1,0:T(8,128)S(1)}, f32[2,32,128]{2,1,0:T(8,128)S(1)}, u32[]{:S(2)}, u32[]{:S(2)}) collective-permute-start(f32[2,32,128]{2,1,0:T(8,128)S(1)} %get-tuple-element.23), channel_id=1, source_target_pairs={{0,1},{1,2},{2,3},{3,0},{4,5},{5,6},{6,7},{7,4},{8,9},{9,10},{10,1... | collective-permute-start | bytes 98312 | tf_op jit(solution)/shard_map/ppermute | solution.py:287
  47.9 13.0 %copy-start.2 = (f32[65536]{0:T(1024)S(1)}, f32[65536]{0:T(1024)}, u32[]{:S(2)}) copy-start(f32[65536]{0:T(1024)} %param.8) | copy-start | bytes 786436
  47.9 5.8 %collective-permute-start.2 = (f32[2,32,128]{2,1,0:T(8,128)S(1)}, f32[2,32,128]{2,1,0:T(8,128)S(1)}, u32[]{:S(2)}, u32[]{:S(2)}) collective-permute-start(f32[2,32,128]{2,1,0:T(8,128)S(1)} %get-tuple-element.25), channel_id=1, source_target_pairs={{0,1},{1,2},{2,3},{3,0},{4,5},{5,6},{6,7},{7,4},{8,9},{9,10},{10,1... | collective-permute-start | bytes 98312 | tf_op jit(solution)/shard_map/ppermute | solution.py:287
  60.8 5.6 %collective-permute-start.3 = (f32[32,128]{1,0:T(8,128)S(1)}, f32[32,128]{1,0:T(8,128)S(1)}, u32[]{:S(2)}, u32[]{:S(2)}) collective-permute-start(f32[32,128]{1,0:T(8,128)S(1)} %get-tuple-element.27), channel_id=1, source_target_pairs={{0,1},{1,2},{2,3},{3,0},{4,5},{5,6},{6,7},{7,4},{8,9},{9,10},{10,1... | collective-permute-start | bytes 49160 | tf_op jit(solution)/shard_map/ppermute | solution.py:287

commit v16 on v15

--- a/solution.py
+++ b/solution.py
@@ -196,7 +196,8 @@
 
 
 def first_kernel(
-    parts_ref, labels_ref, rows_ref, cols_ref, targets_ref, values_ref, state_ref, grad_ref
+    parts_ref, labels_ref, rows_ref, cols_ref, targets_ref, values_ref,
+    residual_ref, weight_ref, grad_ref,
 ):
     group_blocks = parts_ref.shape[1]
     first_row = lax.axis_index("feat") * group_blocks
@@ -209,15 +210,17 @@
     probability = 1.0 / (1.0 + jnp.exp(-margins))
     labels = labels_ref[pl.ds(pl.multiple_of(first_row, 8), group_blocks), :]
     residual = labels.astype(jnp.float32) - probability
-    state_ref[0] = residual
-    state_ref[1] = probability * (1.0 - probability)
+    residual_ref[...] = residual
+    weight_ref[...] = probability * (1.0 - probability)
     grad = gradient_of_all(residual, chosen, values_ref)
     grad_ref[...] = jnp.broadcast_to(grad, grad_ref.shape)
 
 
-def gradient_kernel(section, state_ref, lists_ref, values_ref, grad_ref, rows_ref, total_ref):
-    _, group_blocks, edge = state_ref.shape
-    rows_ref[pl.ds(0, group_blocks), :] = state_ref[0]
+def gradient_kernel(
+    section, residual_ref, lists_ref, values_ref, grad_ref, rows_ref, total_ref
+):
+    group_blocks, edge = residual_ref.shape
+    rows_ref[pl.ds(0, group_blocks), :] = residual_ref[...]
     rows_ref[pl.ds(group_blocks, 8), :] = jnp.zeros((8, edge), jnp.float32)
 
     def run(part):
@@ -235,11 +238,15 @@
     grad_ref[...] = jnp.broadcast_to(total_ref[0:1, :], grad_ref.shape)
 
 
+def joined_kernel(grads_ref, weight_ref, joined_ref):
+    joined_ref[...] = grads_ref[...]
+
+
 def update_kernel(
-    section, grads_ref, state_ref, lists_ref, old_ref, inverses_ref, values_ref,
+    section, grads_ref, residual_ref, weight_ref, lists_ref, old_ref, inverses_ref, values_ref,
     moved_ref, shrunk_ref, landed_ref,
 ):
-    _, group_blocks, edge = state_ref.shape
+    group_blocks, edge = residual_ref.shape
     gradient = jnp.sum(grads_ref[...], axis=0, keepdims=True)
     step = jnp.sum(inverses_ref[section] * gradient, axis=1, keepdims=True)
     square = (edge, edge)
@@ -265,13 +272,8 @@
             landed_ref[pl.ds(place, 1), :] = landed_ref[pl.ds(place, 1), :] + image
 
     for_parts(section, group_blocks, lists_ref, run)
-    weight = state_ref[1]
-    residual = state_ref[0] - weight * landed_ref[pl.ds(0, group_blocks), :]
-    if len(moved_ref.shape) == 3:
-        moved_ref[0] = residual
-        moved_ref[1] = weight
-    else:
-        moved_ref[...] = residual
+    landed = landed_ref[pl.ds(0, group_blocks), :]
+    moved_ref[...] = residual_ref[...] - weight_ref[...] * landed
 
 
 def blocks_kernel(sections, targets_smem, beta_ref, *refs):
@@ -339,9 +341,9 @@
         axis_index_groups=[middle_first(sections)],
     )
     group_shape = (group_blocks, edge)
-    state, grads = call(
+    residual, weight, grads = call(
         first_kernel,
-        (float_of((2, *group_shape)), float_of((samp_count, edge))),
+        (float_of(group_shape), float_of(group_shape), float_of((samp_count, edge))),
         [VMEM] * 6,
         [],
     )(parts, labels.reshape(row_blocks, edge), tile_rows[0], tile_cols[0], block_order, values)
@@ -349,28 +351,33 @@
     shrunk_blocks = []
     for section in range(sections):
         final = section + 1 == sections
+        sums = gathered(grads, "samp")
         moving, shrunk = call(
             functools.partial(update_kernel, section),
-            (float_of(group_shape if final else (2, *group_shape)), float_of((1, edge))),
-            [VMEM] * 6,
+            (float_of(group_shape), float_of((1, edge))),
+            [VMEM] * 7,
             [padded],
-        )(gathered(grads, "samp"), state, lists, old_blocks, inverses, values)
+        )(sums, residual, weight, lists, old_blocks, inverses, values)
         shrunk_blocks.append(shrunk)
-        state = from_behind(moving, "feat", 1)
+        residual = from_behind(moving, "feat", 1)
         if not final:
+            weight = from_behind(weight, "feat", 1)
             grads = call(
                 functools.partial(gradient_kernel, section + 1),
                 float_of((samp_count, edge)),
                 [VMEM] * 3,
                 [padded, pltpu.VMEM((chunk, edge), jnp.float32)],
-            )(state, lists, values)
+            )(residual, lists, values)
+            grads = call(joined_kernel, float_of((samp_count, edge)), [VMEM] * 2, [])(
+                grads, weight
+            )
     blocks = call(
         functools.partial(blocks_kernel, sections),
         float_of(blocks.shape),
         [SMEM] + [VMEM] * (1 + sections),
         [],
     )(block_order, blocks, *shrunk_blocks)
-    return (blocks.reshape(-1), state.reshape(-1))
+    return (blocks.reshape(-1), residual.reshape(-1))
 
 
 def solution(mesh):

time: 67.1 us -> 66.9 us (level)
  starting transfers between devices: 1.14 us -> 3.72 us
  waiting for transfers between devices: 20.4 us -> 18 us
    ppermute x4 -> x7, starting transfers between devices: 1.14 us -> 3.72 us  [from_behind(): return lax.ppermute(value, axis, pairs)]
    ppermute x4 -> x7, waiting for transfers between devices: 20.4 us -> 18 us  [from_behind(): return lax.ppermute(value, axis, pairs)]
    pallas_call x5 -> x8, Pallas kernels: 2.66 us -> 2.29 us  [the longest x4 1.66 us: per_device(): call(functools.partial(update_kernel, section), (float_of(group_shape), f...]
  transfers between devices with their start and end apart: 4 -> 7, of which waited for: 4 -> 5; matrix products, arithmetic and copies ran while one was open for 0% -> 0% of each run, Pallas kernels for 2% -> 3%
where the time goes in v16:
time: 66.9 us; the launch traced here: 66.5 us
  blocking collectives  35.8 us (54%)
  waiting for transfers between devices  18 us (27%)
  Pallas kernels  7.59 us (11%)
  starting transfers between devices  3.72 us (6%)
  between operations  0.79 us (1%)
    all_to_all x4, blocking collectives, gathered(): lax.all_to_all(parts.reshape(count, 1, edge), axis, 0, 0, axis_index_grou...  25.1 us
    ppermute x7, waiting for transfers between devices, from_behind(): return lax.ppermute(value, axis, pairs)  18 us
    all_to_all x1, blocking collectives, per_device(): lax.all_to_all(partial_sum.reshape(sections, group_blocks, edge), 'feat',...  10.7 us
    ppermute x7, starting transfers between devices, from_behind(): return lax.ppermute(value, axis, pairs)  3.72 us
    pallas_call x1, Pallas kernels, per_device(): pl.pallas_call(margins_kernel, out_shape=(float_of((row_blocks, edge)), f...  3.15 us
    pallas_call x4, Pallas kernels, per_device(): call(functools.partial(update_kernel, section), (float_of(group_shape), f...  1.66 us
  transfers between devices with their start and end apart: 7, of which 5 were waited for; matrix products, arithmetic and copies ran while one was open for 0% of the time, Pallas kernels for 3%

profile of v16, /device:TPU:0, one launch (start us, length us, event | category | flops | bytes accessed | tf_op | source)
XLA Modules:
  0.0 66.5 jit_solution(3214609260457820876)
XLA Ops:
  0.6 0.0 copy-start.6
  0.6 0.0 copy-start
  0.7 0.0 copy-start.7
  0.7 0.0 copy-start.8
  0.7 0.0 copy-start.4
  0.7 0.0 copy-start.1
  0.7 3.1 %shard_map.86 = (f32[128,128]{1,0:T(8,128)}, f32[4,128]{1,0:T(4,128)}, s32[4,64]{1,0:T(4,128)}) custom-call(s32[1,64]{1,0:T(1,128)} %bitcast.49, s32[1,4]{1,0:T(1,128)} %targets_smem.1, s32[1,64]{1,0:T(1,128)} %bitcast.51, f32[512,128]{1,0:T(8,128)} %bitcast.38, bf16[64,128,128]{2,1,0:T(8,128)(2,1)} %bitcast.25), custom_call_target="tpu_custom_call" | custom-call | tf_op jit(solution)/shard_map/pallas_call | solution.py:314
  3.8 0.0 copy-start.3
  3.9 0.0 copy-start.5
  3.9 10.7 %all_to_all.25.parts_ref = f32[4,32,128]{2,1,0:T(8,128)S(1)} all-to-all(f32[4,32,128]{2,1,0:T(8,128)} %bitcast.54), channel_id=1, replica_groups={{2,1,3,0},{6,5,7,4},{10,9,11,8},{14,13,15,12},{18,17,19,16},{22,21,23,2..., dimensions={0} | all-to-all | bytes 131072 | tf_op jit(solution)/shard_map/all_to_all | solution.py:336
  14.5 0.0 copy-done.6
  14.6 0.0 copy-done
  14.6 0.0 copy-done.7
  14.6 0.0 copy-done.8
  14.6 0.0 copy-done.4
  14.6 0.6 shard_map.87
  15.2 6.6 %all_to_all.26 = f32[8,1,128]{2,1,0:T(1,128)S(1)} all-to-all(f32[8,1,128]{2,1,0:T(1,128)S(1)} %bitcast.48), channel_id=1, replica_groups={{28,4,20,12,24,0,16,8},{29,5,21,13,25,1,17,9},{30,6,22,14,26,2,18,10},{..., dimensions={0} | all-to-all | bytes 8192 | tf_op jit(solution)/shard_map/all_to_all | solution.py:299
  21.8 0.0 copy-done.1
  21.8 0.0 copy-done.3
  21.8 0.0 copy-done.5
  21.8 0.4 shard_map.88
  22.2 1.0 %collective-permute-start = (f32[32,128]{1,0:T(8,128)S(1)}, f32[32,128]{1,0:T(8,128)S(1)}, u32[]{:S(2)}, u32[]{:S(2)}) collective-permute-start(f32[32,128]{1,0:T(8,128)S(1)} %get-tuple-element.23), channel_id=1, source_target_pairs={{0,1},{1,2},{2,3},{3,0},{4,5},{5,6},{6,7},{7,4},{8,9},{9,10},{10,1... | collective-permute-start | bytes 49160 | tf_op jit(solution)/shard_map/ppermute | solution.py:289
  23.2 1.1 %collective-permute-start.1 = (f32[32,128]{1,0:T(8,128)S(1)}, f32[32,128]{1,0:T(8,128)S(1)}, u32[]{:S(2)}, u32[]{:S(2)}) collective-permute-start(f32[32,128]{1,0:T(8,128)S(1)} %get-tuple-element.19.weight_ref), channel_id=1, source_target_pairs={{0,1},{1,2},{2,3},{3,0},{4,5},{5,6},{6,7},{7,4},{8,9},{9,10},{10,1... | collective-permute-start | bytes 49160 | tf_op jit(solution)/shard_map/ppermute | solution.py:289
  24.3 3.5 %collective-permute-done.residual_ref = f32[32,128]{1,0:T(8,128)S(1)} collective-permute-done((f32[32,128]{1,0:T(8,128)S(1)}, f32[32,128]{1,0:T(8,128)S(1)}, u32[]{:S(2)}, u32[]{:S(2)}) %collective-permute-start) | collective-permute-done | bytes 16416 | tf_op jit(solution)/shard_map/ppermute | solution.py:289
  27.8 0.3 shard_map.89.grads_ref
  28.1 0.6 collective-permute-done.1.weight_ref
  28.7 6.0 %all_to_all.27 = f32[8,1,128]{2,1,0:T(1,128)S(1)} all-to-all(f32[8,1,128]{2,1,0:T(1,128)S(1)} %bitcast.45), channel_id=1, replica_groups={{28,4,20,12,24,0,16,8},{29,5,21,13,25,1,17,9},{30,6,22,14,26,2,18,10},{..., dimensions={0} | all-to-all | bytes 8192 | tf_op jit(solution)/shard_map/all_to_all | solution.py:299
  34.7 0.4 shard_map.91
  35.1 0.1 collective-permute-start.2
  35.2 0.9 %collective-permute-start.3 = (f32[32,128]{1,0:T(8,128)S(1)}, f32[32,128]{1,0:T(8,128)S(1)}, u32[]{:S(2)}, u32[]{:S(2)}) collective-permute-start(f32[32,128]{1,0:T(8,128)S(1)} %collective-permute-done.1.weight_ref), channel_id=1, source_target_pairs={{0,1},{1,2},{2,3},{3,0},{4,5},{5,6},{6,7},{7,4},{8,9},{9,10},{10,1... | collective-permute-start | bytes 49160 | tf_op jit(solution)/shard_map/ppermute | solution.py:289
  36.2 4.6 %collective-permute-done.2.residual_ref = f32[32,128]{1,0:T(8,128)S(1)} collective-permute-done((f32[32,128]{1,0:T(8,128)S(1)}, f32[32,128]{1,0:T(8,128)S(1)}, u32[]{:S(2)}, u32[]{:S(2)}) %collective-permute-start.2) | collective-permute-done | bytes 16416 | tf_op jit(solution)/shard_map/ppermute | solution.py:289
  40.7 0.3 shard_map.92.grads_ref
  41.0 0.0 collective-permute-done.3.weight_ref
  41.0 6.5 %all_to_all.28 = f32[8,1,128]{2,1,0:T(1,128)S(1)} all-to-all(f32[8,1,128]{2,1,0:T(1,128)S(1)} %bitcast.46), channel_id=1, replica_groups={{28,4,20,12,24,0,16,8},{29,5,21,13,25,1,17,9},{30,6,22,14,26,2,18,10},{..., dimensions={0} | all-to-all | bytes 8192 | tf_op jit(solution)/shard_map/all_to_all | solution.py:299
  47.5 0.4 shard_map.94
  47.9 0.0 copy-start.2
  47.9 0.1 collective-permute-start.4
  48.0 0.5 collective-permute-start.5
  48.5 5.0 %collective-permute-done.4.residual_ref = f32[32,128]{1,0:T(8,128)S(1)} collective-permute-done((f32[32,128]{1,0:T(8,128)S(1)}, f32[32,128]{1,0:T(8,128)S(1)}, u32[]{:S(2)}, u32[]{:S(2)}) %collective-permute-start.4) | collective-permute-done | bytes 16416 | tf_op jit(solution)/shard_map/ppermute | solution.py:289
  53.5 0.3 shard_map.95.grads_ref
  53.8 0.0 collective-permute-done.5.weight_ref
  53.8 6.1 %all_to_all.29 = f32[8,1,128]{2,1,0:T(1,128)S(1)} all-to-all(f32[8,1,128]{2,1,0:T(1,128)S(1)} %bitcast.47), channel_id=1, replica_groups={{28,4,20,12,24,0,16,8},{29,5,21,13,25,1,17,9},{30,6,22,14,26,2,18,10},{..., dimensions={0} | all-to-all | bytes 8192 | tf_op jit(solution)/shard_map/all_to_all | solution.py:299
  59.9 0.4 shard_map.97
  60.3 0.1 collective-permute-start.6
  60.4 0.0 copy-done.2
  60.4 1.3 %shard_map.98 = f32[512,128]{1,0:T(8,128)} custom-call(s32[1,4]{1,0:T(1,128)S(1)} %copy-done.6, f32[512,128]{1,0:T(8,128)S(1)} %bitcast.39, f32[1,128]{1,0:T(1,128)S(1)} %get-tuple-element.22.refs_0_, f32[1,128]{1,0:T(1,128)S(1)} %get-tuple-element.24.refs_1_, f32[1,128]{1,0:T(1,128)S(1)} %get-tuple-element.26.refs_2_, f32[1,128]{1,0:T(1,128)S(1)} %get-tuple-element.28.refs_3_), custom_call_target="tpu_custom_call" | custom-call | tf_op jit(solution)/shard_map/pallas_call | solution.py:374
  61.6 4.2 %collective-permute-done.6 = f32[32,128]{1,0:T(8,128)S(1)} collective-permute-done((f32[32,128]{1,0:T(8,128)S(1)}, f32[32,128]{1,0:T(8,128)S(1)}, u32[]{:S(2)}, u32[]{:S(2)}) %collective-permute-start.6) | collective-permute-done | bytes 16416 | tf_op jit(solution)/shard_map/ppermute | solution.py:289
  65.9 0.6 copy.14
  (3 shorter events, 0.0 us)
Async XLA Ops:
  0.6 13.9 %copy-start.6 = (s32[1,4]{1,0:T(1,128)S(1)}, s32[1,4]{1,0:T(1,128)}, u32[]{:S(2)}) copy-start(s32[1,4]{1,0:T(1,128)} %targets_smem.1) | copy-start | bytes 52
  0.6 13.9 %copy-start = (bf16[1,1,64,128,128]{4,3,2,1,0:T(8,128)(2,1)S(1)}, bf16[1,1,64,128,128]{4,3,2,1,0:T(8,128)(2,1)}, u32[]{:S(2)}) copy-start(bf16[1,1,64,128,128]{4,3,2,1,0:T(8,128)(2,1)} %param.11) | copy-start | bytes 6291460
  0.7 13.9 %copy-start.7 = (s32[1,1,64]{2,1,0:T(1,128)S(1)}, s32[1,1,64]{2,1,0:T(1,128)}, u32[]{:S(2)}) copy-start(s32[1,1,64]{2,1,0:T(1,128)} %param.10) | copy-start | bytes 772
  0.7 13.9 %copy-start.8 = (s32[1,1,64]{2,1,0:T(1,128)S(1)}, s32[1,1,64]{2,1,0:T(1,128)}, u32[]{:S(2)}) copy-start(s32[1,1,64]{2,1,0:T(1,128)} %param.9) | copy-start | bytes 772
  0.7 13.9 %copy-start.4 = (s32[16384]{0:T(1024)S(1)}, s32[16384]{0:T(1024)}, u32[]{:S(2)}) copy-start(s32[16384]{0:T(1024)} %param.7) | copy-start | bytes 196612
  0.7 21.1 %copy-start.1 = (f32[1,4,128,128]{3,2,1,0:T(8,128)S(1)}, f32[1,4,128,128]{3,2,1,0:T(8,128)}, u32[]{:S(2)}) copy-start(f32[1,4,128,128]{3,2,1,0:T(8,128)} %param.13) | copy-start | bytes 786436
  3.8 17.9 %copy-start.3 = (s32[4,64]{1,0:T(4,128)S(1)}, s32[4,64]{1,0:T(4,128)}, u32[]{:S(2)}) copy-start(s32[4,64]{1,0:T(4,128)} %get-tuple-element.20.lists_ref) | copy-start | bytes 3076
  3.9 17.9 %copy-start.5 = (f32[4,128]{1,0:T(4,128)S(1)}, f32[4,128]{1,0:T(4,128)}, u32[]{:S(2)}) copy-start(f32[4,128]{1,0:T(4,128)} %get-tuple-element.21.old_ref) | copy-start | bytes 6148
  22.2 5.6 %collective-permute-start = (f32[32,128]{1,0:T(8,128)S(1)}, f32[32,128]{1,0:T(8,128)S(1)}, u32[]{:S(2)}, u32[]{:S(2)}) collective-permute-start(f32[32,128]{1,0:T(8,128)S(1)} %get-tuple-element.23), channel_id=1, source_target_pairs={{0,1},{1,2},{2,3},{3,0},{4,5},{5,6},{6,7},{7,4},{8,9},{9,10},{10,1... | collective-permute-start | bytes 49160 | tf_op jit(solution)/shard_map/ppermute | solution.py:289
  23.2 5.5 %collective-permute-start.1 = (f32[32,128]{1,0:T(8,128)S(1)}, f32[32,128]{1,0:T(8,128)S(1)}, u32[]{:S(2)}, u32[]{:S(2)}) collective-permute-start(f32[32,128]{1,0:T(8,128)S(1)} %get-tuple-element.19.weight_ref), channel_id=1, source_target_pairs={{0,1},{1,2},{2,3},{3,0},{4,5},{5,6},{6,7},{7,4},{8,9},{9,10},{10,1... | collective-permute-start | bytes 49160 | tf_op jit(solution)/shard_map/ppermute | solution.py:289
  35.1 5.6 %collective-permute-start.2 = (f32[32,128]{1,0:T(8,128)S(1)}, f32[32,128]{1,0:T(8,128)S(1)}, u32[]{:S(2)}, u32[]{:S(2)}) collective-permute-start(f32[32,128]{1,0:T(8,128)S(1)} %get-tuple-element.25), channel_id=1, source_target_pairs={{0,1},{1,2},{2,3},{3,0},{4,5},{5,6},{6,7},{7,4},{8,9},{9,10},{10,1... | collective-permute-start | bytes 49160 | tf_op jit(solution)/shard_map/ppermute | solution.py:289
  35.2 5.8 %collective-permute-start.3 = (f32[32,128]{1,0:T(8,128)S(1)}, f32[32,128]{1,0:T(8,128)S(1)}, u32[]{:S(2)}, u32[]{:S(2)}) collective-permute-start(f32[32,128]{1,0:T(8,128)S(1)} %collective-permute-done.1.weight_ref), channel_id=1, source_target_pairs={{0,1},{1,2},{2,3},{3,0},{4,5},{5,6},{6,7},{7,4},{8,9},{9,10},{10,1... | collective-permute-start | bytes 49160 | tf_op jit(solution)/shard_map/ppermute | solution.py:289
  47.9 12.4 %copy-start.2 = (f32[65536]{0:T(1024)S(1)}, f32[65536]{0:T(1024)}, u32[]{:S(2)}) copy-start(f32[65536]{0:T(1024)} %param.8) | copy-start | bytes 786436
  47.9 5.6 %collective-permute-start.4 = (f32[32,128]{1,0:T(8,128)S(1)}, f32[32,128]{1,0:T(8,128)S(1)}, u32[]{:S(2)}, u32[]{:S(2)}) collective-permute-start(f32[32,128]{1,0:T(8,128)S(1)} %get-tuple-element.27), channel_id=1, source_target_pairs={{0,1},{1,2},{2,3},{3,0},{4,5},{5,6},{6,7},{7,4},{8,9},{9,10},{10,1... | collective-permute-start | bytes 49160 | tf_op jit(solution)/shard_map/ppermute | solution.py:289
  48.0 5.8 %collective-permute-start.5 = (f32[32,128]{1,0:T(8,128)S(1)}, f32[32,128]{1,0:T(8,128)S(1)}, u32[]{:S(2)}, u32[]{:S(2)}) collective-permute-start(f32[32,128]{1,0:T(8,128)S(1)} %collective-permute-done.3.weight_ref), channel_id=1, source_target_pairs={{0,1},{1,2},{2,3},{3,0},{4,5},{5,6},{6,7},{7,4},{8,9},{9,10},{10,1... | collective-permute-start | bytes 49160 | tf_op jit(solution)/shard_map/ppermute | solution.py:289
  60.3 5.6 %collective-permute-start.6 = (f32[32,128]{1,0:T(8,128)S(1)}, f32[32,128]{1,0:T(8,128)S(1)}, u32[]{:S(2)}, u32[]{:S(2)}) collective-permute-start(f32[32,128]{1,0:T(8,128)S(1)} %get-tuple-element.29), channel_id=1, source_target_pairs={{0,1},{1,2},{2,3},{3,0},{4,5},{5,6},{6,7},{7,4},{8,9},{9,10},{10,1... | collective-permute-start | bytes 49160 | tf_op jit(solution)/shard_map/ppermute | solution.py:289

commit v17 on v16

--- a/solution.py
+++ b/solution.py
@@ -238,6 +238,17 @@
     grad_ref[...] = jnp.broadcast_to(total_ref[0:1, :], grad_ref.shape)
 
 
+def parted_kernel(
+    section, state_ref, lists_ref, values_ref,
+    residual_ref, weight_ref, grad_ref, rows_ref, total_ref,
+):
+    residual_ref[...] = state_ref[0]
+    weight_ref[...] = state_ref[1]
+    gradient_kernel(
+        section, state_ref.at[0], lists_ref, values_ref, grad_ref, rows_ref, total_ref
+    )
+
+
 def joined_kernel(grads_ref, weight_ref, joined_ref):
     joined_ref[...] = grads_ref[...]
 
@@ -273,7 +284,12 @@
 
     for_parts(section, group_blocks, lists_ref, run)
     landed = landed_ref[pl.ds(0, group_blocks), :]
-    moved_ref[...] = residual_ref[...] - weight_ref[...] * landed
+    residual = residual_ref[...] - weight_ref[...] * landed
+    if len(moved_ref.shape) == 3:
+        moved_ref[0] = residual
+        moved_ref[1] = weight_ref[...]
+    else:
+        moved_ref[...] = residual
 
 
 def blocks_kernel(sections, targets_smem, beta_ref, *refs):
@@ -352,21 +368,30 @@
     for section in range(sections):
         final = section + 1 == sections
         sums = gathered(grads, "samp")
+        together = section == 0 and not final
         moving, shrunk = call(
             functools.partial(update_kernel, section),
-            (float_of(group_shape), float_of((1, edge))),
+            (float_of((2, *group_shape) if together else group_shape), float_of((1, edge))),
             [VMEM] * 7,
             [padded],
         )(sums, residual, weight, lists, old_blocks, inverses, values)
         shrunk_blocks.append(shrunk)
         residual = from_behind(moving, "feat", 1)
-        if not final:
+        scratch = [padded, pltpu.VMEM((chunk, edge), jnp.float32)]
+        if together:
+            residual, weight, grads = call(
+                functools.partial(parted_kernel, section + 1),
+                (float_of(group_shape), float_of(group_shape), float_of((samp_count, edge))),
+                [VMEM] * 3,
+                scratch,
+            )(residual, lists, values)
+        elif not final:
             weight = from_behind(weight, "feat", 1)
             grads = call(
                 functools.partial(gradient_kernel, section + 1),
                 float_of((samp_count, edge)),
                 [VMEM] * 3,
-                [padded, pltpu.VMEM((chunk, edge), jnp.float32)],
+                scratch,
             )(residual, lists, values)
             grads = call(joined_kernel, float_of((samp_count, edge)), [VMEM] * 2, [])(
                 grads, weight

time: 66.9 us -> 66.7 us (level)
  starting transfers between devices: 3.72 us -> 1.88 us
  waiting for transfers between devices: 18 us -> 19.4 us
    ppermute x7 -> x6, starting transfers between devices: 3.72 us -> 1.88 us  [from_behind(): return lax.ppermute(value, axis, pairs)]
    ppermute x7 -> x6, waiting for transfers between devices: 18 us -> 19.4 us  [from_behind(): return lax.ppermute(value, axis, pairs)]
    pallas_call x4 -> x5, Pallas kernels: 1.66 us -> 1.96 us  [the longest x4 1.67 us: per_device(): call(functools.partial(update_kernel, section), (float_of((2, *group_shap...]
  transfers between devices with their start and end apart: 7 -> 6, of which waited for: 5 -> 4; matrix products, arithmetic and copies ran while one was open for 0% -> 0% of each run, Pallas kernels for 3% -> 3%
where the time goes in v17:
time: 66.7 us; the launch traced here: 66.3 us
  blocking collectives  36 us (54%)
  waiting for transfers between devices  19.4 us (29%)
  Pallas kernels  7.59 us (11%)
  starting transfers between devices  1.88 us (3%)
  between operations  0.79 us (1%)
    all_to_all x4, blocking collectives, gathered(): lax.all_to_all(parts.reshape(count, 1, edge), axis, 0, 0, axis_index_grou...  25.4 us
    ppermute x6, waiting for transfers between devices, from_behind(): return lax.ppermute(value, axis, pairs)  19.4 us
    all_to_all x1, blocking collectives, per_device(): lax.all_to_all(partial_sum.reshape(sections, group_blocks, edge), 'feat',...  10.7 us
    pallas_call x1, Pallas kernels, per_device(): pl.pallas_call(margins_kernel, out_shape=(float_of((row_blocks, edge)), f...  3.15 us
    ppermute x6, starting transfers between devices, from_behind(): return lax.ppermute(value, axis, pairs)  1.88 us
    pallas_call x4, Pallas kernels, per_device(): call(functools.partial(update_kernel, section), (float_of((2, *group_shap...  1.67 us
  transfers between devices with their start and end apart: 6, of which 4 were waited for; matrix products, arithmetic and copies ran while one was open for 0% of the time, Pallas kernels for 3%

profile of v17, /device:TPU:0, one launch (start us, length us, event | category | flops | bytes accessed | tf_op | source)
XLA Modules:
  0.0 66.3 jit_solution(13795649685822774652)
XLA Ops:
  0.6 0.0 copy-start.6
  0.6 0.0 copy-start
  0.7 0.0 copy-start.7
  0.7 0.0 copy-start.8
  0.7 0.0 copy-start.4
  0.7 0.0 copy-start.1
  0.7 3.1 %shard_map.86 = (f32[128,128]{1,0:T(8,128)}, f32[4,128]{1,0:T(4,128)}, s32[4,64]{1,0:T(4,128)}) custom-call(s32[1,64]{1,0:T(1,128)} %bitcast.49, s32[1,4]{1,0:T(1,128)} %targets_smem.1, s32[1,64]{1,0:T(1,128)} %bitcast.51, f32[512,128]{1,0:T(8,128)} %bitcast.38, bf16[64,128,128]{2,1,0:T(8,128)(2,1)} %bitcast.25), custom_call_target="tpu_custom_call" | custom-call | tf_op jit(solution)/shard_map/pallas_call | solution.py:330
  3.8 0.0 copy-start.3
  3.9 0.0 copy-start.5
  3.9 10.7 %all_to_all.25.parts_ref = f32[4,32,128]{2,1,0:T(8,128)S(1)} all-to-all(f32[4,32,128]{2,1,0:T(8,128)} %bitcast.54), channel_id=1, replica_groups={{2,1,3,0},{6,5,7,4},{10,9,11,8},{14,13,15,12},{18,17,19,16},{22,21,23,2..., dimensions={0} | all-to-all | bytes 131072 | tf_op jit(solution)/shard_map/all_to_all | solution.py:352
  14.5 0.0 copy-done.6
  14.6 0.0 copy-done
  14.6 0.0 copy-done.7
  14.6 0.0 copy-done.8
  14.6 0.0 copy-done.4
  14.6 0.6 shard_map.87
  15.2 6.6 %all_to_all.26 = f32[8,1,128]{2,1,0:T(1,128)S(1)} all-to-all(f32[8,1,128]{2,1,0:T(1,128)S(1)} %bitcast.47), channel_id=1, replica_groups={{28,4,20,12,24,0,16,8},{29,5,21,13,25,1,17,9},{30,6,22,14,26,2,18,10},{..., dimensions={0} | all-to-all | bytes 8192 | tf_op jit(solution)/shard_map/all_to_all | solution.py:315
  21.8 0.0 copy-done.1
  21.8 0.0 copy-done.3
  21.8 0.0 copy-done.5
  21.8 0.4 shard_map.88
  22.2 1.0 %collective-permute-start = (f32[2,32,128]{2,1,0:T(8,128)S(1)}, f32[2,32,128]{2,1,0:T(8,128)S(1)}, u32[]{:S(2)}, u32[]{:S(2)}) collective-permute-start(f32[2,32,128]{2,1,0:T(8,128)S(1)} %get-tuple-element.26), channel_id=1, source_target_pairs={{0,1},{1,2},{2,3},{3,0},{4,5},{5,6},{6,7},{7,4},{8,9},{9,10},{10,1... | collective-permute-start | bytes 98312 | tf_op jit(solution)/shard_map/ppermute | solution.py:305
  23.2 4.8 %collective-permute-done.state_ref = f32[2,32,128]{2,1,0:T(8,128)S(1)} collective-permute-done((f32[2,32,128]{2,1,0:T(8,128)S(1)}, f32[2,32,128]{2,1,0:T(8,128)S(1)}, u32[]{:S(2)}, u32[]{:S(2)}) %collective-permute-start) | collective-permute-done | bytes 32800 | tf_op jit(solution)/shard_map/ppermute | solution.py:305
  28.0 0.3 shard_map.89
  28.3 6.0 %all_to_all.27 = f32[8,1,128]{2,1,0:T(1,128)S(1)} all-to-all(f32[8,1,128]{2,1,0:T(1,128)S(1)} %bitcast.48), channel_id=1, replica_groups={{28,4,20,12,24,0,16,8},{29,5,21,13,25,1,17,9},{30,6,22,14,26,2,18,10},{..., dimensions={0} | all-to-all | bytes 8192 | tf_op jit(solution)/shard_map/all_to_all | solution.py:315
  34.3 0.4 shard_map.90
  34.7 0.1 collective-permute-start.1
  34.8 0.2 collective-permute-start.2
  35.0 5.3 %collective-permute-done.1.residual_ref = f32[32,128]{1,0:T(8,128)S(1)} collective-permute-done((f32[32,128]{1,0:T(8,128)S(1)}, f32[32,128]{1,0:T(8,128)S(1)}, u32[]{:S(2)}, u32[]{:S(2)}) %collective-permute-start.1) | collective-permute-done | bytes 16416 | tf_op jit(solution)/shard_map/ppermute | solution.py:305
  40.3 0.3 shard_map.91.grads_ref
  40.6 0.0 collective-permute-done.2.weight_ref
  40.6 6.5 %all_to_all.28 = f32[8,1,128]{2,1,0:T(1,128)S(1)} all-to-all(f32[8,1,128]{2,1,0:T(1,128)S(1)} %bitcast.45), channel_id=1, replica_groups={{28,4,20,12,24,0,16,8},{29,5,21,13,25,1,17,9},{30,6,22,14,26,2,18,10},{..., dimensions={0} | all-to-all | bytes 8192 | tf_op jit(solution)/shard_map/all_to_all | solution.py:315
  47.1 0.4 shard_map.93
  47.5 0.0 copy-start.2
  47.5 0.1 collective-permute-start.3
  47.6 0.5 collective-permute-start.4
  48.1 5.0 %collective-permute-done.3.residual_ref = f32[32,128]{1,0:T(8,128)S(1)} collective-permute-done((f32[32,128]{1,0:T(8,128)S(1)}, f32[32,128]{1,0:T(8,128)S(1)}, u32[]{:S(2)}, u32[]{:S(2)}) %collective-permute-start.3) | collective-permute-done | bytes 16416 | tf_op jit(solution)/shard_map/ppermute | solution.py:305
  53.1 0.3 shard_map.94.grads_ref
  53.4 0.0 collective-permute-done.4.weight_ref
  53.4 6.3 %all_to_all.29 = f32[8,1,128]{2,1,0:T(1,128)S(1)} all-to-all(f32[8,1,128]{2,1,0:T(1,128)S(1)} %bitcast.46), channel_id=1, replica_groups={{28,4,20,12,24,0,16,8},{29,5,21,13,25,1,17,9},{30,6,22,14,26,2,18,10},{..., dimensions={0} | all-to-all | bytes 8192 | tf_op jit(solution)/shard_map/all_to_all | solution.py:315
  59.7 0.4 shard_map.96
  60.1 0.1 collective-permute-start.5
  60.2 0.0 copy-done.2
  60.2 1.3 %shard_map.97 = f32[512,128]{1,0:T(8,128)} custom-call(s32[1,4]{1,0:T(1,128)S(1)} %copy-done.6, f32[512,128]{1,0:T(8,128)S(1)} %bitcast.39, f32[1,128]{1,0:T(1,128)S(1)} %get-tuple-element.25.refs_0_, f32[1,128]{1,0:T(1,128)S(1)} %get-tuple-element.30.refs_1_, f32[1,128]{1,0:T(1,128)S(1)} %get-tuple-element.32.refs_2_, f32[1,128]{1,0:T(1,128)S(1)} %get-tuple-element.34.refs_3_), custom_call_target="tpu_custom_call" | custom-call | tf_op jit(solution)/shard_map/pallas_call | solution.py:399
  61.4 4.2 %collective-permute-done.5 = f32[32,128]{1,0:T(8,128)S(1)} collective-permute-done((f32[32,128]{1,0:T(8,128)S(1)}, f32[32,128]{1,0:T(8,128)S(1)}, u32[]{:S(2)}, u32[]{:S(2)}) %collective-permute-start.5) | collective-permute-done | bytes 16416 | tf_op jit(solution)/shard_map/ppermute | solution.py:305
  65.7 0.6 copy.14
  (2 shorter events, 0.0 us)
Async XLA Ops:
  0.6 13.9 %copy-start.6 = (s32[1,4]{1,0:T(1,128)S(1)}, s32[1,4]{1,0:T(1,128)}, u32[]{:S(2)}) copy-start(s32[1,4]{1,0:T(1,128)} %targets_smem.1) | copy-start | bytes 52
  0.6 13.9 %copy-start = (bf16[1,1,64,128,128]{4,3,2,1,0:T(8,128)(2,1)S(1)}, bf16[1,1,64,128,128]{4,3,2,1,0:T(8,128)(2,1)}, u32[]{:S(2)}) copy-start(bf16[1,1,64,128,128]{4,3,2,1,0:T(8,128)(2,1)} %param.11) | copy-start | bytes 6291460
  0.7 13.9 %copy-start.7 = (s32[1,1,64]{2,1,0:T(1,128)S(1)}, s32[1,1,64]{2,1,0:T(1,128)}, u32[]{:S(2)}) copy-start(s32[1,1,64]{2,1,0:T(1,128)} %param.10) | copy-start | bytes 772
  0.7 13.9 %copy-start.8 = (s32[1,1,64]{2,1,0:T(1,128)S(1)}, s32[1,1,64]{2,1,0:T(1,128)}, u32[]{:S(2)}) copy-start(s32[1,1,64]{2,1,0:T(1,128)} %param.9) | copy-start | bytes 772
  0.7 13.9 %copy-start.4 = (s32[16384]{0:T(1024)S(1)}, s32[16384]{0:T(1024)}, u32[]{:S(2)}) copy-start(s32[16384]{0:T(1024)} %param.7) | copy-start | bytes 196612
  0.7 21.1 %copy-start.1 = (f32[1,4,128,128]{3,2,1,0:T(8,128)S(1)}, f32[1,4,128,128]{3,2,1,0:T(8,128)}, u32[]{:S(2)}) copy-start(f32[1,4,128,128]{3,2,1,0:T(8,128)} %param.13) | copy-start | bytes 786436
  3.8 17.9 %copy-start.3 = (s32[4,64]{1,0:T(4,128)S(1)}, s32[4,64]{1,0:T(4,128)}, u32[]{:S(2)}) copy-start(s32[4,64]{1,0:T(4,128)} %get-tuple-element.23.lists_ref) | copy-start | bytes 3076
  3.9 17.9 %copy-start.5 = (f32[4,128]{1,0:T(4,128)S(1)}, f32[4,128]{1,0:T(4,128)}, u32[]{:S(2)}) copy-start(f32[4,128]{1,0:T(4,128)} %get-tuple-element.24.old_ref) | copy-start | bytes 6148
  22.2 5.8 %collective-permute-start = (f32[2,32,128]{2,1,0:T(8,128)S(1)}, f32[2,32,128]{2,1,0:T(8,128)S(1)}, u32[]{:S(2)}, u32[]{:S(2)}) collective-permute-start(f32[2,32,128]{2,1,0:T(8,128)S(1)} %get-tuple-element.26), channel_id=1, source_target_pairs={{0,1},{1,2},{2,3},{3,0},{4,5},{5,6},{6,7},{7,4},{8,9},{9,10},{10,1... | collective-permute-start | bytes 98312 | tf_op jit(solution)/shard_map/ppermute | solution.py:305
  34.7 5.6 %collective-permute-start.1 = (f32[32,128]{1,0:T(8,128)S(1)}, f32[32,128]{1,0:T(8,128)S(1)}, u32[]{:S(2)}, u32[]{:S(2)}) collective-permute-start(f32[32,128]{1,0:T(8,128)S(1)} %get-tuple-element.31), channel_id=1, source_target_pairs={{0,1},{1,2},{2,3},{3,0},{4,5},{5,6},{6,7},{7,4},{8,9},{9,10},{10,1... | collective-permute-start | bytes 49160 | tf_op jit(solution)/shard_map/ppermute | solution.py:305
  34.8 5.8 %collective-permute-start.2 = (f32[32,128]{1,0:T(8,128)S(1)}, f32[32,128]{1,0:T(8,128)S(1)}, u32[]{:S(2)}, u32[]{:S(2)}) collective-permute-start(f32[32,128]{1,0:T(8,128)S(1)} %get-tuple-element.29.weight_ref), channel_id=1, source_target_pairs={{0,1},{1,2},{2,3},{3,0},{4,5},{5,6},{6,7},{7,4},{8,9},{9,10},{10,1... | collective-permute-start | bytes 49160 | tf_op jit(solution)/shard_map/ppermute | solution.py:305
  47.5 12.7 %copy-start.2 = (f32[65536]{0:T(1024)S(1)}, f32[65536]{0:T(1024)}, u32[]{:S(2)}) copy-start(f32[65536]{0:T(1024)} %param.8) | copy-start | bytes 786436
  47.5 5.6 %collective-permute-start.3 = (f32[32,128]{1,0:T(8,128)S(1)}, f32[32,128]{1,0:T(8,128)S(1)}, u32[]{:S(2)}, u32[]{:S(2)}) collective-permute-start(f32[32,128]{1,0:T(8,128)S(1)} %get-tuple-element.33), channel_id=1, source_target_pairs={{0,1},{1,2},{2,3},{3,0},{4,5},{5,6},{6,7},{7,4},{8,9},{9,10},{10,1... | collective-permute-start | bytes 49160 | tf_op jit(solution)/shard_map/ppermute | solution.py:305
  47.6 5.8 %collective-permute-start.4 = (f32[32,128]{1,0:T(8,128)S(1)}, f32[32,128]{1,0:T(8,128)S(1)}, u32[]{:S(2)}, u32[]{:S(2)}) collective-permute-start(f32[32,128]{1,0:T(8,128)S(1)} %collective-permute-done.2.weight_ref), channel_id=1, source_target_pairs={{0,1},{1,2},{2,3},{3,0},{4,5},{5,6},{6,7},{7,4},{8,9},{9,10},{10,1... | collective-permute-start | bytes 49160 | tf_op jit(solution)/shard_map/ppermute | solution.py:305
  60.1 5.6 %collective-permute-start.5 = (f32[32,128]{1,0:T(8,128)S(1)}, f32[32,128]{1,0:T(8,128)S(1)}, u32[]{:S(2)}, u32[]{:S(2)}) collective-permute-start(f32[32,128]{1,0:T(8,128)S(1)} %get-tuple-element.35), channel_id=1, source_target_pairs={{0,1},{1,2},{2,3},{3,0},{4,5},{5,6},{6,7},{7,4},{8,9},{9,10},{10,1... | collective-permute-start | bytes 49160 | tf_op jit(solution)/shard_map/ppermute | solution.py:305
